TPU v7x, 32 devices: a whole 2x2x4 slice. The times are simulated.
32 devices in a mesh: dp: 4 (over x, core), inner: 8 (over z, y).
Axes of the slice: x: 2, y: 2, z: 4, core: 2. Of those that a mesh axis runs over, the one named last changes fastest.
Arguments:
- tokens: bfloat16 [4096, 4096], P(('dp', 'inner')), may hold values from -6 to 6
- key_weight: bfloat16 [4096, 512], P('inner'), may hold values from -0.09375 to 0.09375
- cotangent: bfloat16 [4096, 512], P(('dp', 'inner')), may hold values from -6 to 6
Outputs:
- key_out: bfloat16 [4096, 512], P(('dp', 'inner'))
- input_grad: bfloat16 [4096, 4096], P(('dp', 'inner'))
- weight_grad: float32 [4096, 512], P(('inner', 'dp'))
All inputs are finite; a program needn't handle non-finite values.
Results may differ from a plain program's by a relative error of at most 0.012.
Values may be sent and summed in bfloat16 or wider, within the bound.
No kernel may reach another device: no remote copies, remote signals or barrier semaphores. Data moves between devices by JAX's collectives and lax.ppermute only.
A program may use at most 64 MiB of HBM per device.

v0:
```python
import math

import jax
import jax.numpy as jnp
from jax import lax
from jax.sharding import PartitionSpec as P

HEAD_DIM = 128


epsilon = 1e-06


def per_device(tokens, key_weight, cotangent):
    tok_rows = tokens.shape[0]
    key_cols = key_weight.shape[1]
    gathered = lax.all_gather(key_weight, "inner", axis=0, tiled=True)
    raw = jnp.dot(tokens, gathered, preferred_element_type=jnp.float32)
    per_head = raw.reshape(tok_rows, -1, HEAD_DIM)
    inverse = lax.rsqrt(jnp.mean(per_head * per_head, axis=-1, keepdims=True) + epsilon)
    normed = per_head * inverse
    key_out = normed.reshape(tok_rows, key_cols).astype(jnp.bfloat16)
    upstream = cotangent.astype(jnp.float32).reshape(tok_rows, -1, HEAD_DIM)
    projected = jnp.mean(upstream * normed, axis=-1, keepdims=True)
    key_grad = (
        (inverse * (upstream - normed * projected)).reshape(tok_rows, key_cols).astype(jnp.bfloat16)
    )
    input_grad = lax.dot_general(
        key_grad, gathered, (((1,), (1,)), ((), ())), preferred_element_type=jnp.float32
    ).astype(jnp.bfloat16)
    group_size = lax.axis_size("inner")
    grad_scale = 1.0 / math.sqrt(tok_rows * lax.axis_size("dp") * group_size)
    owned_columns = lax.all_to_all(tokens, "inner", split_axis=1, concat_axis=0, tiled=True)
    group_grads = lax.all_gather(key_grad, "inner", axis=0, tiled=True)
    column_blocks = owned_columns.reshape(group_size, tok_rows, -1)
    grad_blocks = group_grads.reshape(group_size, tok_rows, key_cols)
    block_terms = (
        jnp.einsum("btw,btk->bwk", column_blocks, grad_blocks, preferred_element_type=jnp.float32)
        * grad_scale
    )
    rounded = lax.optimization_barrier(block_terms.astype(jnp.bfloat16))
    inner_total = jnp.sum(rounded.astype(jnp.float32), axis=0)
    weight_grad = lax.psum_scatter(inner_total, "dp", scatter_dimension=0, tiled=True)
    return (key_out, input_grad, weight_grad)


def solution(mesh):
    placed = (P(("dp", "inner"), None), P("inner", None), P(("dp", "inner"), None))
    return jax.shard_map(
        per_device,
        mesh=mesh,
        in_specs=placed,
        out_specs=(P(("dp", "inner"), None), P(("dp", "inner"), None), P(("inner", "dp"), None)),
        check_vma=False,
    )
```

profile of v0, /device:TPU:0, one launch (start us, length us, event | category | flops | bytes accessed | tf_op | source)
XLA Modules:
  0.0 182.8 jit_solution(2906213058440117771)
XLA Ops:
  7.2 0.0 copy-start
  7.2 0.0 copy-start.2
  7.2 0.0 all-gather.3.cloned.1.call-start
  7.2 0.7 all-gather.3.cloned.1.call-update
  7.9 1.6 copy.10
  9.5 1.3 copy.11
  10.9 7.3 %all-to-all-start = ((bf16[128,8,512]{2,0,1:T(8,128)(2,1)}), bf16[128,8,512]{2,0,1:T(8,128)(2,1)S(1)}, u32[]{:S(2)}, u32[]{:S(2)}) async-start(bf16[128,8,512]{2,0,1:T(8,128)(2,1)} %copy.11), calls=%async_computation | async-start | bytes 2097152 | tf_op jit(solution)/shard_map/all_to_all | solution.py:33
  18.1 0.0 all-gather.5.cloned.1.call-start
  18.2 0.0 copy-done.2
  18.2 0.1 reshape.39
  18.3 84.8 %all-gather.3.cloned.1.call-done = bf16[4096,512]{1,0:T(8,128)(2,1)} async-done(((bf16[512,512]{1,0:T(8,128)(2,1)}), bf16[4096,512]{1,0:T(8,128)(2,1)}) %all-gather.3.cloned.1.call-update) | async-done | bytes 4194320 | tf_op jit(solution)/shard_map/all_gather | solution.py:17
  103.1 0.0 copy-done
  103.1 2.9 %fusion.6 = f32[128,512]{1,0:T(8,128)S(1)} fusion(bf16[128,4096]{1,0:T(8,128)(2,1)S(1)} %copy-done, bf16[4096,512]{1,0:T(8,128)(2,1)} %all-gather.3.cloned.1.call-done), kind=kOutput, calls=%fused_computation.15 | convolution fusion | flops 536870912 | bytes 5505024 | tf_op jit(solution)/shard_map/dot_general | solution.py:18
  106.0 0.1 reshape.38
  106.1 0.2 multiply_reduce_fusion.1
  106.4 0.4 multiply_reduce_fusion
  106.8 0.2 mul.46
  107.0 0.2 mul.51
  107.2 0.8 fusion.4
  108.0 0.0 all-gather.5.cloned.1.call-update
  108.0 0.0 reduce-scatter.2.cloned.1.call-start
  108.0 0.0 all-to-all-done
  108.0 38.5 %all-gather.5.cloned.1.call-done = bf16[1024,512]{1,0:T(8,128)(2,1)} async-done(((bf16[128,512]{1,0:T(8,128)(2,1)}), bf16[1024,512]{1,0:T(8,128)(2,1)}) %all-gather.5.cloned.1.call-update) | async-done | bytes 1048592 | tf_op jit(solution)/shard_map/all_gather | solution.py:34
  146.6 2.5 %fusion = bf16[8,512,512]{1,2,0:T(8,128)(2,1)S(1)} fusion(bf16[8,128,512]{2,1,0:T(8,128)(2,1)} %bitcast.32, bf16[128,8,512]{2,0,1:T(8,128)(2,1)S(1)} %all-to-all-done), kind=kOutput, calls=%fused_computation.3 | convolution fusion | flops 541065216 | bytes 6291456 | tf_op jit(solution)/shard_map/btw,btk->bwk/dot_general | solution.py:38
  149.1 0.0 copy-start.1
  149.1 1.6 convert_reduce_fusion
  150.7 0.0 reduce-scatter.2.cloned.1.call-update
  150.7 0.0 copy-done.1
  150.7 4.6 %convolution_convert_fusion = bf16[128,4096]{1,0:T(8,128)(2,1)} fusion(bf16[128,512]{1,0:T(8,128)(2,1)S(1)} %copy-done.1, bf16[4096,512]{1,0:T(8,128)(2,1)} %all-gather.3.cloned.1.call-done), kind=kOutput, calls=%fused_computation.2 | convolution fusion | flops 537395200 | bytes 5373952 | tf_op jit(solution)/shard_map/dot_general | solution.py:28
  155.3 19.2 %reduce-scatter.2.cloned.1.call-done = f32[128,512]{0,1:T(8,128)} async-done(((f32[512,512]{0,1:T(8,128)}), f32[128,512]{0,1:T(8,128)}) %reduce-scatter.2.cloned.1.call-update) | async-done | bytes 262160 | tf_op jit(solution)/shard_map/reduce_scatter | solution.py:43
  174.5 1.8 copy.13
  (2 shorter events, 0.0 us)
Async XLA Ops:
  7.2 96.0 %copy-start = (bf16[128,4096]{1,0:T(8,128)(2,1)S(1)}, bf16[128,4096]{1,0:T(8,128)(2,1)}, u32[]{:S(2)}) copy-start(bf16[128,4096]{1,0:T(8,128)(2,1)} %param.3) | copy-start | bytes 3145732
  7.2 11.0 %copy-start.2 = (bf16[128,512]{1,0:T(8,128)(2,1)S(1)}, bf16[128,512]{1,0:T(8,128)(2,1)}, u32[]{:S(2)}) copy-start(bf16[128,512]{1,0:T(8,128)(2,1)} %param.5) | copy-start | bytes 393220
  7.2 95.9 %all-gather.3.cloned.1.call-start = ((), (), s32[]{:S(2)}) async-start(), calls=%async_computation.2 | async-start | bytes 4718592 | tf_op jit(solution)/shard_map/all_gather | solution.py:17
  10.9 97.2 %all-to-all-start = ((bf16[128,8,512]{2,0,1:T(8,128)(2,1)}), bf16[128,8,512]{2,0,1:T(8,128)(2,1)S(1)}, u32[]{:S(2)}, u32[]{:S(2)}) async-start(bf16[128,8,512]{2,0,1:T(8,128)(2,1)} %copy.11), calls=%async_computation | async-start | bytes 2097152 | tf_op jit(solution)/shard_map/all_to_all | solution.py:33
  18.1 128.4 %all-gather.5.cloned.1.call-start = ((), (), s32[]{:S(2)}) async-start(), calls=%async_computation.3 | async-start | bytes 1179648 | tf_op jit(solution)/shard_map/all_gather | solution.py:34
  108.0 66.5 %reduce-scatter.2.cloned.1.call-start = ((), (), s32[]{:S(2)}) async-start(), calls=%async_computation.4 | async-start | bytes 1310720 | tf_op jit(solution)/shard_map/reduce_scatter | solution.py:43
  149.1 1.6 copy-start.1
Sparse Core Ops, SparseCore 0:
  10.1 92.9 all-gather.2
  108.1 38.4 all-gather.4
  150.8 23.6 reduce-scatter.1
where the time goes:
time: 183 us
  waiting for transfers between devices  143 us (78%)
  between operations  13.9 us (8%)
  matrix products  10.1 us (6%)
  starting transfers between devices  7.4 us (4%)
  local copies, waits for them, and re-layouts  5.3 us (3%)
  other arithmetic  2.96 us (2%)
    all_gather x1, waiting for transfers between devices, per_device(): gathered = lax.all_gather(key_weight, 'inner', axis=0, tiled=True)  84.8 us
    all_gather x1, waiting for transfers between devices, per_device(): group_grads = lax.all_gather(key_grad, 'inner', axis=0, tiled=True)  38.5 us
    reduce_scatter x1, waiting for transfers between devices, per_device(): lax.psum_scatter(inner_total, 'dp', scatter_dimension=0, tiled=True)  19.2 us
    all_to_all x1, starting transfers between devices, per_device(): lax.all_to_all(tokens, 'inner', split_axis=1, concat_axis=0, tiled=True)  7.28 us
    dot_general x1, matrix products, per_device(): lax.dot_general(key_grad, gathered, (((1,), (1,)), ((), ())), preferred_e...  4.65 us
  transfers between devices with their start and end apart: 4, of which 3 were waited for; matrix products, arithmetic and copies ran while one was open for 7% of the time, Pallas kernels for 0%

commit v1 on v0

v1 whole, which is shorter than its diff:
```python
import math

import jax
import jax.numpy as jnp
from jax import lax
from jax.sharding import PartitionSpec as P

HEAD_DIM = 128


epsilon = 1e-06


def per_device(tokens, key_weight, cotangent):
    tok_rows, width = tokens.shape
    key_cols = key_weight.shape[1]
    group = lax.axis_size("inner")
    replicas = lax.axis_size("dp")
    owned_cols = width // group
    grad_scale = 1.0 / math.sqrt(tok_rows * replicas * group)

    by_owner = tokens.reshape(tok_rows, group, owned_cols).transpose(1, 0, 2)
    owned = lax.all_to_all(by_owner, "inner", split_axis=0, concat_axis=0, tiled=True)

    share = jnp.einsum("btw,wk->btk", owned, key_weight, preferred_element_type=jnp.float32)
    shares = lax.all_to_all(share.astype(jnp.bfloat16), "inner", split_axis=0, concat_axis=0, tiled=True)
    raw = jnp.sum(shares.astype(jnp.float32), axis=0)

    per_head = raw.reshape(tok_rows, -1, HEAD_DIM)
    inverse = lax.rsqrt(jnp.mean(per_head * per_head, axis=-1, keepdims=True) + epsilon)
    normed = per_head * inverse
    key_out = normed.reshape(tok_rows, key_cols).astype(jnp.bfloat16)
    upstream = cotangent.astype(jnp.float32).reshape(tok_rows, -1, HEAD_DIM)
    projected = jnp.mean(upstream * normed, axis=-1, keepdims=True)
    key_grad = (
        (inverse * (upstream - normed * projected)).reshape(tok_rows, key_cols).astype(jnp.bfloat16)
    )

    spread = jnp.broadcast_to(key_grad[None], (group, tok_rows, key_cols))
    grads = lax.all_to_all(spread, "inner", split_axis=0, concat_axis=0, tiled=True)

    block_terms = (
        jnp.einsum("btw,btk->bwk", owned, grads, preferred_element_type=jnp.float32) * grad_scale
    )
    rounded = lax.optimization_barrier(block_terms.astype(jnp.bfloat16))
    inner_total = jnp.sum(rounded.astype(jnp.float32), axis=0)
    pieces = lax.all_to_all(
        inner_total.reshape(replicas, -1, key_cols), "dp", split_axis=0, concat_axis=0, tiled=True
    )
    weight_grad = jnp.sum(pieces, axis=0)

    columns = jnp.einsum("btk,wk->btw", grads, key_weight, preferred_element_type=jnp.float32)
    back = lax.all_to_all(columns.astype(jnp.bfloat16), "inner", split_axis=0, concat_axis=0, tiled=True)
    input_grad = back.transpose(1, 0, 2).reshape(tok_rows, width)
    return (key_out, input_grad, weight_grad)


def solution(mesh):
    placed = (P(("dp", "inner"), None), P("inner", None), P(("dp", "inner"), None))
    return jax.shard_map(
        per_device,
        mesh=mesh,
        in_specs=placed,
        out_specs=(P(("dp", "inner"), None), P(("dp", "inner"), None), P(("inner", "dp"), None)),
        check_vma=False,
    )
```

time: 183 us -> 150 us (0.82)
  waiting for transfers between devices: 143 us -> 63 us
  blocking collectives: 0 us -> 62 us
  between operations: 13.9 us -> 0.76 us
  matrix products: 10.1 us -> 4.68 us
  starting transfers between devices: 7.4 us -> 10.7 us
    all_gather x2 -> x0, waiting for transfers between devices: 123 us -> none  [the longest x1 84.8 us: per_device(): gathered = lax.all_gather(key_weight, 'inner', axis=0, tiled=True)]
    all_to_all x1 -> x3, waiting for transfers between devices: 0.01 us -> 63 us  [the longest x1 25.5 us: per_device(): lax.all_to_all(share.astype(jnp.bfloat16), 'inner', split_axis=0, concat_...]
    all_to_all x0 -> x2, blocking collectives: none -> 62 us  [the longest x1 32.8 us: per_device(): lax.all_to_all(by_owner, 'inner', split_axis=0, concat_axis=0, tiled=True)]
    reduce_scatter x1 -> x0, waiting for transfers between devices: 19.2 us -> none  [per_device(): lax.psum_scatter(inner_total, 'dp', scatter_dimension=0, tiled=True)]
    dot_general x3, matrix products: 10.1 us -> 4.68 us  [the longest x1 1.71 us: per_device(): jnp.einsum('btk,wk->btw', grads, key_weight, preferred_element_type=jnp.f...]
    all_to_all x1 -> x3, starting transfers between devices: 7.28 us -> 10.7 us  [the longest x1 3.64 us: per_device(): lax.all_to_all(columns.astype(jnp.bfloat16), 'inner', split_axis=0, conca...]
    unnamed x8 -> x7, local copies, waits for them, and re-layouts: 3.42 us -> 3.84 us
  transfers between devices with their start and end apart: 4 -> 3, of which waited for: 3 -> 3; matrix products, arithmetic and copies ran while one was open for 7% -> 2% of each run, Pallas kernels for 0% -> 0%
where the time goes in v1:
time: 150 us
  waiting for transfers between devices  63 us (42%)
  blocking collectives  62 us (41%)
  starting transfers between devices  10.7 us (7%)
  local copies, waits for them, and re-layouts  6.73 us (4%)
  matrix products  4.68 us (3%)
  other arithmetic  2.15 us (1%)
    all_to_all x1, blocking collectives, per_device(): lax.all_to_all(by_owner, 'inner', split_axis=0, concat_axis=0, tiled=True)  32.8 us
    all_to_all x1, blocking collectives, per_device(): lax.all_to_all(spread, 'inner', split_axis=0, concat_axis=0, tiled=True)  29.1 us
    all_to_all x1, waiting for transfers between devices, per_device(): lax.all_to_all(share.astype(jnp.bfloat16), 'inner', split_axis=0, concat_...  25.5 us
    all_to_all x1, waiting for transfers between devices, per_device(): lax.all_to_all(columns.astype(jnp.bfloat16), 'inner', split_axis=0, conca...  24.8 us
    all_to_all x1, waiting for transfers between devices, per_device(): lax.all_to_all(inner_total.reshape(replicas, -1, key_cols), 'dp', split_a...  12.7 us
    unnamed x7, local copies, waits for them, and re-layouts  3.84 us
    all_to_all x1, starting transfers between devices, per_device(): lax.all_to_all(columns.astype(jnp.bfloat16), 'inner', split_axis=0, conca...  3.64 us
    all_to_all x1, starting transfers between devices, per_device(): lax.all_to_all(share.astype(jnp.bfloat16), 'inner', split_axis=0, concat_...  3.58 us
  transfers between devices with their start and end apart: 3, of which 3 were waited for; matrix products, arithmetic and copies ran while one was open for 2% of the time, Pallas kernels for 0%

profile of v1, /device:TPU:0, one launch (start us, length us, event | category | flops | bytes accessed | tf_op | source)
XLA Modules:
  0.0 150.0 jit_solution(15418753448525891104)
XLA Ops:
  0.6 0.0 copy-start
  0.6 1.7 %copy.17 = bf16[128,4096]{0,1:T(8,128)(2,1)S(1)} copy(bf16[128,4096]{1,0:T(8,128)(2,1)} %param.3) | data formatting | bytes 2097152 | tf_op args[0]
  2.3 0.0 copy-start.1
  2.3 0.5 copy.18
  2.9 32.8 %all_to_all.25 = bf16[8,128,512]{2,1,0:T(8,128)(2,1)S(1)} all-to-all(bf16[8,128,512]{2,1,0:T(8,128)(2,1)S(1)} %bitcast.38), channel_id=1, replica_groups=mesh['dp'=4,'inner'=8] {'inner'}, dimensions={0} | all-to-all | bytes 2097152 | tf_op jit(solution)/shard_map/all_to_all | solution.py:23
  35.7 0.0 copy-done
  35.7 1.7 %convolution_convert_fusion.1 = bf16[8,128,512]{2,1,0:T(8,128)(2,1)} fusion(bf16[8,128,512]{2,1,0:T(8,128)(2,1)S(1)} %all_to_all.25, bf16[512,512]{1,0:T(8,128)(2,1)S(1)} %copy-done), kind=kOutput, calls=%fused_computation.5 | convolution fusion | flops 537395200 | bytes 2621440 | tf_op jit(solution)/shard_map/btw,wk->btk/dot_general | solution.py:25
  37.4 3.6 %all-to-all-start.1 = ((bf16[8,128,512]{2,1,0:T(8,128)(2,1)}), bf16[8,128,512]{2,1,0:T(8,128)(2,1)S(1)}, u32[]{:S(2)}, u32[]{:S(2)}) async-start(bf16[8,128,512]{2,1,0:T(8,128)(2,1)} %convolution_convert_fusion.1), calls=%async_computation.1 | async-start | bytes 2097152 | tf_op jit(solution)/shard_map/all_to_all | solution.py:26
  41.0 0.0 copy-done.1
  41.0 0.1 reshape.42
  41.1 25.5 %all-to-all-done.1 = bf16[8,128,512]{2,1,0:T(8,128)(2,1)S(1)} async-done(((bf16[8,128,512]{2,1,0:T(8,128)(2,1)}), bf16[8,128,512]{2,1,0:T(8,128)(2,1)S(1)}, u32[]{:S(2)}, u32[]{:S(2)}) %all-to-all-start.1) | async-done | bytes 1048608 | tf_op jit(solution)/shard_map/all_to_all | solution.py:26
  66.6 0.1 convert_reduce_fusion.1
  66.7 0.1 reshape.41
  66.8 0.2 multiply_reduce_fusion.1
  67.1 0.4 multiply_reduce_fusion
  67.5 0.2 mul.51
  67.7 0.2 mul.46
  67.9 0.8 fusion.5
  68.6 0.1 broadcast_in_dim.2
  68.7 29.1 %all_to_all.26 = bf16[8,128,512]{2,1,0:T(8,128)(2,1)S(1)} all-to-all(bf16[8,128,512]{2,1,0:T(8,128)(2,1)S(1)} %broadcast_in_dim.2), channel_id=1, replica_groups=mesh['dp'=4,'inner'=8] {'inner'}, dimensions={0} | all-to-all | bytes 2097152 | tf_op jit(solution)/shard_map/all_to_all | solution.py:40
  97.8 1.3 fusion
  99.1 0.6 convert_reduce_fusion
  99.7 1.1 copy_bitcast_fusion
  100.8 3.5 %all-to-all-start.4 = ((f32[4,128,512]{1,2,0:T(8,128)}), f32[4,128,512]{1,2,0:T(8,128)S(1)}, u32[]{:S(2)}, u32[]{:S(2)}) async-start(f32[4,128,512]{1,2,0:T(8,128)} %copy_bitcast_fusion), calls=%async_computation.4 | async-start | bytes 2097152 | tf_op jit(solution)/shard_map/all_to_all | solution.py:47
  104.3 1.7 %convolution_convert_fusion = bf16[8,128,512]{2,1,0:T(8,128)(2,1)} fusion(bf16[8,128,512]{2,1,0:T(8,128)(2,1)S(1)} %all_to_all.26, bf16[512,512]{1,0:T(8,128)(2,1)S(1)} %copy-done), kind=kOutput, calls=%fused_computation.4 | convolution fusion | flops 537395200 | bytes 2621440 | tf_op jit(solution)/shard_map/btk,wk->btw/dot_general | solution.py:52
  106.0 12.7 %all-to-all-done.4 = f32[4,128,512]{1,2,0:T(8,128)S(1)} async-done(((f32[4,128,512]{1,2,0:T(8,128)}), f32[4,128,512]{1,2,0:T(8,128)S(1)}, u32[]{:S(2)}, u32[]{:S(2)}) %all-to-all-start.4) | async-done | bytes 1048608 | tf_op jit(solution)/shard_map/all_to_all | solution.py:47
  118.7 3.6 %all-to-all-start.3 = ((bf16[8,128,512]{2,1,0:T(8,128)(2,1)}), bf16[8,128,512]{2,1,0:T(8,128)(2,1)S(1)}, u32[]{:S(2)}, u32[]{:S(2)}) async-start(bf16[8,128,512]{2,1,0:T(8,128)(2,1)} %convolution_convert_fusion), calls=%async_computation.3 | async-start | bytes 2097152 | tf_op jit(solution)/shard_map/all_to_all | solution.py:53
  122.4 0.1 reduce_sum.49
  122.4 0.8 copy.24
  123.3 24.8 %all-to-all-done.3 = bf16[8,128,512]{2,1,0:T(8,128)(2,1)S(1)} async-done(((bf16[8,128,512]{2,1,0:T(8,128)(2,1)}), bf16[8,128,512]{2,1,0:T(8,128)(2,1)S(1)}, u32[]{:S(2)}, u32[]{:S(2)}) %all-to-all-start.3) | async-done | bytes 1048608 | tf_op jit(solution)/shard_map/all_to_all | solution.py:53
  148.1 0.7 copy.19
  148.7 1.3 copy.23
  (2 shorter events, 0.0 us)
Async XLA Ops:
  0.6 35.1 %copy-start = (bf16[512,512]{1,0:T(8,128)(2,1)S(1)}, bf16[512,512]{1,0:T(8,128)(2,1)}, u32[]{:S(2)}) copy-start(bf16[512,512]{1,0:T(8,128)(2,1)} %param.4) | copy-start | bytes 1572868
  2.3 38.7 %copy-start.1 = (bf16[128,512]{1,0:T(8,128)(2,1)S(1)}, bf16[128,512]{1,0:T(8,128)(2,1)}, u32[]{:S(2)}) copy-start(bf16[128,512]{1,0:T(8,128)(2,1)} %param.5) | copy-start | bytes 393220
  37.4 29.2 %all-to-all-start.1 = ((bf16[8,128,512]{2,1,0:T(8,128)(2,1)}), bf16[8,128,512]{2,1,0:T(8,128)(2,1)S(1)}, u32[]{:S(2)}, u32[]{:S(2)}) async-start(bf16[8,128,512]{2,1,0:T(8,128)(2,1)} %convolution_convert_fusion.1), calls=%async_computation.1 | async-start | bytes 2097152 | tf_op jit(solution)/shard_map/all_to_all | solution.py:26
  100.8 18.0 %all-to-all-start.4 = ((f32[4,128,512]{1,2,0:T(8,128)}), f32[4,128,512]{1,2,0:T(8,128)S(1)}, u32[]{:S(2)}, u32[]{:S(2)}) async-start(f32[4,128,512]{1,2,0:T(8,128)} %copy_bitcast_fusion), calls=%async_computation.4 | async-start | bytes 2097152 | tf_op jit(solution)/shard_map/all_to_all | solution.py:47
  118.7 29.3 %all-to-all-start.3 = ((bf16[8,128,512]{2,1,0:T(8,128)(2,1)}), bf16[8,128,512]{2,1,0:T(8,128)(2,1)S(1)}, u32[]{:S(2)}, u32[]{:S(2)}) async-start(bf16[8,128,512]{2,1,0:T(8,128)(2,1)} %convolution_convert_fusion), calls=%async_computation.3 | async-start | bytes 2097152 | tf_op jit(solution)/shard_map/all_to_all | solution.py:53

commit v2 on v0

v2 whole, which is shorter than its diff:
```python
import math

import jax
import jax.numpy as jnp
from jax import lax
from jax.sharding import Mesh, PartitionSpec as P

HEAD_DIM = 128


epsilon = 1e-06

PLANE = ("near", "pair")


def exchange(blocks, axes):
    return lax.all_to_all(blocks, axes, split_axis=0, concat_axis=0, tiled=True)


def per_device(tokens, key_weight, cotangent):
    tok_rows, width = tokens.shape
    shard_rows, key_cols = key_weight.shape
    outer, near = lax.axis_size("outer"), lax.axis_size("near")
    line, pair = lax.axis_size("line"), lax.axis_size("pair")
    plane = near * pair
    run = shard_rows // (outer * near)
    owned_cols = width // plane
    grad_scale = 1.0 / math.sqrt(tok_rows * outer * near * line * pair)

    runs = key_weight.reshape(outer, near, run * key_cols)
    mine = lax.dynamic_index_in_dim(runs, lax.axis_index("near"), axis=1, keepdims=False)
    mine = mine.reshape(outer * run, key_cols)
    weight = exchange(jnp.broadcast_to(mine[None], (line,) + mine.shape), "line")
    weight = weight.reshape(owned_cols, key_cols)

    by_owner = tokens.reshape(tok_rows, line, pair, outer, near, run)
    by_owner = by_owner.transpose(4, 2, 0, 1, 3, 5).reshape(plane, tok_rows, owned_cols)
    owned = exchange(by_owner, PLANE)

    share = jnp.einsum("btw,wk->btk", owned, weight, preferred_element_type=jnp.float32)
    shares = exchange(share.astype(jnp.bfloat16), PLANE)
    raw = jnp.sum(shares.astype(jnp.float32), axis=0)

    per_head = raw.reshape(tok_rows, -1, HEAD_DIM)
    inverse = lax.rsqrt(jnp.mean(per_head * per_head, axis=-1, keepdims=True) + epsilon)
    normed = per_head * inverse
    key_out = normed.reshape(tok_rows, key_cols).astype(jnp.bfloat16)
    upstream = cotangent.astype(jnp.float32).reshape(tok_rows, -1, HEAD_DIM)
    projected = jnp.mean(upstream * normed, axis=-1, keepdims=True)
    key_grad = (
        (inverse * (upstream - normed * projected)).reshape(tok_rows, key_cols).astype(jnp.bfloat16)
    )

    grads = exchange(jnp.broadcast_to(key_grad[None], (plane,) + key_grad.shape), PLANE)

    columns = jnp.einsum("btk,wk->btw", grads, weight, preferred_element_type=jnp.float32)
    back = exchange(columns.astype(jnp.bfloat16), PLANE)
    back = back.reshape(near, pair, tok_rows, line, outer, run)
    input_grad = back.transpose(2, 3, 1, 4, 0, 5).reshape(tok_rows, width)

    total = jnp.einsum("btw,btk->wk", owned, grads, preferred_element_type=jnp.float32) * grad_scale
    pieces = exchange(total.astype(jnp.bfloat16).reshape(line, outer * run, key_cols), "line")
    weight_grad = jnp.sum(pieces.astype(jnp.float32), axis=0)
    if outer > 1:
        weight_grad = lax.psum_scatter(weight_grad, "outer", scatter_dimension=0, tiled=True)
    return (key_out, input_grad, weight_grad)


def solution(mesh):
    replicas, group = mesh.shape["dp"], mesh.shape["inner"]
    pair = 2 if group % 2 == 0 else 1
    line = group // pair
    near = math.gcd(replicas, line)
    fine = Mesh(
        mesh.devices.reshape(replicas // near, near, line, pair), ("outer", "near", "line", "pair")
    )
    rows = P(("outer", "near", "line", "pair"), None)
    return jax.shard_map(
        per_device,
        mesh=fine,
        in_specs=(rows, P(("line", "pair"), None), rows),
        out_specs=(rows, rows, P(("line", "pair", "outer", "near"), None)),
        check_vma=False,
    )
```

time: 183 us -> 123 us (0.67)
  waiting for transfers between devices: 143 us -> 66.6 us
  blocking collectives: 0 us -> 17 us
  starting transfers between devices: 7.4 us -> 20.9 us
  between operations: 13.9 us -> 0.81 us
  local copies, waits for them, and re-layouts: 5.3 us -> 10.8 us
  matrix products: 10.1 us -> 4.97 us
  other arithmetic: 2.96 us -> 1.08 us
    all_gather x2 -> x0, waiting for transfers between devices: 123 us -> none  [the longest x1 84.8 us: per_device(): gathered = lax.all_gather(key_weight, 'inner', axis=0, tiled=True)]
    all_to_all x1 -> x5, waiting for transfers between devices: 0.01 us -> 66.6 us  [exchange(): return lax.all_to_all(blocks, axes, split_axis=0, concat_axis=0, tiled=True)]
    reduce_scatter x1 -> x0, waiting for transfers between devices: 19.2 us -> none  [per_device(): lax.psum_scatter(inner_total, 'dp', scatter_dimension=0, tiled=True)]
    all_to_all x0 -> x1, blocking collectives: none -> 17 us  [exchange(): return lax.all_to_all(blocks, axes, split_axis=0, concat_axis=0, tiled=True)]
    all_to_all x1 -> x5, starting transfers between devices: 7.28 us -> 20.9 us  [exchange(): return lax.all_to_all(blocks, axes, split_axis=0, concat_axis=0, tiled=True)]
    reshape x2 -> x8, local copies, waits for them, and re-layouts: 0.18 us -> 6.1 us  [the longest x1 1.61 us: per_device(): input_grad = back.transpose(2, 3, 1, 4, 0, 5).reshape(tok_rows, width)]
    dot_general x3, matrix products: 10.1 us -> 4.97 us  [the longest x1 1.71 us: per_device(): jnp.einsum('btk,wk->btw', grads, weight, preferred_element_type=jnp.float32)]
    unnamed x8 -> x10, local copies, waits for them, and re-layouts: 3.42 us -> 0.91 us
  transfers between devices with their start and end apart: 4 -> 5, of which waited for: 3 -> 5; matrix products, arithmetic and copies ran while one was open for 7% -> 5% of each run, Pallas kernels for 0% -> 0%
where the time goes in v2:
time: 123 us; the launch traced here: 122 us
  waiting for transfers between devices  66.6 us (54%)
  starting transfers between devices  20.9 us (17%)
  blocking collectives  17 us (14%)
  local copies, waits for them, and re-layouts  10.8 us (9%)
  matrix products  4.97 us (4%)
    all_to_all x5, waiting for transfers between devices, exchange(): return lax.all_to_all(blocks, axes, split_axis=0, concat_axis=0, tiled=True)  66.6 us
    all_to_all x5, starting transfers between devices, exchange(): return lax.all_to_all(blocks, axes, split_axis=0, concat_axis=0, tiled=True)  20.9 us
    all_to_all x1, blocking collectives, exchange(): return lax.all_to_all(blocks, axes, split_axis=0, concat_axis=0, tiled=True)  17 us
  transfers between devices with their start and end apart: 5, of which 5 were waited for; matrix products, arithmetic and copies ran while one was open for 5% of the time, Pallas kernels for 0%

profile of v2, /device:TPU:0, one launch (start us, length us, event | category | flops | bytes accessed | tf_op | source)
XLA Modules:
  0.0 122.2 jit_solution(16037732031517962063)
XLA Ops:
  0.6 1.4 %reshape.54 = bf16[1,4,65536]{2,1,0:T(4,128)(2,1)S(1)} reshape(bf16[512,512]{1,0:T(8,128)(2,1)} %param.4) | data formatting | bytes 1048576 | tf_op jit(solution)/shard_map/reshape | solution.py:30
  2.1 0.8 dynamic-slice_reduce_fusion
  2.9 0.1 copy.15
  3.1 0.9 broadcast_in_dim.7
  3.9 6.3 %all-to-all-start = ((bf16[4,128,512]{1,2,0:T(8,128)(2,1)}), bf16[4,128,512]{1,2,0:T(8,128)(2,1)S(1)}, u32[]{:S(2)}, u32[]{:S(2)}) async-start(bf16[4,128,512]{1,2,0:T(8,128)(2,1)} %broadcast_in_dim.7), calls=%async_computation | async-start | bytes 1048576 | tf_op jit(solution)/shard_map/all_to_all | solution.py:17
  10.3 0.8 reshape.56
  11.0 0.4 copy.29
  11.4 1.2 reshape.57
  12.6 12.1 %all-to-all-done = bf16[4,128,512]{1,2,0:T(8,128)(2,1)S(1)} async-done(((bf16[4,128,512]{1,2,0:T(8,128)(2,1)}), bf16[4,128,512]{1,2,0:T(8,128)(2,1)S(1)}, u32[]{:S(2)}, u32[]{:S(2)}) %all-to-all-start) | async-done | bytes 524320 | tf_op jit(solution)/shard_map/all_to_all | solution.py:17
  24.7 3.7 %all-to-all-start.1 = ((bf16[8,128,512]{2,1,0:T(8,128)(2,1)}), bf16[8,128,512]{2,1,0:T(8,128)(2,1)S(1)}, u32[]{:S(2)}, u32[]{:S(2)}) async-start(bf16[8,128,512]{2,1,0:T(8,128)(2,1)} %reshape.57), calls=%async_computation.1 | async-start | bytes 2097152 | tf_op jit(solution)/shard_map/all_to_all | solution.py:17
  28.5 0.4 copy.16
  28.9 0.2 reshape.63
  29.1 13.9 %all-to-all-done.1 = bf16[8,128,512]{2,1,0:T(8,128)(2,1)S(1)} async-done(((bf16[8,128,512]{2,1,0:T(8,128)(2,1)}), bf16[8,128,512]{2,1,0:T(8,128)(2,1)S(1)}, u32[]{:S(2)}, u32[]{:S(2)}) %all-to-all-start.1) | async-done | bytes 1048608 | tf_op jit(solution)/shard_map/all_to_all | solution.py:17
  43.0 1.7 %fusion.1 = bf16[8,128,512]{1,2,0:T(8,128)(2,1)} fusion(bf16[512,512,1]{0,1,2:T(8,128)(2,1)S(1)} %reshape.63, bf16[8,128,512]{2,1,0:T(8,128)(2,1)S(1)} %all-to-all-done.1), kind=kOutput, calls=%fused_computation.5 | convolution fusion | flops 537395200 | bytes 2621440 | tf_op jit(solution)/shard_map/btw,wk->btk/dot_general | solution.py:40
  44.7 3.7 %all-to-all-start.2 = ((bf16[8,128,512]{1,2,0:T(8,128)(2,1)}), bf16[8,128,512]{1,2,0:T(8,128)(2,1)S(1)}, u32[]{:S(2)}, u32[]{:S(2)}) async-start(bf16[8,128,512]{1,2,0:T(8,128)(2,1)} %fusion.1), calls=%async_computation.2 | async-start | bytes 2097152 | tf_op jit(solution)/shard_map/all_to_all | solution.py:17
  48.4 0.1 copy.18
  48.6 14.3 %all-to-all-done.2 = bf16[8,128,512]{1,2,0:T(8,128)(2,1)S(1)} async-done(((bf16[8,128,512]{1,2,0:T(8,128)(2,1)}), bf16[8,128,512]{1,2,0:T(8,128)(2,1)S(1)}, u32[]{:S(2)}, u32[]{:S(2)}) %all-to-all-start.2) | async-done | bytes 1048608 | tf_op jit(solution)/shard_map/all_to_all | solution.py:17
  62.9 0.1 convert_reduce_fusion
  63.2 0.1 copy.19
  63.4 17.0 %all_to_all.30 = bf16[8,128,512]{2,1,0:T(8,128)(2,1)S(1)} all-to-all(bf16[8,128,512]{2,1,0:T(8,128)(2,1)S(1)} %broadcast_in_dim.8), channel_id=1, replica_groups=mesh['outer'=1,'near'=4,'line'=4,'pair'=2] {'near','pair'}, dimensions={0} | all-to-all | bytes 2097152 | tf_op jit(solution)/shard_map/all_to_all | solution.py:17
  80.5 1.5 %fusion.2 = bf16[512,512]{0,1:T(8,128)(2,1)} fusion(bf16[8,128,512]{2,1,0:T(8,128)(2,1)S(1)} %all_to_all.30, bf16[8,128,512]{2,1,0:T(8,128)(2,1)S(1)} %all-to-all-done.1), kind=kOutput, calls=%fused_computation.6 | convolution fusion | flops 537395200 | bytes 2621440 | tf_op jit(solution)/shard_map/btw,btk->wk/dot_general | solution.py:61
  82.0 3.6 %all-to-all-start.5 = ((bf16[4,128,512]{2,1,0:T(8,128)(2,1)}), bf16[4,128,512]{2,1,0:T(8,128)(2,1)S(1)}, u32[]{:S(2)}, u32[]{:S(2)}) async-start(bf16[4,128,512]{2,1,0:T(8,128)(2,1)} %bitcast.11), calls=%async_computation.5 | async-start | bytes 1048576 | tf_op jit(solution)/shard_map/all_to_all | solution.py:17
  85.6 0.2 copy.26
  85.8 1.7 %convolution_convert_fusion = bf16[8,128,512]{2,1,0:T(8,128)(2,1)} fusion(bf16[8,128,512]{2,1,0:T(8,128)(2,1)S(1)} %copy-done.2, bf16[512,512,1]{1,0,2:T(8,128)(2,1)S(1)} %bitcast.52), kind=kOutput, calls=%fused_computation.1 | convolution fusion | flops 537395200 | bytes 2621440 | tf_op jit(solution)/shard_map/btk,wk->btw/dot_general | solution.py:56
  87.6 13.3 %all-to-all-done.5 = bf16[4,128,512]{2,1,0:T(8,128)(2,1)S(1)} async-done(((bf16[4,128,512]{2,1,0:T(8,128)(2,1)}), bf16[4,128,512]{2,1,0:T(8,128)(2,1)S(1)}, u32[]{:S(2)}, u32[]{:S(2)}) %all-to-all-start.5) | async-done | bytes 524320 | tf_op jit(solution)/shard_map/all_to_all | solution.py:17
  100.9 3.6 %all-to-all-start.4 = ((bf16[8,128,512]{2,1,0:T(8,128)(2,1)}), bf16[8,128,512]{2,1,0:T(8,128)(2,1)S(1)}, u32[]{:S(2)}, u32[]{:S(2)}) async-start(bf16[8,128,512]{2,1,0:T(8,128)(2,1)} %convolution_convert_fusion), calls=%async_computation.4 | async-start | bytes 2097152 | tf_op jit(solution)/shard_map/all_to_all | solution.py:17
  104.4 0.8 copy.23
  105.2 0.8 convert_reduce_fusion.1
  106.0 12.9 %all-to-all-done.4 = bf16[8,128,512]{2,1,0:T(8,128)(2,1)S(1)} async-done(((bf16[8,128,512]{2,1,0:T(8,128)(2,1)}), bf16[8,128,512]{2,1,0:T(8,128)(2,1)S(1)}, u32[]{:S(2)}, u32[]{:S(2)}) %all-to-all-start.4) | async-done | bytes 1048608 | tf_op jit(solution)/shard_map/all_to_all | solution.py:17
  118.9 0.3 reshape.60
  119.2 1.4 %copy.21 = bf16[128,4,2,1,4,128]{5,4,2,1,0,3:T(4,128)(2,1)S(1)} copy(bf16[128,4,2,1,4,128]{5,1,0,2,4,3:T(4,128)(2,1)S(1)} %bitcast.51) | data formatting | bytes 2097152 | tf_op jit(solution)/shard_map/transpose | solution.py:59
  120.6 1.6 %reshape.61 = bf16[128,4096]{1,0:T(8,128)(2,1)} reshape(bf16[128,4,2,1,4,128]{5,4,2,1,0,3:T(4,128)(2,1)S(1)} %copy.21) | data formatting | bytes 2097152 | tf_op jit(solution)/shard_map/reshape | solution.py:59
  (15 shorter events, 0.4 us)
Async XLA Ops:
  2.8 7.4 %copy-start = (bf16[128,4096]{1,0:T(8,128)(2,1)S(1)}, bf16[128,4096]{1,0:T(8,128)(2,1)}, u32[]{:S(2)}) copy-start(bf16[128,4096]{1,0:T(8,128)(2,1)} %param.3) | copy-start | bytes 3145732
  3.9 20.8 %all-to-all-start = ((bf16[4,128,512]{1,2,0:T(8,128)(2,1)}), bf16[4,128,512]{1,2,0:T(8,128)(2,1)S(1)}, u32[]{:S(2)}, u32[]{:S(2)}) async-start(bf16[4,128,512]{1,2,0:T(8,128)(2,1)} %broadcast_in_dim.7), calls=%async_computation | async-start | bytes 1048576 | tf_op jit(solution)/shard_map/all_to_all | solution.py:17
  24.7 18.3 %all-to-all-start.1 = ((bf16[8,128,512]{2,1,0:T(8,128)(2,1)}), bf16[8,128,512]{2,1,0:T(8,128)(2,1)S(1)}, u32[]{:S(2)}, u32[]{:S(2)}) async-start(bf16[8,128,512]{2,1,0:T(8,128)(2,1)} %reshape.57), calls=%async_computation.1 | async-start | bytes 2097152 | tf_op jit(solution)/shard_map/all_to_all | solution.py:17
  44.7 3.7 %copy-start.3 = (bf16[128,512]{1,0:T(8,128)(2,1)S(1)}, bf16[128,512]{1,0:T(8,128)(2,1)}, u32[]{:S(2)}) copy-start(bf16[128,512]{1,0:T(8,128)(2,1)} %param.5) | copy-start | bytes 393220
  44.7 18.2 %all-to-all-start.2 = ((bf16[8,128,512]{1,2,0:T(8,128)(2,1)}), bf16[8,128,512]{1,2,0:T(8,128)(2,1)S(1)}, u32[]{:S(2)}, u32[]{:S(2)}) async-start(bf16[8,128,512]{1,2,0:T(8,128)(2,1)} %fusion.1), calls=%async_computation.2 | async-start | bytes 2097152 | tf_op jit(solution)/shard_map/all_to_all | solution.py:17
  80.4 1.5 %copy-start.1 = (bf16[8,128,512]{2,1,0:T(8,128)(2,1)}, bf16[8,128,512]{2,1,0:T(8,128)(2,1)S(1)}, u32[]{:S(2)}) copy-start(bf16[8,128,512]{2,1,0:T(8,128)(2,1)S(1)} %all_to_all.30) | copy-start | bytes 3145732
  82.0 3.8 %copy-start.2 = (bf16[8,128,512]{2,1,0:T(8,128)(2,1)S(1)}, bf16[8,128,512]{2,1,0:T(8,128)(2,1)}, u32[]{:S(2)}) copy-start(bf16[8,128,512]{2,1,0:T(8,128)(2,1)} %copy-done.1) | copy-start | bytes 3145732
  82.0 18.9 %all-to-all-start.5 = ((bf16[4,128,512]{2,1,0:T(8,128)(2,1)}), bf16[4,128,512]{2,1,0:T(8,128)(2,1)S(1)}, u32[]{:S(2)}, u32[]{:S(2)}) async-start(bf16[4,128,512]{2,1,0:T(8,128)(2,1)} %bitcast.11), calls=%async_computation.5 | async-start | bytes 1048576 | tf_op jit(solution)/shard_map/all_to_all | solution.py:17
  100.9 18.0 %all-to-all-start.4 = ((bf16[8,128,512]{2,1,0:T(8,128)(2,1)}), bf16[8,128,512]{2,1,0:T(8,128)(2,1)S(1)}, u32[]{:S(2)}, u32[]{:S(2)}) async-start(bf16[8,128,512]{2,1,0:T(8,128)(2,1)} %convolution_convert_fusion), calls=%async_computation.4 | async-start | bytes 2097152 | tf_op jit(solution)/shard_map/all_to_all | solution.py:17

commit v3 on v2

--- a/solution.py
+++ b/solution.py
@@ -10,11 +10,16 @@
 
 epsilon = 1e-06
 
-PLANE = ("near", "pair")
+PLANE = ("pair", "near")
 
 
 def exchange(blocks, axes):
     return lax.all_to_all(blocks, axes, split_axis=0, concat_axis=0, tiled=True)
+
+
+def rotated(block, axis, step):
+    size = lax.axis_size(axis)
+    return lax.ppermute(block, axis, [(i, (i + step) % size) for i in range(size)])
 
 
 def per_device(tokens, key_weight, cotangent):
@@ -30,11 +35,12 @@
     runs = key_weight.reshape(outer, near, run * key_cols)
     mine = lax.dynamic_index_in_dim(runs, lax.axis_index("near"), axis=1, keepdims=False)
     mine = mine.reshape(outer * run, key_cols)
-    weight = exchange(jnp.broadcast_to(mine[None], (line,) + mine.shape), "line")
-    weight = weight.reshape(owned_cols, key_cols)
+    place = lax.axis_index("line")
+    arrived = jnp.stack([mine] + [rotated(mine, "line", step) for step in range(1, line)])
+    weight = arrived[(place - jnp.arange(line)) % line].reshape(owned_cols, key_cols)
 
     by_owner = tokens.reshape(tok_rows, line, pair, outer, near, run)
-    by_owner = by_owner.transpose(4, 2, 0, 1, 3, 5).reshape(plane, tok_rows, owned_cols)
+    by_owner = by_owner.transpose(2, 4, 0, 1, 3, 5).reshape(plane, tok_rows, owned_cols)
     owned = exchange(by_owner, PLANE)
 
     share = jnp.einsum("btw,wk->btk", owned, weight, preferred_element_type=jnp.float32)
@@ -55,12 +61,15 @@
 
     columns = jnp.einsum("btk,wk->btw", grads, weight, preferred_element_type=jnp.float32)
     back = exchange(columns.astype(jnp.bfloat16), PLANE)
-    back = back.reshape(near, pair, tok_rows, line, outer, run)
-    input_grad = back.transpose(2, 3, 1, 4, 0, 5).reshape(tok_rows, width)
+    back = back.reshape(pair, near, tok_rows, line, outer, run)
+    input_grad = back.transpose(2, 3, 0, 4, 1, 5).reshape(tok_rows, width)
 
     total = jnp.einsum("btw,btk->wk", owned, grads, preferred_element_type=jnp.float32) * grad_scale
-    pieces = exchange(total.astype(jnp.bfloat16).reshape(line, outer * run, key_cols), "line")
-    weight_grad = jnp.sum(pieces.astype(jnp.float32), axis=0)
+    pieces = total.astype(jnp.bfloat16).reshape(line, outer * run, key_cols)
+    weight_grad = lax.dynamic_index_in_dim(pieces, place, axis=0, keepdims=False).astype(jnp.float32)
+    for step in range(1, line):
+        leaving = lax.dynamic_index_in_dim(pieces, (place + step) % line, axis=0, keepdims=False)
+        weight_grad += rotated(leaving, "line", step).astype(jnp.float32)
     if outer > 1:
         weight_grad = lax.psum_scatter(weight_grad, "outer", scatter_dimension=0, tiled=True)
     return (key_out, input_grad, weight_grad)

time: 123 us -> 91.4 us (0.74)
  waiting for transfers between devices: 66.6 us -> 30.7 us
  starting transfers between devices: 20.9 us -> 24.2 us
    all_to_all x5 -> x3, waiting for transfers between devices: 66.6 us -> 15.3 us  [exchange(): return lax.all_to_all(blocks, axes, split_axis=0, concat_axis=0, tiled=True)]
    ppermute x0 -> x6, waiting for transfers between devices: none -> 15.4 us  [rotated(): lax.ppermute(block, axis, [(i, (i + step) % size) for i in range(size)])]
    ppermute x0 -> x6, starting transfers between devices: none -> 11.4 us  [rotated(): lax.ppermute(block, axis, [(i, (i + step) % size) for i in range(size)])]
    all_to_all x5 -> x3, starting transfers between devices: 20.9 us -> 12.9 us  [exchange(): return lax.all_to_all(blocks, axes, split_axis=0, concat_axis=0, tiled=True)]
    add x0 -> x1, other arithmetic: none -> 1.67 us  [per_device(): weight_grad += rotated(leaving, 'line', step).astype(jnp.float32)]
    reshape x5 -> x4, local copies, waits for them, and re-layouts: 3.51 us -> 3.19 us  [the longest x1 1.61 us: per_device(): input_grad = back.transpose(2, 3, 0, 4, 1, 5).reshape(tok_rows, width)]
  transfers between devices with their start and end apart: 5 -> 9, of which waited for: 5 -> 5; matrix products, arithmetic and copies ran while one was open for 5% -> 6% of each run, Pallas kernels for 0% -> 0%
where the time goes in v3:
time: 91.4 us; the launch traced here: 90.4 us
  waiting for transfers between devices  30.7 us (34%)
  starting transfers between devices  24.2 us (26%)
  blocking collectives  17.9 us (20%)
  local copies, waits for them, and re-layouts  10.5 us (11%)
  matrix products  4.2 us (5%)
  other arithmetic  2.07 us (2%)
    all_to_all x1, blocking collectives, exchange(): return lax.all_to_all(blocks, axes, split_axis=0, concat_axis=0, tiled=True)  17.9 us
    ppermute x6, waiting for transfers between devices, rotated(): lax.ppermute(block, axis, [(i, (i + step) % size) for i in range(size)])  15.4 us
    all_to_all x3, waiting for transfers between devices, exchange(): return lax.all_to_all(blocks, axes, split_axis=0, concat_axis=0, tiled=True)  15.3 us
    all_to_all x3, starting transfers between devices, exchange(): return lax.all_to_all(blocks, axes, split_axis=0, concat_axis=0, tiled=True)  12.9 us
    ppermute x6, starting transfers between devices, rotated(): lax.ppermute(block, axis, [(i, (i + step) % size) for i in range(size)])  11.4 us
    reshape x2, local copies, waits for them, and re-layouts, per_device(): by_owner = tokens.reshape(tok_rows, line, pair, outer, near, run)  2.2 us
  transfers between devices with their start and end apart: 9, of which 5 were waited for; matrix products, arithmetic and copies ran while one was open for 6% of the time, Pallas kernels for 0%

profile of v3, /device:TPU:0, one launch (start us, length us, event | category | flops | bytes accessed | tf_op | source)
XLA Modules:
  0.0 90.4 jit_solution(17614589190869590619)
XLA Ops:
  0.6 1.8 %reshape.111 = bf16[128,4,2,1,4,128]{5,4,2,1,0,3:T(4,128)(2,1)S(1)} reshape(bf16[128,4096]{1,0:T(8,128)(2,1)} %param.3) | data formatting | bytes 2097152 | tf_op jit(solution)/shard_map/reshape | solution.py:42
  2.4 0.4 copy.21
  2.8 1.2 %reshape.112 = bf16[8,128,512]{2,1,0:T(8,128)(2,1)} reshape(bf16[2,4,128,4,1,128]{5,3,2,1,0,4:T(4,128)(2,1)S(1)} %bitcast.63) | data formatting | bytes 2097152 | tf_op jit(solution)/shard_map/reshape | solution.py:43
  4.1 5.3 %all-to-all-start = ((bf16[8,128,512]{2,1,0:T(8,128)(2,1)}), bf16[8,128,512]{2,1,0:T(8,128)(2,1)S(1)}, u32[]{:S(2)}, u32[]{:S(2)}) async-start(bf16[8,128,512]{2,1,0:T(8,128)(2,1)} %reshape.112), calls=%async_computation | async-start | bytes 2097152 | tf_op jit(solution)/shard_map/all_to_all | solution.py:17
  9.4 0.4 reshape.108
  9.8 0.8 dynamic-slice_reduce_fusion
  10.6 1.6 %collective-permute-start = (bf16[128,512]{1,0:T(8,128)(2,1)S(1)}, bf16[128,512]{1,0:T(8,128)(2,1)S(1)}, u32[]{:S(2)}, u32[]{:S(2)}) collective-permute-start(bf16[128,512]{1,0:T(8,128)(2,1)S(1)} %reshape.109), channel_id=1, source_target_pairs={{0,2},{2,4},{4,6},{6,0},{1,3},{3,5},{5,7},{7,1},{8,10},{10,12},{12... | collective-permute-start | bytes 393224 | tf_op jit(solution)/shard_map/ppermute | solution.py:22
  12.3 2.6 %collective-permute-start.1 = (bf16[128,512]{1,0:T(8,128)(2,1)S(1)}, bf16[128,512]{1,0:T(8,128)(2,1)S(1)}, u32[]{:S(2)}, u32[]{:S(2)}) collective-permute-start(bf16[128,512]{1,0:T(8,128)(2,1)S(1)} %reshape.109), channel_id=1, source_target_pairs={{0,4},{2,6},{4,0},{6,2},{1,5},{3,7},{5,1},{7,3},{8,12},{10,14},{12... | collective-permute-start | bytes 393224 | tf_op jit(solution)/shard_map/ppermute | solution.py:22
  14.8 1.3 %collective-permute-start.2 = (bf16[128,512]{1,0:T(8,128)(2,1)S(1)}, bf16[128,512]{1,0:T(8,128)(2,1)S(1)}, u32[]{:S(2)}, u32[]{:S(2)}) collective-permute-start(bf16[128,512]{1,0:T(8,128)(2,1)S(1)} %reshape.109), channel_id=1, source_target_pairs={{0,6},{2,0},{4,2},{6,4},{1,7},{3,1},{5,3},{7,5},{8,14},{10,8},{12,... | collective-permute-start | bytes 393224 | tf_op jit(solution)/shard_map/ppermute | solution.py:22
  16.3 2.5 %collective-permute-done = bf16[128,512]{1,0:T(8,128)(2,1)S(1)} collective-permute-done((bf16[128,512]{1,0:T(8,128)(2,1)S(1)}, bf16[128,512]{1,0:T(8,128)(2,1)S(1)}, u32[]{:S(2)}, u32[]{:S(2)}) %collective-permute-start) | collective-permute-done | bytes 131104 | tf_op jit(solution)/shard_map/ppermute | solution.py:22
  18.9 5.3 %collective-permute-done.1 = bf16[128,512]{1,0:T(8,128)(2,1)S(1)} collective-permute-done((bf16[128,512]{1,0:T(8,128)(2,1)S(1)}, bf16[128,512]{1,0:T(8,128)(2,1)S(1)}, u32[]{:S(2)}, u32[]{:S(2)}) %collective-permute-start.1) | collective-permute-done | bytes 131104 | tf_op jit(solution)/shard_map/ppermute | solution.py:22
  24.2 0.6 gather_fusion
  24.8 1.7 %fusion.1 = bf16[8,128,512]{1,2,0:T(8,128)(2,1)} fusion(bf16[512,512,1]{1,0,2:T(8,128)(2,1)S(1)} %bitcast.67, bf16[8,128,512]{2,1,0:T(8,128)(2,1)S(1)} %all-to-all-done), kind=kOutput, calls=%fused_computation.6 | convolution fusion | flops 537395200 | bytes 2621440 | tf_op jit(solution)/shard_map/btw,wk->btk/dot_general | solution.py:46
  26.6 4.0 %all-to-all-start.1 = ((bf16[8,128,512]{1,2,0:T(8,128)(2,1)}), bf16[8,128,512]{1,2,0:T(8,128)(2,1)S(1)}, u32[]{:S(2)}, u32[]{:S(2)}) async-start(bf16[8,128,512]{1,2,0:T(8,128)(2,1)} %fusion.1), calls=%async_computation.1 | async-start | bytes 2097152 | tf_op jit(solution)/shard_map/all_to_all | solution.py:17
  30.6 0.1 copy.12
  30.7 15.3 %all-to-all-done.1 = bf16[8,128,512]{1,2,0:T(8,128)(2,1)S(1)} async-done(((bf16[8,128,512]{1,2,0:T(8,128)(2,1)}), bf16[8,128,512]{1,2,0:T(8,128)(2,1)S(1)}, u32[]{:S(2)}, u32[]{:S(2)}) %all-to-all-start.1) | async-done | bytes 1048608 | tf_op jit(solution)/shard_map/all_to_all | solution.py:17
  46.0 0.1 convert_reduce_fusion
  46.5 17.9 %all_to_all.20 = bf16[8,128,512]{2,1,0:T(8,128)(2,1)S(1)} all-to-all(bf16[8,128,512]{2,1,0:T(8,128)(2,1)S(1)} %broadcast_in_dim.2), channel_id=1, replica_groups=mesh['outer'=1,'near'=4,'line'=4,'pair'=2] {'pair','near'}, dimensions={0} | all-to-all | bytes 2097152 | tf_op jit(solution)/shard_map/all_to_all | solution.py:17
  64.4 1.7 %convolution_convert_fusion = bf16[8,128,512]{2,1,0:T(8,128)(2,1)} fusion(bf16[8,128,512]{2,1,0:T(8,128)(2,1)S(1)} %all_to_all.20, bf16[512,512,1]{1,0,2:T(8,128)(2,1)S(1)} %bitcast.68), kind=kOutput, calls=%fused_computation.2 | convolution fusion | flops 537395200 | bytes 2621440 | tf_op jit(solution)/shard_map/btk,wk->btw/dot_general | solution.py:62
  66.2 3.6 %all-to-all-start.3 = ((bf16[8,128,512]{2,1,0:T(8,128)(2,1)}), bf16[8,128,512]{2,1,0:T(8,128)(2,1)S(1)}, u32[]{:S(2)}, u32[]{:S(2)}) async-start(bf16[8,128,512]{2,1,0:T(8,128)(2,1)} %convolution_convert_fusion), calls=%async_computation.3 | async-start | bytes 2097152 | tf_op jit(solution)/shard_map/all_to_all | solution.py:17
  69.8 0.8 fusion.2
  70.5 0.8 copy-done.1
  71.3 3.3 %collective-permute-start.3 = (bf16[128,512]{1,0:T(8,128)(2,1)S(1)}, bf16[128,512]{1,0:T(8,128)(2,1)S(1)}, u32[]{:S(2)}, u32[]{:S(2)}) collective-permute-start(bf16[128,512]{1,0:T(8,128)(2,1)S(1)} %get-tuple-element.6), channel_id=1, source_target_pairs={{0,2},{2,4},{4,6},{6,0},{1,3},{3,5},{5,7},{7,1},{8,10},{10,12},{12... | collective-permute-start | bytes 393224 | tf_op jit(solution)/shard_map/ppermute | solution.py:22
  74.7 1.6 %collective-permute-start.4 = (bf16[128,512]{1,0:T(8,128)(2,1)S(1)}, bf16[128,512]{1,0:T(8,128)(2,1)S(1)}, u32[]{:S(2)}, u32[]{:S(2)}) collective-permute-start(bf16[128,512]{1,0:T(8,128)(2,1)S(1)} %get-tuple-element.8), channel_id=1, source_target_pairs={{0,4},{2,6},{4,0},{6,2},{1,5},{3,7},{5,1},{7,3},{8,12},{10,14},{12... | collective-permute-start | bytes 393224 | tf_op jit(solution)/shard_map/ppermute | solution.py:22
  76.3 0.8 collective-permute-start.5
  77.1 0.8 copy.16
  77.9 2.3 %collective-permute-done.3 = bf16[128,512]{1,0:T(8,128)(2,1)S(1)} collective-permute-done((bf16[128,512]{1,0:T(8,128)(2,1)S(1)}, bf16[128,512]{1,0:T(8,128)(2,1)S(1)}, u32[]{:S(2)}, u32[]{:S(2)}) %collective-permute-start.3) | collective-permute-done | bytes 131104 | tf_op jit(solution)/shard_map/ppermute | solution.py:22
  80.2 5.3 %collective-permute-done.4 = bf16[128,512]{1,0:T(8,128)(2,1)S(1)} collective-permute-done((bf16[128,512]{1,0:T(8,128)(2,1)S(1)}, bf16[128,512]{1,0:T(8,128)(2,1)S(1)}, u32[]{:S(2)}, u32[]{:S(2)}) %collective-permute-start.4) | collective-permute-done | bytes 131104 | tf_op jit(solution)/shard_map/ppermute | solution.py:22
  85.5 1.7 %fusion.5 = f32[128,512]{1,0:T(8,128)} fusion(bf16[128,512]{1,0:T(8,128)(2,1)S(1)} %collective-permute-done.5, bf16[128,512]{1,0:T(8,128)(2,1)S(1)} %collective-permute-done.4, bf16[128,512]{1,0:T(8,128)(2,1)S(1)} %collective-permute-done.3, bf16[4,128,512]{2,1,0:T(8,128)(2,1)} %bitcast.66, s32[]{:T(128)S(6)} %select_n.58), kind=kLoop, calls=%fused_computation.15 | loop fusion | flops 458752 | bytes 786436 | tf_op jit(solution)/shard_map/add | solution.py:72
  87.1 0.3 reshape.115
  87.4 1.4 %copy.14 = bf16[128,4,2,1,4,128]{5,4,2,1,0,3:T(4,128)(2,1)S(1)} copy(bf16[128,4,2,1,4,128]{5,1,0,4,2,3:T(4,128)(2,1)S(1)} %bitcast.64) | data formatting | bytes 2097152 | tf_op jit(solution)/shard_map/transpose | solution.py:65
  88.8 1.6 %reshape.116 = bf16[128,4096]{1,0:T(8,128)(2,1)} reshape(bf16[128,4,2,1,4,128]{5,4,2,1,0,3:T(4,128)(2,1)S(1)} %copy.14) | data formatting | bytes 2097152 | tf_op jit(solution)/shard_map/reshape | solution.py:65
  (26 shorter events, 0.7 us)
Async XLA Ops:
  4.1 5.3 %copy-start = (bf16[512,512]{1,0:T(8,128)(2,1)S(1)}, bf16[512,512]{1,0:T(8,128)(2,1)}, u32[]{:S(2)}) copy-start(bf16[512,512]{1,0:T(8,128)(2,1)} %param.4) | copy-start | bytes 1572868
  4.1 20.7 %all-to-all-start = ((bf16[8,128,512]{2,1,0:T(8,128)(2,1)}), bf16[8,128,512]{2,1,0:T(8,128)(2,1)S(1)}, u32[]{:S(2)}, u32[]{:S(2)}) async-start(bf16[8,128,512]{2,1,0:T(8,128)(2,1)} %reshape.112), calls=%async_computation | async-start | bytes 2097152 | tf_op jit(solution)/shard_map/all_to_all | solution.py:17
  10.6 8.2 %collective-permute-start = (bf16[128,512]{1,0:T(8,128)(2,1)S(1)}, bf16[128,512]{1,0:T(8,128)(2,1)S(1)}, u32[]{:S(2)}, u32[]{:S(2)}) collective-permute-start(bf16[128,512]{1,0:T(8,128)(2,1)S(1)} %reshape.109), channel_id=1, source_target_pairs={{0,2},{2,4},{4,6},{6,0},{1,3},{3,5},{5,7},{7,1},{8,10},{10,12},{12... | collective-permute-start | bytes 393224 | tf_op jit(solution)/shard_map/ppermute | solution.py:22
  12.3 11.9 %collective-permute-start.1 = (bf16[128,512]{1,0:T(8,128)(2,1)S(1)}, bf16[128,512]{1,0:T(8,128)(2,1)S(1)}, u32[]{:S(2)}, u32[]{:S(2)}) collective-permute-start(bf16[128,512]{1,0:T(8,128)(2,1)S(1)} %reshape.109), channel_id=1, source_target_pairs={{0,4},{2,6},{4,0},{6,2},{1,5},{3,7},{5,1},{7,3},{8,12},{10,14},{12... | collective-permute-start | bytes 393224 | tf_op jit(solution)/shard_map/ppermute | solution.py:22
  14.8 9.3 %collective-permute-start.2 = (bf16[128,512]{1,0:T(8,128)(2,1)S(1)}, bf16[128,512]{1,0:T(8,128)(2,1)S(1)}, u32[]{:S(2)}, u32[]{:S(2)}) collective-permute-start(bf16[128,512]{1,0:T(8,128)(2,1)S(1)} %reshape.109), channel_id=1, source_target_pairs={{0,6},{2,0},{4,2},{6,4},{1,7},{3,1},{5,3},{7,5},{8,14},{10,8},{12,... | collective-permute-start | bytes 393224 | tf_op jit(solution)/shard_map/ppermute | solution.py:22
  24.8 1.8 %copy-start.2 = (bf16[4,128,512]{2,1,0:T(8,128)(2,1)}, bf16[4,128,512]{2,1,0:T(8,128)(2,1)S(1)}, u32[]{:S(2)}) copy-start(bf16[4,128,512]{2,1,0:T(8,128)(2,1)S(1)} %gather_fusion) | copy-start | bytes 1572868
  26.5 4.0 %copy-start.4 = (bf16[128,512]{1,0:T(8,128)(2,1)S(1)}, bf16[128,512]{1,0:T(8,128)(2,1)}, u32[]{:S(2)}) copy-start(bf16[128,512]{1,0:T(8,128)(2,1)} %param.5) | copy-start | bytes 393220
  26.6 19.4 %all-to-all-start.1 = ((bf16[8,128,512]{1,2,0:T(8,128)(2,1)}), bf16[8,128,512]{1,2,0:T(8,128)(2,1)S(1)}, u32[]{:S(2)}, u32[]{:S(2)}) async-start(bf16[8,128,512]{1,2,0:T(8,128)(2,1)} %fusion.1), calls=%async_computation.1 | async-start | bytes 2097152 | tf_op jit(solution)/shard_map/all_to_all | solution.py:17
  46.5 17.9 %copy-start.3 = (bf16[4,128,512]{2,1,0:T(8,128)(2,1)S(1)}, bf16[4,128,512]{2,1,0:T(8,128)(2,1)}, u32[]{:S(2)}) copy-start(bf16[4,128,512]{2,1,0:T(8,128)(2,1)} %copy-done.2) | copy-start | bytes 1572868
  66.2 21.0 %all-to-all-start.3 = ((bf16[8,128,512]{2,1,0:T(8,128)(2,1)}), bf16[8,128,512]{2,1,0:T(8,128)(2,1)S(1)}, u32[]{:S(2)}, u32[]{:S(2)}) async-start(bf16[8,128,512]{2,1,0:T(8,128)(2,1)} %convolution_convert_fusion), calls=%async_computation.3 | async-start | bytes 2097152 | tf_op jit(solution)/shard_map/all_to_all | solution.py:17
  70.5 0.8 copy-start.1
  71.3 8.8 %collective-permute-start.3 = (bf16[128,512]{1,0:T(8,128)(2,1)S(1)}, bf16[128,512]{1,0:T(8,128)(2,1)S(1)}, u32[]{:S(2)}, u32[]{:S(2)}) collective-permute-start(bf16[128,512]{1,0:T(8,128)(2,1)S(1)} %get-tuple-element.6), channel_id=1, source_target_pairs={{0,2},{2,4},{4,6},{6,0},{1,3},{3,5},{5,7},{7,1},{8,10},{10,12},{12... | collective-permute-start | bytes 393224 | tf_op jit(solution)/shard_map/ppermute | solution.py:22
  74.7 10.8 %collective-permute-start.4 = (bf16[128,512]{1,0:T(8,128)(2,1)S(1)}, bf16[128,512]{1,0:T(8,128)(2,1)S(1)}, u32[]{:S(2)}, u32[]{:S(2)}) collective-permute-start(bf16[128,512]{1,0:T(8,128)(2,1)S(1)} %get-tuple-element.8), channel_id=1, source_target_pairs={{0,4},{2,6},{4,0},{6,2},{1,5},{3,7},{5,1},{7,3},{8,12},{10,14},{12... | collective-permute-start | bytes 393224 | tf_op jit(solution)/shard_map/ppermute | solution.py:22
  76.3 9.1 %collective-permute-start.5 = (bf16[128,512]{1,0:T(8,128)(2,1)S(1)}, bf16[128,512]{1,0:T(8,128)(2,1)S(1)}, u32[]{:S(2)}, u32[]{:S(2)}) collective-permute-start(bf16[128,512]{1,0:T(8,128)(2,1)S(1)} %get-tuple-element.7), channel_id=1, source_target_pairs={{0,6},{2,0},{4,2},{6,4},{1,7},{3,1},{5,3},{7,5},{8,14},{10,8},{12,... | collective-permute-start | bytes 393224 | tf_op jit(solution)/shard_map/ppermute | solution.py:22

commit v4 on v2

v4 whole, which is shorter than its diff:
```python
import functools
import itertools
import math

import jax
import jax.numpy as jnp
from jax import lax
from jax.experimental import pallas as pl
from jax.experimental.pallas import tpu as pltpu
from jax.sharding import Mesh, PartitionSpec as P

HEAD_DIM = 128


epsilon = 1e-06

MEMBERS = ("side", "pair")
bf16, f32 = jnp.bfloat16, jnp.float32


def local_call(body, out_shapes, *args, flops=0):
    vmem = pl.BlockSpec(memory_space=pltpu.VMEM)
    many = isinstance(out_shapes, (list, tuple))
    moved = sum(math.prod(a.shape) * a.dtype.itemsize for a in args)
    return pl.pallas_call(
        body,
        out_shape=out_shapes,
        in_specs=[vmem] * len(args),
        out_specs=[vmem] * len(out_shapes) if many else vmem,
        compiler_params=pltpu.CompilerParams(vmem_limit_bytes=32 << 20),
        cost_estimate=pl.CostEstimate(flops=flops, bytes_accessed=moved, transcendentals=0),
    )(*args)


def rotated(block, axis, step):
    size = lax.axis_size(axis)
    return lax.ppermute(block, axis, [(i, (i + step) % size) for i in range(size)])


def flipped(block, axes, mask):
    size = lax.axis_size(axes)
    return lax.ppermute(block, axes, [(i, i ^ mask) for i in range(size)])


def run_of(part, mask):
    side, twin = lax.axis_size("side"), lax.axis_size("twin")
    line, pair = lax.axis_size("line"), lax.axis_size("pair")
    member = (lax.axis_index("side") * pair + lax.axis_index("pair")) ^ mask
    place = lax.rem(lax.axis_index("line") + line - part // twin, line)
    core = lax.axis_index("twin") ^ (part % twin)
    return (place * pair + lax.rem(member, pair)) * side * twin + member // pair * twin + core


def pack_body(masks, parts, tokens, *blocks):
    run = blocks[0].shape[1] // parts
    for mask, block in zip(masks, blocks):
        for part in range(parts):
            start = pl.multiple_of(run_of(part, mask) * run, run)
            block[:, part * run : (part + 1) * run] = tokens[:, pl.ds(start, run)]


def unpack_body(masks, parts, *refs):
    blocks, whole = refs[:-1], refs[-1]
    run = blocks[0].shape[1] // parts
    for mask, block in zip(masks, blocks):
        for part in range(parts):
            start = pl.multiple_of(run_of(part, mask) * run, run)
            whole[:, pl.ds(start, run)] = block[:, part * run : (part + 1) * run]


def split_runs(tokens, outer):
    tok_rows, width = tokens.shape
    inner = lax.axis_size("line") * lax.axis_size("pair")
    near = lax.axis_size("side") * lax.axis_size("twin")
    cut = tokens.reshape(tok_rows, inner, outer, near, width // (inner * outer * near))
    return cut.transpose(0, 1, 3, 2, 4).reshape(tok_rows, width)


def join_runs(tokens, outer):
    tok_rows, width = tokens.shape
    inner = lax.axis_size("line") * lax.axis_size("pair")
    near = lax.axis_size("side") * lax.axis_size("twin")
    cut = tokens.reshape(tok_rows, inner, near, outer, width // (inner * outer * near))
    return cut.transpose(0, 1, 3, 2, 4).reshape(tok_rows, width)


def join_body(*refs):
    whole = refs[-1]
    rows = refs[0].shape[0]
    for i, ref in enumerate(refs[:-1]):
        whole[i * rows : (i + 1) * rows, :] = ref[...]


def share_body(block, weight, out):
    out[...] = jnp.dot(block[...], weight[...], preferred_element_type=f32).astype(out.dtype)


def columns_body(grad, weight, out):
    out[...] = lax.dot_general(
        grad[...], weight[...], (((1,), (1,)), ((), ())), preferred_element_type=f32
    ).astype(out.dtype)


def norm_body(*refs):
    *shares, cotangent, key_out, key_grad = refs
    for head in range(key_out.shape[1] // HEAD_DIM):
        at = slice(head * HEAD_DIM, (head + 1) * HEAD_DIM)
        raw = sum(share[:, at].astype(f32) for share in shares)
        inverse = lax.rsqrt(jnp.mean(raw * raw, axis=-1, keepdims=True) + epsilon)
        normed = raw * inverse
        upstream = cotangent[:, at].astype(f32)
        projected = jnp.mean(upstream * normed, axis=-1, keepdims=True)
        key_out[:, at] = normed.astype(bf16)
        key_grad[:, at] = (inverse * (upstream - normed * projected)).astype(bf16)


def terms_body(members, twin, grad_scale, *refs):
    blocks, grads, (kept, *leaving) = refs[:members], refs[members : 2 * members], refs[2 * members :]
    tokens = jnp.concatenate([block[...] for block in blocks], axis=0)
    grad = jnp.concatenate([grad[...] for grad in grads], axis=0)
    rows = kept.shape[1]
    total = lax.dot_general(tokens, grad, (((0,), (0,)), ((), ())), preferred_element_type=f32)
    total = total * grad_scale
    for part in range(total.shape[0] // rows):
        piece = total[part * rows : (part + 1) * rows]
        if part % twin == 0:
            kept[part // twin] = piece
        else:
            leaving[0][part // twin] = piece.astype(bf16)


def merge_body(kept, arrived, own, *leaving):
    for step in range(kept.shape[0]):
        piece = kept[step] + arrived[step].astype(f32)
        if step == 0:
            own[...] = piece
        else:
            leaving[step - 1][...] = piece.astype(bf16)


def sum_body(*refs):
    refs[-1][...] = sum(ref[...].astype(f32) for ref in refs[:-1])


def per_device(tokens, key_weight, cotangent):
    tok_rows, width = tokens.shape
    shard_rows, key_cols = key_weight.shape
    outer, side, twin = (lax.axis_size(a) for a in ("outer", "side", "twin"))
    line, pair = lax.axis_size("line"), lax.axis_size("pair")
    members = pair * side
    masks = list(range(members))
    rows = shard_rows // (side * twin)
    parts = line * twin
    owned = width // members
    grad_scale = 1.0 / math.sqrt(tok_rows * outer * side * twin * line * pair)
    shape = jax.ShapeDtypeStruct

    if outer > 1:
        cut = key_weight.reshape(outer, side * twin, rows // outer, key_cols)
        runs = cut.transpose(1, 0, 2, 3).reshape(shard_rows, key_cols)
    else:
        runs = key_weight
    first = lax.axis_index("side") * twin + lax.axis_index("twin")
    mine = lax.dynamic_slice_in_dim(runs, first * rows, rows, axis=0)
    passed = [mine] + [rotated(mine, "line", step) for step in range(1, line)]
    pieces = []
    for step, piece in enumerate(passed):
        pieces.append(piece)
        if twin > 1:
            if step == 0:
                pieces.append(lax.dynamic_slice_in_dim(runs, (first ^ 1) * rows, rows, axis=0))
            else:
                pieces.append(flipped(piece, "twin", 1))

    if outer > 1:
        tokens = split_runs(tokens, outer)
    packed = local_call(
        functools.partial(pack_body, masks, parts), [shape((tok_rows, owned), bf16)] * members, tokens
    )
    blocks = [packed[0]] + [flipped(packed[mask], MEMBERS, mask) for mask in masks[1:]]
    weight = local_call(join_body, shape((owned, key_cols), bf16), *pieces)

    flops = 2 * tok_rows * owned * key_cols
    shares = []
    for mask in masks:
        kind = bf16 if mask else f32
        share = local_call(share_body, shape((tok_rows, key_cols), kind), blocks[mask], weight, flops=flops)
        shares.append(flipped(share, MEMBERS, mask) if mask else share)
    key_out, key_grad = local_call(
        norm_body, [shape((tok_rows, key_cols), bf16)] * 2, *shares, cotangent
    )

    grads = [key_grad] + [flipped(key_grad, MEMBERS, mask) for mask in masks[1:]]
    columns = []
    for mask in masks:
        column = local_call(columns_body, shape((tok_rows, owned), bf16), grads[mask], weight, flops=flops)
        columns.append(flipped(column, MEMBERS, mask) if mask else column)

    terms = local_call(
        functools.partial(terms_body, members, twin, grad_scale),
        [shape((line, rows, key_cols), f32)] + [shape((line, rows, key_cols), bf16)] * (twin - 1),
        *blocks,
        *grads,
        flops=members * flops,
    )
    arrived = flipped(terms[1], "twin", 1) if twin > 1 else jnp.zeros_like(terms[0])
    sums = local_call(
        merge_body,
        [shape((rows, key_cols), f32)] + [shape((rows, key_cols), bf16)] * (line - 1),
        terms[0],
        arrived,
    )
    met = [sums[0]] + [rotated(sums[step], "line", -step) for step in range(1, line)]
    weight_grad = local_call(sum_body, shape((rows, key_cols), f32), *met)
    if outer > 1:
        weight_grad = lax.psum_scatter(weight_grad, "outer", scatter_dimension=0, tiled=True)

    input_grad = local_call(
        functools.partial(unpack_body, masks, parts), shape((tok_rows, width), bf16), *columns
    )
    if outer > 1:
        input_grad = join_runs(input_grad, outer)
    return (key_out, input_grad, weight_grad)


def halves(size):
    return 2 if size % 2 == 0 else 1


def solution(mesh):
    replicas, group = mesh.shape["dp"], mesh.shape["inner"]
    twin, pair = halves(replicas), halves(group)
    side = halves(replicas // twin)
    fine = Mesh(
        mesh.devices.reshape(replicas // (side * twin), side, twin, group // pair, pair),
        ("outer", "side", "twin", "line", "pair"),
    )
    rows = P(("outer", "side", "twin", "line", "pair"), None)
    return jax.shard_map(
        per_device,
        mesh=fine,
        in_specs=(rows, P(("line", "pair"), None), rows),
        out_specs=(rows, rows, P(("line", "pair", "outer", "side", "twin"), None)),
        check_vma=False,
    )
```

time: 123 us -> 65.9 us (0.54)
  waiting for transfers between devices: 66.6 us -> 27.2 us
  blocking collectives: 17 us -> 0 us
  local copies, waits for them, and re-layouts: 10.8 us -> 2.22 us
  starting transfers between devices: 20.9 us -> 28.4 us
  Pallas kernels: 0 us -> 7.11 us
  matrix products: 4.97 us -> 0 us
    all_to_all x5 -> x0, waiting for transfers between devices: 66.6 us -> none  [exchange(): return lax.all_to_all(blocks, axes, split_axis=0, concat_axis=0, tiled=True)]
    ppermute x0 -> x22, starting transfers between devices: none -> 28.4 us  [the longest x16 17.9 us: flipped(): return lax.ppermute(block, axes, [(i, i ^ mask) for i in range(size)])]
    ppermute x0 -> x22, waiting for transfers between devices: none -> 27.2 us  [the longest x16 18 us: flipped(): return lax.ppermute(block, axes, [(i, i ^ mask) for i in range(size)])]
    all_to_all x5 -> x0, starting transfers between devices: 20.9 us -> none  [exchange(): return lax.all_to_all(blocks, axes, split_axis=0, concat_axis=0, tiled=True)]
    all_to_all x1 -> x0, blocking collectives: 17 us -> none  [exchange(): return lax.all_to_all(blocks, axes, split_axis=0, concat_axis=0, tiled=True)]
    pallas_call x0 -> x15, Pallas kernels: none -> 7.11 us  [local_call(): pl.pallas_call(body, out_shape=out_shapes, in_specs=[vmem] * len(args), o...]
    reshape x8 -> x0, local copies, waits for them, and re-layouts: 6.1 us -> none  [the longest x1 1.61 us: per_device(): input_grad = back.transpose(2, 3, 1, 4, 0, 5).reshape(tok_rows, width)]
    dot_general x3 -> x0, matrix products: 4.97 us -> none  [the longest x1 1.71 us: per_device(): jnp.einsum('btk,wk->btw', grads, weight, preferred_element_type=jnp.float32)]
  transfers between devices with their start and end apart: 5 -> 22, of which waited for: 5 -> 13; matrix products, arithmetic and copies ran while one was open for 5% -> 0% of each run, Pallas kernels for 0% -> 7%
where the time goes in v4:
time: 65.9 us; the launch traced here: 65.7 us
  starting transfers between devices  28.4 us (43%)
  waiting for transfers between devices  27.2 us (41%)
  Pallas kernels  7.11 us (11%)
  local copies, waits for them, and re-layouts  2.22 us (3%)
  between operations  0.79 us (1%)
    ppermute x16, waiting for transfers between devices, flipped(): return lax.ppermute(block, axes, [(i, i ^ mask) for i in range(size)])  18 us
    ppermute x16, starting transfers between devices, flipped(): return lax.ppermute(block, axes, [(i, i ^ mask) for i in range(size)])  17.9 us
    ppermute x6, starting transfers between devices, rotated(): lax.ppermute(block, axis, [(i, (i + step) % size) for i in range(size)])  10.5 us
    ppermute x6, waiting for transfers between devices, rotated(): lax.ppermute(block, axis, [(i, (i + step) % size) for i in range(size)])  9.22 us
    pallas_call x15, Pallas kernels, local_call(): pl.pallas_call(body, out_shape=out_shapes, in_specs=[vmem] * len(args), o...  7.11 us
  transfers between devices with their start and end apart: 22, of which 13 were waited for; matrix products, arithmetic and copies ran while one was open for 0% of the time, Pallas kernels for 7%

profile of v4, /device:TPU:0, one launch (start us, length us, event | category | flops | bytes accessed | tf_op | source)
XLA Modules:
  0.0 65.7 jit_solution(6921525313835748872)
XLA Ops:
  0.6 1.0 %constant_dynamic-slice_fusion = (bf16[128,512]{1,0:T(8,128)(2,1)S(1)}, bf16[128,512]{1,0:T(8,128)(2,1)S(1)}) fusion(bf16[512,512]{1,0:T(8,128)(2,1)} %param.4, s32[]{:T(128)S(6)} %select_n.7, s32[]{:T(128)S(6)} %select_n.6), kind=kLoop, calls=%fused_computation | loop fusion | bytes 524296 | tf_op jit(solution)/shard_map/dynamic_slice | solution.py:171
  1.6 5.1 %collective-permute-start.4 = (bf16[128,512]{1,0:T(8,128)(2,1)S(1)}, bf16[128,512]{1,0:T(8,128)(2,1)S(1)}, u32[]{:S(2)}, u32[]{:S(2)}) collective-permute-start(bf16[128,512]{1,0:T(8,128)(2,1)S(1)} %get-tuple-element.28.refs_0_), channel_id=1, source_target_pairs={{0,6},{2,0},{4,2},{6,4},{1,7},{3,1},{5,3},{7,5},{8,14},{10,8},{12,... | collective-permute-start | bytes 393224 | tf_op jit(solution)/shard_map/ppermute | solution.py:37
  6.7 1.0 %collective-permute-start = (bf16[128,512]{1,0:T(8,128)(2,1)S(1)}, bf16[128,512]{1,0:T(8,128)(2,1)S(1)}, u32[]{:S(2)}, u32[]{:S(2)}) collective-permute-start(bf16[128,512]{1,0:T(8,128)(2,1)S(1)} %get-tuple-element.28.refs_0_), channel_id=1, source_target_pairs={{0,2},{2,4},{4,6},{6,0},{1,3},{3,5},{5,7},{7,1},{8,10},{10,12},{12... | collective-permute-start | bytes 393224 | tf_op jit(solution)/shard_map/ppermute | solution.py:37
  7.8 2.9 %collective-permute-done.4.refs_6_ = bf16[128,512]{1,0:T(8,128)(2,1)S(1)} collective-permute-done((bf16[128,512]{1,0:T(8,128)(2,1)S(1)}, bf16[128,512]{1,0:T(8,128)(2,1)S(1)}, u32[]{:S(2)}, u32[]{:S(2)}) %collective-permute-start.4) | collective-permute-done | bytes 131104 | tf_op jit(solution)/shard_map/ppermute | solution.py:37
  10.7 1.2 %copy-done = bf16[128,4096]{1,0:T(8,128)(2,1)S(1)} copy-done((bf16[128,4096]{1,0:T(8,128)(2,1)S(1)}, bf16[128,4096]{1,0:T(8,128)(2,1)}, u32[]{:S(2)}) %copy-start) | copy-done | bytes 1048600
  12.2 1.6 %collective-permute-start.6 = (bf16[128,1024]{1,0:T(8,128)(2,1)S(1)}, bf16[128,1024]{1,0:T(8,128)(2,1)S(1)}, u32[]{:S(2)}, u32[]{:S(2)}) collective-permute-start(bf16[128,1024]{1,0:T(8,128)(2,1)S(1)} %get-tuple-element.16), channel_id=1, source_target_pairs={{0,1},{1,0},{16,17},{17,16},{2,3},{3,2},{18,19},{19,18},{4,5},{5,4... | collective-permute-start | bytes 786440 | tf_op jit(solution)/shard_map/ppermute | solution.py:42
  13.8 1.5 %collective-permute-start.8 = (bf16[128,1024]{1,0:T(8,128)(2,1)S(1)}, bf16[128,1024]{1,0:T(8,128)(2,1)S(1)}, u32[]{:S(2)}, u32[]{:S(2)}) collective-permute-start(bf16[128,1024]{1,0:T(8,128)(2,1)S(1)} %get-tuple-element.17), channel_id=1, source_target_pairs={{0,16},{1,17},{16,0},{17,1},{2,18},{3,19},{18,2},{19,3},{4,20},{5,... | collective-permute-start | bytes 786440 | tf_op jit(solution)/shard_map/ppermute | solution.py:42
  15.2 2.7 %collective-permute-done.2.refs_4_ = bf16[128,512]{1,0:T(8,128)(2,1)S(1)} collective-permute-done((bf16[128,512]{1,0:T(8,128)(2,1)S(1)}, bf16[128,512]{1,0:T(8,128)(2,1)S(1)}, u32[]{:S(2)}, u32[]{:S(2)}) %collective-permute-start.2) | collective-permute-done | bytes 131104 | tf_op jit(solution)/shard_map/ppermute | solution.py:37
  17.9 2.4 %collective-permute-start.10 = (bf16[128,1024]{1,0:T(8,128)(2,1)S(1)}, bf16[128,1024]{1,0:T(8,128)(2,1)S(1)}, u32[]{:S(2)}, u32[]{:S(2)}) collective-permute-start(bf16[128,1024]{1,0:T(8,128)(2,1)S(1)} %get-tuple-element.18), channel_id=1, source_target_pairs={{0,17},{1,16},{16,1},{17,0},{2,19},{3,18},{18,3},{19,2},{4,21},{5,... | collective-permute-start | bytes 786440 | tf_op jit(solution)/shard_map/ppermute | solution.py:42
  20.9 0.8 %collective-permute-done.3.refs_5_ = bf16[128,512]{1,0:T(8,128)(2,1)S(1)} collective-permute-done((bf16[128,512]{1,0:T(8,128)(2,1)S(1)}, bf16[128,512]{1,0:T(8,128)(2,1)S(1)}, u32[]{:S(2)}, u32[]{:S(2)}) %collective-permute-start.3) | collective-permute-done | bytes 131104 | tf_op jit(solution)/shard_map/ppermute | solution.py:42
  22.3 0.6 collective-permute-start.7
  23.2 1.5 %collective-permute-start.9 = (bf16[128,512]{1,0:T(8,128)(2,1)S(1)}, bf16[128,512]{1,0:T(8,128)(2,1)S(1)}, u32[]{:S(2)}, u32[]{:S(2)}) collective-permute-start(bf16[128,512]{1,0:T(8,128)(2,1)S(1)} %shard_map.62), channel_id=1, source_target_pairs={{0,16},{1,17},{16,0},{17,1},{2,18},{3,19},{18,2},{19,3},{4,20},{5,... | collective-permute-start | bytes 393224 | tf_op jit(solution)/shard_map/ppermute | solution.py:42
  24.8 3.7 %collective-permute-done.10.block.refs_3_ = bf16[128,1024]{1,0:T(8,128)(2,1)S(1)} collective-permute-done((bf16[128,1024]{1,0:T(8,128)(2,1)S(1)}, bf16[128,1024]{1,0:T(8,128)(2,1)S(1)}, u32[]{:S(2)}, u32[]{:S(2)}) %collective-permute-start.10) | collective-permute-done | bytes 262176 | tf_op jit(solution)/shard_map/ppermute | solution.py:42
  28.8 2.5 %collective-permute-start.11 = (bf16[128,512]{1,0:T(8,128)(2,1)S(1)}, bf16[128,512]{1,0:T(8,128)(2,1)S(1)}, u32[]{:S(2)}, u32[]{:S(2)}) collective-permute-start(bf16[128,512]{1,0:T(8,128)(2,1)S(1)} %shard_map.63), channel_id=1, source_target_pairs={{0,17},{1,16},{16,1},{17,0},{2,19},{3,18},{18,3},{19,2},{4,21},{5,... | collective-permute-start | bytes 393224 | tf_op jit(solution)/shard_map/ppermute | solution.py:42
  31.7 3.1 %collective-permute-done.11.refs_3_ = bf16[128,512]{1,0:T(8,128)(2,1)S(1)} collective-permute-done((bf16[128,512]{1,0:T(8,128)(2,1)S(1)}, bf16[128,512]{1,0:T(8,128)(2,1)S(1)}, u32[]{:S(2)}, u32[]{:S(2)}) %collective-permute-start.11) | collective-permute-done | bytes 131104 | tf_op jit(solution)/shard_map/ppermute | solution.py:42
  34.7 0.8 %shard_map.64 = (bf16[128,512]{1,0:T(8,128)(2,1)}, bf16[128,512]{1,0:T(8,128)(2,1)S(1)}) custom-call(f32[128,512]{1,0:T(8,128)S(1)} %shard_map.60.refs_0_, bf16[128,512]{1,0:T(8,128)(2,1)S(1)} %collective-permute-done.7.refs_1_, bf16[128,512]{1,0:T(8,128)(2,1)S(1)} %collective-permute-done.9.refs_2_, bf16[128,512]{1,0:T(8,128)(2,1)S(1)} %collective-permute-done.11.refs_3_, ...), custom_call_target="tpu_custom_call" | custom-call | bytes 786432 | tf_op jit(solution)/shard_map/pallas_call | solution.py:25
  35.6 2.5 %collective-permute-start.16 = (bf16[128,512]{1,0:T(8,128)(2,1)S(1)}, bf16[128,512]{1,0:T(8,128)(2,1)S(1)}, u32[]{:S(2)}, u32[]{:S(2)}) collective-permute-start(bf16[128,512]{1,0:T(8,128)(2,1)S(1)} %get-tuple-element.20.grad.refs_4_), channel_id=1, source_target_pairs={{0,17},{1,16},{16,1},{17,0},{2,19},{3,18},{18,3},{19,2},{4,21},{5,... | collective-permute-start | bytes 393224 | tf_op jit(solution)/shard_map/ppermute | solution.py:42
  38.0 0.5 collective-permute-start.14
  39.0 2.4 %collective-permute-done.16.grad.refs_7_ = bf16[128,512]{1,0:T(8,128)(2,1)S(1)} collective-permute-done((bf16[128,512]{1,0:T(8,128)(2,1)S(1)}, bf16[128,512]{1,0:T(8,128)(2,1)S(1)}, u32[]{:S(2)}, u32[]{:S(2)}) %collective-permute-start.16) | collective-permute-done | bytes 131104 | tf_op jit(solution)/shard_map/ppermute | solution.py:42
  41.4 1.6 %collective-permute-done.14.grad.refs_6_ = bf16[128,512]{1,0:T(8,128)(2,1)S(1)} collective-permute-done((bf16[128,512]{1,0:T(8,128)(2,1)S(1)}, bf16[128,512]{1,0:T(8,128)(2,1)S(1)}, u32[]{:S(2)}, u32[]{:S(2)}) %collective-permute-start.14) | collective-permute-done | bytes 131104 | tf_op jit(solution)/shard_map/ppermute | solution.py:42
  43.0 0.5 collective-permute-done.12.grad.refs_5_
  43.5 0.7 %shard_map.70 = (f32[4,128,512]{2,1,0:T(8,128)S(1)}, bf16[4,128,512]{2,1,0:T(8,128)(2,1)S(1)}) custom-call(bf16[128,1024]{1,0:T(8,128)(2,1)S(1)} %get-tuple-element.15.block.refs_0_, bf16[128,1024]{1,0:T(8,128)(2,1)S(1)} %collective-permute-done.6.block.refs_1_, bf16[128,1024]{1,0:T(8,128)(2,1)S(1)} %collective-permute-done.8.block.refs_2_, ...), custom_call_target="tpu_custom_call" | custom-call | flops 536870912 | bytes 1572864 | tf_op jit(solution)/shard_map/pallas_call | solution.py:25
  44.8 1.8 %collective-permute-start.17 = (bf16[128,1024]{1,0:T(8,128)(2,1)S(1)}, bf16[128,1024]{1,0:T(8,128)(2,1)S(1)}, u32[]{:S(2)}, u32[]{:S(2)}) collective-permute-start(bf16[128,1024]{1,0:T(8,128)(2,1)S(1)} %shard_map.68), channel_id=1, source_target_pairs={{0,17},{1,16},{16,1},{17,0},{2,19},{3,18},{18,3},{19,2},{4,21},{5,... | collective-permute-start | bytes 786440 | tf_op jit(solution)/shard_map/ppermute | solution.py:42
  47.1 0.6 collective-permute-start.15
  48.2 1.2 %collective-permute-start.13 = (bf16[128,1024]{1,0:T(8,128)(2,1)S(1)}, bf16[128,1024]{1,0:T(8,128)(2,1)S(1)}, u32[]{:S(2)}, u32[]{:S(2)}) collective-permute-start(bf16[128,1024]{1,0:T(8,128)(2,1)S(1)} %shard_map.66), channel_id=1, source_target_pairs={{0,1},{1,0},{16,17},{17,16},{2,3},{3,2},{18,19},{19,18},{4,5},{5,4... | collective-permute-start | bytes 786440 | tf_op jit(solution)/shard_map/ppermute | solution.py:42
  49.6 4.4 %collective-permute-start.19 = (bf16[128,512]{1,0:T(8,128)(2,1)S(1)}, bf16[128,512]{1,0:T(8,128)(2,1)S(1)}, u32[]{:S(2)}, u32[]{:S(2)}) collective-permute-start(bf16[128,512]{1,0:T(8,128)(2,1)S(1)} %get-tuple-element.24), channel_id=1, source_target_pairs={{0,6},{2,0},{4,2},{6,4},{1,7},{3,1},{5,3},{7,5},{8,14},{10,8},{12,... | collective-permute-start | bytes 393224 | tf_op jit(solution)/shard_map/ppermute | solution.py:37
  54.0 1.0 %collective-permute-done.17.refs_3_ = bf16[128,1024]{1,0:T(8,128)(2,1)S(1)} collective-permute-done((bf16[128,1024]{1,0:T(8,128)(2,1)S(1)}, bf16[128,1024]{1,0:T(8,128)(2,1)S(1)}, u32[]{:S(2)}, u32[]{:S(2)}) %collective-permute-start.17) | collective-permute-done | bytes 262176 | tf_op jit(solution)/shard_map/ppermute | solution.py:42
  55.4 4.1 %collective-permute-done.15.refs_2_ = bf16[128,1024]{1,0:T(8,128)(2,1)S(1)} collective-permute-done((bf16[128,1024]{1,0:T(8,128)(2,1)S(1)}, bf16[128,1024]{1,0:T(8,128)(2,1)S(1)}, u32[]{:S(2)}, u32[]{:S(2)}) %collective-permute-start.15) | collective-permute-done | bytes 262176 | tf_op jit(solution)/shard_map/ppermute | solution.py:42
  59.5 0.6 collective-permute-done.13.refs_1_
  60.1 1.2 %shard_map.69 = bf16[128,4096]{1,0:T(8,128)(2,1)} custom-call(bf16[128,1024]{1,0:T(8,128)(2,1)S(1)} %shard_map.65.refs_0_, bf16[128,1024]{1,0:T(8,128)(2,1)S(1)} %collective-permute-done.13.refs_1_, bf16[128,1024]{1,0:T(8,128)(2,1)S(1)} %collective-permute-done.15.refs_2_, bf16[128,1024]{1,0:T(8,128)(2,1)S(1)} %collective-permute-done.17.refs_3_), custom_call_target="tpu_custom_call" | custom-call | bytes 1048576 | tf_op jit(solution)/shard_map/pallas_call | solution.py:25
  61.3 3.6 %collective-permute-done.20.refs_2_ = bf16[128,512]{1,0:T(8,128)(2,1)S(1)} collective-permute-done((bf16[128,512]{1,0:T(8,128)(2,1)S(1)}, bf16[128,512]{1,0:T(8,128)(2,1)S(1)}, u32[]{:S(2)}, u32[]{:S(2)}) %collective-permute-start.20) | collective-permute-done | bytes 131104 | tf_op jit(solution)/shard_map/ppermute | solution.py:37
  65.0 0.8 %shard_map.72 = f32[128,512]{1,0:T(8,128)} custom-call(f32[128,512]{1,0:T(8,128)S(1)} %get-tuple-element.23.refs_0_, bf16[128,512]{1,0:T(8,128)(2,1)S(1)} %collective-permute-done.19.refs_1_, bf16[128,512]{1,0:T(8,128)(2,1)S(1)} %collective-permute-done.20.refs_2_, bf16[128,512]{1,0:T(8,128)(2,1)S(1)} %collective-permute-done.21.refs_3_), custom_call_target="tpu_custom_call" | custom-call | bytes 655360 | tf_op jit(solution)/shard_map/pallas_call | solution.py:25
  (32 shorter events, 4.9 us)
Async XLA Ops:
  1.6 9.0 %collective-permute-start.4 = (bf16[128,512]{1,0:T(8,128)(2,1)S(1)}, bf16[128,512]{1,0:T(8,128)(2,1)S(1)}, u32[]{:S(2)}, u32[]{:S(2)}) collective-permute-start(bf16[128,512]{1,0:T(8,128)(2,1)S(1)} %get-tuple-element.28.refs_0_), channel_id=1, source_target_pairs={{0,6},{2,0},{4,2},{6,4},{1,7},{3,1},{5,3},{7,5},{8,14},{10,8},{12,... | collective-permute-start | bytes 393224 | tf_op jit(solution)/shard_map/ppermute | solution.py:37
  6.7 11.2 %collective-permute-start.2 = (bf16[128,512]{1,0:T(8,128)(2,1)S(1)}, bf16[128,512]{1,0:T(8,128)(2,1)S(1)}, u32[]{:S(2)}, u32[]{:S(2)}) collective-permute-start(bf16[128,512]{1,0:T(8,128)(2,1)S(1)} %get-tuple-element.28.refs_0_), channel_id=1, source_target_pairs={{0,4},{2,6},{4,0},{6,2},{1,5},{3,7},{5,1},{7,3},{8,12},{10,14},{12... | collective-permute-start | bytes 393224 | tf_op jit(solution)/shard_map/ppermute | solution.py:37
  6.7 13.7 %collective-permute-start = (bf16[128,512]{1,0:T(8,128)(2,1)S(1)}, bf16[128,512]{1,0:T(8,128)(2,1)S(1)}, u32[]{:S(2)}, u32[]{:S(2)}) collective-permute-start(bf16[128,512]{1,0:T(8,128)(2,1)S(1)} %get-tuple-element.28.refs_0_), channel_id=1, source_target_pairs={{0,2},{2,4},{4,6},{6,0},{1,3},{3,5},{5,7},{7,1},{8,10},{10,12},{12... | collective-permute-start | bytes 393224 | tf_op jit(solution)/shard_map/ppermute | solution.py:37
  10.6 9.8 %collective-permute-start.5 = (bf16[128,512]{1,0:T(8,128)(2,1)S(1)}, bf16[128,512]{1,0:T(8,128)(2,1)S(1)}, u32[]{:S(2)}, u32[]{:S(2)}) collective-permute-start(bf16[128,512]{1,0:T(8,128)(2,1)S(1)} %collective-permute-done.4.refs_6_), channel_id=1, source_target_pairs={{0,8},{8,0},{1,9},{9,1},{2,10},{10,2},{3,11},{11,3},{4,12},{12,4},... | collective-permute-start | bytes 393224 | tf_op jit(solution)/shard_map/ppermute | solution.py:42
  10.6 1.2 %copy-start = (bf16[128,4096]{1,0:T(8,128)(2,1)S(1)}, bf16[128,4096]{1,0:T(8,128)(2,1)}, u32[]{:S(2)}) copy-start(bf16[128,4096]{1,0:T(8,128)(2,1)} %tokens.1) | copy-start | bytes 3145732
  12.2 9.8 %collective-permute-start.6 = (bf16[128,1024]{1,0:T(8,128)(2,1)S(1)}, bf16[128,1024]{1,0:T(8,128)(2,1)S(1)}, u32[]{:S(2)}, u32[]{:S(2)}) collective-permute-start(bf16[128,1024]{1,0:T(8,128)(2,1)S(1)} %get-tuple-element.16), channel_id=1, source_target_pairs={{0,1},{1,0},{16,17},{17,16},{2,3},{3,2},{18,19},{19,18},{4,5},{5,4... | collective-permute-start | bytes 786440 | tf_op jit(solution)/shard_map/ppermute | solution.py:42
  13.8 9.2 %collective-permute-start.8 = (bf16[128,1024]{1,0:T(8,128)(2,1)S(1)}, bf16[128,1024]{1,0:T(8,128)(2,1)S(1)}, u32[]{:S(2)}, u32[]{:S(2)}) collective-permute-start(bf16[128,1024]{1,0:T(8,128)(2,1)S(1)} %get-tuple-element.17), channel_id=1, source_target_pairs={{0,16},{1,17},{16,0},{17,1},{2,18},{3,19},{18,2},{19,3},{4,20},{5,... | collective-permute-start | bytes 786440 | tf_op jit(solution)/shard_map/ppermute | solution.py:42
  17.9 10.5 %collective-permute-start.10 = (bf16[128,1024]{1,0:T(8,128)(2,1)S(1)}, bf16[128,1024]{1,0:T(8,128)(2,1)S(1)}, u32[]{:S(2)}, u32[]{:S(2)}) collective-permute-start(bf16[128,1024]{1,0:T(8,128)(2,1)S(1)} %get-tuple-element.18), channel_id=1, source_target_pairs={{0,17},{1,16},{16,1},{17,0},{2,19},{3,18},{18,3},{19,2},{4,21},{5,... | collective-permute-start | bytes 786440 | tf_op jit(solution)/shard_map/ppermute | solution.py:42
  20.4 1.3 %collective-permute-start.3 = (bf16[128,512]{1,0:T(8,128)(2,1)S(1)}, bf16[128,512]{1,0:T(8,128)(2,1)S(1)}, u32[]{:S(2)}, u32[]{:S(2)}) collective-permute-start(bf16[128,512]{1,0:T(8,128)(2,1)S(1)} %collective-permute-done.2.refs_4_), channel_id=1, source_target_pairs={{0,8},{8,0},{1,9},{9,1},{2,10},{10,2},{3,11},{11,3},{4,12},{12,4},... | collective-permute-start | bytes 393224 | tf_op jit(solution)/shard_map/ppermute | solution.py:42
  20.4 1.5 %collective-permute-start.1 = (bf16[128,512]{1,0:T(8,128)(2,1)S(1)}, bf16[128,512]{1,0:T(8,128)(2,1)S(1)}, u32[]{:S(2)}, u32[]{:S(2)}) collective-permute-start(bf16[128,512]{1,0:T(8,128)(2,1)S(1)} %collective-permute-done.refs_2_), channel_id=1, source_target_pairs={{0,8},{8,0},{1,9},{9,1},{2,10},{10,2},{3,11},{11,3},{4,12},{12,4},... | collective-permute-start | bytes 393224 | tf_op jit(solution)/shard_map/ppermute | solution.py:42
  22.3 9.3 %collective-permute-start.7 = (bf16[128,512]{1,0:T(8,128)(2,1)S(1)}, bf16[128,512]{1,0:T(8,128)(2,1)S(1)}, u32[]{:S(2)}, u32[]{:S(2)}) collective-permute-start(bf16[128,512]{1,0:T(8,128)(2,1)S(1)} %shard_map.61), channel_id=1, source_target_pairs={{0,1},{1,0},{16,17},{17,16},{2,3},{3,2},{18,19},{19,18},{4,5},{5,4... | collective-permute-start | bytes 393224 | tf_op jit(solution)/shard_map/ppermute | solution.py:42
  23.2 8.4 %collective-permute-start.9 = (bf16[128,512]{1,0:T(8,128)(2,1)S(1)}, bf16[128,512]{1,0:T(8,128)(2,1)S(1)}, u32[]{:S(2)}, u32[]{:S(2)}) collective-permute-start(bf16[128,512]{1,0:T(8,128)(2,1)S(1)} %shard_map.62), channel_id=1, source_target_pairs={{0,16},{1,17},{16,0},{17,1},{2,18},{3,19},{18,2},{19,3},{4,20},{5,... | collective-permute-start | bytes 393224 | tf_op jit(solution)/shard_map/ppermute | solution.py:42
  28.8 5.9 %collective-permute-start.11 = (bf16[128,512]{1,0:T(8,128)(2,1)S(1)}, bf16[128,512]{1,0:T(8,128)(2,1)S(1)}, u32[]{:S(2)}, u32[]{:S(2)}) collective-permute-start(bf16[128,512]{1,0:T(8,128)(2,1)S(1)} %shard_map.63), channel_id=1, source_target_pairs={{0,17},{1,16},{16,1},{17,0},{2,19},{3,18},{18,3},{19,2},{4,21},{5,... | collective-permute-start | bytes 393224 | tf_op jit(solution)/shard_map/ppermute | solution.py:42
  31.3 3.4 %copy-start.1 = (bf16[128,512]{1,0:T(8,128)(2,1)S(1)}, bf16[128,512]{1,0:T(8,128)(2,1)}, u32[]{:S(2)}) copy-start(bf16[128,512]{1,0:T(8,128)(2,1)} %refs_4_.1) | copy-start | bytes 393220
  35.6 5.9 %collective-permute-start.16 = (bf16[128,512]{1,0:T(8,128)(2,1)S(1)}, bf16[128,512]{1,0:T(8,128)(2,1)S(1)}, u32[]{:S(2)}, u32[]{:S(2)}) collective-permute-start(bf16[128,512]{1,0:T(8,128)(2,1)S(1)} %get-tuple-element.20.grad.refs_4_), channel_id=1, source_target_pairs={{0,17},{1,16},{16,1},{17,0},{2,19},{3,18},{18,3},{19,2},{4,21},{5,... | collective-permute-start | bytes 393224 | tf_op jit(solution)/shard_map/ppermute | solution.py:42
  38.0 5.0 %collective-permute-start.14 = (bf16[128,512]{1,0:T(8,128)(2,1)S(1)}, bf16[128,512]{1,0:T(8,128)(2,1)S(1)}, u32[]{:S(2)}, u32[]{:S(2)}) collective-permute-start(bf16[128,512]{1,0:T(8,128)(2,1)S(1)} %get-tuple-element.20.grad.refs_4_), channel_id=1, source_target_pairs={{0,16},{1,17},{16,0},{17,1},{2,18},{3,19},{18,2},{19,3},{4,20},{5,... | collective-permute-start | bytes 393224 | tf_op jit(solution)/shard_map/ppermute | solution.py:42
  38.5 5.0 %collective-permute-start.12 = (bf16[128,512]{1,0:T(8,128)(2,1)S(1)}, bf16[128,512]{1,0:T(8,128)(2,1)S(1)}, u32[]{:S(2)}, u32[]{:S(2)}) collective-permute-start(bf16[128,512]{1,0:T(8,128)(2,1)S(1)} %get-tuple-element.20.grad.refs_4_), channel_id=1, source_target_pairs={{0,1},{1,0},{16,17},{17,16},{2,3},{3,2},{18,19},{19,18},{4,5},{5,4... | collective-permute-start | bytes 393224 | tf_op jit(solution)/shard_map/ppermute | solution.py:42
  44.3 5.2 %collective-permute-start.18 = (bf16[4,128,512]{2,1,0:T(8,128)(2,1)S(1)}, bf16[4,128,512]{2,1,0:T(8,128)(2,1)S(1)}, u32[]{:S(2)}, u32[]{:S(2)}) collective-permute-start(bf16[4,128,512]{2,1,0:T(8,128)(2,1)S(1)} %get-tuple-element.22), channel_id=1, source_target_pairs={{0,8},{8,0},{1,9},{9,1},{2,10},{10,2},{3,11},{11,3},{4,12},{12,4},... | collective-permute-start | bytes 1572872 | tf_op jit(solution)/shard_map/ppermute | solution.py:42
  44.8 10.1 %collective-permute-start.17 = (bf16[128,1024]{1,0:T(8,128)(2,1)S(1)}, bf16[128,1024]{1,0:T(8,128)(2,1)S(1)}, u32[]{:S(2)}, u32[]{:S(2)}) collective-permute-start(bf16[128,1024]{1,0:T(8,128)(2,1)S(1)} %shard_map.68), channel_id=1, source_target_pairs={{0,17},{1,16},{16,1},{17,0},{2,19},{3,18},{18,3},{19,2},{4,21},{5,... | collective-permute-start | bytes 786440 | tf_op jit(solution)/shard_map/ppermute | solution.py:42
  47.1 12.4 %collective-permute-start.15 = (bf16[128,1024]{1,0:T(8,128)(2,1)S(1)}, bf16[128,1024]{1,0:T(8,128)(2,1)S(1)}, u32[]{:S(2)}, u32[]{:S(2)}) collective-permute-start(bf16[128,1024]{1,0:T(8,128)(2,1)S(1)} %shard_map.67), channel_id=1, source_target_pairs={{0,16},{1,17},{16,0},{17,1},{2,18},{3,19},{18,2},{19,3},{4,20},{5,... | collective-permute-start | bytes 786440 | tf_op jit(solution)/shard_map/ppermute | solution.py:42
  48.2 11.9 %collective-permute-start.13 = (bf16[128,1024]{1,0:T(8,128)(2,1)S(1)}, bf16[128,1024]{1,0:T(8,128)(2,1)S(1)}, u32[]{:S(2)}, u32[]{:S(2)}) collective-permute-start(bf16[128,1024]{1,0:T(8,128)(2,1)S(1)} %shard_map.66), channel_id=1, source_target_pairs={{0,1},{1,0},{16,17},{17,16},{2,3},{3,2},{18,19},{19,18},{4,5},{5,4... | collective-permute-start | bytes 786440 | tf_op jit(solution)/shard_map/ppermute | solution.py:42
  49.6 11.8 %collective-permute-start.19 = (bf16[128,512]{1,0:T(8,128)(2,1)S(1)}, bf16[128,512]{1,0:T(8,128)(2,1)S(1)}, u32[]{:S(2)}, u32[]{:S(2)}) collective-permute-start(bf16[128,512]{1,0:T(8,128)(2,1)S(1)} %get-tuple-element.24), channel_id=1, source_target_pairs={{0,6},{2,0},{4,2},{6,4},{1,7},{3,1},{5,3},{7,5},{8,14},{10,8},{12,... | collective-permute-start | bytes 393224 | tf_op jit(solution)/shard_map/ppermute | solution.py:37
  54.0 11.0 %collective-permute-start.20 = (bf16[128,512]{1,0:T(8,128)(2,1)S(1)}, bf16[128,512]{1,0:T(8,128)(2,1)S(1)}, u32[]{:S(2)}, u32[]{:S(2)}) collective-permute-start(bf16[128,512]{1,0:T(8,128)(2,1)S(1)} %get-tuple-element.25), channel_id=1, source_target_pairs={{0,4},{2,6},{4,0},{6,2},{1,5},{3,7},{5,1},{7,3},{8,12},{10,14},{12... | collective-permute-start | bytes 393224 | tf_op jit(solution)/shard_map/ppermute | solution.py:37
  54.9 10.0 %collective-permute-start.21 = (bf16[128,512]{1,0:T(8,128)(2,1)S(1)}, bf16[128,512]{1,0:T(8,128)(2,1)S(1)}, u32[]{:S(2)}, u32[]{:S(2)}) collective-permute-start(bf16[128,512]{1,0:T(8,128)(2,1)S(1)} %get-tuple-element.26), channel_id=1, source_target_pairs={{0,2},{2,4},{4,6},{6,0},{1,3},{3,5},{5,7},{7,1},{8,10},{10,12},{12... | collective-permute-start | bytes 393224 | tf_op jit(solution)/shard_map/ppermute | solution.py:37

commit v5 on v4

v5 whole, which is shorter than its diff:
```python
import functools
import math

import jax
import jax.numpy as jnp
from jax import lax
from jax.experimental import pallas as pl
from jax.experimental.pallas import tpu as pltpu
from jax.sharding import Mesh, PartitionSpec as P

HEAD_DIM = 128


epsilon = 1e-06

MEMBERS = ("side", "pair")
TWIN = 2
bf16, f32 = jnp.bfloat16, jnp.float32


def local_call(body, out_shapes, *args, flops=0):
    vmem = pl.BlockSpec(memory_space=pltpu.VMEM)
    many = isinstance(out_shapes, (list, tuple))
    moved = sum(math.prod(a.shape) * a.dtype.itemsize for a in args)
    return pl.pallas_call(
        body,
        out_shape=out_shapes,
        in_specs=[vmem] * len(args),
        out_specs=[vmem] * len(out_shapes) if many else vmem,
        compiler_params=pltpu.CompilerParams(vmem_limit_bytes=32 << 20),
        cost_estimate=pl.CostEstimate(flops=flops, bytes_accessed=moved, transcendentals=0),
    )(*args)


def rotated(block, axis, step):
    size = lax.axis_size(axis)
    return lax.ppermute(block, axis, [(i, (i + step) % size) for i in range(size)])


def flipped(block, axes, mask):
    size = lax.axis_size(axes)
    return lax.ppermute(block, axes, [(i, i ^ mask) for i in range(size)])


def run_of(part, mask):
    side, line, pair = lax.axis_size("side"), lax.axis_size("line"), lax.axis_size("pair")
    member = (lax.axis_index("side") * pair + lax.axis_index("pair")) ^ mask
    place = lax.rem(lax.axis_index("line") + line - part // TWIN, line)
    core = lax.axis_index("twin") ^ (part % TWIN)
    return (place * pair + lax.rem(member, pair)) * side * TWIN + member // pair * TWIN + core


def pack(mask, tokens, block):
    parts = lax.axis_size("line") * TWIN
    run = block.shape[1] // parts
    for part in range(parts):
        start = pl.multiple_of(run_of(part, mask) * run, run)
        block[:, part * run : (part + 1) * run] = tokens[:, pl.ds(start, run)]


def first_body(mask, tokens, shard, both, block):
    rows = both.shape[0]
    both[...] = shard[pl.ds(pl.multiple_of(lax.axis_index("side") * rows, rows), rows), :]
    pack(mask, tokens, block)


def second_body(masks, tokens, both, _, mine, *blocks):
    rows = mine.shape[0]
    mine[...] = both[pl.ds(pl.multiple_of(lax.axis_index("twin") * rows, rows), rows), :]
    for mask, block in zip(masks, blocks):
        pack(mask, tokens, block)


def unpack_body(masks, *refs):
    blocks, whole = refs[:-1], refs[-1]
    parts = lax.axis_size("line") * TWIN
    run = blocks[0].shape[1] // parts
    for mask, block in zip(masks, blocks):
        for part in range(parts):
            start = pl.multiple_of(run_of(part, mask) * run, run)
            whole[:, pl.ds(start, run)] = block[:, part * run : (part + 1) * run]


def split_runs(tokens, outer):
    tok_rows, width = tokens.shape
    inner = lax.axis_size("line") * lax.axis_size("pair")
    near = lax.axis_size("side") * TWIN
    cut = tokens.reshape(tok_rows, inner, outer, near, width // (inner * outer * near))
    return cut.transpose(0, 1, 3, 2, 4).reshape(tok_rows, width)


def join_runs(tokens, outer):
    tok_rows, width = tokens.shape
    inner = lax.axis_size("line") * lax.axis_size("pair")
    near = lax.axis_size("side") * TWIN
    cut = tokens.reshape(tok_rows, inner, near, outer, width // (inner * outer * near))
    return cut.transpose(0, 1, 3, 2, 4).reshape(tok_rows, width)


def parted(block, step):
    line = lax.axis_size("line")
    to = [core * line + (i + (line - step if core else step)) % line for core in range(TWIN) for i in range(line)]
    return lax.ppermute(block, ("twin", "line"), list(enumerate(to)))


def join_body(line, *refs):
    *pieces, whole = refs
    rows = whole.shape[0] // (line * TWIN)
    core = lax.axis_index("twin")

    def put(step, twin_run, piece):
        part = step * TWIN + (twin_run ^ core)
        whole[pl.ds(pl.multiple_of(part * rows, rows), rows), :] = piece

    def put_both(step, piece):
        for twin_run in range(TWIN):
            put(step, twin_run, piece[twin_run * rows : (twin_run + 1) * rows, :])

    pieces = iter(pieces)
    put_both(0, next(pieces))
    for step in range(1, (line + 1) // 2):
        put_both(jnp.where(core == 0, step, line - step), next(pieces))
        put_both(jnp.where(core == 0, line - step, step), next(pieces))
    if line % 2 == 0:
        put(line // 2, core, next(pieces)[...])
        put(line // 2, 1 - core, next(pieces)[...])


def share_body(block, weight, out):
    out[...] = jnp.dot(block[...], weight[...], preferred_element_type=f32).astype(out.dtype)


def columns_body(grad, weight, out):
    out[...] = lax.dot_general(
        grad[...], weight[...], (((1,), (1,)), ((), ())), preferred_element_type=f32
    ).astype(out.dtype)


def norm_body(*refs):
    *shares, cotangent, key_out, key_grad = refs
    for head in range(key_out.shape[1] // HEAD_DIM):
        at = slice(head * HEAD_DIM, (head + 1) * HEAD_DIM)
        raw = sum(share[:, at].astype(f32) for share in shares)
        inverse = lax.rsqrt(jnp.mean(raw * raw, axis=-1, keepdims=True) + epsilon)
        normed = raw * inverse
        upstream = cotangent[:, at].astype(f32)
        projected = jnp.mean(upstream * normed, axis=-1, keepdims=True)
        key_out[:, at] = normed.astype(bf16)
        key_grad[:, at] = (inverse * (upstream - normed * projected)).astype(bf16)


def terms_body(members, grad_scale, *refs):
    blocks, grads, (kept, leaving) = refs[:members], refs[members : 2 * members], refs[2 * members :]
    tokens = jnp.concatenate([block[...] for block in blocks], axis=0)
    grad = jnp.concatenate([grad[...] for grad in grads], axis=0)
    rows = kept.shape[1]
    total = lax.dot_general(tokens, grad, (((0,), (0,)), ((), ())), preferred_element_type=f32)
    total = total * grad_scale
    for part in range(total.shape[0] // rows):
        piece = total[part * rows : (part + 1) * rows]
        if part % TWIN == 0:
            kept[part // TWIN] = piece
        else:
            leaving[part // TWIN] = piece.astype(bf16)


def merge_body(kept, arrived, own, *leaving):
    for step in range(kept.shape[0]):
        piece = kept[step] + arrived[step].astype(f32)
        if step == 0:
            own[...] = piece
        else:
            leaving[step - 1][...] = piece.astype(bf16)


def sum_body(*refs):
    refs[-1][...] = sum(ref[...].astype(f32) for ref in refs[:-1])


def per_device(tokens, key_weight, cotangent):
    tok_rows, width = tokens.shape
    shard_rows, key_cols = key_weight.shape
    outer, side = lax.axis_size("outer"), lax.axis_size("side")
    line, pair = lax.axis_size("line"), lax.axis_size("pair")
    members = pair * side
    masks = list(range(members))
    rows = shard_rows // (side * TWIN)
    owned = width // members
    grad_scale = 1.0 / math.sqrt(tok_rows * outer * side * TWIN * line * pair)
    shape = jax.ShapeDtypeStruct
    block_shape = shape((tok_rows, owned), bf16)
    if outer > 1:
        cut = key_weight.reshape(outer, side * TWIN, rows // outer, key_cols)
        key_weight = cut.transpose(1, 0, 2, 3).reshape(shard_rows, key_cols)
        tokens = split_runs(tokens, outer)

    both, *far = local_call(
        functools.partial(first_body, masks[-1]),
        [shape((TWIN * rows, key_cols), bf16), block_shape],
        tokens,
        key_weight,
    )
    mine, *packed = local_call(
        functools.partial(second_body, masks[:-1]),
        [shape((rows, key_cols), bf16)] + [block_shape] * (members - 1),
        tokens,
        both,
        *far,
    )
    packed += far
    blocks = [packed[0]] + [flipped(packed[mask], MEMBERS, mask) for mask in masks[1:]]
    passed = [parted(both, step) for step in range(1, (line + 1) // 2)]
    if line % 2 == 0:
        passed.append(rotated(mine, "line", line // 2))
    pieces = [both]
    *passed, blocks = lax.optimization_barrier((*passed, blocks))
    for piece in passed:
        pieces += [piece, flipped(piece, "twin", 1)]
    weight = local_call(
        functools.partial(join_body, line), shape((owned, key_cols), bf16), *pieces
    )

    flops = 2 * tok_rows * owned * key_cols
    shares = []
    for mask in masks:
        kind = bf16 if mask else f32
        share = local_call(share_body, shape((tok_rows, key_cols), kind), blocks[mask], weight, flops=flops)
        shares.append(flipped(share, MEMBERS, mask) if mask else share)
    key_out, key_grad = local_call(
        norm_body, [shape((tok_rows, key_cols), bf16)] * 2, *shares, cotangent
    )

    grads = [key_grad] + [flipped(key_grad, MEMBERS, mask) for mask in masks[1:]]
    columns = []
    for mask in masks:
        column = local_call(columns_body, shape((tok_rows, owned), bf16), grads[mask], weight, flops=flops)
        columns.append(flipped(column, MEMBERS, mask) if mask else column)

    terms = local_call(
        functools.partial(terms_body, members, grad_scale),
        [shape((line, rows, key_cols), kind) for kind in (f32, bf16)],
        *blocks,
        *grads,
        flops=members * flops,
    )
    sums = local_call(
        merge_body,
        [shape((rows, key_cols), f32)] + [shape((rows, key_cols), bf16)] * (line - 1),
        terms[0],
        flipped(terms[1], "twin", 1),
    )
    met = [sums[0]] + [rotated(sums[step], "line", -step) for step in range(1, line)]
    weight_grad = local_call(sum_body, shape((rows, key_cols), f32), *met)
    if outer > 1:
        weight_grad = lax.psum_scatter(weight_grad, "outer", scatter_dimension=0, tiled=True)

    input_grad = local_call(
        functools.partial(unpack_body, masks), shape((tok_rows, width), bf16), *columns
    )
    if outer > 1:
        input_grad = join_runs(input_grad, outer)
    return (key_out, input_grad, weight_grad)


def solution(mesh):
    replicas, group = mesh.shape["dp"], mesh.shape["inner"]
    near = math.gcd(replicas, 2 * TWIN)
    pair = math.gcd(group, 2)
    fine = Mesh(
        mesh.devices.reshape(replicas // near, near // TWIN, TWIN, group // pair, pair),
        ("outer", "side", "twin", "line", "pair"),
    )
    rows = P(("outer", "side", "twin", "line", "pair"), None)
    return jax.shard_map(
        per_device,
        mesh=fine,
        in_specs=(rows, P(("line", "pair"), None), rows),
        out_specs=(rows, rows, P(("line", "pair", "outer", "side", "twin"), None)),
        check_vma=False,
    )
```

time: 65.9 us -> 64.7 us (0.982)
  starting transfers between devices: 28.4 us -> 25 us
  waiting for transfers between devices: 27.2 us -> 29.3 us
    ppermute x6 -> x4, starting transfers between devices: 10.5 us -> 7 us  [rotated(): lax.ppermute(block, axis, [(i, (i + step) % size) for i in range(size)])]
    ppermute x6 -> x4, waiting for transfers between devices: 9.22 us -> 12.1 us  [rotated(): lax.ppermute(block, axis, [(i, (i + step) % size) for i in range(size)])]
    ppermute x0 -> x1, starting transfers between devices: none -> 1.58 us  [parted(): return lax.ppermute(block, ('twin', 'line'), list(enumerate(to)))]
    ppermute x16 -> x15, starting transfers between devices: 17.9 us -> 16.4 us  [flipped(): return lax.ppermute(block, axes, [(i, i ^ mask) for i in range(size)])]
    unnamed x4 -> x6, local copies, waits for them, and re-layouts: 1.23 us -> 2.27 us
    dynamic_slice x1 -> x0, local copies, waits for them, and re-layouts: 0.99 us -> none  [per_device(): lax.dynamic_slice_in_dim(runs, (first ^ 1) * rows, rows, axis=0)]
    ppermute x16 -> x15, waiting for transfers between devices: 18 us -> 17.2 us  [flipped(): return lax.ppermute(block, axes, [(i, i ^ mask) for i in range(size)])]
    pallas_call x15 -> x16, Pallas kernels: 7.11 us -> 7.16 us  [local_call(): pl.pallas_call(body, out_shape=out_shapes, in_specs=[vmem] * len(args), o...]
  transfers between devices with their start and end apart: 22 -> 20, of which waited for: 13 -> 12; matrix products, arithmetic and copies ran while one was open for 0% -> 0% of each run, Pallas kernels for 7% -> 6%
where the time goes in v5:
time: 64.7 us; the launch traced here: 64.5 us
  waiting for transfers between devices  29.3 us (45%)
  starting transfers between devices  25 us (39%)
  Pallas kernels  7.16 us (11%)
  local copies, waits for them, and re-layouts  2.27 us (4%)
  between operations  0.78 us (1%)
    ppermute x15, waiting for transfers between devices, flipped(): return lax.ppermute(block, axes, [(i, i ^ mask) for i in range(size)])  17.2 us
    ppermute x15, starting transfers between devices, flipped(): return lax.ppermute(block, axes, [(i, i ^ mask) for i in range(size)])  16.4 us
    ppermute x4, waiting for transfers between devices, rotated(): lax.ppermute(block, axis, [(i, (i + step) % size) for i in range(size)])  12.1 us
    pallas_call x16, Pallas kernels, local_call(): pl.pallas_call(body, out_shape=out_shapes, in_specs=[vmem] * len(args), o...  7.16 us
    ppermute x4, starting transfers between devices, rotated(): lax.ppermute(block, axis, [(i, (i + step) % size) for i in range(size)])  7 us
    unnamed x6, local copies, waits for them, and re-layouts  2.27 us
    ppermute x1, starting transfers between devices, parted(): return lax.ppermute(block, ('twin', 'line'), list(enumerate(to)))  1.58 us
  transfers between devices with their start and end apart: 20, of which 12 were waited for; matrix products, arithmetic and copies ran while one was open for 0% of the time, Pallas kernels for 6%

profile of v5, /device:TPU:0, one launch (start us, length us, event | category | flops | bytes accessed | tf_op | source)
XLA Modules:
  0.0 64.5 jit_solution(15946195414589649853)
XLA Ops:
  0.6 1.2 %copy-done = bf16[128,4096]{1,0:T(8,128)(2,1)S(1)} copy-done((bf16[128,4096]{1,0:T(8,128)(2,1)S(1)}, bf16[128,4096]{1,0:T(8,128)(2,1)}, u32[]{:S(2)}) %copy-start) | copy-done | bytes 1048600
  1.9 1.0 %copy-done.1 = bf16[512,512]{1,0:T(8,128)(2,1)S(1)} copy-done((bf16[512,512]{1,0:T(8,128)(2,1)S(1)}, bf16[512,512]{1,0:T(8,128)(2,1)}, u32[]{:S(2)}) %copy-start.1) | copy-done | bytes 524312
  3.0 4.0 %collective-permute-start.4 = (bf16[128,1024]{1,0:T(8,128)(2,1)S(1)}, bf16[128,1024]{1,0:T(8,128)(2,1)S(1)}, u32[]{:S(2)}, u32[]{:S(2)}) collective-permute-start(bf16[128,1024]{1,0:T(8,128)(2,1)S(1)} %get-tuple-element.24._), channel_id=1, source_target_pairs={{0,17},{1,16},{16,1},{17,0},{2,19},{3,18},{18,3},{19,2},{4,21},{5,... | collective-permute-start | bytes 786440 | tf_op jit(solution)/shard_map/ppermute | solution.py:42
  7.0 1.6 %collective-permute-start = (bf16[256,512]{1,0:T(8,128)(2,1)S(1)}, bf16[256,512]{1,0:T(8,128)(2,1)S(1)}, u32[]{:S(2)}, u32[]{:S(2)}) collective-permute-start(bf16[256,512]{1,0:T(8,128)(2,1)S(1)} %get-tuple-element.23.both.refs_0_), channel_id=1, source_target_pairs={{0,2},{2,4},{4,6},{6,0},{8,14},{10,8},{12,10},{14,12},{1,3},{3,5},... | collective-permute-start | bytes 786440 | tf_op jit(solution)/shard_map/ppermute | solution.py:103
  8.8 0.6 collective-permute-start.2
  9.3 0.5 collective-permute-start.3
  9.9 2.6 %collective-permute-start.1 = (bf16[128,512]{1,0:T(8,128)(2,1)S(1)}, bf16[128,512]{1,0:T(8,128)(2,1)S(1)}, u32[]{:S(2)}, u32[]{:S(2)}) collective-permute-start(bf16[128,512]{1,0:T(8,128)(2,1)S(1)} %get-tuple-element.25), channel_id=1, source_target_pairs={{0,4},{2,6},{4,0},{6,2},{1,5},{3,7},{5,1},{7,3},{8,12},{10,14},{12... | collective-permute-start | bytes 393224 | tf_op jit(solution)/shard_map/ppermute | solution.py:37
  12.5 9.2 %collective-permute-done.1.refs_3_ = bf16[128,512]{1,0:T(8,128)(2,1)S(1)} collective-permute-done((bf16[128,512]{1,0:T(8,128)(2,1)S(1)}, bf16[128,512]{1,0:T(8,128)(2,1)S(1)}, u32[]{:S(2)}, u32[]{:S(2)}) %collective-permute-start.1) | collective-permute-done | bytes 131104 | tf_op jit(solution)/shard_map/ppermute | solution.py:37
  22.2 1.2 %collective-permute-done.6.refs_4_ = bf16[128,512]{1,0:T(8,128)(2,1)S(1)} collective-permute-done((bf16[128,512]{1,0:T(8,128)(2,1)S(1)}, bf16[128,512]{1,0:T(8,128)(2,1)S(1)}, u32[]{:S(2)}, u32[]{:S(2)}) %collective-permute-start.6) | collective-permute-done | bytes 131104 | tf_op jit(solution)/shard_map/ppermute | solution.py:42
  24.5 1.1 %collective-permute-start.7 = (bf16[128,512]{1,0:T(8,128)(2,1)S(1)}, bf16[128,512]{1,0:T(8,128)(2,1)S(1)}, u32[]{:S(2)}, u32[]{:S(2)}) collective-permute-start(bf16[128,512]{1,0:T(8,128)(2,1)S(1)} %shard_map.62), channel_id=1, source_target_pairs={{0,1},{1,0},{16,17},{17,16},{2,3},{3,2},{18,19},{19,18},{4,5},{5,4... | collective-permute-start | bytes 393224 | tf_op jit(solution)/shard_map/ppermute | solution.py:42
  25.6 0.7 %collective-permute-start.8 = (bf16[128,512]{1,0:T(8,128)(2,1)S(1)}, bf16[128,512]{1,0:T(8,128)(2,1)S(1)}, u32[]{:S(2)}, u32[]{:S(2)}) collective-permute-start(bf16[128,512]{1,0:T(8,128)(2,1)S(1)} %shard_map.63), channel_id=1, source_target_pairs={{0,16},{1,17},{16,0},{17,1},{2,18},{3,19},{18,2},{19,3},{4,20},{5,... | collective-permute-start | bytes 393224 | tf_op jit(solution)/shard_map/ppermute | solution.py:42
  26.3 1.7 %collective-permute-start.9 = (bf16[128,512]{1,0:T(8,128)(2,1)S(1)}, bf16[128,512]{1,0:T(8,128)(2,1)S(1)}, u32[]{:S(2)}, u32[]{:S(2)}) collective-permute-start(bf16[128,512]{1,0:T(8,128)(2,1)S(1)} %shard_map.64), channel_id=1, source_target_pairs={{0,17},{1,16},{16,1},{17,0},{2,19},{3,18},{18,3},{19,2},{4,21},{5,... | collective-permute-start | bytes 393224 | tf_op jit(solution)/shard_map/ppermute | solution.py:42
  28.4 1.7 %collective-permute-done.7.refs_1_ = bf16[128,512]{1,0:T(8,128)(2,1)S(1)} collective-permute-done((bf16[128,512]{1,0:T(8,128)(2,1)S(1)}, bf16[128,512]{1,0:T(8,128)(2,1)S(1)}, u32[]{:S(2)}, u32[]{:S(2)}) %collective-permute-start.7) | collective-permute-done | bytes 131104 | tf_op jit(solution)/shard_map/ppermute | solution.py:42
  30.1 1.9 %collective-permute-done.8.refs_2_ = bf16[128,512]{1,0:T(8,128)(2,1)S(1)} collective-permute-done((bf16[128,512]{1,0:T(8,128)(2,1)S(1)}, bf16[128,512]{1,0:T(8,128)(2,1)S(1)}, u32[]{:S(2)}, u32[]{:S(2)}) %collective-permute-start.8) | collective-permute-done | bytes 131104 | tf_op jit(solution)/shard_map/ppermute | solution.py:42
  32.0 2.1 %collective-permute-done.9.refs_3_ = bf16[128,512]{1,0:T(8,128)(2,1)S(1)} collective-permute-done((bf16[128,512]{1,0:T(8,128)(2,1)S(1)}, bf16[128,512]{1,0:T(8,128)(2,1)S(1)}, u32[]{:S(2)}, u32[]{:S(2)}) %collective-permute-start.9) | collective-permute-done | bytes 131104 | tf_op jit(solution)/shard_map/ppermute | solution.py:42
  34.1 0.8 %shard_map.65 = (bf16[128,512]{1,0:T(8,128)(2,1)}, bf16[128,512]{1,0:T(8,128)(2,1)S(1)}) custom-call(f32[128,512]{1,0:T(8,128)S(1)} %shard_map.61.refs_0_, bf16[128,512]{1,0:T(8,128)(2,1)S(1)} %collective-permute-done.7.refs_1_, bf16[128,512]{1,0:T(8,128)(2,1)S(1)} %collective-permute-done.8.refs_2_, bf16[128,512]{1,0:T(8,128)(2,1)S(1)} %collective-permute-done.9.refs_3_, ...), custom_call_target="tpu_custom_call" | custom-call | bytes 786432 | tf_op jit(solution)/shard_map/pallas_call | solution.py:25
  34.9 1.2 %collective-permute-start.14 = (bf16[128,512]{1,0:T(8,128)(2,1)S(1)}, bf16[128,512]{1,0:T(8,128)(2,1)S(1)}, u32[]{:S(2)}, u32[]{:S(2)}) collective-permute-start(bf16[128,512]{1,0:T(8,128)(2,1)S(1)} %get-tuple-element.36.grad.refs_4_), channel_id=1, source_target_pairs={{0,17},{1,16},{16,1},{17,0},{2,19},{3,18},{18,3},{19,2},{4,21},{5,... | collective-permute-start | bytes 393224 | tf_op jit(solution)/shard_map/ppermute | solution.py:42
  36.1 1.3 %collective-permute-start.12 = (bf16[128,512]{1,0:T(8,128)(2,1)S(1)}, bf16[128,512]{1,0:T(8,128)(2,1)S(1)}, u32[]{:S(2)}, u32[]{:S(2)}) collective-permute-start(bf16[128,512]{1,0:T(8,128)(2,1)S(1)} %get-tuple-element.36.grad.refs_4_), channel_id=1, source_target_pairs={{0,16},{1,17},{16,0},{17,1},{2,18},{3,19},{18,2},{19,3},{4,20},{5,... | collective-permute-start | bytes 393224 | tf_op jit(solution)/shard_map/ppermute | solution.py:42
  37.4 1.0 %collective-permute-start.10 = (bf16[128,512]{1,0:T(8,128)(2,1)S(1)}, bf16[128,512]{1,0:T(8,128)(2,1)S(1)}, u32[]{:S(2)}, u32[]{:S(2)}) collective-permute-start(bf16[128,512]{1,0:T(8,128)(2,1)S(1)} %get-tuple-element.36.grad.refs_4_), channel_id=1, source_target_pairs={{0,1},{1,0},{16,17},{17,16},{2,3},{3,2},{18,19},{19,18},{4,5},{5,4... | collective-permute-start | bytes 393224 | tf_op jit(solution)/shard_map/ppermute | solution.py:42
  38.4 3.3 %collective-permute-done.14.grad.refs_7_ = bf16[128,512]{1,0:T(8,128)(2,1)S(1)} collective-permute-done((bf16[128,512]{1,0:T(8,128)(2,1)S(1)}, bf16[128,512]{1,0:T(8,128)(2,1)S(1)}, u32[]{:S(2)}, u32[]{:S(2)}) %collective-permute-start.14) | collective-permute-done | bytes 131104 | tf_op jit(solution)/shard_map/ppermute | solution.py:42
  41.7 0.9 %collective-permute-done.12.grad.refs_6_ = bf16[128,512]{1,0:T(8,128)(2,1)S(1)} collective-permute-done((bf16[128,512]{1,0:T(8,128)(2,1)S(1)}, bf16[128,512]{1,0:T(8,128)(2,1)S(1)}, u32[]{:S(2)}, u32[]{:S(2)}) %collective-permute-start.12) | collective-permute-done | bytes 131104 | tf_op jit(solution)/shard_map/ppermute | solution.py:42
  43.0 0.7 %shard_map.71 = (f32[4,128,512]{2,1,0:T(8,128)S(1)}, bf16[4,128,512]{2,1,0:T(8,128)(2,1)S(1)}) custom-call(bf16[128,1024]{1,0:T(8,128)(2,1)S(1)} %get-tuple-element.29.block.refs_0_, bf16[128,1024]{1,0:T(8,128)(2,1)S(1)} %collective-permute-done.2.block.refs_1_, bf16[128,1024]{1,0:T(8,128)(2,1)S(1)} %collective-permute-done.3.block.refs_2_, ...), custom_call_target="tpu_custom_call" | custom-call | flops 536870912 | bytes 1572864 | tf_op jit(solution)/shard_map/pallas_call | solution.py:25
  44.3 1.2 %collective-permute-start.15 = (bf16[128,1024]{1,0:T(8,128)(2,1)S(1)}, bf16[128,1024]{1,0:T(8,128)(2,1)S(1)}, u32[]{:S(2)}, u32[]{:S(2)}) collective-permute-start(bf16[128,1024]{1,0:T(8,128)(2,1)S(1)} %shard_map.69), channel_id=1, source_target_pairs={{0,17},{1,16},{16,1},{17,0},{2,19},{3,18},{18,3},{19,2},{4,21},{5,... | collective-permute-start | bytes 786440 | tf_op jit(solution)/shard_map/ppermute | solution.py:42
  46.0 1.4 %collective-permute-start.13 = (bf16[128,1024]{1,0:T(8,128)(2,1)S(1)}, bf16[128,1024]{1,0:T(8,128)(2,1)S(1)}, u32[]{:S(2)}, u32[]{:S(2)}) collective-permute-start(bf16[128,1024]{1,0:T(8,128)(2,1)S(1)} %shard_map.68), channel_id=1, source_target_pairs={{0,16},{1,17},{16,0},{17,1},{2,18},{3,19},{18,2},{19,3},{4,20},{5,... | collective-permute-start | bytes 786440 | tf_op jit(solution)/shard_map/ppermute | solution.py:42
  47.9 1.1 %collective-permute-start.11 = (bf16[128,1024]{1,0:T(8,128)(2,1)S(1)}, bf16[128,1024]{1,0:T(8,128)(2,1)S(1)}, u32[]{:S(2)}, u32[]{:S(2)}) collective-permute-start(bf16[128,1024]{1,0:T(8,128)(2,1)S(1)} %shard_map.67), channel_id=1, source_target_pairs={{0,1},{1,0},{16,17},{17,16},{2,3},{3,2},{18,19},{19,18},{4,5},{5,4... | collective-permute-start | bytes 786440 | tf_op jit(solution)/shard_map/ppermute | solution.py:42
  49.1 3.6 %collective-permute-start.17 = (bf16[128,512]{1,0:T(8,128)(2,1)S(1)}, bf16[128,512]{1,0:T(8,128)(2,1)S(1)}, u32[]{:S(2)}, u32[]{:S(2)}) collective-permute-start(bf16[128,512]{1,0:T(8,128)(2,1)S(1)} %get-tuple-element.40), channel_id=1, source_target_pairs={{0,6},{2,0},{4,2},{6,4},{1,7},{3,1},{5,3},{7,5},{8,14},{10,8},{12,... | collective-permute-start | bytes 393224 | tf_op jit(solution)/shard_map/ppermute | solution.py:37
  52.7 1.7 %collective-permute-done.15.refs_3_ = bf16[128,1024]{1,0:T(8,128)(2,1)S(1)} collective-permute-done((bf16[128,1024]{1,0:T(8,128)(2,1)S(1)}, bf16[128,1024]{1,0:T(8,128)(2,1)S(1)}, u32[]{:S(2)}, u32[]{:S(2)}) %collective-permute-start.15) | collective-permute-done | bytes 262176 | tf_op jit(solution)/shard_map/ppermute | solution.py:42
  54.4 0.8 %collective-permute-start.19 = (bf16[128,512]{1,0:T(8,128)(2,1)S(1)}, bf16[128,512]{1,0:T(8,128)(2,1)S(1)}, u32[]{:S(2)}, u32[]{:S(2)}) collective-permute-start(bf16[128,512]{1,0:T(8,128)(2,1)S(1)} %get-tuple-element.42), channel_id=1, source_target_pairs={{0,2},{2,4},{4,6},{6,0},{1,3},{3,5},{5,7},{7,1},{8,10},{10,12},{12... | collective-permute-start | bytes 393224 | tf_op jit(solution)/shard_map/ppermute | solution.py:37
  55.7 3.5 %collective-permute-done.13.refs_2_ = bf16[128,1024]{1,0:T(8,128)(2,1)S(1)} collective-permute-done((bf16[128,1024]{1,0:T(8,128)(2,1)S(1)}, bf16[128,1024]{1,0:T(8,128)(2,1)S(1)}, u32[]{:S(2)}, u32[]{:S(2)}) %collective-permute-start.13) | collective-permute-done | bytes 262176 | tf_op jit(solution)/shard_map/ppermute | solution.py:42
  59.6 1.2 %shard_map.70 = bf16[128,4096]{1,0:T(8,128)(2,1)} custom-call(bf16[128,1024]{1,0:T(8,128)(2,1)S(1)} %shard_map.66.refs_0_, bf16[128,1024]{1,0:T(8,128)(2,1)S(1)} %collective-permute-done.11.refs_1_, bf16[128,1024]{1,0:T(8,128)(2,1)S(1)} %collective-permute-done.13.refs_2_, bf16[128,1024]{1,0:T(8,128)(2,1)S(1)} %collective-permute-done.15.refs_3_), custom_call_target="tpu_custom_call" | custom-call | bytes 1048576 | tf_op jit(solution)/shard_map/pallas_call | solution.py:25
  60.8 2.9 %collective-permute-done.18.refs_2_ = bf16[128,512]{1,0:T(8,128)(2,1)S(1)} collective-permute-done((bf16[128,512]{1,0:T(8,128)(2,1)S(1)}, bf16[128,512]{1,0:T(8,128)(2,1)S(1)}, u32[]{:S(2)}, u32[]{:S(2)}) %collective-permute-start.18) | collective-permute-done | bytes 131104 | tf_op jit(solution)/shard_map/ppermute | solution.py:37
  63.7 0.8 %shard_map.73 = f32[128,512]{1,0:T(8,128)} custom-call(f32[128,512]{1,0:T(8,128)S(1)} %get-tuple-element.39.refs_0_, bf16[128,512]{1,0:T(8,128)(2,1)S(1)} %collective-permute-done.17.refs_1_, bf16[128,512]{1,0:T(8,128)(2,1)S(1)} %collective-permute-done.18.refs_2_, bf16[128,512]{1,0:T(8,128)(2,1)S(1)} %collective-permute-done.19.refs_3_), custom_call_target="tpu_custom_call" | custom-call | bytes 655360 | tf_op jit(solution)/shard_map/pallas_call | solution.py:25
  (30 shorter events, 5.1 us)
Async XLA Ops:
  0.6 1.2 %copy-start = (bf16[128,4096]{1,0:T(8,128)(2,1)S(1)}, bf16[128,4096]{1,0:T(8,128)(2,1)}, u32[]{:S(2)}) copy-start(bf16[128,4096]{1,0:T(8,128)(2,1)} %tokens.3) | copy-start | bytes 3145732
  1.9 1.0 %copy-start.1 = (bf16[512,512]{1,0:T(8,128)(2,1)S(1)}, bf16[512,512]{1,0:T(8,128)(2,1)}, u32[]{:S(2)}) copy-start(bf16[512,512]{1,0:T(8,128)(2,1)} %shard.1) | copy-start | bytes 1572868
  3.0 18.7 %collective-permute-start.4 = (bf16[128,1024]{1,0:T(8,128)(2,1)S(1)}, bf16[128,1024]{1,0:T(8,128)(2,1)S(1)}, u32[]{:S(2)}, u32[]{:S(2)}) collective-permute-start(bf16[128,1024]{1,0:T(8,128)(2,1)S(1)} %get-tuple-element.24._), channel_id=1, source_target_pairs={{0,17},{1,16},{16,1},{17,0},{2,19},{3,18},{18,3},{19,2},{4,21},{5,... | collective-permute-start | bytes 786440 | tf_op jit(solution)/shard_map/ppermute | solution.py:42
  7.0 14.7 %collective-permute-start = (bf16[256,512]{1,0:T(8,128)(2,1)S(1)}, bf16[256,512]{1,0:T(8,128)(2,1)S(1)}, u32[]{:S(2)}, u32[]{:S(2)}) collective-permute-start(bf16[256,512]{1,0:T(8,128)(2,1)S(1)} %get-tuple-element.23.both.refs_0_), channel_id=1, source_target_pairs={{0,2},{2,4},{4,6},{6,0},{8,14},{10,8},{12,10},{14,12},{1,3},{3,5},... | collective-permute-start | bytes 786440 | tf_op jit(solution)/shard_map/ppermute | solution.py:103
  8.8 12.9 %collective-permute-start.2 = (bf16[128,1024]{1,0:T(8,128)(2,1)S(1)}, bf16[128,1024]{1,0:T(8,128)(2,1)S(1)}, u32[]{:S(2)}, u32[]{:S(2)}) collective-permute-start(bf16[128,1024]{1,0:T(8,128)(2,1)S(1)} %get-tuple-element.27), channel_id=1, source_target_pairs={{0,1},{1,0},{16,17},{17,16},{2,3},{3,2},{18,19},{19,18},{4,5},{5,4... | collective-permute-start | bytes 786440 | tf_op jit(solution)/shard_map/ppermute | solution.py:42
  9.3 12.3 %collective-permute-start.3 = (bf16[128,1024]{1,0:T(8,128)(2,1)S(1)}, bf16[128,1024]{1,0:T(8,128)(2,1)S(1)}, u32[]{:S(2)}, u32[]{:S(2)}) collective-permute-start(bf16[128,1024]{1,0:T(8,128)(2,1)S(1)} %get-tuple-element.28), channel_id=1, source_target_pairs={{0,16},{1,17},{16,0},{17,1},{2,18},{3,19},{18,2},{19,3},{4,20},{5,... | collective-permute-start | bytes 786440 | tf_op jit(solution)/shard_map/ppermute | solution.py:42
  9.9 11.8 %collective-permute-start.1 = (bf16[128,512]{1,0:T(8,128)(2,1)S(1)}, bf16[128,512]{1,0:T(8,128)(2,1)S(1)}, u32[]{:S(2)}, u32[]{:S(2)}) collective-permute-start(bf16[128,512]{1,0:T(8,128)(2,1)S(1)} %get-tuple-element.25), channel_id=1, source_target_pairs={{0,4},{2,6},{4,0},{6,2},{1,5},{3,7},{5,1},{7,3},{8,12},{10,14},{12... | collective-permute-start | bytes 393224 | tf_op jit(solution)/shard_map/ppermute | solution.py:37
  21.7 1.8 %collective-permute-start.5 = (bf16[256,512]{1,0:T(8,128)(2,1)S(1)}, bf16[256,512]{1,0:T(8,128)(2,1)S(1)}, u32[]{:S(2)}, u32[]{:S(2)}) collective-permute-start(bf16[256,512]{1,0:T(8,128)(2,1)S(1)} %collective-permute-done.refs_1_), channel_id=1, source_target_pairs={{0,8},{8,0},{1,9},{9,1},{2,10},{10,2},{3,11},{11,3},{4,12},{12,4},... | collective-permute-start | bytes 786440 | tf_op jit(solution)/shard_map/ppermute | solution.py:42
  21.7 1.7 %collective-permute-start.6 = (bf16[128,512]{1,0:T(8,128)(2,1)S(1)}, bf16[128,512]{1,0:T(8,128)(2,1)S(1)}, u32[]{:S(2)}, u32[]{:S(2)}) collective-permute-start(bf16[128,512]{1,0:T(8,128)(2,1)S(1)} %collective-permute-done.1.refs_3_), channel_id=1, source_target_pairs={{0,8},{8,0},{1,9},{9,1},{2,10},{10,2},{3,11},{11,3},{4,12},{12,4},... | collective-permute-start | bytes 393224 | tf_op jit(solution)/shard_map/ppermute | solution.py:42
  24.5 9.6 %copy-start.2 = (bf16[128,512]{1,0:T(8,128)(2,1)S(1)}, bf16[128,512]{1,0:T(8,128)(2,1)}, u32[]{:S(2)}) copy-start(bf16[128,512]{1,0:T(8,128)(2,1)} %refs_4_.1) | copy-start | bytes 393220
  24.5 5.6 %collective-permute-start.7 = (bf16[128,512]{1,0:T(8,128)(2,1)S(1)}, bf16[128,512]{1,0:T(8,128)(2,1)S(1)}, u32[]{:S(2)}, u32[]{:S(2)}) collective-permute-start(bf16[128,512]{1,0:T(8,128)(2,1)S(1)} %shard_map.62), channel_id=1, source_target_pairs={{0,1},{1,0},{16,17},{17,16},{2,3},{3,2},{18,19},{19,18},{4,5},{5,4... | collective-permute-start | bytes 393224 | tf_op jit(solution)/shard_map/ppermute | solution.py:42
  25.6 6.4 %collective-permute-start.8 = (bf16[128,512]{1,0:T(8,128)(2,1)S(1)}, bf16[128,512]{1,0:T(8,128)(2,1)S(1)}, u32[]{:S(2)}, u32[]{:S(2)}) collective-permute-start(bf16[128,512]{1,0:T(8,128)(2,1)S(1)} %shard_map.63), channel_id=1, source_target_pairs={{0,16},{1,17},{16,0},{17,1},{2,18},{3,19},{18,2},{19,3},{4,20},{5,... | collective-permute-start | bytes 393224 | tf_op jit(solution)/shard_map/ppermute | solution.py:42
  26.3 7.8 %collective-permute-start.9 = (bf16[128,512]{1,0:T(8,128)(2,1)S(1)}, bf16[128,512]{1,0:T(8,128)(2,1)S(1)}, u32[]{:S(2)}, u32[]{:S(2)}) collective-permute-start(bf16[128,512]{1,0:T(8,128)(2,1)S(1)} %shard_map.64), channel_id=1, source_target_pairs={{0,17},{1,16},{16,1},{17,0},{2,19},{3,18},{18,3},{19,2},{4,21},{5,... | collective-permute-start | bytes 393224 | tf_op jit(solution)/shard_map/ppermute | solution.py:42
  34.9 6.8 %collective-permute-start.14 = (bf16[128,512]{1,0:T(8,128)(2,1)S(1)}, bf16[128,512]{1,0:T(8,128)(2,1)S(1)}, u32[]{:S(2)}, u32[]{:S(2)}) collective-permute-start(bf16[128,512]{1,0:T(8,128)(2,1)S(1)} %get-tuple-element.36.grad.refs_4_), channel_id=1, source_target_pairs={{0,17},{1,16},{16,1},{17,0},{2,19},{3,18},{18,3},{19,2},{4,21},{5,... | collective-permute-start | bytes 393224 | tf_op jit(solution)/shard_map/ppermute | solution.py:42
  36.1 6.5 %collective-permute-start.12 = (bf16[128,512]{1,0:T(8,128)(2,1)S(1)}, bf16[128,512]{1,0:T(8,128)(2,1)S(1)}, u32[]{:S(2)}, u32[]{:S(2)}) collective-permute-start(bf16[128,512]{1,0:T(8,128)(2,1)S(1)} %get-tuple-element.36.grad.refs_4_), channel_id=1, source_target_pairs={{0,16},{1,17},{16,0},{17,1},{2,18},{3,19},{18,2},{19,3},{4,20},{5,... | collective-permute-start | bytes 393224 | tf_op jit(solution)/shard_map/ppermute | solution.py:42
  37.4 5.6 %collective-permute-start.10 = (bf16[128,512]{1,0:T(8,128)(2,1)S(1)}, bf16[128,512]{1,0:T(8,128)(2,1)S(1)}, u32[]{:S(2)}, u32[]{:S(2)}) collective-permute-start(bf16[128,512]{1,0:T(8,128)(2,1)S(1)} %get-tuple-element.36.grad.refs_4_), channel_id=1, source_target_pairs={{0,1},{1,0},{16,17},{17,16},{2,3},{3,2},{18,19},{19,18},{4,5},{5,4... | collective-permute-start | bytes 393224 | tf_op jit(solution)/shard_map/ppermute | solution.py:42
  43.8 5.2 %collective-permute-start.16 = (bf16[4,128,512]{2,1,0:T(8,128)(2,1)S(1)}, bf16[4,128,512]{2,1,0:T(8,128)(2,1)S(1)}, u32[]{:S(2)}, u32[]{:S(2)}) collective-permute-start(bf16[4,128,512]{2,1,0:T(8,128)(2,1)S(1)} %get-tuple-element.38), channel_id=1, source_target_pairs={{0,8},{8,0},{1,9},{9,1},{2,10},{10,2},{3,11},{11,3},{4,12},{12,4},... | collective-permute-start | bytes 1572872 | tf_op jit(solution)/shard_map/ppermute | solution.py:42
  44.3 10.1 %collective-permute-start.15 = (bf16[128,1024]{1,0:T(8,128)(2,1)S(1)}, bf16[128,1024]{1,0:T(8,128)(2,1)S(1)}, u32[]{:S(2)}, u32[]{:S(2)}) collective-permute-start(bf16[128,1024]{1,0:T(8,128)(2,1)S(1)} %shard_map.69), channel_id=1, source_target_pairs={{0,17},{1,16},{16,1},{17,0},{2,19},{3,18},{18,3},{19,2},{4,21},{5,... | collective-permute-start | bytes 786440 | tf_op jit(solution)/shard_map/ppermute | solution.py:42
  46.0 13.2 %collective-permute-start.13 = (bf16[128,1024]{1,0:T(8,128)(2,1)S(1)}, bf16[128,1024]{1,0:T(8,128)(2,1)S(1)}, u32[]{:S(2)}, u32[]{:S(2)}) collective-permute-start(bf16[128,1024]{1,0:T(8,128)(2,1)S(1)} %shard_map.68), channel_id=1, source_target_pairs={{0,16},{1,17},{16,0},{17,1},{2,18},{3,19},{18,2},{19,3},{4,20},{5,... | collective-permute-start | bytes 786440 | tf_op jit(solution)/shard_map/ppermute | solution.py:42
  47.9 11.7 %collective-permute-start.11 = (bf16[128,1024]{1,0:T(8,128)(2,1)S(1)}, bf16[128,1024]{1,0:T(8,128)(2,1)S(1)}, u32[]{:S(2)}, u32[]{:S(2)}) collective-permute-start(bf16[128,1024]{1,0:T(8,128)(2,1)S(1)} %shard_map.67), channel_id=1, source_target_pairs={{0,1},{1,0},{16,17},{17,16},{2,3},{3,2},{18,19},{19,18},{4,5},{5,4... | collective-permute-start | bytes 786440 | tf_op jit(solution)/shard_map/ppermute | solution.py:42
  49.1 11.8 %collective-permute-start.17 = (bf16[128,512]{1,0:T(8,128)(2,1)S(1)}, bf16[128,512]{1,0:T(8,128)(2,1)S(1)}, u32[]{:S(2)}, u32[]{:S(2)}) collective-permute-start(bf16[128,512]{1,0:T(8,128)(2,1)S(1)} %get-tuple-element.40), channel_id=1, source_target_pairs={{0,6},{2,0},{4,2},{6,4},{1,7},{3,1},{5,3},{7,5},{8,14},{10,8},{12,... | collective-permute-start | bytes 393224 | tf_op jit(solution)/shard_map/ppermute | solution.py:37
  52.7 11.0 %collective-permute-start.18 = (bf16[128,512]{1,0:T(8,128)(2,1)S(1)}, bf16[128,512]{1,0:T(8,128)(2,1)S(1)}, u32[]{:S(2)}, u32[]{:S(2)}) collective-permute-start(bf16[128,512]{1,0:T(8,128)(2,1)S(1)} %get-tuple-element.41), channel_id=1, source_target_pairs={{0,4},{2,6},{4,0},{6,2},{1,5},{3,7},{5,1},{7,3},{8,12},{10,14},{12... | collective-permute-start | bytes 393224 | tf_op jit(solution)/shard_map/ppermute | solution.py:37
  54.4 9.3 %collective-permute-start.19 = (bf16[128,512]{1,0:T(8,128)(2,1)S(1)}, bf16[128,512]{1,0:T(8,128)(2,1)S(1)}, u32[]{:S(2)}, u32[]{:S(2)}) collective-permute-start(bf16[128,512]{1,0:T(8,128)(2,1)S(1)} %get-tuple-element.42), channel_id=1, source_target_pairs={{0,2},{2,4},{4,6},{6,0},{1,3},{3,5},{5,7},{7,1},{8,10},{10,12},{12... | collective-permute-start | bytes 393224 | tf_op jit(solution)/shard_map/ppermute | solution.py:37

commit v6 on v5

--- a/solution.py
+++ b/solution.py
@@ -18,16 +18,17 @@
 bf16, f32 = jnp.bfloat16, jnp.float32
 
 
-def local_call(body, out_shapes, *args, flops=0):
+def local_call(body, out_shapes, *args, flops=0, space=pltpu.VMEM, scratch=(), room=32):
     vmem = pl.BlockSpec(memory_space=pltpu.VMEM)
     many = isinstance(out_shapes, (list, tuple))
     moved = sum(math.prod(a.shape) * a.dtype.itemsize for a in args)
     return pl.pallas_call(
         body,
         out_shape=out_shapes,
-        in_specs=[vmem] * len(args),
+        in_specs=[pl.BlockSpec(memory_space=space)] * len(args),
         out_specs=[vmem] * len(out_shapes) if many else vmem,
-        compiler_params=pltpu.CompilerParams(vmem_limit_bytes=32 << 20),
+        scratch_shapes=scratch,
+        compiler_params=pltpu.CompilerParams(vmem_limit_bytes=room << 20),
         cost_estimate=pl.CostEstimate(flops=flops, bytes_accessed=moved, transcendentals=0),
     )(*args)
 
@@ -58,17 +59,21 @@
         block[:, part * run : (part + 1) * run] = tokens[:, pl.ds(start, run)]
 
 
-def first_body(mask, tokens, shard, both, block):
-    rows = both.shape[0]
-    both[...] = shard[pl.ds(pl.multiple_of(lax.axis_index("side") * rows, rows), rows), :]
-    pack(mask, tokens, block)
-
-
-def second_body(masks, tokens, both, _, mine, *blocks):
-    rows = mine.shape[0]
-    mine[...] = both[pl.ds(pl.multiple_of(lax.axis_index("twin") * rows, rows), rows), :]
+def front_body(masks, tokens_hbm, shard, both, mine, *refs):
+    *blocks, tokens, arrived = refs
+    copies = [pltpu.make_async_copy(tokens_hbm, tokens, arrived.at[0])]
+    rows, half = mine.shape[0], both.shape[0]
+    first = lax.axis_index("side") * half
+    for i, (target, start) in enumerate(((both, first), (mine, first + lax.axis_index("twin") * rows))):
+        source = shard.at[pl.ds(pl.multiple_of(start, rows), target.shape[0])]
+        copies.append(pltpu.make_async_copy(source, target, arrived.at[1 + i]))
+    for copy in copies:
+        copy.start()
+    copies[0].wait()
     for mask, block in zip(masks, blocks):
         pack(mask, tokens, block)
+    for copy in copies[1:]:
+        copy.wait()
 
 
 def unpack_body(masks, *refs):
@@ -194,20 +199,15 @@
         key_weight = cut.transpose(1, 0, 2, 3).reshape(shard_rows, key_cols)
         tokens = split_runs(tokens, outer)
 
-    both, *far = local_call(
-        functools.partial(first_body, masks[-1]),
-        [shape((TWIN * rows, key_cols), bf16), block_shape],
+    both, mine, *packed = local_call(
+        functools.partial(front_body, masks),
+        [shape((TWIN * rows, key_cols), bf16), shape((rows, key_cols), bf16)] + [block_shape] * members,
         tokens,
         key_weight,
-    )
-    mine, *packed = local_call(
-        functools.partial(second_body, masks[:-1]),
-        [shape((rows, key_cols), bf16)] + [block_shape] * (members - 1),
-        tokens,
-        both,
-        *far,
-    )
-    packed += far
+        space=pltpu.HBM,
+        room=53,
+        scratch=[pltpu.VMEM(tokens.shape, bf16), pltpu.SemaphoreType.DMA((3,))],
+    )
     blocks = [packed[0]] + [flipped(packed[mask], MEMBERS, mask) for mask in masks[1:]]
     passed = [parted(both, step) for step in range(1, (line + 1) // 2)]
     if line % 2 == 0:
@@ -222,7 +222,7 @@
 
     flops = 2 * tok_rows * owned * key_cols
     shares = []
-    for mask in masks:
+    for mask in reversed(masks):
         kind = bf16 if mask else f32
         share = local_call(share_body, shape((tok_rows, key_cols), kind), blocks[mask], weight, flops=flops)
         shares.append(flipped(share, MEMBERS, mask) if mask else share)
@@ -231,11 +231,10 @@
     )
 
     grads = [key_grad] + [flipped(key_grad, MEMBERS, mask) for mask in masks[1:]]
-    columns = []
-    for mask in masks:
-        column = local_call(columns_body, shape((tok_rows, owned), bf16), grads[mask], weight, flops=flops)
-        columns.append(flipped(column, MEMBERS, mask) if mask else column)
-
+    columns = [
+        local_call(columns_body, block_shape, grad, weight, flops=flops) for grad in grads[:-1]
+    ]
+    columns, grads[-1] = lax.optimization_barrier((columns, grads[-1]))
     terms = local_call(
         functools.partial(terms_body, members, grad_scale),
         [shape((line, rows, key_cols), kind) for kind in (f32, bf16)],
@@ -243,17 +242,22 @@
         *grads,
         flops=members * flops,
     )
+    columns = columns[:1] + [flipped(columns[mask], MEMBERS, mask) for mask in masks[1:-1]]
     sums = local_call(
         merge_body,
         [shape((rows, key_cols), f32)] + [shape((rows, key_cols), bf16)] * (line - 1),
         terms[0],
         flipped(terms[1], "twin", 1),
     )
+
     met = [sums[0]] + [rotated(sums[step], "line", -step) for step in range(1, line)]
-    weight_grad = local_call(sum_body, shape((rows, key_cols), f32), *met)
+    column = local_call(columns_body, block_shape, grads[-1], weight, flops=flops)
+    column, columns, _ = lax.optimization_barrier((column, columns, sums))
+    columns.append(flipped(column, MEMBERS, masks[-1]) if len(masks) > 1 else column)
+    weight_grad = local_call(sum_body, shape((rows, key_cols), f32), *met, flops=32 * flops)
+    columns, weight_grad = lax.optimization_barrier((columns, weight_grad))
     if outer > 1:
         weight_grad = lax.psum_scatter(weight_grad, "outer", scatter_dimension=0, tiled=True)
-
     input_grad = local_call(
         functools.partial(unpack_body, masks), shape((tok_rows, width), bf16), *columns
     )

time: 64.7 us -> 65.4 us (1.011)
  local copies, waits for them, and re-layouts: 2.27 us -> 0.01 us
  Pallas kernels: 7.16 us -> 9.17 us
    ppermute x4, waiting for transfers between devices: 12.1 us -> 16.6 us  [rotated(): lax.ppermute(block, axis, [(i, (i + step) % size) for i in range(size)])]
    ppermute x15, waiting for transfers between devices: 17.2 us -> 13.3 us  [flipped(): return lax.ppermute(block, axes, [(i, i ^ mask) for i in range(size)])]
    unnamed x6 -> x2, local copies, waits for them, and re-layouts: 2.27 us -> 0.01 us
    pallas_call x16 -> x15, Pallas kernels: 7.16 us -> 9.17 us  [local_call(): pl.pallas_call(body, out_shape=out_shapes, in_specs=[pl.BlockSpec(memory_...]
  transfers between devices with their start and end apart: 20 -> 20, of which waited for: 12 -> 10; matrix products, arithmetic and copies ran while one was open for 0% -> 0% of each run, Pallas kernels for 6% -> 5%
where the time goes in v6:
time: 65.4 us; the launch traced here: 65.3 us
  waiting for transfers between devices  29.9 us (46%)
  starting transfers between devices  25.4 us (39%)
  Pallas kernels  9.17 us (14%)
  between operations  0.77 us (1%)
    ppermute x15, starting transfers between devices, flipped(): return lax.ppermute(block, axes, [(i, i ^ mask) for i in range(size)])  16.7 us
    ppermute x4, waiting for transfers between devices, rotated(): lax.ppermute(block, axis, [(i, (i + step) % size) for i in range(size)])  16.6 us
    ppermute x15, waiting for transfers between devices, flipped(): return lax.ppermute(block, axes, [(i, i ^ mask) for i in range(size)])  13.3 us
    pallas_call x15, Pallas kernels, local_call(): pl.pallas_call(body, out_shape=out_shapes, in_specs=[pl.BlockSpec(memory_...  9.17 us
    ppermute x4, starting transfers between devices, rotated(): lax.ppermute(block, axis, [(i, (i + step) % size) for i in range(size)])  6.73 us
    ppermute x1, starting transfers between devices, parted(): return lax.ppermute(block, ('twin', 'line'), list(enumerate(to)))  2.01 us
  transfers between devices with their start and end apart: 20, of which 10 were waited for; matrix products, arithmetic and copies ran while one was open for 0% of the time, Pallas kernels for 5%

profile of v6, /device:TPU:0, one launch (start us, length us, event | category | flops | bytes accessed | tf_op | source)
XLA Modules:
  0.0 65.3 jit_solution(4300451971603553534)
XLA Ops:
  0.6 2.3 %shard_map.58 = (bf16[256,512]{1,0:T(8,128)(2,1)S(1)}, bf16[128,512]{1,0:T(8,128)(2,1)S(1)}, bf16[128,1024]{1,0:T(8,128)(2,1)S(1)}, bf16[128,1024]{1,0:T(8,128)(...) custom-call(bf16[128,4096]{1,0:T(8,128)(2,1)} %tokens_hbm.1, bf16[512,512]{1,0:T(8,128)(2,1)} %shard.1), custom_call_target="tpu_custom_call" | custom-call | bytes 1572864 | tf_op jit(solution)/shard_map/pallas_call | solution.py:25
  3.0 3.0 %collective-permute-start.2 = (bf16[128,1024]{1,0:T(8,128)(2,1)S(1)}, bf16[128,1024]{1,0:T(8,128)(2,1)S(1)}, u32[]{:S(2)}, u32[]{:S(2)}) collective-permute-start(bf16[128,1024]{1,0:T(8,128)(2,1)S(1)} %get-tuple-element.39), channel_id=1, source_target_pairs={{0,1},{1,0},{16,17},{17,16},{2,3},{3,2},{18,19},{19,18},{4,5},{5,4... | collective-permute-start | bytes 786440 | tf_op jit(solution)/shard_map/ppermute | solution.py:43
  6.0 1.5 %collective-permute-start.3 = (bf16[128,1024]{1,0:T(8,128)(2,1)}, bf16[128,1024]{1,0:T(8,128)(2,1)S(1)}, u32[]{:S(2)}, u32[]{:S(2)}) collective-permute-start(bf16[128,1024]{1,0:T(8,128)(2,1)} %get-tuple-element.40), channel_id=1, source_target_pairs={{0,16},{1,17},{16,0},{17,1},{2,18},{3,19},{18,2},{19,3},{4,20},{5,... | collective-permute-start | bytes 786440 | tf_op jit(solution)/shard_map/ppermute | solution.py:43
  7.5 2.0 %collective-permute-start = (bf16[256,512]{1,0:T(8,128)(2,1)S(1)}, bf16[256,512]{1,0:T(8,128)(2,1)S(1)}, u32[]{:S(2)}, u32[]{:S(2)}) collective-permute-start(bf16[256,512]{1,0:T(8,128)(2,1)S(1)} %get-tuple-element.36.refs_0_), channel_id=1, source_target_pairs={{0,2},{2,4},{4,6},{6,0},{8,14},{10,8},{12,10},{14,12},{1,3},{3,5},... | collective-permute-start | bytes 786440 | tf_op jit(solution)/shard_map/ppermute | solution.py:108
  9.5 2.6 %collective-permute-start.1 = (bf16[128,512]{1,0:T(8,128)(2,1)S(1)}, bf16[128,512]{1,0:T(8,128)(2,1)S(1)}, u32[]{:S(2)}, u32[]{:S(2)}) collective-permute-start(bf16[128,512]{1,0:T(8,128)(2,1)S(1)} %get-tuple-element.37), channel_id=1, source_target_pairs={{0,4},{2,6},{4,0},{6,2},{1,5},{3,7},{5,1},{7,3},{8,12},{10,14},{12... | collective-permute-start | bytes 393224 | tf_op jit(solution)/shard_map/ppermute | solution.py:38
  12.1 9.8 %collective-permute-done.1.refs_3_ = bf16[128,512]{1,0:T(8,128)(2,1)S(1)} collective-permute-done((bf16[128,512]{1,0:T(8,128)(2,1)S(1)}, bf16[128,512]{1,0:T(8,128)(2,1)S(1)}, u32[]{:S(2)}, u32[]{:S(2)}) %collective-permute-start.1) | collective-permute-done | bytes 131104 | tf_op jit(solution)/shard_map/ppermute | solution.py:38
  22.0 0.5 collective-permute-start.6
  22.5 1.2 %collective-permute-done.6.refs_4_ = bf16[128,512]{1,0:T(8,128)(2,1)S(1)} collective-permute-done((bf16[128,512]{1,0:T(8,128)(2,1)S(1)}, bf16[128,512]{1,0:T(8,128)(2,1)S(1)}, u32[]{:S(2)}, u32[]{:S(2)}) %collective-permute-start.6) | collective-permute-done | bytes 131104 | tf_op jit(solution)/shard_map/ppermute | solution.py:43
  24.8 2.6 %collective-permute-start.7 = (bf16[128,512]{1,0:T(8,128)(2,1)S(1)}, bf16[128,512]{1,0:T(8,128)(2,1)S(1)}, u32[]{:S(2)}, u32[]{:S(2)}) collective-permute-start(bf16[128,512]{1,0:T(8,128)(2,1)S(1)} %shard_map.60), channel_id=1, source_target_pairs={{0,17},{1,16},{16,1},{17,0},{2,19},{3,18},{18,3},{19,2},{4,21},{5,... | collective-permute-start | bytes 393224 | tf_op jit(solution)/shard_map/ppermute | solution.py:43
  27.4 0.5 collective-permute-start.8
  28.6 3.4 %collective-permute-done.7.refs_0_ = bf16[128,512]{1,0:T(8,128)(2,1)S(1)} collective-permute-done((bf16[128,512]{1,0:T(8,128)(2,1)S(1)}, bf16[128,512]{1,0:T(8,128)(2,1)S(1)}, u32[]{:S(2)}, u32[]{:S(2)}) %collective-permute-start.7) | collective-permute-done | bytes 131104 | tf_op jit(solution)/shard_map/ppermute | solution.py:43
  32.1 2.2 %collective-permute-done.8.refs_1_ = bf16[128,512]{1,0:T(8,128)(2,1)S(1)} collective-permute-done((bf16[128,512]{1,0:T(8,128)(2,1)S(1)}, bf16[128,512]{1,0:T(8,128)(2,1)S(1)}, u32[]{:S(2)}, u32[]{:S(2)}) %collective-permute-start.8) | collective-permute-done | bytes 131104 | tf_op jit(solution)/shard_map/ppermute | solution.py:43
  34.3 0.8 %shard_map.64 = (bf16[128,512]{1,0:T(8,128)(2,1)}, bf16[128,512]{1,0:T(8,128)(2,1)S(1)}) custom-call(bf16[128,512]{1,0:T(8,128)(2,1)S(1)} %collective-permute-done.7.refs_0_, bf16[128,512]{1,0:T(8,128)(2,1)S(1)} %collective-permute-done.8.refs_1_, bf16[128,512]{1,0:T(8,128)(2,1)S(1)} %collective-permute-done.9.refs_2_, f32[128,512]{1,0:T(8,128)S(1)} %shard_map.63.refs_3_, ...), custom_call_target="tpu_custom_call" | custom-call | bytes 786432 | tf_op jit(solution)/shard_map/pallas_call | solution.py:25
  35.1 1.4 %collective-permute-start.10 = (bf16[128,512]{1,0:T(8,128)(2,1)S(1)}, bf16[128,512]{1,0:T(8,128)(2,1)S(1)}, u32[]{:S(2)}, u32[]{:S(2)}) collective-permute-start(bf16[128,512]{1,0:T(8,128)(2,1)S(1)} %get-tuple-element.49.grad.refs_4_), channel_id=1, source_target_pairs={{0,1},{1,0},{16,17},{17,16},{2,3},{3,2},{18,19},{19,18},{4,5},{5,4... | collective-permute-start | bytes 393224 | tf_op jit(solution)/shard_map/ppermute | solution.py:43
  36.5 1.5 %collective-permute-start.11 = (bf16[128,512]{1,0:T(8,128)(2,1)S(1)}, bf16[128,512]{1,0:T(8,128)(2,1)S(1)}, u32[]{:S(2)}, u32[]{:S(2)}) collective-permute-start(bf16[128,512]{1,0:T(8,128)(2,1)S(1)} %get-tuple-element.49.grad.refs_4_), channel_id=1, source_target_pairs={{0,16},{1,17},{16,0},{17,1},{2,18},{3,19},{18,2},{19,3},{4,20},{5,... | collective-permute-start | bytes 393224 | tf_op jit(solution)/shard_map/ppermute | solution.py:43
  38.0 0.5 collective-permute-start.12
  38.6 0.5 shard_map.65.refs_0_
  39.1 1.1 %collective-permute-done.10.grad.refs_5_ = bf16[128,512]{1,0:T(8,128)(2,1)S(1)} collective-permute-done((bf16[128,512]{1,0:T(8,128)(2,1)S(1)}, bf16[128,512]{1,0:T(8,128)(2,1)S(1)}, u32[]{:S(2)}, u32[]{:S(2)}) %collective-permute-start.10) | collective-permute-done | bytes 131104 | tf_op jit(solution)/shard_map/ppermute | solution.py:43
  40.2 0.5 shard_map.66
  40.7 2.2 %collective-permute-done.11.grad.refs_6_ = bf16[128,512]{1,0:T(8,128)(2,1)S(1)} collective-permute-done((bf16[128,512]{1,0:T(8,128)(2,1)S(1)}, bf16[128,512]{1,0:T(8,128)(2,1)S(1)}, u32[]{:S(2)}, u32[]{:S(2)}) %collective-permute-start.11) | collective-permute-done | bytes 131104 | tf_op jit(solution)/shard_map/ppermute | solution.py:43
  43.4 0.9 %collective-permute-done.12.grad.refs_7_ = bf16[128,512]{1,0:T(8,128)(2,1)S(1)} collective-permute-done((bf16[128,512]{1,0:T(8,128)(2,1)S(1)}, bf16[128,512]{1,0:T(8,128)(2,1)S(1)}, u32[]{:S(2)}, u32[]{:S(2)}) %collective-permute-start.12) | collective-permute-done | bytes 131104 | tf_op jit(solution)/shard_map/ppermute | solution.py:43
  44.3 0.7 %shard_map.69 = (f32[4,128,512]{2,1,0:T(8,128)S(1)}, bf16[4,128,512]{2,1,0:T(8,128)(2,1)S(1)}) custom-call(bf16[128,1024]{1,0:T(8,128)(2,1)S(1)} %get-tuple-element.47.block.refs_0_, bf16[128,1024]{1,0:T(8,128)(2,1)S(1)} %collective-permute-done.2.block.refs_1_, bf16[128,1024]{1,0:T(8,128)(2,1)S(1)} %collective-permute-done.3.block.refs_2_, ...), custom_call_target="tpu_custom_call" | custom-call | flops 536870912 | bytes 1572864 | tf_op jit(solution)/shard_map/pallas_call | solution.py:25
  45.1 1.7 %collective-permute-start.13 = (bf16[128,1024]{1,0:T(8,128)(2,1)S(1)}, bf16[128,1024]{1,0:T(8,128)(2,1)S(1)}, u32[]{:S(2)}, u32[]{:S(2)}) collective-permute-start(bf16[128,1024]{1,0:T(8,128)(2,1)S(1)} %shard_map.66), channel_id=1, source_target_pairs={{0,1},{1,0},{16,17},{17,16},{2,3},{3,2},{18,19},{19,18},{4,5},{5,4... | collective-permute-start | bytes 786440 | tf_op jit(solution)/shard_map/ppermute | solution.py:43
  46.8 1.5 %collective-permute-start.14 = (bf16[128,1024]{1,0:T(8,128)(2,1)S(1)}, bf16[128,1024]{1,0:T(8,128)(2,1)S(1)}, u32[]{:S(2)}, u32[]{:S(2)}) collective-permute-start(bf16[128,1024]{1,0:T(8,128)(2,1)S(1)} %shard_map.67), channel_id=1, source_target_pairs={{0,16},{1,17},{16,0},{17,1},{2,18},{3,19},{18,2},{19,3},{4,20},{5,... | collective-permute-start | bytes 786440 | tf_op jit(solution)/shard_map/ppermute | solution.py:43
  48.4 3.5 %collective-permute-start.17 = (bf16[128,512]{1,0:T(8,128)(2,1)S(1)}, bf16[128,512]{1,0:T(8,128)(2,1)S(1)}, u32[]{:S(2)}, u32[]{:S(2)}) collective-permute-start(bf16[128,512]{1,0:T(8,128)(2,1)S(1)} %get-tuple-element.57), channel_id=1, source_target_pairs={{0,6},{2,0},{4,2},{6,4},{1,7},{3,1},{5,3},{7,5},{8,14},{10,8},{12,... | collective-permute-start | bytes 393224 | tf_op jit(solution)/shard_map/ppermute | solution.py:38
  51.9 0.6 collective-permute-start.19
  53.0 0.8 %collective-permute-done.13.refs_1_ = bf16[128,1024]{1,0:T(8,128)(2,1)S(1)} collective-permute-done((bf16[128,1024]{1,0:T(8,128)(2,1)S(1)}, bf16[128,1024]{1,0:T(8,128)(2,1)S(1)}, u32[]{:S(2)}, u32[]{:S(2)}) %collective-permute-start.13) | collective-permute-done | bytes 262176 | tf_op jit(solution)/shard_map/ppermute | solution.py:43
  53.9 1.3 %collective-permute-done.14.refs_2_ = bf16[128,1024]{1,0:T(8,128)(2,1)S(1)} collective-permute-done((bf16[128,1024]{1,0:T(8,128)(2,1)S(1)}, bf16[128,1024]{1,0:T(8,128)(2,1)S(1)}, u32[]{:S(2)}, u32[]{:S(2)}) %collective-permute-start.14) | collective-permute-done | bytes 262176 | tf_op jit(solution)/shard_map/ppermute | solution.py:43
  55.2 1.2 %collective-permute-start.16 = (bf16[128,1024]{1,0:T(8,128)(2,1)S(1)}, bf16[128,1024]{1,0:T(8,128)(2,1)S(1)}, u32[]{:S(2)}, u32[]{:S(2)}) collective-permute-start(bf16[128,1024]{1,0:T(8,128)(2,1)S(1)} %shard_map.68), channel_id=1, source_target_pairs={{0,17},{1,16},{16,1},{17,0},{2,19},{3,18},{18,3},{19,2},{4,21},{5,... | collective-permute-start | bytes 786440 | tf_op jit(solution)/shard_map/ppermute | solution.py:43
  56.5 6.8 %collective-permute-done.18.refs_2_ = bf16[128,512]{1,0:T(8,128)(2,1)S(1)} collective-permute-done((bf16[128,512]{1,0:T(8,128)(2,1)S(1)}, bf16[128,512]{1,0:T(8,128)(2,1)S(1)}, u32[]{:S(2)}, u32[]{:S(2)}) %collective-permute-start.18) | collective-permute-done | bytes 131104 | tf_op jit(solution)/shard_map/ppermute | solution.py:38
  63.3 0.8 %shard_map.71 = f32[128,512]{1,0:T(8,128)} custom-call(f32[128,512]{1,0:T(8,128)S(1)} %get-tuple-element.56.refs_0_, bf16[128,512]{1,0:T(8,128)(2,1)S(1)} %collective-permute-done.17.refs_1_, bf16[128,512]{1,0:T(8,128)(2,1)S(1)} %collective-permute-done.18.refs_2_, bf16[128,512]{1,0:T(8,128)(2,1)S(1)} %collective-permute-done.19.refs_3_), custom_call_target="tpu_custom_call" | custom-call | flops 4294967296 | bytes 655360 | tf_op jit(solution)/shard_map/pallas_call | solution.py:25
  64.0 1.2 %shard_map.72 = bf16[128,4096]{1,0:T(8,128)(2,1)} custom-call(bf16[128,1024]{1,0:T(8,128)(2,1)S(1)} %shard_map.65.refs_0_, bf16[128,1024]{1,0:T(8,128)(2,1)S(1)} %collective-permute-done.13.refs_1_, bf16[128,1024]{1,0:T(8,128)(2,1)S(1)} %collective-permute-done.14.refs_2_, bf16[128,1024]{1,0:T(8,128)(2,1)S(1)} %collective-permute-done.16.refs_3_), custom_call_target="tpu_custom_call" | custom-call | bytes 1048576 | tf_op jit(solution)/shard_map/pallas_call | solution.py:25
  (25 shorter events, 3.0 us)
Async XLA Ops:
  3.0 18.9 %collective-permute-start.2 = (bf16[128,1024]{1,0:T(8,128)(2,1)S(1)}, bf16[128,1024]{1,0:T(8,128)(2,1)S(1)}, u32[]{:S(2)}, u32[]{:S(2)}) collective-permute-start(bf16[128,1024]{1,0:T(8,128)(2,1)S(1)} %get-tuple-element.39), channel_id=1, source_target_pairs={{0,1},{1,0},{16,17},{17,16},{2,3},{3,2},{18,19},{19,18},{4,5},{5,4... | collective-permute-start | bytes 786440 | tf_op jit(solution)/shard_map/ppermute | solution.py:43
  6.0 15.9 %collective-permute-start.3 = (bf16[128,1024]{1,0:T(8,128)(2,1)}, bf16[128,1024]{1,0:T(8,128)(2,1)S(1)}, u32[]{:S(2)}, u32[]{:S(2)}) collective-permute-start(bf16[128,1024]{1,0:T(8,128)(2,1)} %get-tuple-element.40), channel_id=1, source_target_pairs={{0,16},{1,17},{16,0},{17,1},{2,18},{3,19},{18,2},{19,3},{4,20},{5,... | collective-permute-start | bytes 786440 | tf_op jit(solution)/shard_map/ppermute | solution.py:43
  7.5 14.4 %collective-permute-start.4 = (bf16[128,1024]{1,0:T(8,128)(2,1)}, bf16[128,1024]{1,0:T(8,128)(2,1)S(1)}, u32[]{:S(2)}, u32[]{:S(2)}) collective-permute-start(bf16[128,1024]{1,0:T(8,128)(2,1)} %get-tuple-element.41), channel_id=1, source_target_pairs={{0,17},{1,16},{16,1},{17,0},{2,19},{3,18},{18,3},{19,2},{4,21},{5,... | collective-permute-start | bytes 786440 | tf_op jit(solution)/shard_map/ppermute | solution.py:43
  7.5 14.4 %collective-permute-start = (bf16[256,512]{1,0:T(8,128)(2,1)S(1)}, bf16[256,512]{1,0:T(8,128)(2,1)S(1)}, u32[]{:S(2)}, u32[]{:S(2)}) collective-permute-start(bf16[256,512]{1,0:T(8,128)(2,1)S(1)} %get-tuple-element.36.refs_0_), channel_id=1, source_target_pairs={{0,2},{2,4},{4,6},{6,0},{8,14},{10,8},{12,10},{14,12},{1,3},{3,5},... | collective-permute-start | bytes 786440 | tf_op jit(solution)/shard_map/ppermute | solution.py:108
  9.5 12.4 %collective-permute-start.1 = (bf16[128,512]{1,0:T(8,128)(2,1)S(1)}, bf16[128,512]{1,0:T(8,128)(2,1)S(1)}, u32[]{:S(2)}, u32[]{:S(2)}) collective-permute-start(bf16[128,512]{1,0:T(8,128)(2,1)S(1)} %get-tuple-element.37), channel_id=1, source_target_pairs={{0,4},{2,6},{4,0},{6,2},{1,5},{3,7},{5,1},{7,3},{8,12},{10,14},{12... | collective-permute-start | bytes 393224 | tf_op jit(solution)/shard_map/ppermute | solution.py:38
  21.9 1.8 %collective-permute-start.5 = (bf16[256,512]{1,0:T(8,128)(2,1)S(1)}, bf16[256,512]{1,0:T(8,128)(2,1)S(1)}, u32[]{:S(2)}, u32[]{:S(2)}) collective-permute-start(bf16[256,512]{1,0:T(8,128)(2,1)S(1)} %collective-permute-done.refs_1_), channel_id=1, source_target_pairs={{0,8},{8,0},{1,9},{9,1},{2,10},{10,2},{3,11},{11,3},{4,12},{12,4},... | collective-permute-start | bytes 786440 | tf_op jit(solution)/shard_map/ppermute | solution.py:43
  22.0 1.7 %collective-permute-start.6 = (bf16[128,512]{1,0:T(8,128)(2,1)S(1)}, bf16[128,512]{1,0:T(8,128)(2,1)S(1)}, u32[]{:S(2)}, u32[]{:S(2)}) collective-permute-start(bf16[128,512]{1,0:T(8,128)(2,1)S(1)} %collective-permute-done.1.refs_3_), channel_id=1, source_target_pairs={{0,8},{8,0},{1,9},{9,1},{2,10},{10,2},{3,11},{11,3},{4,12},{12,4},... | collective-permute-start | bytes 393224 | tf_op jit(solution)/shard_map/ppermute | solution.py:43
  24.8 9.5 %copy-start = (bf16[128,512]{1,0:T(8,128)(2,1)S(1)}, bf16[128,512]{1,0:T(8,128)(2,1)}, u32[]{:S(2)}) copy-start(bf16[128,512]{1,0:T(8,128)(2,1)} %refs_4_.1) | copy-start | bytes 393220
  24.8 7.3 %collective-permute-start.7 = (bf16[128,512]{1,0:T(8,128)(2,1)S(1)}, bf16[128,512]{1,0:T(8,128)(2,1)S(1)}, u32[]{:S(2)}, u32[]{:S(2)}) collective-permute-start(bf16[128,512]{1,0:T(8,128)(2,1)S(1)} %shard_map.60), channel_id=1, source_target_pairs={{0,17},{1,16},{16,1},{17,0},{2,19},{3,18},{18,3},{19,2},{4,21},{5,... | collective-permute-start | bytes 393224 | tf_op jit(solution)/shard_map/ppermute | solution.py:43
  27.4 6.9 %collective-permute-start.8 = (bf16[128,512]{1,0:T(8,128)(2,1)S(1)}, bf16[128,512]{1,0:T(8,128)(2,1)S(1)}, u32[]{:S(2)}, u32[]{:S(2)}) collective-permute-start(bf16[128,512]{1,0:T(8,128)(2,1)S(1)} %shard_map.61), channel_id=1, source_target_pairs={{0,16},{1,17},{16,0},{17,1},{2,18},{3,19},{18,2},{19,3},{4,20},{5,... | collective-permute-start | bytes 393224 | tf_op jit(solution)/shard_map/ppermute | solution.py:43
  27.9 6.3 %collective-permute-start.9 = (bf16[128,512]{1,0:T(8,128)(2,1)S(1)}, bf16[128,512]{1,0:T(8,128)(2,1)S(1)}, u32[]{:S(2)}, u32[]{:S(2)}) collective-permute-start(bf16[128,512]{1,0:T(8,128)(2,1)S(1)} %shard_map.62), channel_id=1, source_target_pairs={{0,1},{1,0},{16,17},{17,16},{2,3},{3,2},{18,19},{19,18},{4,5},{5,4... | collective-permute-start | bytes 393224 | tf_op jit(solution)/shard_map/ppermute | solution.py:43
  35.1 5.1 %collective-permute-start.10 = (bf16[128,512]{1,0:T(8,128)(2,1)S(1)}, bf16[128,512]{1,0:T(8,128)(2,1)S(1)}, u32[]{:S(2)}, u32[]{:S(2)}) collective-permute-start(bf16[128,512]{1,0:T(8,128)(2,1)S(1)} %get-tuple-element.49.grad.refs_4_), channel_id=1, source_target_pairs={{0,1},{1,0},{16,17},{17,16},{2,3},{3,2},{18,19},{19,18},{4,5},{5,4... | collective-permute-start | bytes 393224 | tf_op jit(solution)/shard_map/ppermute | solution.py:43
  36.5 6.4 %collective-permute-start.11 = (bf16[128,512]{1,0:T(8,128)(2,1)S(1)}, bf16[128,512]{1,0:T(8,128)(2,1)S(1)}, u32[]{:S(2)}, u32[]{:S(2)}) collective-permute-start(bf16[128,512]{1,0:T(8,128)(2,1)S(1)} %get-tuple-element.49.grad.refs_4_), channel_id=1, source_target_pairs={{0,16},{1,17},{16,0},{17,1},{2,18},{3,19},{18,2},{19,3},{4,20},{5,... | collective-permute-start | bytes 393224 | tf_op jit(solution)/shard_map/ppermute | solution.py:43
  38.0 6.3 %collective-permute-start.12 = (bf16[128,512]{1,0:T(8,128)(2,1)S(1)}, bf16[128,512]{1,0:T(8,128)(2,1)S(1)}, u32[]{:S(2)}, u32[]{:S(2)}) collective-permute-start(bf16[128,512]{1,0:T(8,128)(2,1)S(1)} %get-tuple-element.49.grad.refs_4_), channel_id=1, source_target_pairs={{0,17},{1,16},{16,1},{17,0},{2,19},{3,18},{18,3},{19,2},{4,21},{5,... | collective-permute-start | bytes 393224 | tf_op jit(solution)/shard_map/ppermute | solution.py:43
  45.1 3.3 %collective-permute-start.15 = (bf16[4,128,512]{2,1,0:T(8,128)(2,1)S(1)}, bf16[4,128,512]{2,1,0:T(8,128)(2,1)S(1)}, u32[]{:S(2)}, u32[]{:S(2)}) collective-permute-start(bf16[4,128,512]{2,1,0:T(8,128)(2,1)S(1)} %get-tuple-element.55), channel_id=1, source_target_pairs={{0,8},{8,0},{1,9},{9,1},{2,10},{10,2},{3,11},{11,3},{4,12},{12,4},... | collective-permute-start | bytes 1572872 | tf_op jit(solution)/shard_map/ppermute | solution.py:43
  45.1 8.7 %collective-permute-start.13 = (bf16[128,1024]{1,0:T(8,128)(2,1)S(1)}, bf16[128,1024]{1,0:T(8,128)(2,1)S(1)}, u32[]{:S(2)}, u32[]{:S(2)}) collective-permute-start(bf16[128,1024]{1,0:T(8,128)(2,1)S(1)} %shard_map.66), channel_id=1, source_target_pairs={{0,1},{1,0},{16,17},{17,16},{2,3},{3,2},{18,19},{19,18},{4,5},{5,4... | collective-permute-start | bytes 786440 | tf_op jit(solution)/shard_map/ppermute | solution.py:43
  46.8 8.4 %collective-permute-start.14 = (bf16[128,1024]{1,0:T(8,128)(2,1)S(1)}, bf16[128,1024]{1,0:T(8,128)(2,1)S(1)}, u32[]{:S(2)}, u32[]{:S(2)}) collective-permute-start(bf16[128,1024]{1,0:T(8,128)(2,1)S(1)} %shard_map.67), channel_id=1, source_target_pairs={{0,16},{1,17},{16,0},{17,1},{2,18},{3,19},{18,2},{19,3},{4,20},{5,... | collective-permute-start | bytes 786440 | tf_op jit(solution)/shard_map/ppermute | solution.py:43
  48.4 8.0 %collective-permute-start.17 = (bf16[128,512]{1,0:T(8,128)(2,1)S(1)}, bf16[128,512]{1,0:T(8,128)(2,1)S(1)}, u32[]{:S(2)}, u32[]{:S(2)}) collective-permute-start(bf16[128,512]{1,0:T(8,128)(2,1)S(1)} %get-tuple-element.57), channel_id=1, source_target_pairs={{0,6},{2,0},{4,2},{6,4},{1,7},{3,1},{5,3},{7,5},{8,14},{10,8},{12,... | collective-permute-start | bytes 393224 | tf_op jit(solution)/shard_map/ppermute | solution.py:38
  51.9 11.4 %collective-permute-start.18 = (bf16[128,512]{1,0:T(8,128)(2,1)S(1)}, bf16[128,512]{1,0:T(8,128)(2,1)S(1)}, u32[]{:S(2)}, u32[]{:S(2)}) collective-permute-start(bf16[128,512]{1,0:T(8,128)(2,1)S(1)} %get-tuple-element.58), channel_id=1, source_target_pairs={{0,4},{2,6},{4,0},{6,2},{1,5},{3,7},{5,1},{7,3},{8,12},{10,14},{12... | collective-permute-start | bytes 393224 | tf_op jit(solution)/shard_map/ppermute | solution.py:38
  51.9 11.4 %collective-permute-start.19 = (bf16[128,512]{1,0:T(8,128)(2,1)S(1)}, bf16[128,512]{1,0:T(8,128)(2,1)S(1)}, u32[]{:S(2)}, u32[]{:S(2)}) collective-permute-start(bf16[128,512]{1,0:T(8,128)(2,1)S(1)} %get-tuple-element.59), channel_id=1, source_target_pairs={{0,2},{2,4},{4,6},{6,0},{1,3},{3,5},{5,7},{7,1},{8,10},{10,12},{12... | collective-permute-start | bytes 393224 | tf_op jit(solution)/shard_map/ppermute | solution.py:38
  55.2 8.8 %collective-permute-start.16 = (bf16[128,1024]{1,0:T(8,128)(2,1)S(1)}, bf16[128,1024]{1,0:T(8,128)(2,1)S(1)}, u32[]{:S(2)}, u32[]{:S(2)}) collective-permute-start(bf16[128,1024]{1,0:T(8,128)(2,1)S(1)} %shard_map.68), channel_id=1, source_target_pairs={{0,17},{1,16},{16,1},{17,0},{2,19},{3,18},{18,3},{19,2},{4,21},{5,... | collective-permute-start | bytes 786440 | tf_op jit(solution)/shard_map/ppermute | solution.py:43

commit v7 on v6

--- a/solution.py
+++ b/solution.py
@@ -18,12 +18,14 @@
 bf16, f32 = jnp.bfloat16, jnp.float32
 
 
-def local_call(body, out_shapes, *args, flops=0, space=pltpu.VMEM, scratch=(), room=32):
+def local_call(name, body, out_shapes, *args, flops=0, space=pltpu.VMEM, scratch=(), room=32, moved=None):
     vmem = pl.BlockSpec(memory_space=pltpu.VMEM)
     many = isinstance(out_shapes, (list, tuple))
-    moved = sum(math.prod(a.shape) * a.dtype.itemsize for a in args)
+    if moved is None:
+        moved = sum(math.prod(a.shape) * a.dtype.itemsize for a in args)
     return pl.pallas_call(
         body,
+        name=name,
         out_shape=out_shapes,
         in_specs=[pl.BlockSpec(memory_space=space)] * len(args),
         out_specs=[vmem] * len(out_shapes) if many else vmem,
@@ -51,28 +53,23 @@
     return (place * pair + lax.rem(member, pair)) * side * TWIN + member // pair * TWIN + core
 
 
-def pack(mask, tokens, block):
-    parts = lax.axis_size("line") * TWIN
-    run = block.shape[1] // parts
-    for part in range(parts):
-        start = pl.multiple_of(run_of(part, mask) * run, run)
-        block[:, part * run : (part + 1) * run] = tokens[:, pl.ds(start, run)]
-
-
-def front_body(masks, tokens_hbm, shard, both, mine, *refs):
-    *blocks, tokens, arrived = refs
-    copies = [pltpu.make_async_copy(tokens_hbm, tokens, arrived.at[0])]
+def front_body(masks, tokens, shard, both, mine, *refs):
+    *blocks, arrived = refs
     rows, half = mine.shape[0], both.shape[0]
     first = lax.axis_index("side") * half
-    for i, (target, start) in enumerate(((both, first), (mine, first + lax.axis_index("twin") * rows))):
-        source = shard.at[pl.ds(pl.multiple_of(start, rows), target.shape[0])]
-        copies.append(pltpu.make_async_copy(source, target, arrived.at[1 + i]))
+    moves = []
+    for target, start in ((both, first), (mine, first + lax.axis_index("twin") * rows)):
+        moves.append((shard.at[pl.ds(pl.multiple_of(start, rows), target.shape[0])], target))
+    parts = lax.axis_size("line") * TWIN
+    run = blocks[0].shape[1] // parts
+    for mask, block in zip(masks, blocks):
+        for part in range(parts):
+            start = pl.multiple_of(run_of(part, mask) * run, run)
+            moves.append((tokens.at[:, pl.ds(start, run)], block.at[:, pl.ds(part * run, run)]))
+    copies = [pltpu.make_async_copy(*move, arrived.at[i]) for i, move in enumerate(moves)]
     for copy in copies:
         copy.start()
-    copies[0].wait()
-    for mask, block in zip(masks, blocks):
-        pack(mask, tokens, block)
-    for copy in copies[1:]:
+    for copy in copies:
         copy.wait()
 
 
@@ -108,8 +105,22 @@
     return lax.ppermute(block, ("twin", "line"), list(enumerate(to)))
 
 
-def join_body(line, *refs):
-    *pieces, whole = refs
+def cuts(rows, count):
+    unit = math.gcd(rows, 64)
+    ends = [-(-rows // unit * i // count) * unit for i in range(count + 1)]
+    return list(zip(ends, ends[1:]))
+
+
+def relay_body(count, *refs):
+    rows = jnp.concatenate([ref[...] for ref in refs[:-count]], axis=0)
+    for (start, end), out in zip(cuts(rows.shape[0], count), refs[-count:]):
+        out[...] = rows[start:end]
+
+
+def join_body(line, count, *refs):
+    both, *pieces, whole = refs
+    others = jnp.concatenate([piece[...] for piece in pieces[-count:]], axis=0)
+    pieces = pieces[:-count]
     rows = whole.shape[0] // (line * TWIN)
     core = lax.axis_index("twin")
 
@@ -119,16 +130,16 @@
 
     def put_both(step, piece):
         for twin_run in range(TWIN):
-            put(step, twin_run, piece[twin_run * rows : (twin_run + 1) * rows, :])
-
-    pieces = iter(pieces)
-    put_both(0, next(pieces))
+            put(step, twin_run, piece[twin_run * rows : (twin_run + 1) * rows])
+
+    put_both(0, both[...])
     for step in range(1, (line + 1) // 2):
-        put_both(jnp.where(core == 0, step, line - step), next(pieces))
-        put_both(jnp.where(core == 0, line - step, step), next(pieces))
+        at = (step - 1) * TWIN * rows
+        put_both(jnp.where(core == 0, step, line - step), pieces[step - 1][...])
+        put_both(jnp.where(core == 0, line - step, step), others[at : at + TWIN * rows])
     if line % 2 == 0:
-        put(line // 2, core, next(pieces)[...])
-        put(line // 2, 1 - core, next(pieces)[...])
+        put(line // 2, core, pieces[-1][...])
+        put(line // 2, 1 - core, others[others.shape[0] - rows :])
 
 
 def share_body(block, weight, out):
@@ -155,23 +166,28 @@
 
 
 def terms_body(members, grad_scale, *refs):
-    blocks, grads, (kept, leaving) = refs[:members], refs[members : 2 * members], refs[2 * members :]
+    blocks, grads, (kept, *leaving) = refs[:members], refs[members : 2 * members], refs[2 * members :]
     tokens = jnp.concatenate([block[...] for block in blocks], axis=0)
     grad = jnp.concatenate([grad[...] for grad in grads], axis=0)
-    rows = kept.shape[1]
+    line, rows, _ = kept.shape
     total = lax.dot_general(tokens, grad, (((0,), (0,)), ((), ())), preferred_element_type=f32)
     total = total * grad_scale
-    for part in range(total.shape[0] // rows):
-        piece = total[part * rows : (part + 1) * rows]
-        if part % TWIN == 0:
-            kept[part // TWIN] = piece
-        else:
-            leaving[part // TWIN] = piece.astype(bf16)
-
-
-def merge_body(kept, arrived, own, *leaving):
+    others = []
+    for step in range(line):
+        start = step * TWIN * rows
+        kept[step] = total[start : start + rows]
+        others.append(total[start + rows : start + TWIN * rows].astype(bf16))
+    others = jnp.concatenate(others, axis=0)
+    for (start, end), piece in zip(cuts(line * rows, len(leaving)), leaving):
+        piece[...] = others[start:end]
+
+
+def merge_body(count, kept, *refs):
+    others = jnp.concatenate([piece[...] for piece in refs[:count]], axis=0)
+    own, *leaving = refs[count:]
+    rows = own.shape[0]
     for step in range(kept.shape[0]):
-        piece = kept[step] + arrived[step].astype(f32)
+        piece = kept[step] + others[step * rows : (step + 1) * rows].astype(f32)
         if step == 0:
             own[...] = piece
         else:
@@ -193,6 +209,8 @@
     owned = width // members
     grad_scale = 1.0 / math.sqrt(tok_rows * outer * side * TWIN * line * pair)
     shape = jax.ShapeDtypeStruct
+    parts = line * TWIN
+    flops = 2 * tok_rows * owned * key_cols
     block_shape = shape((tok_rows, owned), bf16)
     if outer > 1:
         cut = key_weight.reshape(outer, side * TWIN, rows // outer, key_cols)
@@ -200,65 +218,80 @@
         tokens = split_runs(tokens, outer)
 
     both, mine, *packed = local_call(
+        "front",
         functools.partial(front_body, masks),
         [shape((TWIN * rows, key_cols), bf16), shape((rows, key_cols), bf16)] + [block_shape] * members,
         tokens,
         key_weight,
         space=pltpu.HBM,
         room=53,
-        scratch=[pltpu.VMEM(tokens.shape, bf16), pltpu.SemaphoreType.DMA((3,))],
+        scratch=[pltpu.SemaphoreType.DMA((2 + members * parts,))],
     )
     blocks = [packed[0]] + [flipped(packed[mask], MEMBERS, mask) for mask in masks[1:]]
     passed = [parted(both, step) for step in range(1, (line + 1) // 2)]
     if line % 2 == 0:
         passed.append(rotated(mine, "line", line // 2))
     pieces = [both]
-    *passed, blocks = lax.optimization_barrier((*passed, blocks))
-    for piece in passed:
-        pieces += [piece, flipped(piece, "twin", 1)]
+    reach = shard_rows // side * (line - 1) // TWIN
+    relayed = local_call(
+        "relay",
+        functools.partial(relay_body, 2),
+        [shape((end - start, key_cols), bf16) for start, end in cuts(reach, 2)],
+        *passed,
+        flops=8 * flops,
+    )
     weight = local_call(
-        functools.partial(join_body, line), shape((owned, key_cols), bf16), *pieces
-    )
-
-    flops = 2 * tok_rows * owned * key_cols
+        "join",
+        functools.partial(join_body, line, 2),
+        shape((owned, key_cols), bf16),
+        both,
+        *passed,
+        *[flipped(piece, "twin", 1) for piece in relayed],
+    )
+
     shares = []
-    for mask in reversed(masks):
+    for mask in masks:
         kind = bf16 if mask else f32
-        share = local_call(share_body, shape((tok_rows, key_cols), kind), blocks[mask], weight, flops=flops)
+        share = local_call("share", share_body, shape((tok_rows, key_cols), kind), blocks[mask], weight, flops=flops)
         shares.append(flipped(share, MEMBERS, mask) if mask else share)
     key_out, key_grad = local_call(
-        norm_body, [shape((tok_rows, key_cols), bf16)] * 2, *shares, cotangent
+        "norm", norm_body, [shape((tok_rows, key_cols), bf16)] * 2, *shares, cotangent
     )
 
     grads = [key_grad] + [flipped(key_grad, MEMBERS, mask) for mask in masks[1:]]
     columns = [
-        local_call(columns_body, block_shape, grad, weight, flops=flops) for grad in grads[:-1]
+        local_call("columns", columns_body, block_shape, grad, weight, flops=flops) for grad in grads[:-1]
     ]
     columns, grads[-1] = lax.optimization_barrier((columns, grads[-1]))
     terms = local_call(
+        "terms",
         functools.partial(terms_body, members, grad_scale),
-        [shape((line, rows, key_cols), kind) for kind in (f32, bf16)],
+        [shape((line, rows, key_cols), f32)]
+        + [shape((end - start, key_cols), bf16) for start, end in cuts(line * rows, 3)],
         *blocks,
         *grads,
         flops=members * flops,
     )
     columns = columns[:1] + [flipped(columns[mask], MEMBERS, mask) for mask in masks[1:-1]]
     sums = local_call(
-        merge_body,
+        "merge",
+        functools.partial(merge_body, 3),
         [shape((rows, key_cols), f32)] + [shape((rows, key_cols), bf16)] * (line - 1),
         terms[0],
-        flipped(terms[1], "twin", 1),
+        *[flipped(piece, "twin", 1) for piece in terms[1:]],
+        moved=0,
     )
 
     met = [sums[0]] + [rotated(sums[step], "line", -step) for step in range(1, line)]
-    column = local_call(columns_body, block_shape, grads[-1], weight, flops=flops)
+    column = local_call("columns", columns_body, block_shape, grads[-1], weight, flops=flops)
     column, columns, _ = lax.optimization_barrier((column, columns, sums))
     columns.append(flipped(column, MEMBERS, masks[-1]) if len(masks) > 1 else column)
-    weight_grad = local_call(sum_body, shape((rows, key_cols), f32), *met, flops=32 * flops)
+    weight_grad = local_call("final_sum", sum_body, shape((rows, key_cols), f32), *met, flops=32 * flops)
     columns, weight_grad = lax.optimization_barrier((columns, weight_grad))
     if outer > 1:
         weight_grad = lax.psum_scatter(weight_grad, "outer", scatter_dimension=0, tiled=True)
     input_grad = local_call(
+        "unpack",
         functools.partial(unpack_body, masks), shape((tok_rows, width), bf16), *columns
     )
     if outer > 1:

time: 65.4 us -> 62.5 us (0.956)
  waiting for transfers between devices: 29.9 us -> 26 us
  starting transfers between devices: 25.4 us -> 26.4 us
    ppermute x4, waiting for transfers between devices: 16.6 us -> 13.6 us  [rotated(): lax.ppermute(block, axis, [(i, (i + step) % size) for i in range(size)])]
    ppermute x1, starting transfers between devices: 2.01 us -> 3.08 us  [parted(): return lax.ppermute(block, ('twin', 'line'), list(enumerate(to)))]
    ppermute x15 -> x17, waiting for transfers between devices: 13.3 us -> 12.4 us  [flipped(): return lax.ppermute(block, axes, [(i, i ^ mask) for i in range(size)])]
    ppermute x15 -> x17, starting transfers between devices: 16.7 us -> 16 us  [flipped(): return lax.ppermute(block, axes, [(i, i ^ mask) for i in range(size)])]
    pallas_call x15 -> x16, Pallas kernels: 9.17 us -> 9.22 us  [local_call(): pl.pallas_call(body, name=name, out_shape=out_shapes, in_specs=[pl.BlockS...]
  transfers between devices with their start and end apart: 20 -> 22, of which waited for: 10 -> 12; matrix products, arithmetic and copies ran while one was open for 0% -> 0% of each run, Pallas kernels for 5% -> 7%
where the time goes in v7:
time: 62.5 us; the launch traced here: 62.3 us
  starting transfers between devices  26.4 us (42%)
  waiting for transfers between devices  26 us (42%)
  Pallas kernels  9.22 us (15%)
  between operations  0.77 us (1%)
    ppermute x17, starting transfers between devices, flipped(): return lax.ppermute(block, axes, [(i, i ^ mask) for i in range(size)])  16 us
    ppermute x4, waiting for transfers between devices, rotated(): lax.ppermute(block, axis, [(i, (i + step) % size) for i in range(size)])  13.6 us
    ppermute x17, waiting for transfers between devices, flipped(): return lax.ppermute(block, axes, [(i, i ^ mask) for i in range(size)])  12.4 us
    pallas_call x16, Pallas kernels, local_call(): pl.pallas_call(body, name=name, out_shape=out_shapes, in_specs=[pl.BlockS...  9.22 us
    ppermute x4, starting transfers between devices, rotated(): lax.ppermute(block, axis, [(i, (i + step) % size) for i in range(size)])  7.25 us
    ppermute x1, starting transfers between devices, parted(): return lax.ppermute(block, ('twin', 'line'), list(enumerate(to)))  3.08 us
  transfers between devices with their start and end apart: 22, of which 12 were waited for; matrix products, arithmetic and copies ran while one was open for 0% of the time, Pallas kernels for 7%

profile of v7, /device:TPU:0, one launch (start us, length us, event | category | flops | bytes accessed | tf_op | source)
XLA Modules:
  0.0 62.3 jit_solution(3865566858067232026)
XLA Ops:
  0.6 2.4 %front.1 = (bf16[256,512]{1,0:T(8,128)(2,1)S(1)}, bf16[128,512]{1,0:T(8,128)(2,1)S(1)}, bf16[128,1024]{1,0:T(8,128)(2,1)S(1)}, bf16[128,1024]{1,0:T(8,128)(2,1)S...) custom-call(bf16[128,4096]{1,0:T(8,128)(2,1)} %tokens.1, bf16[512,512]{1,0:T(8,128)(2,1)} %shard.1), custom_call_target="tpu_custom_call" | custom-call | bytes 1572864 | tf_op jit(solution)/shard_map/front/pallas_call | solution.py:26
  3.0 3.1 %collective-permute-start = (bf16[256,512]{1,0:T(8,128)(2,1)S(1)}, bf16[256,512]{1,0:T(8,128)(2,1)S(1)}, u32[]{:S(2)}, u32[]{:S(2)}) collective-permute-start(bf16[256,512]{1,0:T(8,128)(2,1)S(1)} %get-tuple-element.35.refs_0_), channel_id=1, source_target_pairs={{0,2},{2,4},{4,6},{6,0},{8,14},{10,8},{12,10},{14,12},{1,3},{3,5},... | collective-permute-start | bytes 786440 | tf_op jit(solution)/shard_map/ppermute | solution.py:105
  6.1 2.6 %collective-permute-start.1 = (bf16[128,512]{1,0:T(8,128)(2,1)S(1)}, bf16[128,512]{1,0:T(8,128)(2,1)S(1)}, u32[]{:S(2)}, u32[]{:S(2)}) collective-permute-start(bf16[128,512]{1,0:T(8,128)(2,1)S(1)} %get-tuple-element.36), channel_id=1, source_target_pairs={{0,4},{2,6},{4,0},{6,2},{1,5},{3,7},{5,1},{7,3},{8,12},{10,14},{12... | collective-permute-start | bytes 393224 | tf_op jit(solution)/shard_map/ppermute | solution.py:40
  8.7 1.5 %collective-permute-start.4 = (bf16[128,1024]{1,0:T(8,128)(2,1)S(1)}, bf16[128,1024]{1,0:T(8,128)(2,1)S(1)}, u32[]{:S(2)}, u32[]{:S(2)}) collective-permute-start(bf16[128,1024]{1,0:T(8,128)(2,1)S(1)} %get-tuple-element.39), channel_id=1, source_target_pairs={{0,1},{1,0},{16,17},{17,16},{2,3},{3,2},{18,19},{19,18},{4,5},{5,4... | collective-permute-start | bytes 786440 | tf_op jit(solution)/shard_map/ppermute | solution.py:45
  10.2 1.5 %collective-permute-start.6 = (bf16[128,1024]{1,0:T(8,128)(2,1)}, bf16[128,1024]{1,0:T(8,128)(2,1)S(1)}, u32[]{:S(2)}, u32[]{:S(2)}) collective-permute-start(bf16[128,1024]{1,0:T(8,128)(2,1)} %get-tuple-element.40), channel_id=1, source_target_pairs={{0,16},{1,17},{16,0},{17,1},{2,18},{3,19},{18,2},{19,3},{4,20},{5,... | collective-permute-start | bytes 786440 | tf_op jit(solution)/shard_map/ppermute | solution.py:45
  12.2 6.4 %collective-permute-done.1.refs_1_.refs_2_ = bf16[128,512]{1,0:T(8,128)(2,1)S(1)} collective-permute-done((bf16[128,512]{1,0:T(8,128)(2,1)S(1)}, bf16[128,512]{1,0:T(8,128)(2,1)S(1)}, u32[]{:S(2)}, u32[]{:S(2)}) %collective-permute-start.1) | collective-permute-done | bytes 131104 | tf_op jit(solution)/shard_map/ppermute | solution.py:40
  18.6 0.5 collective-permute-start.2
  19.2 1.0 %collective-permute-done.2.refs_3_ = bf16[192,512]{1,0:T(8,128)(2,1)S(1)} collective-permute-done((bf16[192,512]{1,0:T(8,128)(2,1)S(1)}, bf16[192,512]{1,0:T(8,128)(2,1)S(1)}, u32[]{:S(2)}, u32[]{:S(2)}) %collective-permute-start.2) | collective-permute-done | bytes 196640 | tf_op jit(solution)/shard_map/ppermute | solution.py:45
  21.0 1.6 %collective-permute-start.5 = (bf16[128,512]{1,0:T(8,128)(2,1)S(1)}, bf16[128,512]{1,0:T(8,128)(2,1)S(1)}, u32[]{:S(2)}, u32[]{:S(2)}) collective-permute-start(bf16[128,512]{1,0:T(8,128)(2,1)S(1)} %share.5), channel_id=1, source_target_pairs={{0,1},{1,0},{16,17},{17,16},{2,3},{3,2},{18,19},{19,18},{4,5},{5,4... | collective-permute-start | bytes 393224 | tf_op jit(solution)/shard_map/ppermute | solution.py:45
  22.9 1.6 %collective-permute-start.7 = (bf16[128,512]{1,0:T(8,128)(2,1)S(1)}, bf16[128,512]{1,0:T(8,128)(2,1)S(1)}, u32[]{:S(2)}, u32[]{:S(2)}) collective-permute-start(bf16[128,512]{1,0:T(8,128)(2,1)S(1)} %share.6), channel_id=1, source_target_pairs={{0,16},{1,17},{16,0},{17,1},{2,18},{3,19},{18,2},{19,3},{4,20},{5,... | collective-permute-start | bytes 393224 | tf_op jit(solution)/shard_map/ppermute | solution.py:45
  24.7 1.0 %collective-permute-start.9 = (bf16[128,512]{1,0:T(8,128)(2,1)S(1)}, bf16[128,512]{1,0:T(8,128)(2,1)S(1)}, u32[]{:S(2)}, u32[]{:S(2)}) collective-permute-start(bf16[128,512]{1,0:T(8,128)(2,1)S(1)} %share.7), channel_id=1, source_target_pairs={{0,17},{1,16},{16,1},{17,0},{2,19},{3,18},{18,3},{19,2},{4,21},{5,... | collective-permute-start | bytes 393224 | tf_op jit(solution)/shard_map/ppermute | solution.py:45
  26.0 0.7 %collective-permute-done.5.refs_1_ = bf16[128,512]{1,0:T(8,128)(2,1)S(1)} collective-permute-done((bf16[128,512]{1,0:T(8,128)(2,1)S(1)}, bf16[128,512]{1,0:T(8,128)(2,1)S(1)}, u32[]{:S(2)}, u32[]{:S(2)}) %collective-permute-start.5) | collective-permute-done | bytes 131104 | tf_op jit(solution)/shard_map/ppermute | solution.py:45
  26.7 2.6 %collective-permute-done.7.refs_2_ = bf16[128,512]{1,0:T(8,128)(2,1)S(1)} collective-permute-done((bf16[128,512]{1,0:T(8,128)(2,1)S(1)}, bf16[128,512]{1,0:T(8,128)(2,1)S(1)}, u32[]{:S(2)}, u32[]{:S(2)}) %collective-permute-start.7) | collective-permute-done | bytes 131104 | tf_op jit(solution)/shard_map/ppermute | solution.py:45
  29.3 1.8 %collective-permute-done.9.refs_3_ = bf16[128,512]{1,0:T(8,128)(2,1)S(1)} collective-permute-done((bf16[128,512]{1,0:T(8,128)(2,1)S(1)}, bf16[128,512]{1,0:T(8,128)(2,1)S(1)}, u32[]{:S(2)}, u32[]{:S(2)}) %collective-permute-start.9) | collective-permute-done | bytes 131104 | tf_op jit(solution)/shard_map/ppermute | solution.py:45
  31.1 0.8 %norm.1 = (bf16[128,512]{1,0:T(8,128)(2,1)}, bf16[128,512]{1,0:T(8,128)(2,1)S(1)}) custom-call(f32[128,512]{1,0:T(8,128)S(1)} %share.4.refs_0_, bf16[128,512]{1,0:T(8,128)(2,1)S(1)} %collective-permute-done.5.refs_1_, bf16[128,512]{1,0:T(8,128)(2,1)S(1)} %collective-permute-done.7.refs_2_, bf16[128,512]{1,0:T(8,128)(2,1)S(1)} %collective-permute-done.9.refs_3_, ...), custom_call_target="tpu_custom_call" | custom-call | bytes 786432 | tf_op jit(solution)/shard_map/norm/pallas_call | solution.py:26
  31.9 1.5 %collective-permute-start.10 = (bf16[128,512]{1,0:T(8,128)(2,1)S(1)}, bf16[128,512]{1,0:T(8,128)(2,1)S(1)}, u32[]{:S(2)}, u32[]{:S(2)}) collective-permute-start(bf16[128,512]{1,0:T(8,128)(2,1)S(1)} %get-tuple-element.43.grad.refs_4_), channel_id=1, source_target_pairs={{0,1},{1,0},{16,17},{17,16},{2,3},{3,2},{18,19},{19,18},{4,5},{5,4... | collective-permute-start | bytes 393224 | tf_op jit(solution)/shard_map/ppermute | solution.py:45
  33.4 1.5 %collective-permute-start.11 = (bf16[128,512]{1,0:T(8,128)(2,1)S(1)}, bf16[128,512]{1,0:T(8,128)(2,1)S(1)}, u32[]{:S(2)}, u32[]{:S(2)}) collective-permute-start(bf16[128,512]{1,0:T(8,128)(2,1)S(1)} %get-tuple-element.43.grad.refs_4_), channel_id=1, source_target_pairs={{0,16},{1,17},{16,0},{17,1},{2,18},{3,19},{18,2},{19,3},{4,20},{5,... | collective-permute-start | bytes 393224 | tf_op jit(solution)/shard_map/ppermute | solution.py:45
  35.9 1.3 %collective-permute-done.10.grad.refs_5_ = bf16[128,512]{1,0:T(8,128)(2,1)S(1)} collective-permute-done((bf16[128,512]{1,0:T(8,128)(2,1)S(1)}, bf16[128,512]{1,0:T(8,128)(2,1)S(1)}, u32[]{:S(2)}, u32[]{:S(2)}) %collective-permute-start.10) | collective-permute-done | bytes 131104 | tf_op jit(solution)/shard_map/ppermute | solution.py:45
  37.6 1.5 %collective-permute-done.11.grad.refs_6_ = bf16[128,512]{1,0:T(8,128)(2,1)S(1)} collective-permute-done((bf16[128,512]{1,0:T(8,128)(2,1)S(1)}, bf16[128,512]{1,0:T(8,128)(2,1)S(1)}, u32[]{:S(2)}, u32[]{:S(2)}) %collective-permute-start.11) | collective-permute-done | bytes 131104 | tf_op jit(solution)/shard_map/ppermute | solution.py:45
  39.6 1.6 %collective-permute-done.12.grad.refs_7_ = bf16[128,512]{1,0:T(8,128)(2,1)S(1)} collective-permute-done((bf16[128,512]{1,0:T(8,128)(2,1)S(1)}, bf16[128,512]{1,0:T(8,128)(2,1)S(1)}, u32[]{:S(2)}, u32[]{:S(2)}) %collective-permute-start.12) | collective-permute-done | bytes 131104 | tf_op jit(solution)/shard_map/ppermute | solution.py:45
  41.1 0.7 %terms.1 = (f32[4,128,512]{2,1,0:T(8,128)S(1)}, bf16[192,512]{1,0:T(8,128)(2,1)S(1)}, bf16[192,512]{1,0:T(8,128)(2,1)S(1)}, bf16[128,512]{1,0:T(8,128)(2,1)S(1)}) custom-call(bf16[128,1024]{1,0:T(8,128)(2,1)S(1)} %get-tuple-element.34.block.refs_0_, bf16[128,1024]{1,0:T(8,128)(2,1)S(1)} %collective-permute-done.4.block.refs_1_, ...), custom_call_target="tpu_custom_call" | custom-call | flops 536870912 | bytes 1572864 | tf_op jit(solution)/shard_map/terms/pallas_call | solution.py:26
  42.0 0.5 collective-permute-start.16
  42.6 0.8 %collective-permute-start.13 = (bf16[128,1024]{1,0:T(8,128)(2,1)S(1)}, bf16[128,1024]{1,0:T(8,128)(2,1)S(1)}, u32[]{:S(2)}, u32[]{:S(2)}) collective-permute-start(bf16[128,1024]{1,0:T(8,128)(2,1)S(1)} %columns.5), channel_id=1, source_target_pairs={{0,1},{1,0},{16,17},{17,16},{2,3},{3,2},{18,19},{19,18},{4,5},{5,4... | collective-permute-start | bytes 786440 | tf_op jit(solution)/shard_map/ppermute | solution.py:45
  43.4 1.5 %collective-permute-start.14 = (bf16[128,1024]{1,0:T(8,128)(2,1)S(1)}, bf16[128,1024]{1,0:T(8,128)(2,1)S(1)}, u32[]{:S(2)}, u32[]{:S(2)}) collective-permute-start(bf16[128,1024]{1,0:T(8,128)(2,1)S(1)} %columns.6), channel_id=1, source_target_pairs={{0,16},{1,17},{16,0},{17,1},{2,18},{3,19},{18,2},{19,3},{4,20},{5,... | collective-permute-start | bytes 786440 | tf_op jit(solution)/shard_map/ppermute | solution.py:45
  45.0 4.0 %collective-permute-start.19 = (bf16[128,512]{1,0:T(8,128)(2,1)S(1)}, bf16[128,512]{1,0:T(8,128)(2,1)S(1)}, u32[]{:S(2)}, u32[]{:S(2)}) collective-permute-start(bf16[128,512]{1,0:T(8,128)(2,1)S(1)} %get-tuple-element.53), channel_id=1, source_target_pairs={{0,6},{2,0},{4,2},{6,4},{1,7},{3,1},{5,3},{7,5},{8,14},{10,8},{12,... | collective-permute-start | bytes 393224 | tf_op jit(solution)/shard_map/ppermute | solution.py:40
  49.0 0.6 %collective-permute-start.21 = (bf16[128,512]{1,0:T(8,128)(2,1)S(1)}, bf16[128,512]{1,0:T(8,128)(2,1)S(1)}, u32[]{:S(2)}, u32[]{:S(2)}) collective-permute-start(bf16[128,512]{1,0:T(8,128)(2,1)S(1)} %get-tuple-element.55), channel_id=1, source_target_pairs={{0,2},{2,4},{4,6},{6,0},{1,3},{3,5},{5,7},{7,1},{8,10},{10,12},{12... | collective-permute-start | bytes 393224 | tf_op jit(solution)/shard_map/ppermute | solution.py:40
  50.1 1.1 %collective-permute-done.13.refs_1_ = bf16[128,1024]{1,0:T(8,128)(2,1)S(1)} collective-permute-done((bf16[128,1024]{1,0:T(8,128)(2,1)S(1)}, bf16[128,1024]{1,0:T(8,128)(2,1)S(1)}, u32[]{:S(2)}, u32[]{:S(2)}) %collective-permute-start.13) | collective-permute-done | bytes 262176 | tf_op jit(solution)/shard_map/ppermute | solution.py:45
  51.2 0.5 collective-permute-done.14.refs_2_
  51.8 1.4 %collective-permute-start.18 = (bf16[128,1024]{1,0:T(8,128)(2,1)S(1)}, bf16[128,1024]{1,0:T(8,128)(2,1)S(1)}, u32[]{:S(2)}, u32[]{:S(2)}) collective-permute-start(bf16[128,1024]{1,0:T(8,128)(2,1)S(1)} %columns.7), channel_id=1, source_target_pairs={{0,17},{1,16},{16,1},{17,0},{2,19},{3,18},{18,3},{19,2},{4,21},{5,... | collective-permute-start | bytes 786440 | tf_op jit(solution)/shard_map/ppermute | solution.py:45
  53.2 7.2 %collective-permute-done.20.refs_2_ = bf16[128,512]{1,0:T(8,128)(2,1)S(1)} collective-permute-done((bf16[128,512]{1,0:T(8,128)(2,1)S(1)}, bf16[128,512]{1,0:T(8,128)(2,1)S(1)}, u32[]{:S(2)}, u32[]{:S(2)}) %collective-permute-start.20) | collective-permute-done | bytes 131104 | tf_op jit(solution)/shard_map/ppermute | solution.py:40
  60.3 0.8 %final_sum.1 = f32[128,512]{1,0:T(8,128)} custom-call(f32[128,512]{1,0:T(8,128)S(1)} %get-tuple-element.52.refs_0_, bf16[128,512]{1,0:T(8,128)(2,1)S(1)} %collective-permute-done.19.refs_1_, bf16[128,512]{1,0:T(8,128)(2,1)S(1)} %collective-permute-done.20.refs_2_, bf16[128,512]{1,0:T(8,128)(2,1)S(1)} %collective-permute-done.21.refs_3_), custom_call_target="tpu_custom_call" | custom-call | flops 4294967296 | bytes 655360 | tf_op jit(solution)/shard_map/final_sum/pallas_call | solution.py:26
  61.1 1.2 %unpack.1 = bf16[128,4096]{1,0:T(8,128)(2,1)} custom-call(bf16[128,1024]{1,0:T(8,128)(2,1)S(1)} %columns.4.refs_0_, bf16[128,1024]{1,0:T(8,128)(2,1)S(1)} %collective-permute-done.13.refs_1_, bf16[128,1024]{1,0:T(8,128)(2,1)S(1)} %collective-permute-done.14.refs_2_, bf16[128,1024]{1,0:T(8,128)(2,1)S(1)} %collective-permute-done.18.refs_3_), custom_call_target="tpu_custom_call" | custom-call | bytes 1048576 | tf_op jit(solution)/shard_map/unpack/pallas_call | solution.py:26
  (30 shorter events, 4.9 us)
Async XLA Ops:
  3.0 15.6 %collective-permute-start = (bf16[256,512]{1,0:T(8,128)(2,1)S(1)}, bf16[256,512]{1,0:T(8,128)(2,1)S(1)}, u32[]{:S(2)}, u32[]{:S(2)}) collective-permute-start(bf16[256,512]{1,0:T(8,128)(2,1)S(1)} %get-tuple-element.35.refs_0_), channel_id=1, source_target_pairs={{0,2},{2,4},{4,6},{6,0},{8,14},{10,8},{12,10},{14,12},{1,3},{3,5},... | collective-permute-start | bytes 786440 | tf_op jit(solution)/shard_map/ppermute | solution.py:105
  6.1 12.5 %collective-permute-start.1 = (bf16[128,512]{1,0:T(8,128)(2,1)S(1)}, bf16[128,512]{1,0:T(8,128)(2,1)S(1)}, u32[]{:S(2)}, u32[]{:S(2)}) collective-permute-start(bf16[128,512]{1,0:T(8,128)(2,1)S(1)} %get-tuple-element.36), channel_id=1, source_target_pairs={{0,4},{2,6},{4,0},{6,2},{1,5},{3,7},{5,1},{7,3},{8,12},{10,14},{12... | collective-permute-start | bytes 393224 | tf_op jit(solution)/shard_map/ppermute | solution.py:40
  8.7 12.0 %collective-permute-start.4 = (bf16[128,1024]{1,0:T(8,128)(2,1)S(1)}, bf16[128,1024]{1,0:T(8,128)(2,1)S(1)}, u32[]{:S(2)}, u32[]{:S(2)}) collective-permute-start(bf16[128,1024]{1,0:T(8,128)(2,1)S(1)} %get-tuple-element.39), channel_id=1, source_target_pairs={{0,1},{1,0},{16,17},{17,16},{2,3},{3,2},{18,19},{19,18},{4,5},{5,4... | collective-permute-start | bytes 786440 | tf_op jit(solution)/shard_map/ppermute | solution.py:45
  10.2 12.4 %collective-permute-start.6 = (bf16[128,1024]{1,0:T(8,128)(2,1)}, bf16[128,1024]{1,0:T(8,128)(2,1)S(1)}, u32[]{:S(2)}, u32[]{:S(2)}) collective-permute-start(bf16[128,1024]{1,0:T(8,128)(2,1)} %get-tuple-element.40), channel_id=1, source_target_pairs={{0,16},{1,17},{16,0},{17,1},{2,18},{3,19},{18,2},{19,3},{4,20},{5,... | collective-permute-start | bytes 786440 | tf_op jit(solution)/shard_map/ppermute | solution.py:45
  11.7 12.7 %collective-permute-start.8 = (bf16[128,1024]{1,0:T(8,128)(2,1)}, bf16[128,1024]{1,0:T(8,128)(2,1)S(1)}, u32[]{:S(2)}, u32[]{:S(2)}) collective-permute-start(bf16[128,1024]{1,0:T(8,128)(2,1)} %get-tuple-element.41), channel_id=1, source_target_pairs={{0,17},{1,16},{16,1},{17,0},{2,19},{3,18},{18,3},{19,2},{4,21},{5,... | collective-permute-start | bytes 786440 | tf_op jit(solution)/shard_map/ppermute | solution.py:45
  18.6 1.6 %collective-permute-start.2 = (bf16[192,512]{1,0:T(8,128)(2,1)S(1)}, bf16[192,512]{1,0:T(8,128)(2,1)S(1)}, u32[]{:S(2)}, u32[]{:S(2)}) collective-permute-start(bf16[192,512]{1,0:T(8,128)(2,1)S(1)} %get-tuple-element.37), channel_id=1, source_target_pairs={{0,8},{8,0},{1,9},{9,1},{2,10},{10,2},{3,11},{11,3},{4,12},{12,4},... | collective-permute-start | bytes 589832 | tf_op jit(solution)/shard_map/ppermute | solution.py:45
  19.1 1.4 %collective-permute-start.3 = (bf16[192,512]{1,0:T(8,128)(2,1)S(1)}, bf16[192,512]{1,0:T(8,128)(2,1)S(1)}, u32[]{:S(2)}, u32[]{:S(2)}) collective-permute-start(bf16[192,512]{1,0:T(8,128)(2,1)S(1)} %get-tuple-element.38), channel_id=1, source_target_pairs={{0,8},{8,0},{1,9},{9,1},{2,10},{10,2},{3,11},{11,3},{4,12},{12,4},... | collective-permute-start | bytes 589832 | tf_op jit(solution)/shard_map/ppermute | solution.py:45
  21.0 5.8 %collective-permute-start.5 = (bf16[128,512]{1,0:T(8,128)(2,1)S(1)}, bf16[128,512]{1,0:T(8,128)(2,1)S(1)}, u32[]{:S(2)}, u32[]{:S(2)}) collective-permute-start(bf16[128,512]{1,0:T(8,128)(2,1)S(1)} %share.5), channel_id=1, source_target_pairs={{0,1},{1,0},{16,17},{17,16},{2,3},{3,2},{18,19},{19,18},{4,5},{5,4... | collective-permute-start | bytes 393224 | tf_op jit(solution)/shard_map/ppermute | solution.py:45
  22.9 6.4 %collective-permute-start.7 = (bf16[128,512]{1,0:T(8,128)(2,1)S(1)}, bf16[128,512]{1,0:T(8,128)(2,1)S(1)}, u32[]{:S(2)}, u32[]{:S(2)}) collective-permute-start(bf16[128,512]{1,0:T(8,128)(2,1)S(1)} %share.6), channel_id=1, source_target_pairs={{0,16},{1,17},{16,0},{17,1},{2,18},{3,19},{18,2},{19,3},{4,20},{5,... | collective-permute-start | bytes 393224 | tf_op jit(solution)/shard_map/ppermute | solution.py:45
  24.7 6.3 %collective-permute-start.9 = (bf16[128,512]{1,0:T(8,128)(2,1)S(1)}, bf16[128,512]{1,0:T(8,128)(2,1)S(1)}, u32[]{:S(2)}, u32[]{:S(2)}) collective-permute-start(bf16[128,512]{1,0:T(8,128)(2,1)S(1)} %share.7), channel_id=1, source_target_pairs={{0,17},{1,16},{16,1},{17,0},{2,19},{3,18},{18,3},{19,2},{4,21},{5,... | collective-permute-start | bytes 393224 | tf_op jit(solution)/shard_map/ppermute | solution.py:45
  25.7 5.4 %copy-start = (bf16[128,512]{1,0:T(8,128)(2,1)S(1)}, bf16[128,512]{1,0:T(8,128)(2,1)}, u32[]{:S(2)}) copy-start(bf16[128,512]{1,0:T(8,128)(2,1)} %refs_4_.1) | copy-start | bytes 393220
  31.9 5.2 %collective-permute-start.10 = (bf16[128,512]{1,0:T(8,128)(2,1)S(1)}, bf16[128,512]{1,0:T(8,128)(2,1)S(1)}, u32[]{:S(2)}, u32[]{:S(2)}) collective-permute-start(bf16[128,512]{1,0:T(8,128)(2,1)S(1)} %get-tuple-element.43.grad.refs_4_), channel_id=1, source_target_pairs={{0,1},{1,0},{16,17},{17,16},{2,3},{3,2},{18,19},{19,18},{4,5},{5,4... | collective-permute-start | bytes 393224 | tf_op jit(solution)/shard_map/ppermute | solution.py:45
  33.4 5.7 %collective-permute-start.11 = (bf16[128,512]{1,0:T(8,128)(2,1)S(1)}, bf16[128,512]{1,0:T(8,128)(2,1)S(1)}, u32[]{:S(2)}, u32[]{:S(2)}) collective-permute-start(bf16[128,512]{1,0:T(8,128)(2,1)S(1)} %get-tuple-element.43.grad.refs_4_), channel_id=1, source_target_pairs={{0,16},{1,17},{16,0},{17,1},{2,18},{3,19},{18,2},{19,3},{4,20},{5,... | collective-permute-start | bytes 393224 | tf_op jit(solution)/shard_map/ppermute | solution.py:45
  34.9 6.2 %collective-permute-start.12 = (bf16[128,512]{1,0:T(8,128)(2,1)S(1)}, bf16[128,512]{1,0:T(8,128)(2,1)S(1)}, u32[]{:S(2)}, u32[]{:S(2)}) collective-permute-start(bf16[128,512]{1,0:T(8,128)(2,1)S(1)} %get-tuple-element.43.grad.refs_4_), channel_id=1, source_target_pairs={{0,17},{1,16},{16,1},{17,0},{2,19},{3,18},{18,3},{19,2},{4,21},{5,... | collective-permute-start | bytes 393224 | tf_op jit(solution)/shard_map/ppermute | solution.py:45
  41.9 3.0 %collective-permute-start.15 = (bf16[192,512]{1,0:T(8,128)(2,1)S(1)}, bf16[192,512]{1,0:T(8,128)(2,1)S(1)}, u32[]{:S(2)}, u32[]{:S(2)}) collective-permute-start(bf16[192,512]{1,0:T(8,128)(2,1)S(1)} %get-tuple-element.49), channel_id=1, source_target_pairs={{0,8},{8,0},{1,9},{9,1},{2,10},{10,2},{3,11},{11,3},{4,12},{12,4},... | collective-permute-start | bytes 589832 | tf_op jit(solution)/shard_map/ppermute | solution.py:45
  42.0 2.9 %collective-permute-start.16 = (bf16[192,512]{1,0:T(8,128)(2,1)S(1)}, bf16[192,512]{1,0:T(8,128)(2,1)S(1)}, u32[]{:S(2)}, u32[]{:S(2)}) collective-permute-start(bf16[192,512]{1,0:T(8,128)(2,1)S(1)} %get-tuple-element.50), channel_id=1, source_target_pairs={{0,8},{8,0},{1,9},{9,1},{2,10},{10,2},{3,11},{11,3},{4,12},{12,4},... | collective-permute-start | bytes 589832 | tf_op jit(solution)/shard_map/ppermute | solution.py:45
  42.5 2.4 %collective-permute-start.17 = (bf16[128,512]{1,0:T(8,128)(2,1)S(1)}, bf16[128,512]{1,0:T(8,128)(2,1)S(1)}, u32[]{:S(2)}, u32[]{:S(2)}) collective-permute-start(bf16[128,512]{1,0:T(8,128)(2,1)S(1)} %get-tuple-element.51), channel_id=1, source_target_pairs={{0,8},{8,0},{1,9},{9,1},{2,10},{10,2},{3,11},{11,3},{4,12},{12,4},... | collective-permute-start | bytes 393224 | tf_op jit(solution)/shard_map/ppermute | solution.py:45
  42.6 8.7 %collective-permute-start.13 = (bf16[128,1024]{1,0:T(8,128)(2,1)S(1)}, bf16[128,1024]{1,0:T(8,128)(2,1)S(1)}, u32[]{:S(2)}, u32[]{:S(2)}) collective-permute-start(bf16[128,1024]{1,0:T(8,128)(2,1)S(1)} %columns.5), channel_id=1, source_target_pairs={{0,1},{1,0},{16,17},{17,16},{2,3},{3,2},{18,19},{19,18},{4,5},{5,4... | collective-permute-start | bytes 786440 | tf_op jit(solution)/shard_map/ppermute | solution.py:45
  43.4 8.4 %collective-permute-start.14 = (bf16[128,1024]{1,0:T(8,128)(2,1)S(1)}, bf16[128,1024]{1,0:T(8,128)(2,1)S(1)}, u32[]{:S(2)}, u32[]{:S(2)}) collective-permute-start(bf16[128,1024]{1,0:T(8,128)(2,1)S(1)} %columns.6), channel_id=1, source_target_pairs={{0,16},{1,17},{16,0},{17,1},{2,18},{3,19},{18,2},{19,3},{4,20},{5,... | collective-permute-start | bytes 786440 | tf_op jit(solution)/shard_map/ppermute | solution.py:45
  45.0 8.2 %collective-permute-start.19 = (bf16[128,512]{1,0:T(8,128)(2,1)S(1)}, bf16[128,512]{1,0:T(8,128)(2,1)S(1)}, u32[]{:S(2)}, u32[]{:S(2)}) collective-permute-start(bf16[128,512]{1,0:T(8,128)(2,1)S(1)} %get-tuple-element.53), channel_id=1, source_target_pairs={{0,6},{2,0},{4,2},{6,4},{1,7},{3,1},{5,3},{7,5},{8,14},{10,8},{12,... | collective-permute-start | bytes 393224 | tf_op jit(solution)/shard_map/ppermute | solution.py:40
  49.0 11.4 %collective-permute-start.20 = (bf16[128,512]{1,0:T(8,128)(2,1)S(1)}, bf16[128,512]{1,0:T(8,128)(2,1)S(1)}, u32[]{:S(2)}, u32[]{:S(2)}) collective-permute-start(bf16[128,512]{1,0:T(8,128)(2,1)S(1)} %get-tuple-element.54), channel_id=1, source_target_pairs={{0,4},{2,6},{4,0},{6,2},{1,5},{3,7},{5,1},{7,3},{8,12},{10,14},{12... | collective-permute-start | bytes 393224 | tf_op jit(solution)/shard_map/ppermute | solution.py:40
  49.0 11.4 %collective-permute-start.21 = (bf16[128,512]{1,0:T(8,128)(2,1)S(1)}, bf16[128,512]{1,0:T(8,128)(2,1)S(1)}, u32[]{:S(2)}, u32[]{:S(2)}) collective-permute-start(bf16[128,512]{1,0:T(8,128)(2,1)S(1)} %get-tuple-element.55), channel_id=1, source_target_pairs={{0,2},{2,4},{4,6},{6,0},{1,3},{3,5},{5,7},{7,1},{8,10},{10,12},{12... | collective-permute-start | bytes 393224 | tf_op jit(solution)/shard_map/ppermute | solution.py:40
  51.8 9.4 %collective-permute-start.18 = (bf16[128,1024]{1,0:T(8,128)(2,1)S(1)}, bf16[128,1024]{1,0:T(8,128)(2,1)S(1)}, u32[]{:S(2)}, u32[]{:S(2)}) collective-permute-start(bf16[128,1024]{1,0:T(8,128)(2,1)S(1)} %columns.7), channel_id=1, source_target_pairs={{0,17},{1,16},{16,1},{17,0},{2,19},{3,18},{18,3},{19,2},{4,21},{5,... | collective-permute-start | bytes 786440 | tf_op jit(solution)/shard_map/ppermute | solution.py:45

commit v8 on v7

--- a/solution.py
+++ b/solution.py
@@ -1,4 +1,5 @@
 import functools
+import itertools
 import math
 
 import jax
@@ -13,8 +14,9 @@
 
 epsilon = 1e-06
 
-MEMBERS = ("side", "pair")
+SPLIT = 2
 TWIN = 2
+MEMBERS = SPLIT * SPLIT
 bf16, f32 = jnp.bfloat16, jnp.float32
 
 
@@ -40,20 +42,34 @@
     return lax.ppermute(block, axis, [(i, (i + step) % size) for i in range(size)])
 
 
-def flipped(block, axes, mask):
-    size = lax.axis_size(axes)
-    return lax.ppermute(block, axes, [(i, i ^ mask) for i in range(size)])
-
-
-def run_of(part, mask):
-    side, line, pair = lax.axis_size("side"), lax.axis_size("line"), lax.axis_size("pair")
-    member = (lax.axis_index("side") * pair + lax.axis_index("pair")) ^ mask
+def to_twin(block):
+    return lax.ppermute(block, "twin", [(0, 1), (1, 0)])
+
+
+def flips(far, core):
+    return (0, 0) if far == 0 else (1, 1) if far == 3 else (core, 1 - core) if far == 1 else (1 - core, core)
+
+
+def to_member(block, far):
+    def index(side, core, pair):
+        return (side * TWIN + core) * SPLIT + pair
+
+    pairs = []
+    for side, core, pair in itertools.product(range(SPLIT), range(TWIN), range(SPLIT)):
+        over, across = flips(far, core)
+        pairs.append((index(side, core, pair), index(side ^ over, core, pair ^ across)))
+    return lax.ppermute(block, ("side", "twin", "pair"), pairs)
+
+
+def run_of(part, far):
+    line, core = lax.axis_size("line"), lax.axis_index("twin")
+    over, across = flips(far, core)
     place = lax.rem(lax.axis_index("line") + line - part // TWIN, line)
-    core = lax.axis_index("twin") ^ (part % TWIN)
-    return (place * pair + lax.rem(member, pair)) * side * TWIN + member // pair * TWIN + core
-
-
-def front_body(masks, tokens, shard, both, mine, *refs):
+    side, pair = lax.axis_index("side") ^ over, lax.axis_index("pair") ^ across
+    return ((place * SPLIT + pair) * SPLIT + side) * TWIN + (core ^ (part % TWIN))
+
+
+def front_body(tokens, shard, both, mine, *refs):
     *blocks, arrived = refs
     rows, half = mine.shape[0], both.shape[0]
     first = lax.axis_index("side") * half
@@ -62,9 +78,9 @@
         moves.append((shard.at[pl.ds(pl.multiple_of(start, rows), target.shape[0])], target))
     parts = lax.axis_size("line") * TWIN
     run = blocks[0].shape[1] // parts
-    for mask, block in zip(masks, blocks):
+    for far, block in enumerate(blocks):
         for part in range(parts):
-            start = pl.multiple_of(run_of(part, mask) * run, run)
+            start = pl.multiple_of(run_of(part, far) * run, run)
             moves.append((tokens.at[:, pl.ds(start, run)], block.at[:, pl.ds(part * run, run)]))
     copies = [pltpu.make_async_copy(*move, arrived.at[i]) for i, move in enumerate(moves)]
     for copy in copies:
@@ -73,20 +89,43 @@
         copy.wait()
 
 
-def unpack_body(masks, *refs):
-    blocks, whole = refs[:-1], refs[-1]
+def unpack_body(fars, *refs):
+    blocks = refs[: len(fars)]
+    whole, done = refs[-2:]
     parts = lax.axis_size("line") * TWIN
     run = blocks[0].shape[1] // parts
-    for mask, block in zip(masks, blocks):
+    moves = []
+    for far, block in zip(fars, blocks):
         for part in range(parts):
-            start = pl.multiple_of(run_of(part, mask) * run, run)
-            whole[:, pl.ds(start, run)] = block[:, part * run : (part + 1) * run]
+            start = pl.multiple_of(run_of(part, far) * run, run)
+            moves.append((block.at[:, pl.ds(part * run, run)], whole.at[:, pl.ds(start, run)]))
+    copies = [pltpu.make_async_copy(*move, done.at[i]) for i, move in enumerate(moves)]
+    for copy in copies:
+        copy.start()
+    for copy in copies:
+        copy.wait()
+
+
+def unpack(fars, blocks, shape, whole=None):
+    vmem, hbm = pl.BlockSpec(memory_space=pltpu.VMEM), pl.BlockSpec(memory_space=pl.ANY)
+    held = [] if whole is None else [whole]
+    return pl.pallas_call(
+        functools.partial(unpack_body, fars),
+        name="unpack",
+        out_shape=shape,
+        in_specs=[vmem] * len(blocks) + [hbm] * len(held),
+        out_specs=hbm,
+        input_output_aliases={len(blocks): 0} if held else {},
+        scratch_shapes=[pltpu.SemaphoreType.DMA((len(blocks) * lax.axis_size("line") * TWIN,))],
+        compiler_params=pltpu.CompilerParams(vmem_limit_bytes=32 << 20),
+        cost_estimate=pl.CostEstimate(flops=0, bytes_accessed=0, transcendentals=0),
+    )(*blocks, *held)
 
 
 def split_runs(tokens, outer):
     tok_rows, width = tokens.shape
     inner = lax.axis_size("line") * lax.axis_size("pair")
-    near = lax.axis_size("side") * TWIN
+    near = SPLIT * TWIN
     cut = tokens.reshape(tok_rows, inner, outer, near, width // (inner * outer * near))
     return cut.transpose(0, 1, 3, 2, 4).reshape(tok_rows, width)
 
@@ -94,7 +133,7 @@
 def join_runs(tokens, outer):
     tok_rows, width = tokens.shape
     inner = lax.axis_size("line") * lax.axis_size("pair")
-    near = lax.axis_size("side") * TWIN
+    near = SPLIT * TWIN
     cut = tokens.reshape(tok_rows, inner, near, outer, width // (inner * outer * near))
     return cut.transpose(0, 1, 3, 2, 4).reshape(tok_rows, width)
 
@@ -150,6 +189,14 @@
     out[...] = lax.dot_general(
         grad[...], weight[...], (((1,), (1,)), ((), ())), preferred_element_type=f32
     ).astype(out.dtype)
+
+
+def add_body(first, second, out):
+    out[...] = (first[...].astype(f32) + second[...].astype(f32)).astype(out.dtype)
+
+
+def emit_body(held, out):
+    out[...] = held[...]
 
 
 def norm_body(*refs):
@@ -165,8 +212,8 @@
         key_grad[:, at] = (inverse * (upstream - normed * projected)).astype(bf16)
 
 
-def terms_body(members, grad_scale, *refs):
-    blocks, grads, (kept, *leaving) = refs[:members], refs[members : 2 * members], refs[2 * members :]
+def terms_body(grad_scale, *refs):
+    blocks, grads, (kept, *leaving) = refs[:MEMBERS], refs[MEMBERS : 2 * MEMBERS], refs[2 * MEMBERS :]
     tokens = jnp.concatenate([block[...] for block in blocks], axis=0)
     grad = jnp.concatenate([grad[...] for grad in grads], axis=0)
     line, rows, _ = kept.shape
@@ -201,38 +248,35 @@
 def per_device(tokens, key_weight, cotangent):
     tok_rows, width = tokens.shape
     shard_rows, key_cols = key_weight.shape
-    outer, side = lax.axis_size("outer"), lax.axis_size("side")
-    line, pair = lax.axis_size("line"), lax.axis_size("pair")
-    members = pair * side
-    masks = list(range(members))
-    rows = shard_rows // (side * TWIN)
-    owned = width // members
-    grad_scale = 1.0 / math.sqrt(tok_rows * outer * side * TWIN * line * pair)
+    outer, line = lax.axis_size("outer"), lax.axis_size("line")
+    parts = line * TWIN
+    rows = shard_rows // (SPLIT * TWIN)
+    owned = width // MEMBERS
+    grad_scale = 1.0 / math.sqrt(tok_rows * outer * TWIN * MEMBERS * line)
+    flops = 2 * tok_rows * owned * key_cols
     shape = jax.ShapeDtypeStruct
-    parts = line * TWIN
-    flops = 2 * tok_rows * owned * key_cols
-    block_shape = shape((tok_rows, owned), bf16)
+    block_shape, head_shape = shape((tok_rows, owned), bf16), shape((tok_rows, key_cols), bf16)
     if outer > 1:
-        cut = key_weight.reshape(outer, side * TWIN, rows // outer, key_cols)
+        cut = key_weight.reshape(outer, SPLIT * TWIN, rows // outer, key_cols)
         key_weight = cut.transpose(1, 0, 2, 3).reshape(shard_rows, key_cols)
         tokens = split_runs(tokens, outer)
 
     both, mine, *packed = local_call(
         "front",
-        functools.partial(front_body, masks),
-        [shape((TWIN * rows, key_cols), bf16), shape((rows, key_cols), bf16)] + [block_shape] * members,
+        front_body,
+        [shape((TWIN * rows, key_cols), bf16), shape((rows, key_cols), bf16)] + [block_shape] * MEMBERS,
         tokens,
         key_weight,
         space=pltpu.HBM,
         room=53,
-        scratch=[pltpu.SemaphoreType.DMA((2 + members * parts,))],
-    )
-    blocks = [packed[0]] + [flipped(packed[mask], MEMBERS, mask) for mask in masks[1:]]
+        scratch=[pltpu.SemaphoreType.DMA((2 + MEMBERS * parts,))],
+    )
+    blocks = packed[:1] + [to_member(packed[far], far) for far in range(1, MEMBERS)]
     passed = [parted(both, step) for step in range(1, (line + 1) // 2)]
     if line % 2 == 0:
         passed.append(rotated(mine, "line", line // 2))
     pieces = [both]
-    reach = shard_rows // side * (line - 1) // TWIN
+    reach = shard_rows // SPLIT * (line - 1) // TWIN
     relayed = local_call(
         "relay",
         functools.partial(relay_body, 2),
@@ -240,60 +284,71 @@
         *passed,
         flops=8 * flops,
     )
+    theirs = [to_twin(piece) for piece in relayed]
+    theirs, blocks = lax.optimization_barrier((theirs, blocks))
     weight = local_call(
         "join",
         functools.partial(join_body, line, 2),
         shape((owned, key_cols), bf16),
         both,
         *passed,
-        *[flipped(piece, "twin", 1) for piece in relayed],
-    )
-
-    shares = []
-    for mask in masks:
-        kind = bf16 if mask else f32
-        share = local_call("share", share_body, shape((tok_rows, key_cols), kind), blocks[mask], weight, flops=flops)
-        shares.append(flipped(share, MEMBERS, mask) if mask else share)
-    key_out, key_grad = local_call(
-        "norm", norm_body, [shape((tok_rows, key_cols), bf16)] * 2, *shares, cotangent
-    )
-
-    grads = [key_grad] + [flipped(key_grad, MEMBERS, mask) for mask in masks[1:]]
-    columns = [
-        local_call("columns", columns_body, block_shape, grad, weight, flops=flops) for grad in grads[:-1]
-    ]
-    columns, grads[-1] = lax.optimization_barrier((columns, grads[-1]))
+        *theirs,
+    )
+
+    def share(far, kind):
+        shaped = shape((tok_rows, key_cols), kind)
+        return local_call("share", share_body, shaped, blocks[far], weight, flops=flops)
+
+    passing = to_member(share(3, bf16), 2)
+    second = to_member(share(2, bf16), 2)
+    first = to_member(local_call("add", add_body, head_shape, share(1, f32), passing), 1)
+    normed, key_grad = local_call("norm", norm_body, [head_shape] * 2, share(0, f32), second, first, cotangent)
+    key_out = local_call("emit", emit_body, head_shape, normed)
+
+    grad_1 = to_member(key_grad, 1)
+    grad_2 = to_member(key_grad, 2)
+    grad_3 = to_member(grad_1, 2)
+
+    def columns(grad):
+        return local_call("columns", columns_body, block_shape, grad, weight, moved=0)
+
+    seen_1, grad_2 = lax.optimization_barrier((grad_1, grad_2))
+    column_0, column_1 = columns(key_grad), columns(seen_1)
+    column_0, column_1, key_out, grad_3 = lax.optimization_barrier((column_0, column_1, key_out, grad_3))
+    back_1 = to_member(column_1, 1)
     terms = local_call(
         "terms",
-        functools.partial(terms_body, members, grad_scale),
+        functools.partial(terms_body, grad_scale),
         [shape((line, rows, key_cols), f32)]
         + [shape((end - start, key_cols), bf16) for start, end in cuts(line * rows, 3)],
         *blocks,
-        *grads,
-        flops=members * flops,
-    )
-    columns = columns[:1] + [flipped(columns[mask], MEMBERS, mask) for mask in masks[1:-1]]
+        key_grad,
+        grad_1,
+        grad_2,
+        grad_3,
+        flops=MEMBERS * flops,
+    )
+    kept, *theirs = terms
+    theirs = [to_twin(piece) for piece in theirs]
+    column_2, column_3 = columns(grad_2), columns(grad_3)
+    theirs, back_1, column_2, column_3 = lax.optimization_barrier((theirs, back_1, column_2, column_3))
     sums = local_call(
         "merge",
         functools.partial(merge_body, 3),
         [shape((rows, key_cols), f32)] + [shape((rows, key_cols), bf16)] * (line - 1),
-        terms[0],
-        *[flipped(piece, "twin", 1) for piece in terms[1:]],
+        kept,
+        *theirs,
         moved=0,
     )
-
     met = [sums[0]] + [rotated(sums[step], "line", -step) for step in range(1, line)]
-    column = local_call("columns", columns_body, block_shape, grads[-1], weight, flops=flops)
-    column, columns, _ = lax.optimization_barrier((column, columns, sums))
-    columns.append(flipped(column, MEMBERS, masks[-1]) if len(masks) > 1 else column)
     weight_grad = local_call("final_sum", sum_body, shape((rows, key_cols), f32), *met, flops=32 * flops)
-    columns, weight_grad = lax.optimization_barrier((columns, weight_grad))
     if outer > 1:
         weight_grad = lax.psum_scatter(weight_grad, "outer", scatter_dimension=0, tiled=True)
-    input_grad = local_call(
-        "unpack",
-        functools.partial(unpack_body, masks), shape((tok_rows, width), bf16), *columns
-    )
+
+    back_2, back_3 = to_member(column_2, 2), to_member(column_3, 3)
+    input_grad = unpack((0, 1), (column_0, back_1), shape((tok_rows, width), bf16))
+    back_2, back_3, weight_grad = lax.optimization_barrier((back_2, back_3, weight_grad))
+    input_grad = unpack((2, 3), (back_2, back_3), shape((tok_rows, width), bf16), input_grad)
     if outer > 1:
         input_grad = join_runs(input_grad, outer)
     return (key_out, input_grad, weight_grad)
@@ -301,10 +356,8 @@
 
 def solution(mesh):
     replicas, group = mesh.shape["dp"], mesh.shape["inner"]
-    near = math.gcd(replicas, 2 * TWIN)
-    pair = math.gcd(group, 2)
     fine = Mesh(
-        mesh.devices.reshape(replicas // near, near // TWIN, TWIN, group // pair, pair),
+        mesh.devices.reshape(replicas // (SPLIT * TWIN), SPLIT, TWIN, group // SPLIT, SPLIT),
         ("outer", "side", "twin", "line", "pair"),
     )
     rows = P(("outer", "side", "twin", "line", "pair"), None)

time: 62.5 us -> 66.9 us (1.070)
  waiting for transfers between devices: 26 us -> 31.5 us
  starting transfers between devices: 26.4 us -> 24.5 us
  Pallas kernels: 9.22 us -> 9.92 us
    ppermute x17, waiting for transfers between devices: 12.4 us -> 19.6 us  [the longest x12 19.2 us: to_member(): return lax.ppermute(block, ('side', 'twin', 'pair'), pairs)]
    pallas_call x0 -> x2, Pallas kernels: none -> 1.83 us  [unpack(): pl.pallas_call(functools.partial(unpack_body, fars), name='unpack', out_s...]
    ppermute x4, waiting for transfers between devices: 13.6 us -> 11.9 us  [rotated(): lax.ppermute(block, axis, [(i, (i + step) % size) for i in range(size)])]
    pallas_call x16 -> x17, Pallas kernels: 9.22 us -> 8.1 us  [local_call(): pl.pallas_call(body, name=name, out_shape=out_shapes, in_specs=[pl.BlockS...]
    ppermute x17, starting transfers between devices: 16 us -> 15 us  [the longest x12 13.8 us: to_member(): return lax.ppermute(block, ('side', 'twin', 'pair'), pairs)]
    ppermute x4, starting transfers between devices: 7.25 us -> 6.35 us  [rotated(): lax.ppermute(block, axis, [(i, (i + step) % size) for i in range(size)])]
  transfers between devices with their start and end apart: 22 -> 22, of which waited for: 12 -> 11; matrix products, arithmetic and copies ran while one was open for 0% -> 0% of each run, Pallas kernels for 7% -> 9%
where the time goes in v8:
time: 66.9 us; the launch traced here: 66.7 us
  waiting for transfers between devices  31.5 us (47%)
  starting transfers between devices  24.5 us (37%)
  Pallas kernels  9.92 us (15%)
  between operations  0.8 us (1%)
    ppermute x12, waiting for transfers between devices, to_member(): return lax.ppermute(block, ('side', 'twin', 'pair'), pairs)  19.2 us
    ppermute x12, starting transfers between devices, to_member(): return lax.ppermute(block, ('side', 'twin', 'pair'), pairs)  13.8 us
    ppermute x4, waiting for transfers between devices, rotated(): lax.ppermute(block, axis, [(i, (i + step) % size) for i in range(size)])  11.9 us
    pallas_call x17, Pallas kernels, local_call(): pl.pallas_call(body, name=name, out_shape=out_shapes, in_specs=[pl.BlockS...  8.1 us
    ppermute x4, starting transfers between devices, rotated(): lax.ppermute(block, axis, [(i, (i + step) % size) for i in range(size)])  6.35 us
    ppermute x1, starting transfers between devices, parted(): return lax.ppermute(block, ('twin', 'line'), list(enumerate(to)))  3.08 us
    pallas_call x2, Pallas kernels, unpack(): pl.pallas_call(functools.partial(unpack_body, fars), name='unpack', out_s...  1.83 us
  transfers between devices with their start and end apart: 22, of which 11 were waited for; matrix products, arithmetic and copies ran while one was open for 0% of the time, Pallas kernels for 9%

profile of v8, /device:TPU:0, one launch (start us, length us, event | category | flops | bytes accessed | tf_op | source)
XLA Modules:
  0.0 66.7 jit_solution(5607365710665927092)
XLA Ops:
  0.6 2.4 %front.1 = (bf16[256,512]{1,0:T(8,128)(2,1)S(1)}, bf16[128,512]{1,0:T(8,128)(2,1)S(1)}, bf16[128,1024]{1,0:T(8,128)(2,1)S(1)}, bf16[128,1024]{1,0:T(8,128)(2,1)S...) custom-call(bf16[128,4096]{1,0:T(8,128)(2,1)} %tokens.1, bf16[512,512]{1,0:T(8,128)(2,1)} %shard.1), custom_call_target="tpu_custom_call" | custom-call | bytes 1572864 | tf_op jit(solution)/shard_map/front/pallas_call | solution.py:28
  3.0 3.1 %collective-permute-start = (bf16[256,512]{1,0:T(8,128)(2,1)S(1)}, bf16[256,512]{1,0:T(8,128)(2,1)S(1)}, u32[]{:S(2)}, u32[]{:S(2)}) collective-permute-start(bf16[256,512]{1,0:T(8,128)(2,1)S(1)} %get-tuple-element.42.refs_0_), channel_id=1, source_target_pairs={{0,2},{2,4},{4,6},{6,0},{8,14},{10,8},{12,10},{14,12},{1,3},{3,5},... | collective-permute-start | bytes 786440 | tf_op jit(solution)/shard_map/ppermute | solution.py:144
  6.1 2.6 %collective-permute-start.1 = (bf16[128,512]{1,0:T(8,128)(2,1)S(1)}, bf16[128,512]{1,0:T(8,128)(2,1)S(1)}, u32[]{:S(2)}, u32[]{:S(2)}) collective-permute-start(bf16[128,512]{1,0:T(8,128)(2,1)S(1)} %get-tuple-element.43), channel_id=1, source_target_pairs={{0,4},{2,6},{4,0},{6,2},{1,5},{3,7},{5,1},{7,3},{8,12},{10,14},{12... | collective-permute-start | bytes 393224 | tf_op jit(solution)/shard_map/ppermute | solution.py:42
  8.7 1.5 %collective-permute-start.4 = (bf16[128,1024]{1,0:T(8,128)(2,1)S(1)}, bf16[128,1024]{1,0:T(8,128)(2,1)S(1)}, u32[]{:S(2)}, u32[]{:S(2)}) collective-permute-start(bf16[128,1024]{1,0:T(8,128)(2,1)S(1)} %get-tuple-element.47), channel_id=1, source_target_pairs={{0,1},{1,0},{8,24},{9,25},{16,17},{17,16},{24,8},{25,9},{2,3},{3,2... | collective-permute-start | bytes 786440 | tf_op jit(solution)/shard_map/ppermute | solution.py:61
  10.2 1.5 %collective-permute-start.5 = (bf16[128,1024]{1,0:T(8,128)(2,1)}, bf16[128,1024]{1,0:T(8,128)(2,1)S(1)}, u32[]{:S(2)}, u32[]{:S(2)}) collective-permute-start(bf16[128,1024]{1,0:T(8,128)(2,1)} %get-tuple-element.48), channel_id=1, source_target_pairs={{0,16},{1,17},{8,9},{9,8},{16,0},{17,1},{24,25},{25,24},{2,18},{3,... | collective-permute-start | bytes 786440 | tf_op jit(solution)/shard_map/ppermute | solution.py:61
  11.7 0.5 collective-permute-start.6
  12.2 6.4 %collective-permute-done.1.refs_1_.refs_2_ = bf16[128,512]{1,0:T(8,128)(2,1)S(1)} collective-permute-done((bf16[128,512]{1,0:T(8,128)(2,1)S(1)}, bf16[128,512]{1,0:T(8,128)(2,1)S(1)}, u32[]{:S(2)}, u32[]{:S(2)}) %collective-permute-start.1) | collective-permute-done | bytes 131104 | tf_op jit(solution)/shard_map/ppermute | solution.py:42
  18.6 0.5 collective-permute-start.2
  19.2 3.7 %collective-permute-done.4.block.refs_1_ = bf16[128,1024]{1,0:T(8,128)(2,1)S(1)} collective-permute-done((bf16[128,1024]{1,0:T(8,128)(2,1)S(1)}, bf16[128,1024]{1,0:T(8,128)(2,1)S(1)}, u32[]{:S(2)}, u32[]{:S(2)}) %collective-permute-start.4) | collective-permute-done | bytes 262176 | tf_op jit(solution)/shard_map/ppermute | solution.py:61
  23.3 1.1 %collective-permute-start.8 = (bf16[128,512]{1,0:T(8,128)(2,1)S(1)}, bf16[128,512]{1,0:T(8,128)(2,1)S(1)}, u32[]{:S(2)}, u32[]{:S(2)}) collective-permute-start(bf16[128,512]{1,0:T(8,128)(2,1)S(1)} %share.7), channel_id=1, source_target_pairs={{0,16},{1,17},{8,9},{9,8},{16,0},{17,1},{24,25},{25,24},{2,18},{3,... | collective-permute-start | bytes 393224 | tf_op jit(solution)/shard_map/ppermute | solution.py:61
  24.7 1.1 %collective-permute-start.7 = (bf16[128,512]{1,0:T(8,128)(2,1)S(1)}, bf16[128,512]{1,0:T(8,128)(2,1)S(1)}, u32[]{:S(2)}, u32[]{:S(2)}) collective-permute-start(bf16[128,512]{1,0:T(8,128)(2,1)S(1)} %share.5), channel_id=1, source_target_pairs={{0,16},{1,17},{8,9},{9,8},{16,0},{17,1},{24,25},{25,24},{2,18},{3,... | collective-permute-start | bytes 393224 | tf_op jit(solution)/shard_map/ppermute | solution.py:61
  26.1 2.2 %collective-permute-done.8.second = bf16[128,512]{1,0:T(8,128)(2,1)S(1)} collective-permute-done((bf16[128,512]{1,0:T(8,128)(2,1)S(1)}, bf16[128,512]{1,0:T(8,128)(2,1)S(1)}, u32[]{:S(2)}, u32[]{:S(2)}) %collective-permute-start.8) | collective-permute-done | bytes 131104 | tf_op jit(solution)/shard_map/ppermute | solution.py:61
  28.4 1.6 %collective-permute-start.9 = (bf16[128,512]{1,0:T(8,128)(2,1)S(1)}, bf16[128,512]{1,0:T(8,128)(2,1)S(1)}, u32[]{:S(2)}, u32[]{:S(2)}) collective-permute-start(bf16[128,512]{1,0:T(8,128)(2,1)S(1)} %add.1), channel_id=1, source_target_pairs={{0,1},{1,0},{8,24},{9,25},{16,17},{17,16},{24,8},{25,9},{2,3},{3,2... | collective-permute-start | bytes 393224 | tf_op jit(solution)/shard_map/ppermute | solution.py:61
  30.3 3.1 %collective-permute-done.9.refs_2_ = bf16[128,512]{1,0:T(8,128)(2,1)S(1)} collective-permute-done((bf16[128,512]{1,0:T(8,128)(2,1)S(1)}, bf16[128,512]{1,0:T(8,128)(2,1)S(1)}, u32[]{:S(2)}, u32[]{:S(2)}) %collective-permute-start.9) | collective-permute-done | bytes 131104 | tf_op jit(solution)/shard_map/ppermute | solution.py:61
  33.7 1.6 %collective-permute-start.10 = (bf16[128,512]{1,0:T(8,128)(2,1)S(1)}, bf16[128,512]{1,0:T(8,128)(2,1)S(1)}, u32[]{:S(2)}, u32[]{:S(2)}) collective-permute-start(bf16[128,512]{1,0:T(8,128)(2,1)S(1)} %get-tuple-element.56.grad.refs_4_), channel_id=1, source_target_pairs={{0,1},{1,0},{8,24},{9,25},{16,17},{17,16},{24,8},{25,9},{2,3},{3,2... | collective-permute-start | bytes 393224 | tf_op jit(solution)/shard_map/ppermute | solution.py:61
  35.3 0.5 collective-permute-start.11
  35.8 4.0 %collective-permute-done.10.grad.refs_5_ = bf16[128,512]{1,0:T(8,128)(2,1)S(1)} collective-permute-done((bf16[128,512]{1,0:T(8,128)(2,1)S(1)}, bf16[128,512]{1,0:T(8,128)(2,1)S(1)}, u32[]{:S(2)}, u32[]{:S(2)}) %collective-permute-start.10) | collective-permute-done | bytes 131104 | tf_op jit(solution)/shard_map/ppermute | solution.py:61
  39.8 1.0 %collective-permute-start.12 = (bf16[128,512]{1,0:T(8,128)(2,1)S(1)}, bf16[128,512]{1,0:T(8,128)(2,1)S(1)}, u32[]{:S(2)}, u32[]{:S(2)}) collective-permute-start(bf16[128,512]{1,0:T(8,128)(2,1)S(1)} %collective-permute-done.10.grad.refs_5_), channel_id=1, source_target_pairs={{0,16},{1,17},{8,9},{9,8},{16,0},{17,1},{24,25},{25,24},{2,18},{3,... | collective-permute-start | bytes 393224 | tf_op jit(solution)/shard_map/ppermute | solution.py:61
  41.3 0.7 emit.1
  42.4 3.7 %collective-permute-done.12.refs_7_.grad = bf16[128,512]{1,0:T(8,128)(2,1)S(1)} collective-permute-done((bf16[128,512]{1,0:T(8,128)(2,1)S(1)}, bf16[128,512]{1,0:T(8,128)(2,1)S(1)}, u32[]{:S(2)}, u32[]{:S(2)}) %collective-permute-start.12) | collective-permute-done | bytes 131104 | tf_op jit(solution)/shard_map/ppermute | solution.py:61
  46.1 1.5 %collective-permute-start.16 = (bf16[128,1024]{1,0:T(8,128)(2,1)S(1)}, bf16[128,1024]{1,0:T(8,128)(2,1)S(1)}, u32[]{:S(2)}, u32[]{:S(2)}) collective-permute-start(bf16[128,1024]{1,0:T(8,128)(2,1)S(1)} %columns.5), channel_id=1, source_target_pairs={{0,1},{1,0},{8,24},{9,25},{16,17},{17,16},{24,8},{25,9},{2,3},{3,2... | collective-permute-start | bytes 786440 | tf_op jit(solution)/shard_map/ppermute | solution.py:61
  47.6 0.7 %terms.1 = (f32[4,128,512]{2,1,0:T(8,128)S(1)}, bf16[192,512]{1,0:T(8,128)(2,1)S(1)}, bf16[192,512]{1,0:T(8,128)(2,1)S(1)}, bf16[128,512]{1,0:T(8,128)(2,1)S(1)}) custom-call(bf16[128,1024]{1,0:T(8,128)(2,1)S(1)} %get-tuple-element.50.block.refs_0_, bf16[128,1024]{1,0:T(8,128)(2,1)S(1)} %collective-permute-done.4.block.refs_1_, ...), custom_call_target="tpu_custom_call" | custom-call | flops 536870912 | bytes 1572864 | tf_op jit(solution)/shard_map/terms/pallas_call | solution.py:28
  48.4 0.5 collective-permute-start.14
  50.3 2.2 %collective-permute-done.16.refs_1_ = bf16[128,1024]{1,0:T(8,128)(2,1)S(1)} collective-permute-done((bf16[128,1024]{1,0:T(8,128)(2,1)S(1)}, bf16[128,1024]{1,0:T(8,128)(2,1)S(1)}, u32[]{:S(2)}, u32[]{:S(2)}) %collective-permute-start.16) | collective-permute-done | bytes 262176 | tf_op jit(solution)/shard_map/ppermute | solution.py:61
  52.6 0.8 %collective-permute-start.19 = (bf16[128,512]{1,0:T(8,128)(2,1)S(1)}, bf16[128,512]{1,0:T(8,128)(2,1)S(1)}, u32[]{:S(2)}, u32[]{:S(2)}) collective-permute-start(bf16[128,512]{1,0:T(8,128)(2,1)S(1)} %get-tuple-element.73), channel_id=1, source_target_pairs={{0,6},{2,0},{4,2},{6,4},{1,7},{3,1},{5,3},{7,5},{8,14},{10,8},{12,... | collective-permute-start | bytes 393224 | tf_op jit(solution)/shard_map/ppermute | solution.py:42
  53.4 1.0 %collective-permute-start.20 = (bf16[128,512]{1,0:T(8,128)(2,1)S(1)}, bf16[128,512]{1,0:T(8,128)(2,1)S(1)}, u32[]{:S(2)}, u32[]{:S(2)}) collective-permute-start(bf16[128,512]{1,0:T(8,128)(2,1)S(1)} %get-tuple-element.74), channel_id=1, source_target_pairs={{0,4},{2,6},{4,0},{6,2},{1,5},{3,7},{5,1},{7,3},{8,12},{10,14},{12... | collective-permute-start | bytes 393224 | tf_op jit(solution)/shard_map/ppermute | solution.py:42
  54.4 1.9 %collective-permute-start.21 = (bf16[128,512]{1,0:T(8,128)(2,1)S(1)}, bf16[128,512]{1,0:T(8,128)(2,1)S(1)}, u32[]{:S(2)}, u32[]{:S(2)}) collective-permute-start(bf16[128,512]{1,0:T(8,128)(2,1)S(1)} %get-tuple-element.75), channel_id=1, source_target_pairs={{0,2},{2,4},{4,6},{6,0},{1,3},{3,5},{5,7},{7,1},{8,10},{10,12},{12... | collective-permute-start | bytes 393224 | tf_op jit(solution)/shard_map/ppermute | solution.py:42
  56.3 1.7 %collective-permute-start.17 = (bf16[128,1024]{1,0:T(8,128)(2,1)S(1)}, bf16[128,1024]{1,0:T(8,128)(2,1)S(1)}, u32[]{:S(2)}, u32[]{:S(2)}) collective-permute-start(bf16[128,1024]{1,0:T(8,128)(2,1)S(1)} %columns.6), channel_id=1, source_target_pairs={{0,16},{1,17},{8,9},{9,8},{16,0},{17,1},{24,25},{25,24},{2,18},{3,... | collective-permute-start | bytes 786440 | tf_op jit(solution)/shard_map/ppermute | solution.py:61
  58.3 0.9 %unpack.2.refs_2_ = bf16[128,4096]{1,0:T(8,128)(2,1)} custom-call(bf16[128,1024]{1,0:T(8,128)(2,1)S(1)} %columns.4.refs_0_, bf16[128,1024]{1,0:T(8,128)(2,1)S(1)} %collective-permute-done.16.refs_1_), custom_call_target="tpu_custom_call" | custom-call | tf_op jit(solution)/shard_map/unpack/pallas_call | solution.py:112
  59.7 5.1 %collective-permute-done.20.refs_2_ = bf16[128,512]{1,0:T(8,128)(2,1)S(1)} collective-permute-done((bf16[128,512]{1,0:T(8,128)(2,1)S(1)}, bf16[128,512]{1,0:T(8,128)(2,1)S(1)}, u32[]{:S(2)}, u32[]{:S(2)}) %collective-permute-start.20) | collective-permute-done | bytes 131104 | tf_op jit(solution)/shard_map/ppermute | solution.py:42
  64.8 0.8 %final_sum.1 = f32[128,512]{1,0:T(8,128)} custom-call(f32[128,512]{1,0:T(8,128)S(1)} %get-tuple-element.72.refs_0_, bf16[128,512]{1,0:T(8,128)(2,1)S(1)} %collective-permute-done.19.refs_1_, bf16[128,512]{1,0:T(8,128)(2,1)S(1)} %collective-permute-done.20.refs_2_, bf16[128,512]{1,0:T(8,128)(2,1)S(1)} %collective-permute-done.21.refs_3_), custom_call_target="tpu_custom_call" | custom-call | flops 4294967296 | bytes 655360 | tf_op jit(solution)/shard_map/final_sum/pallas_call | solution.py:28
  65.8 0.9 %unpack.3 = bf16[128,4096]{1,0:T(8,128)(2,1)} custom-call(bf16[128,1024]{1,0:T(8,128)(2,1)S(1)} %collective-permute-done.17.refs_0_, bf16[128,1024]{1,0:T(8,128)(2,1)S(1)} %collective-permute-done.18.refs_1_, bf16[128,4096]{1,0:T(8,128)(2,1)} %unpack.2.refs_2_), custom_call_target="tpu_custom_call", output_to_operand_aliasing={{}: (2, {})} | custom-call | tf_op jit(solution)/shard_map/unpack/pallas_call | solution.py:112
  (33 shorter events, 5.2 us)
Async XLA Ops:
  3.0 15.6 %collective-permute-start = (bf16[256,512]{1,0:T(8,128)(2,1)S(1)}, bf16[256,512]{1,0:T(8,128)(2,1)S(1)}, u32[]{:S(2)}, u32[]{:S(2)}) collective-permute-start(bf16[256,512]{1,0:T(8,128)(2,1)S(1)} %get-tuple-element.42.refs_0_), channel_id=1, source_target_pairs={{0,2},{2,4},{4,6},{6,0},{8,14},{10,8},{12,10},{14,12},{1,3},{3,5},... | collective-permute-start | bytes 786440 | tf_op jit(solution)/shard_map/ppermute | solution.py:144
  6.1 12.5 %collective-permute-start.1 = (bf16[128,512]{1,0:T(8,128)(2,1)S(1)}, bf16[128,512]{1,0:T(8,128)(2,1)S(1)}, u32[]{:S(2)}, u32[]{:S(2)}) collective-permute-start(bf16[128,512]{1,0:T(8,128)(2,1)S(1)} %get-tuple-element.43), channel_id=1, source_target_pairs={{0,4},{2,6},{4,0},{6,2},{1,5},{3,7},{5,1},{7,3},{8,12},{10,14},{12... | collective-permute-start | bytes 393224 | tf_op jit(solution)/shard_map/ppermute | solution.py:42
  8.7 14.2 %collective-permute-start.4 = (bf16[128,1024]{1,0:T(8,128)(2,1)S(1)}, bf16[128,1024]{1,0:T(8,128)(2,1)S(1)}, u32[]{:S(2)}, u32[]{:S(2)}) collective-permute-start(bf16[128,1024]{1,0:T(8,128)(2,1)S(1)} %get-tuple-element.47), channel_id=1, source_target_pairs={{0,1},{1,0},{8,24},{9,25},{16,17},{17,16},{24,8},{25,9},{2,3},{3,2... | collective-permute-start | bytes 786440 | tf_op jit(solution)/shard_map/ppermute | solution.py:61
  10.2 12.7 %collective-permute-start.5 = (bf16[128,1024]{1,0:T(8,128)(2,1)}, bf16[128,1024]{1,0:T(8,128)(2,1)S(1)}, u32[]{:S(2)}, u32[]{:S(2)}) collective-permute-start(bf16[128,1024]{1,0:T(8,128)(2,1)} %get-tuple-element.48), channel_id=1, source_target_pairs={{0,16},{1,17},{8,9},{9,8},{16,0},{17,1},{24,25},{25,24},{2,18},{3,... | collective-permute-start | bytes 786440 | tf_op jit(solution)/shard_map/ppermute | solution.py:61
  11.7 11.2 %collective-permute-start.6 = (bf16[128,1024]{1,0:T(8,128)(2,1)}, bf16[128,1024]{1,0:T(8,128)(2,1)S(1)}, u32[]{:S(2)}, u32[]{:S(2)}) collective-permute-start(bf16[128,1024]{1,0:T(8,128)(2,1)} %get-tuple-element.49), channel_id=1, source_target_pairs={{0,17},{1,16},{8,25},{9,24},{16,1},{17,0},{24,9},{25,8},{2,19},{3,... | collective-permute-start | bytes 786440 | tf_op jit(solution)/shard_map/ppermute | solution.py:61
  18.6 4.3 %collective-permute-start.2 = (bf16[192,512]{1,0:T(8,128)(2,1)S(1)}, bf16[192,512]{1,0:T(8,128)(2,1)S(1)}, u32[]{:S(2)}, u32[]{:S(2)}) collective-permute-start(bf16[192,512]{1,0:T(8,128)(2,1)S(1)} %get-tuple-element.44), channel_id=1, source_target_pairs={{0,8},{8,0},{1,9},{9,1},{2,10},{10,2},{3,11},{11,3},{4,12},{12,4},... | collective-permute-start | bytes 589832 | tf_op jit(solution)/shard_map/ppermute | solution.py:46
  19.1 3.8 %collective-permute-start.3 = (bf16[192,512]{1,0:T(8,128)(2,1)S(1)}, bf16[192,512]{1,0:T(8,128)(2,1)S(1)}, u32[]{:S(2)}, u32[]{:S(2)}) collective-permute-start(bf16[192,512]{1,0:T(8,128)(2,1)S(1)} %get-tuple-element.45), channel_id=1, source_target_pairs={{0,8},{8,0},{1,9},{9,1},{2,10},{10,2},{3,11},{11,3},{4,12},{12,4},... | collective-permute-start | bytes 589832 | tf_op jit(solution)/shard_map/ppermute | solution.py:46
  23.3 5.0 %collective-permute-start.8 = (bf16[128,512]{1,0:T(8,128)(2,1)S(1)}, bf16[128,512]{1,0:T(8,128)(2,1)S(1)}, u32[]{:S(2)}, u32[]{:S(2)}) collective-permute-start(bf16[128,512]{1,0:T(8,128)(2,1)S(1)} %share.7), channel_id=1, source_target_pairs={{0,16},{1,17},{8,9},{9,8},{16,0},{17,1},{24,25},{25,24},{2,18},{3,... | collective-permute-start | bytes 393224 | tf_op jit(solution)/shard_map/ppermute | solution.py:61
  24.7 5.6 %collective-permute-start.7 = (bf16[128,512]{1,0:T(8,128)(2,1)S(1)}, bf16[128,512]{1,0:T(8,128)(2,1)S(1)}, u32[]{:S(2)}, u32[]{:S(2)}) collective-permute-start(bf16[128,512]{1,0:T(8,128)(2,1)S(1)} %share.5), channel_id=1, source_target_pairs={{0,16},{1,17},{8,9},{9,8},{16,0},{17,1},{24,25},{25,24},{2,18},{3,... | collective-permute-start | bytes 393224 | tf_op jit(solution)/shard_map/ppermute | solution.py:61
  28.4 5.0 %copy-start = (bf16[128,512]{1,0:T(8,128)(2,1)S(1)}, bf16[128,512]{1,0:T(8,128)(2,1)}, u32[]{:S(2)}) copy-start(bf16[128,512]{1,0:T(8,128)(2,1)} %refs_3_.1) | copy-start | bytes 393220
  28.4 5.0 %collective-permute-start.9 = (bf16[128,512]{1,0:T(8,128)(2,1)S(1)}, bf16[128,512]{1,0:T(8,128)(2,1)S(1)}, u32[]{:S(2)}, u32[]{:S(2)}) collective-permute-start(bf16[128,512]{1,0:T(8,128)(2,1)S(1)} %add.1), channel_id=1, source_target_pairs={{0,1},{1,0},{8,24},{9,25},{16,17},{17,16},{24,8},{25,9},{2,3},{3,2... | collective-permute-start | bytes 393224 | tf_op jit(solution)/shard_map/ppermute | solution.py:61
  33.7 6.1 %collective-permute-start.10 = (bf16[128,512]{1,0:T(8,128)(2,1)S(1)}, bf16[128,512]{1,0:T(8,128)(2,1)S(1)}, u32[]{:S(2)}, u32[]{:S(2)}) collective-permute-start(bf16[128,512]{1,0:T(8,128)(2,1)S(1)} %get-tuple-element.56.grad.refs_4_), channel_id=1, source_target_pairs={{0,1},{1,0},{8,24},{9,25},{16,17},{17,16},{24,8},{25,9},{2,3},{3,2... | collective-permute-start | bytes 393224 | tf_op jit(solution)/shard_map/ppermute | solution.py:61
  35.3 6.7 %collective-permute-start.11 = (bf16[128,512]{1,0:T(8,128)(2,1)S(1)}, bf16[128,512]{1,0:T(8,128)(2,1)S(1)}, u32[]{:S(2)}, u32[]{:S(2)}) collective-permute-start(bf16[128,512]{1,0:T(8,128)(2,1)S(1)} %get-tuple-element.56.grad.refs_4_), channel_id=1, source_target_pairs={{0,16},{1,17},{8,9},{9,8},{16,0},{17,1},{24,25},{25,24},{2,18},{3,... | collective-permute-start | bytes 393224 | tf_op jit(solution)/shard_map/ppermute | solution.py:61
  39.8 6.3 %collective-permute-start.12 = (bf16[128,512]{1,0:T(8,128)(2,1)S(1)}, bf16[128,512]{1,0:T(8,128)(2,1)S(1)}, u32[]{:S(2)}, u32[]{:S(2)}) collective-permute-start(bf16[128,512]{1,0:T(8,128)(2,1)S(1)} %collective-permute-done.10.grad.refs_5_), channel_id=1, source_target_pairs={{0,16},{1,17},{8,9},{9,8},{16,0},{17,1},{24,25},{25,24},{2,18},{3,... | collective-permute-start | bytes 393224 | tf_op jit(solution)/shard_map/ppermute | solution.py:61
  46.1 6.4 %collective-permute-start.16 = (bf16[128,1024]{1,0:T(8,128)(2,1)S(1)}, bf16[128,1024]{1,0:T(8,128)(2,1)S(1)}, u32[]{:S(2)}, u32[]{:S(2)}) collective-permute-start(bf16[128,1024]{1,0:T(8,128)(2,1)S(1)} %columns.5), channel_id=1, source_target_pairs={{0,1},{1,0},{8,24},{9,25},{16,17},{17,16},{24,8},{25,9},{2,3},{3,2... | collective-permute-start | bytes 786440 | tf_op jit(solution)/shard_map/ppermute | solution.py:61
  48.4 2.0 %collective-permute-start.13 = (bf16[192,512]{1,0:T(8,128)(2,1)S(1)}, bf16[192,512]{1,0:T(8,128)(2,1)S(1)}, u32[]{:S(2)}, u32[]{:S(2)}) collective-permute-start(bf16[192,512]{1,0:T(8,128)(2,1)S(1)} %get-tuple-element.62), channel_id=1, source_target_pairs={{0,8},{8,0},{1,9},{9,1},{2,10},{10,2},{3,11},{11,3},{4,12},{12,4},... | collective-permute-start | bytes 589832 | tf_op jit(solution)/shard_map/ppermute | solution.py:46
  48.4 1.9 %collective-permute-start.14 = (bf16[192,512]{1,0:T(8,128)(2,1)S(1)}, bf16[192,512]{1,0:T(8,128)(2,1)S(1)}, u32[]{:S(2)}, u32[]{:S(2)}) collective-permute-start(bf16[192,512]{1,0:T(8,128)(2,1)S(1)} %get-tuple-element.63), channel_id=1, source_target_pairs={{0,8},{8,0},{1,9},{9,1},{2,10},{10,2},{3,11},{11,3},{4,12},{12,4},... | collective-permute-start | bytes 589832 | tf_op jit(solution)/shard_map/ppermute | solution.py:46
  48.9 1.4 %collective-permute-start.15 = (bf16[128,512]{1,0:T(8,128)(2,1)S(1)}, bf16[128,512]{1,0:T(8,128)(2,1)S(1)}, u32[]{:S(2)}, u32[]{:S(2)}) collective-permute-start(bf16[128,512]{1,0:T(8,128)(2,1)S(1)} %get-tuple-element.64), channel_id=1, source_target_pairs={{0,8},{8,0},{1,9},{9,1},{2,10},{10,2},{3,11},{11,3},{4,12},{12,4},... | collective-permute-start | bytes 393224 | tf_op jit(solution)/shard_map/ppermute | solution.py:46
  52.6 7.1 %collective-permute-start.19 = (bf16[128,512]{1,0:T(8,128)(2,1)S(1)}, bf16[128,512]{1,0:T(8,128)(2,1)S(1)}, u32[]{:S(2)}, u32[]{:S(2)}) collective-permute-start(bf16[128,512]{1,0:T(8,128)(2,1)S(1)} %get-tuple-element.73), channel_id=1, source_target_pairs={{0,6},{2,0},{4,2},{6,4},{1,7},{3,1},{5,3},{7,5},{8,14},{10,8},{12,... | collective-permute-start | bytes 393224 | tf_op jit(solution)/shard_map/ppermute | solution.py:42
  53.4 11.4 %collective-permute-start.20 = (bf16[128,512]{1,0:T(8,128)(2,1)S(1)}, bf16[128,512]{1,0:T(8,128)(2,1)S(1)}, u32[]{:S(2)}, u32[]{:S(2)}) collective-permute-start(bf16[128,512]{1,0:T(8,128)(2,1)S(1)} %get-tuple-element.74), channel_id=1, source_target_pairs={{0,4},{2,6},{4,0},{6,2},{1,5},{3,7},{5,1},{7,3},{8,12},{10,14},{12... | collective-permute-start | bytes 393224 | tf_op jit(solution)/shard_map/ppermute | solution.py:42
  54.4 10.4 %collective-permute-start.21 = (bf16[128,512]{1,0:T(8,128)(2,1)S(1)}, bf16[128,512]{1,0:T(8,128)(2,1)S(1)}, u32[]{:S(2)}, u32[]{:S(2)}) collective-permute-start(bf16[128,512]{1,0:T(8,128)(2,1)S(1)} %get-tuple-element.75), channel_id=1, source_target_pairs={{0,2},{2,4},{4,6},{6,0},{1,3},{3,5},{5,7},{7,1},{8,10},{10,12},{12... | collective-permute-start | bytes 393224 | tf_op jit(solution)/shard_map/ppermute | solution.py:42
  56.3 9.2 %collective-permute-start.17 = (bf16[128,1024]{1,0:T(8,128)(2,1)S(1)}, bf16[128,1024]{1,0:T(8,128)(2,1)S(1)}, u32[]{:S(2)}, u32[]{:S(2)}) collective-permute-start(bf16[128,1024]{1,0:T(8,128)(2,1)S(1)} %columns.6), channel_id=1, source_target_pairs={{0,16},{1,17},{8,9},{9,8},{16,0},{17,1},{24,25},{25,24},{2,18},{3,... | collective-permute-start | bytes 786440 | tf_op jit(solution)/shard_map/ppermute | solution.py:61
  58.0 7.8 %collective-permute-start.18 = (bf16[128,1024]{1,0:T(8,128)(2,1)S(1)}, bf16[128,1024]{1,0:T(8,128)(2,1)S(1)}, u32[]{:S(2)}, u32[]{:S(2)}) collective-permute-start(bf16[128,1024]{1,0:T(8,128)(2,1)S(1)} %columns.7), channel_id=1, source_target_pairs={{0,17},{1,16},{8,25},{9,24},{16,1},{17,0},{24,9},{25,8},{2,19},{3,... | collective-permute-start | bytes 786440 | tf_op jit(solution)/shard_map/ppermute | solution.py:61

commit v9 on v8

--- a/solution.py
+++ b/solution.py
@@ -32,7 +32,7 @@
         in_specs=[pl.BlockSpec(memory_space=space)] * len(args),
         out_specs=[vmem] * len(out_shapes) if many else vmem,
         scratch_shapes=scratch,
-        compiler_params=pltpu.CompilerParams(vmem_limit_bytes=room << 20),
+        compiler_params=pltpu.CompilerParams(vmem_limit_bytes=int(room * 2**20)),
         cost_estimate=pl.CostEstimate(flops=flops, bytes_accessed=moved, transcendentals=0),
     )(*args)
 
@@ -69,24 +69,26 @@
     return ((place * SPLIT + pair) * SPLIT + side) * TWIN + (core ^ (part % TWIN))
 
 
-def front_body(tokens, shard, both, mine, *refs):
-    *blocks, arrived = refs
+def front_body(shard, both, mine, arrived):
     rows, half = mine.shape[0], both.shape[0]
     first = lax.axis_index("side") * half
-    moves = []
+    copies = []
     for target, start in ((both, first), (mine, first + lax.axis_index("twin") * rows)):
-        moves.append((shard.at[pl.ds(pl.multiple_of(start, rows), target.shape[0])], target))
+        source = shard.at[pl.ds(pl.multiple_of(start, rows), target.shape[0])]
+        copies.append(pltpu.make_async_copy(source, target, arrived.at[len(copies)]))
+    for copy in copies:
+        copy.start()
+    for copy in copies:
+        copy.wait()
+
+
+def pack_body(tokens, *blocks):
     parts = lax.axis_size("line") * TWIN
     run = blocks[0].shape[1] // parts
     for far, block in enumerate(blocks):
         for part in range(parts):
             start = pl.multiple_of(run_of(part, far) * run, run)
-            moves.append((tokens.at[:, pl.ds(start, run)], block.at[:, pl.ds(part * run, run)]))
-    copies = [pltpu.make_async_copy(*move, arrived.at[i]) for i, move in enumerate(moves)]
-    for copy in copies:
-        copy.start()
-    for copy in copies:
-        copy.wait()
+            block[:, part * run : (part + 1) * run] = tokens[:, pl.ds(start, run)]
 
 
 def unpack_body(fars, *refs):
@@ -261,17 +263,17 @@
         key_weight = cut.transpose(1, 0, 2, 3).reshape(shard_rows, key_cols)
         tokens = split_runs(tokens, outer)
 
-    both, mine, *packed = local_call(
+    both, mine = local_call(
         "front",
         front_body,
-        [shape((TWIN * rows, key_cols), bf16), shape((rows, key_cols), bf16)] + [block_shape] * MEMBERS,
-        tokens,
+        [shape((TWIN * rows, key_cols), bf16), shape((rows, key_cols), bf16)],
         key_weight,
         space=pltpu.HBM,
-        room=53,
-        scratch=[pltpu.SemaphoreType.DMA((2 + MEMBERS * parts,))],
-    )
-    blocks = packed[:1] + [to_member(packed[far], far) for far in range(1, MEMBERS)]
+        scratch=[pltpu.SemaphoreType.DMA((2,))],
+        room=53.4,
+    )
+    packed = local_call("pack", pack_body, [block_shape] * MEMBERS, tokens)
+    blocks = [packed[0]] + [to_member(packed[far], far) for far in range(1, MEMBERS)]
     passed = [parted(both, step) for step in range(1, (line + 1) // 2)]
     if line % 2 == 0:
         passed.append(rotated(mine, "line", line // 2))
@@ -299,23 +301,20 @@
         shaped = shape((tok_rows, key_cols), kind)
         return local_call("share", share_body, shaped, blocks[far], weight, flops=flops)
 
-    passing = to_member(share(3, bf16), 2)
-    second = to_member(share(2, bf16), 2)
-    first = to_member(local_call("add", add_body, head_shape, share(1, f32), passing), 1)
-    normed, key_grad = local_call("norm", norm_body, [head_shape] * 2, share(0, f32), second, first, cotangent)
+    shares = [to_member(share(far, bf16), far) for far in (3, 1, 2)]
+    normed, key_grad = local_call("norm", norm_body, [head_shape] * 2, share(0, f32), *shares, cotangent)
     key_out = local_call("emit", emit_body, head_shape, normed)
 
-    grad_1 = to_member(key_grad, 1)
-    grad_2 = to_member(key_grad, 2)
-    grad_3 = to_member(grad_1, 2)
+    grad_3, grad_1, grad_2 = (to_member(key_grad, far) for far in (3, 1, 2))
 
     def columns(grad):
         return local_call("columns", columns_body, block_shape, grad, weight, moved=0)
 
-    seen_1, grad_2 = lax.optimization_barrier((grad_1, grad_2))
-    column_0, column_1 = columns(key_grad), columns(seen_1)
-    column_0, column_1, key_out, grad_3 = lax.optimization_barrier((column_0, column_1, key_out, grad_3))
+    column_0, column_1 = columns(key_grad), columns(grad_1)
     back_1 = to_member(column_1, 1)
+    column_0, _, key_out, grad_2, grad_3 = lax.optimization_barrier(
+        (column_0, column_1, key_out, grad_2, grad_3)
+    )
     terms = local_call(
         "terms",
         functools.partial(terms_body, grad_scale),
@@ -326,7 +325,7 @@
         grad_1,
         grad_2,
         grad_3,
-        flops=MEMBERS * flops,
+        moved=0,
     )
     kept, *theirs = terms
     theirs = [to_twin(piece) for piece in theirs]
@@ -341,12 +340,15 @@
         moved=0,
     )
     met = [sums[0]] + [rotated(sums[step], "line", -step) for step in range(1, line)]
-    weight_grad = local_call("final_sum", sum_body, shape((rows, key_cols), f32), *met, flops=32 * flops)
+    input_grad = unpack((0, 1), (column_0, back_1), shape((tok_rows, width), bf16))
+    met, input_grad = lax.optimization_barrier((met, input_grad))
+    weight_grad = local_call("final_sum", sum_body, shape((rows, key_cols), f32), *met, flops=16 * flops)
     if outer > 1:
         weight_grad = lax.psum_scatter(weight_grad, "outer", scatter_dimension=0, tiled=True)
 
-    back_2, back_3 = to_member(column_2, 2), to_member(column_3, 3)
-    input_grad = unpack((0, 1), (column_0, back_1), shape((tok_rows, width), bf16))
+    back_2 = to_member(column_2, 2)
+    column_3, back_1, back_2 = lax.optimization_barrier((column_3, back_1, back_2))
+    back_3 = to_member(column_3, 3)
     back_2, back_3, weight_grad = lax.optimization_barrier((back_2, back_3, weight_grad))
     input_grad = unpack((2, 3), (back_2, back_3), shape((tok_rows, width), bf16), input_grad)
     if outer > 1:

time: 66.9 us -> 65.2 us (0.975)
  waiting for transfers between devices: 31.5 us -> 26.7 us
  starting transfers between devices: 24.5 us -> 27.5 us
  local copies, waits for them, and re-layouts: 0.01 us -> 1.23 us
  Pallas kernels: 9.92 us -> 8.85 us
    ppermute x12, waiting for transfers between devices: 19.2 us -> 15.1 us  [to_member(): return lax.ppermute(block, ('side', 'twin', 'pair'), pairs)]
    ppermute x4, starting transfers between devices: 6.35 us -> 9.48 us  [rotated(): lax.ppermute(block, axis, [(i, (i + step) % size) for i in range(size)])]
    unnamed x2 -> x4, local copies, waits for them, and re-layouts: 0.01 us -> 1.23 us
    pallas_call x17, Pallas kernels: 8.1 us -> 7.02 us  [local_call(): pl.pallas_call(body, name=name, out_shape=out_shapes, in_specs=[pl.BlockS...]
    ppermute x4, waiting for transfers between devices: 11.9 us -> 11.3 us  [rotated(): lax.ppermute(block, axis, [(i, (i + step) % size) for i in range(size)])]
  transfers between devices with their start and end apart: 22 -> 22, of which waited for: 11 -> 8; matrix products, arithmetic and copies ran while one was open for 0% -> 0% of each run, Pallas kernels for 9% -> 9%
where the time goes in v9:
time: 65.2 us; the launch traced here: 65 us
  starting transfers between devices  27.5 us (42%)
  waiting for transfers between devices  26.7 us (41%)
  Pallas kernels  8.85 us (14%)
  local copies, waits for them, and re-layouts  1.23 us (2%)
  between operations  0.8 us (1%)
    ppermute x12, waiting for transfers between devices, to_member(): return lax.ppermute(block, ('side', 'twin', 'pair'), pairs)  15.1 us
    ppermute x12, starting transfers between devices, to_member(): return lax.ppermute(block, ('side', 'twin', 'pair'), pairs)  13.7 us
    ppermute x4, waiting for transfers between devices, rotated(): lax.ppermute(block, axis, [(i, (i + step) % size) for i in range(size)])  11.3 us
    ppermute x4, starting transfers between devices, rotated(): lax.ppermute(block, axis, [(i, (i + step) % size) for i in range(size)])  9.48 us
    pallas_call x17, Pallas kernels, local_call(): pl.pallas_call(body, name=name, out_shape=out_shapes, in_specs=[pl.BlockS...  7.02 us
    ppermute x1, starting transfers between devices, parted(): return lax.ppermute(block, ('twin', 'line'), list(enumerate(to)))  3.08 us
    pallas_call x2, Pallas kernels, unpack(): pl.pallas_call(functools.partial(unpack_body, fars), name='unpack', out_s...  1.83 us
  transfers between devices with their start and end apart: 22, of which 8 were waited for; matrix products, arithmetic and copies ran while one was open for 0% of the time, Pallas kernels for 9%

profile of v9, /device:TPU:0, one launch (start us, length us, event | category | flops | bytes accessed | tf_op | source)
XLA Modules:
  0.0 65.0 jit_solution(10843355952454892233)
XLA Ops:
  0.6 1.0 %front.1 = (bf16[256,512]{1,0:T(8,128)(2,1)S(1)}, bf16[128,512]{1,0:T(8,128)(2,1)S(1)}) custom-call(bf16[512,512]{1,0:T(8,128)(2,1)} %shard.1), custom_call_target="tpu_custom_call" | custom-call | bytes 524288 | tf_op jit(solution)/shard_map/front/pallas_call | solution.py:28
  1.6 3.1 %collective-permute-start = (bf16[256,512]{1,0:T(8,128)(2,1)S(1)}, bf16[256,512]{1,0:T(8,128)(2,1)S(1)}, u32[]{:S(2)}, u32[]{:S(2)}) collective-permute-start(bf16[256,512]{1,0:T(8,128)(2,1)S(1)} %get-tuple-element.47.refs_0_), channel_id=1, source_target_pairs={{0,2},{2,4},{4,6},{6,0},{8,14},{10,8},{12,10},{14,12},{1,3},{3,5},... | collective-permute-start | bytes 786440 | tf_op jit(solution)/shard_map/ppermute | solution.py:146
  4.7 2.6 %collective-permute-start.1 = (bf16[128,512]{1,0:T(8,128)(2,1)S(1)}, bf16[128,512]{1,0:T(8,128)(2,1)S(1)}, u32[]{:S(2)}, u32[]{:S(2)}) collective-permute-start(bf16[128,512]{1,0:T(8,128)(2,1)S(1)} %get-tuple-element.48), channel_id=1, source_target_pairs={{0,4},{2,6},{4,0},{6,2},{1,5},{3,7},{5,1},{7,3},{8,12},{10,14},{12... | collective-permute-start | bytes 393224 | tf_op jit(solution)/shard_map/ppermute | solution.py:42
  7.3 1.2 %copy-done = bf16[128,4096]{1,0:T(8,128)(2,1)S(1)} copy-done((bf16[128,4096]{1,0:T(8,128)(2,1)S(1)}, bf16[128,4096]{1,0:T(8,128)(2,1)}, u32[]{:S(2)}) %copy-start) | copy-done | bytes 1048600
  8.8 1.6 %collective-permute-start.4 = (bf16[128,1024]{1,0:T(8,128)(2,1)S(1)}, bf16[128,1024]{1,0:T(8,128)(2,1)S(1)}, u32[]{:S(2)}, u32[]{:S(2)}) collective-permute-start(bf16[128,1024]{1,0:T(8,128)(2,1)S(1)} %get-tuple-element.52), channel_id=1, source_target_pairs={{0,1},{1,0},{8,24},{9,25},{16,17},{17,16},{24,8},{25,9},{2,3},{3,2... | collective-permute-start | bytes 786440 | tf_op jit(solution)/shard_map/ppermute | solution.py:61
  10.4 1.5 %collective-permute-start.5 = (bf16[128,1024]{1,0:T(8,128)(2,1)S(1)}, bf16[128,1024]{1,0:T(8,128)(2,1)S(1)}, u32[]{:S(2)}, u32[]{:S(2)}) collective-permute-start(bf16[128,1024]{1,0:T(8,128)(2,1)S(1)} %get-tuple-element.53), channel_id=1, source_target_pairs={{0,16},{1,17},{8,9},{9,8},{16,0},{17,1},{24,25},{25,24},{2,18},{3,... | collective-permute-start | bytes 786440 | tf_op jit(solution)/shard_map/ppermute | solution.py:61
  11.9 0.5 collective-permute-start.6
  12.4 4.8 %collective-permute-done.1.refs_1_.refs_2_ = bf16[128,512]{1,0:T(8,128)(2,1)S(1)} collective-permute-done((bf16[128,512]{1,0:T(8,128)(2,1)S(1)}, bf16[128,512]{1,0:T(8,128)(2,1)S(1)}, u32[]{:S(2)}, u32[]{:S(2)}) %collective-permute-start.1) | collective-permute-done | bytes 131104 | tf_op jit(solution)/shard_map/ppermute | solution.py:42
  17.2 0.5 collective-permute-start.2
  17.8 5.1 %collective-permute-done.4.block.refs_1_ = bf16[128,1024]{1,0:T(8,128)(2,1)S(1)} collective-permute-done((bf16[128,1024]{1,0:T(8,128)(2,1)S(1)}, bf16[128,1024]{1,0:T(8,128)(2,1)S(1)}, u32[]{:S(2)}, u32[]{:S(2)}) %collective-permute-start.4) | collective-permute-done | bytes 262176 | tf_op jit(solution)/shard_map/ppermute | solution.py:61
  24.0 1.5 %collective-permute-start.7 = (bf16[128,512]{1,0:T(8,128)(2,1)S(1)}, bf16[128,512]{1,0:T(8,128)(2,1)S(1)}, u32[]{:S(2)}, u32[]{:S(2)}) collective-permute-start(bf16[128,512]{1,0:T(8,128)(2,1)S(1)} %share.5), channel_id=1, source_target_pairs={{0,17},{1,16},{8,25},{9,24},{16,1},{17,0},{24,9},{25,8},{2,19},{3,... | collective-permute-start | bytes 393224 | tf_op jit(solution)/shard_map/ppermute | solution.py:61
  25.6 1.2 %collective-permute-start.8 = (bf16[128,512]{1,0:T(8,128)(2,1)S(1)}, bf16[128,512]{1,0:T(8,128)(2,1)S(1)}, u32[]{:S(2)}, u32[]{:S(2)}) collective-permute-start(bf16[128,512]{1,0:T(8,128)(2,1)S(1)} %share.6), channel_id=1, source_target_pairs={{0,1},{1,0},{8,24},{9,25},{16,17},{17,16},{24,8},{25,9},{2,3},{3,2... | collective-permute-start | bytes 393224 | tf_op jit(solution)/shard_map/ppermute | solution.py:61
  26.7 0.8 %collective-permute-start.9 = (bf16[128,512]{1,0:T(8,128)(2,1)S(1)}, bf16[128,512]{1,0:T(8,128)(2,1)S(1)}, u32[]{:S(2)}, u32[]{:S(2)}) collective-permute-start(bf16[128,512]{1,0:T(8,128)(2,1)S(1)} %share.7), channel_id=1, source_target_pairs={{0,16},{1,17},{8,9},{9,8},{16,0},{17,1},{24,25},{25,24},{2,18},{3,... | collective-permute-start | bytes 393224 | tf_op jit(solution)/shard_map/ppermute | solution.py:61
  27.9 2.3 %collective-permute-done.7.refs_1_ = bf16[128,512]{1,0:T(8,128)(2,1)S(1)} collective-permute-done((bf16[128,512]{1,0:T(8,128)(2,1)S(1)}, bf16[128,512]{1,0:T(8,128)(2,1)S(1)}, u32[]{:S(2)}, u32[]{:S(2)}) %collective-permute-start.7) | collective-permute-done | bytes 131104 | tf_op jit(solution)/shard_map/ppermute | solution.py:61
  30.1 2.5 %collective-permute-done.8.refs_2_ = bf16[128,512]{1,0:T(8,128)(2,1)S(1)} collective-permute-done((bf16[128,512]{1,0:T(8,128)(2,1)S(1)}, bf16[128,512]{1,0:T(8,128)(2,1)S(1)}, u32[]{:S(2)}, u32[]{:S(2)}) %collective-permute-start.8) | collective-permute-done | bytes 131104 | tf_op jit(solution)/shard_map/ppermute | solution.py:61
  32.9 1.5 %collective-permute-start.10 = (bf16[128,512]{1,0:T(8,128)(2,1)S(1)}, bf16[128,512]{1,0:T(8,128)(2,1)S(1)}, u32[]{:S(2)}, u32[]{:S(2)}) collective-permute-start(bf16[128,512]{1,0:T(8,128)(2,1)S(1)} %get-tuple-element.61.grad.refs_4_), channel_id=1, source_target_pairs={{0,1},{1,0},{8,24},{9,25},{16,17},{17,16},{24,8},{25,9},{2,3},{3,2... | collective-permute-start | bytes 393224 | tf_op jit(solution)/shard_map/ppermute | solution.py:61
  34.7 1.7 %collective-permute-start.11 = (bf16[128,512]{1,0:T(8,128)(2,1)S(1)}, bf16[128,512]{1,0:T(8,128)(2,1)S(1)}, u32[]{:S(2)}, u32[]{:S(2)}) collective-permute-start(bf16[128,512]{1,0:T(8,128)(2,1)S(1)} %get-tuple-element.61.grad.refs_4_), channel_id=1, source_target_pairs={{0,16},{1,17},{8,9},{9,8},{16,0},{17,1},{24,25},{25,24},{2,18},{3,... | collective-permute-start | bytes 393224 | tf_op jit(solution)/shard_map/ppermute | solution.py:61
  36.5 4.7 %collective-permute-done.10.grad.refs_5_ = bf16[128,512]{1,0:T(8,128)(2,1)S(1)} collective-permute-done((bf16[128,512]{1,0:T(8,128)(2,1)S(1)}, bf16[128,512]{1,0:T(8,128)(2,1)S(1)}, u32[]{:S(2)}, u32[]{:S(2)}) %collective-permute-start.10) | collective-permute-done | bytes 131104 | tf_op jit(solution)/shard_map/ppermute | solution.py:61
  41.6 2.2 %collective-permute-start.16 = (bf16[128,1024]{1,0:T(8,128)(2,1)S(1)}, bf16[128,1024]{1,0:T(8,128)(2,1)S(1)}, u32[]{:S(2)}, u32[]{:S(2)}) collective-permute-start(bf16[128,1024]{1,0:T(8,128)(2,1)S(1)} %columns.5), channel_id=1, source_target_pairs={{0,1},{1,0},{8,24},{9,25},{16,17},{17,16},{24,8},{25,9},{2,3},{3,2... | collective-permute-start | bytes 786440 | tf_op jit(solution)/shard_map/ppermute | solution.py:61
  44.3 0.7 %emit.1 = bf16[128,512]{1,0:T(8,128)(2,1)} custom-call(bf16[128,512]{1,0:T(8,128)(2,1)S(1)} %get-tuple-element.62.held), custom_call_target="tpu_custom_call" | custom-call | bytes 131072 | tf_op jit(solution)/shard_map/emit/pallas_call | solution.py:28
  45.0 0.7 %terms.1 = (f32[4,128,512]{2,1,0:T(8,128)S(1)}, bf16[192,512]{1,0:T(8,128)(2,1)S(1)}, bf16[192,512]{1,0:T(8,128)(2,1)S(1)}, bf16[128,512]{1,0:T(8,128)(2,1)S(1)}) custom-call(bf16[128,1024]{1,0:T(8,128)(2,1)S(1)} %get-tuple-element.55.block.refs_0_, bf16[128,1024]{1,0:T(8,128)(2,1)S(1)} %collective-permute-done.4.block.refs_1_, ...), custom_call_target="tpu_custom_call" | custom-call | tf_op jit(solution)/shard_map/terms/pallas_call | solution.py:28
  45.8 0.5 collective-permute-start.14
  46.4 0.5 columns.6
  46.8 0.5 columns.7
  48.3 2.4 %collective-permute-start.19 = (bf16[128,512]{1,0:T(8,128)(2,1)S(1)}, bf16[128,512]{1,0:T(8,128)(2,1)S(1)}, u32[]{:S(2)}, u32[]{:S(2)}) collective-permute-start(bf16[128,512]{1,0:T(8,128)(2,1)S(1)} %get-tuple-element.79), channel_id=1, source_target_pairs={{0,6},{2,0},{4,2},{6,4},{1,7},{3,1},{5,3},{7,5},{8,14},{10,8},{12,... | collective-permute-start | bytes 393224 | tf_op jit(solution)/shard_map/ppermute | solution.py:42
  50.8 2.5 %collective-permute-start.20 = (bf16[128,512]{1,0:T(8,128)(2,1)S(1)}, bf16[128,512]{1,0:T(8,128)(2,1)S(1)}, u32[]{:S(2)}, u32[]{:S(2)}) collective-permute-start(bf16[128,512]{1,0:T(8,128)(2,1)S(1)} %get-tuple-element.80), channel_id=1, source_target_pairs={{0,4},{2,6},{4,0},{6,2},{1,5},{3,7},{5,1},{7,3},{8,12},{10,14},{12... | collective-permute-start | bytes 393224 | tf_op jit(solution)/shard_map/ppermute | solution.py:42
  53.3 1.9 %collective-permute-start.21 = (bf16[128,512]{1,0:T(8,128)(2,1)S(1)}, bf16[128,512]{1,0:T(8,128)(2,1)S(1)}, u32[]{:S(2)}, u32[]{:S(2)}) collective-permute-start(bf16[128,512]{1,0:T(8,128)(2,1)S(1)} %get-tuple-element.81), channel_id=1, source_target_pairs={{0,2},{2,4},{4,6},{6,0},{1,3},{3,5},{5,7},{7,1},{8,10},{10,12},{12... | collective-permute-start | bytes 393224 | tf_op jit(solution)/shard_map/ppermute | solution.py:42
  55.2 0.7 %collective-permute-start.18 = (bf16[128,1024]{1,0:T(8,128)(2,1)S(1)}, bf16[128,1024]{1,0:T(8,128)(2,1)S(1)}, u32[]{:S(2)}, u32[]{:S(2)}) collective-permute-start(bf16[128,1024]{1,0:T(8,128)(2,1)S(1)} %columns.7), channel_id=1, source_target_pairs={{0,17},{1,16},{8,25},{9,24},{16,1},{17,0},{24,9},{25,8},{2,19},{3,... | collective-permute-start | bytes 786440 | tf_op jit(solution)/shard_map/ppermute | solution.py:61
  56.0 0.9 %unpack.2.refs_2_ = bf16[128,4096]{1,0:T(8,128)(2,1)} custom-call(bf16[128,1024]{1,0:T(8,128)(2,1)S(1)} %columns.4.refs_0_, bf16[128,1024]{1,0:T(8,128)(2,1)S(1)} %collective-permute-done.16.refs_1_), custom_call_target="tpu_custom_call" | custom-call | tf_op jit(solution)/shard_map/unpack/pallas_call | solution.py:114
  56.9 6.4 %collective-permute-done.20.refs_2_ = bf16[128,512]{1,0:T(8,128)(2,1)S(1)} collective-permute-done((bf16[128,512]{1,0:T(8,128)(2,1)S(1)}, bf16[128,512]{1,0:T(8,128)(2,1)S(1)}, u32[]{:S(2)}, u32[]{:S(2)}) %collective-permute-start.20) | collective-permute-done | bytes 131104 | tf_op jit(solution)/shard_map/ppermute | solution.py:42
  63.4 0.8 %final_sum.1 = f32[128,512]{1,0:T(8,128)} custom-call(f32[128,512]{1,0:T(8,128)S(1)} %get-tuple-element.83.refs_0_, bf16[128,512]{1,0:T(8,128)(2,1)S(1)} %collective-permute-done.19.refs_1_, bf16[128,512]{1,0:T(8,128)(2,1)S(1)} %collective-permute-done.20.refs_2_, bf16[128,512]{1,0:T(8,128)(2,1)S(1)} %collective-permute-done.21.refs_3_), custom_call_target="tpu_custom_call" | custom-call | flops 2147483648 | bytes 655360 | tf_op jit(solution)/shard_map/final_sum/pallas_call | solution.py:28
  64.1 0.9 %unpack.3 = bf16[128,4096]{1,0:T(8,128)(2,1)} custom-call(bf16[128,1024]{1,0:T(8,128)(2,1)S(1)} %collective-permute-done.17.refs_0_, bf16[128,1024]{1,0:T(8,128)(2,1)S(1)} %collective-permute-done.18.refs_1_, bf16[128,4096]{1,0:T(8,128)(2,1)} %unpack.2.refs_2_), custom_call_target="tpu_custom_call", output_to_operand_aliasing={{}: (2, {})} | custom-call | tf_op jit(solution)/shard_map/unpack/pallas_call | solution.py:114
  (35 shorter events, 4.4 us)
Async XLA Ops:
  1.6 15.6 %collective-permute-start = (bf16[256,512]{1,0:T(8,128)(2,1)S(1)}, bf16[256,512]{1,0:T(8,128)(2,1)S(1)}, u32[]{:S(2)}, u32[]{:S(2)}) collective-permute-start(bf16[256,512]{1,0:T(8,128)(2,1)S(1)} %get-tuple-element.47.refs_0_), channel_id=1, source_target_pairs={{0,2},{2,4},{4,6},{6,0},{8,14},{10,8},{12,10},{14,12},{1,3},{3,5},... | collective-permute-start | bytes 786440 | tf_op jit(solution)/shard_map/ppermute | solution.py:146
  4.7 12.5 %collective-permute-start.1 = (bf16[128,512]{1,0:T(8,128)(2,1)S(1)}, bf16[128,512]{1,0:T(8,128)(2,1)S(1)}, u32[]{:S(2)}, u32[]{:S(2)}) collective-permute-start(bf16[128,512]{1,0:T(8,128)(2,1)S(1)} %get-tuple-element.48), channel_id=1, source_target_pairs={{0,4},{2,6},{4,0},{6,2},{1,5},{3,7},{5,1},{7,3},{8,12},{10,14},{12... | collective-permute-start | bytes 393224 | tf_op jit(solution)/shard_map/ppermute | solution.py:42
  7.3 1.2 %copy-start = (bf16[128,4096]{1,0:T(8,128)(2,1)S(1)}, bf16[128,4096]{1,0:T(8,128)(2,1)}, u32[]{:S(2)}) copy-start(bf16[128,4096]{1,0:T(8,128)(2,1)} %tokens.1) | copy-start | bytes 3145732
  8.8 14.1 %collective-permute-start.4 = (bf16[128,1024]{1,0:T(8,128)(2,1)S(1)}, bf16[128,1024]{1,0:T(8,128)(2,1)S(1)}, u32[]{:S(2)}, u32[]{:S(2)}) collective-permute-start(bf16[128,1024]{1,0:T(8,128)(2,1)S(1)} %get-tuple-element.52), channel_id=1, source_target_pairs={{0,1},{1,0},{8,24},{9,25},{16,17},{17,16},{24,8},{25,9},{2,3},{3,2... | collective-permute-start | bytes 786440 | tf_op jit(solution)/shard_map/ppermute | solution.py:61
  10.4 12.5 %collective-permute-start.5 = (bf16[128,1024]{1,0:T(8,128)(2,1)S(1)}, bf16[128,1024]{1,0:T(8,128)(2,1)S(1)}, u32[]{:S(2)}, u32[]{:S(2)}) collective-permute-start(bf16[128,1024]{1,0:T(8,128)(2,1)S(1)} %get-tuple-element.53), channel_id=1, source_target_pairs={{0,16},{1,17},{8,9},{9,8},{16,0},{17,1},{24,25},{25,24},{2,18},{3,... | collective-permute-start | bytes 786440 | tf_op jit(solution)/shard_map/ppermute | solution.py:61
  11.9 11.0 %collective-permute-start.6 = (bf16[128,1024]{1,0:T(8,128)(2,1)S(1)}, bf16[128,1024]{1,0:T(8,128)(2,1)S(1)}, u32[]{:S(2)}, u32[]{:S(2)}) collective-permute-start(bf16[128,1024]{1,0:T(8,128)(2,1)S(1)} %get-tuple-element.54), channel_id=1, source_target_pairs={{0,17},{1,16},{8,25},{9,24},{16,1},{17,0},{24,9},{25,8},{2,19},{3,... | collective-permute-start | bytes 786440 | tf_op jit(solution)/shard_map/ppermute | solution.py:61
  17.2 5.7 %collective-permute-start.2 = (bf16[192,512]{1,0:T(8,128)(2,1)S(1)}, bf16[192,512]{1,0:T(8,128)(2,1)S(1)}, u32[]{:S(2)}, u32[]{:S(2)}) collective-permute-start(bf16[192,512]{1,0:T(8,128)(2,1)S(1)} %get-tuple-element.49), channel_id=1, source_target_pairs={{0,8},{8,0},{1,9},{9,1},{2,10},{10,2},{3,11},{11,3},{4,12},{12,4},... | collective-permute-start | bytes 589832 | tf_op jit(solution)/shard_map/ppermute | solution.py:46
  17.7 5.2 %collective-permute-start.3 = (bf16[192,512]{1,0:T(8,128)(2,1)S(1)}, bf16[192,512]{1,0:T(8,128)(2,1)S(1)}, u32[]{:S(2)}, u32[]{:S(2)}) collective-permute-start(bf16[192,512]{1,0:T(8,128)(2,1)S(1)} %get-tuple-element.50), channel_id=1, source_target_pairs={{0,8},{8,0},{1,9},{9,1},{2,10},{10,2},{3,11},{11,3},{4,12},{12,4},... | collective-permute-start | bytes 589832 | tf_op jit(solution)/shard_map/ppermute | solution.py:46
  24.0 8.7 %copy-start.1 = (bf16[128,512]{1,0:T(8,128)(2,1)S(1)}, bf16[128,512]{1,0:T(8,128)(2,1)}, u32[]{:S(2)}) copy-start(bf16[128,512]{1,0:T(8,128)(2,1)} %refs_4_.1) | copy-start | bytes 393220
  24.0 6.1 %collective-permute-start.7 = (bf16[128,512]{1,0:T(8,128)(2,1)S(1)}, bf16[128,512]{1,0:T(8,128)(2,1)S(1)}, u32[]{:S(2)}, u32[]{:S(2)}) collective-permute-start(bf16[128,512]{1,0:T(8,128)(2,1)S(1)} %share.5), channel_id=1, source_target_pairs={{0,17},{1,16},{8,25},{9,24},{16,1},{17,0},{24,9},{25,8},{2,19},{3,... | collective-permute-start | bytes 393224 | tf_op jit(solution)/shard_map/ppermute | solution.py:61
  25.6 7.1 %collective-permute-start.8 = (bf16[128,512]{1,0:T(8,128)(2,1)S(1)}, bf16[128,512]{1,0:T(8,128)(2,1)S(1)}, u32[]{:S(2)}, u32[]{:S(2)}) collective-permute-start(bf16[128,512]{1,0:T(8,128)(2,1)S(1)} %share.6), channel_id=1, source_target_pairs={{0,1},{1,0},{8,24},{9,25},{16,17},{17,16},{24,8},{25,9},{2,3},{3,2... | collective-permute-start | bytes 393224 | tf_op jit(solution)/shard_map/ppermute | solution.py:61
  26.7 5.9 %collective-permute-start.9 = (bf16[128,512]{1,0:T(8,128)(2,1)S(1)}, bf16[128,512]{1,0:T(8,128)(2,1)S(1)}, u32[]{:S(2)}, u32[]{:S(2)}) collective-permute-start(bf16[128,512]{1,0:T(8,128)(2,1)S(1)} %share.7), channel_id=1, source_target_pairs={{0,16},{1,17},{8,9},{9,8},{16,0},{17,1},{24,25},{25,24},{2,18},{3,... | collective-permute-start | bytes 393224 | tf_op jit(solution)/shard_map/ppermute | solution.py:61
  32.9 8.2 %collective-permute-start.10 = (bf16[128,512]{1,0:T(8,128)(2,1)S(1)}, bf16[128,512]{1,0:T(8,128)(2,1)S(1)}, u32[]{:S(2)}, u32[]{:S(2)}) collective-permute-start(bf16[128,512]{1,0:T(8,128)(2,1)S(1)} %get-tuple-element.61.grad.refs_4_), channel_id=1, source_target_pairs={{0,1},{1,0},{8,24},{9,25},{16,17},{17,16},{24,8},{25,9},{2,3},{3,2... | collective-permute-start | bytes 393224 | tf_op jit(solution)/shard_map/ppermute | solution.py:61
  34.4 10.6 %collective-permute-start.12 = (bf16[128,512]{1,0:T(8,128)(2,1)S(1)}, bf16[128,512]{1,0:T(8,128)(2,1)S(1)}, u32[]{:S(2)}, u32[]{:S(2)}) collective-permute-start(bf16[128,512]{1,0:T(8,128)(2,1)S(1)} %get-tuple-element.61.grad.refs_4_), channel_id=1, source_target_pairs={{0,17},{1,16},{8,25},{9,24},{16,1},{17,0},{24,9},{25,8},{2,19},{3,... | collective-permute-start | bytes 393224 | tf_op jit(solution)/shard_map/ppermute | solution.py:61
  34.7 10.2 %collective-permute-start.11 = (bf16[128,512]{1,0:T(8,128)(2,1)S(1)}, bf16[128,512]{1,0:T(8,128)(2,1)S(1)}, u32[]{:S(2)}, u32[]{:S(2)}) collective-permute-start(bf16[128,512]{1,0:T(8,128)(2,1)S(1)} %get-tuple-element.61.grad.refs_4_), channel_id=1, source_target_pairs={{0,16},{1,17},{8,9},{9,8},{16,0},{17,1},{24,25},{25,24},{2,18},{3,... | collective-permute-start | bytes 393224 | tf_op jit(solution)/shard_map/ppermute | solution.py:61
  41.6 6.5 %collective-permute-start.16 = (bf16[128,1024]{1,0:T(8,128)(2,1)S(1)}, bf16[128,1024]{1,0:T(8,128)(2,1)S(1)}, u32[]{:S(2)}, u32[]{:S(2)}) collective-permute-start(bf16[128,1024]{1,0:T(8,128)(2,1)S(1)} %columns.5), channel_id=1, source_target_pairs={{0,1},{1,0},{8,24},{9,25},{16,17},{17,16},{24,8},{25,9},{2,3},{3,2... | collective-permute-start | bytes 786440 | tf_op jit(solution)/shard_map/ppermute | solution.py:61
  45.7 2.0 %collective-permute-start.13 = (bf16[192,512]{1,0:T(8,128)(2,1)S(1)}, bf16[192,512]{1,0:T(8,128)(2,1)S(1)}, u32[]{:S(2)}, u32[]{:S(2)}) collective-permute-start(bf16[192,512]{1,0:T(8,128)(2,1)S(1)} %get-tuple-element.66), channel_id=1, source_target_pairs={{0,8},{8,0},{1,9},{9,1},{2,10},{10,2},{3,11},{11,3},{4,12},{12,4},... | collective-permute-start | bytes 589832 | tf_op jit(solution)/shard_map/ppermute | solution.py:46
  45.8 1.9 %collective-permute-start.14 = (bf16[192,512]{1,0:T(8,128)(2,1)S(1)}, bf16[192,512]{1,0:T(8,128)(2,1)S(1)}, u32[]{:S(2)}, u32[]{:S(2)}) collective-permute-start(bf16[192,512]{1,0:T(8,128)(2,1)S(1)} %get-tuple-element.67), channel_id=1, source_target_pairs={{0,8},{8,0},{1,9},{9,1},{2,10},{10,2},{3,11},{11,3},{4,12},{12,4},... | collective-permute-start | bytes 589832 | tf_op jit(solution)/shard_map/ppermute | solution.py:46
  46.3 1.4 %collective-permute-start.15 = (bf16[128,512]{1,0:T(8,128)(2,1)S(1)}, bf16[128,512]{1,0:T(8,128)(2,1)S(1)}, u32[]{:S(2)}, u32[]{:S(2)}) collective-permute-start(bf16[128,512]{1,0:T(8,128)(2,1)S(1)} %get-tuple-element.68), channel_id=1, source_target_pairs={{0,8},{8,0},{1,9},{9,1},{2,10},{10,2},{3,11},{11,3},{4,12},{12,4},... | collective-permute-start | bytes 393224 | tf_op jit(solution)/shard_map/ppermute | solution.py:46
  48.2 7.1 %collective-permute-start.17 = (bf16[128,1024]{1,0:T(8,128)(2,1)S(1)}, bf16[128,1024]{1,0:T(8,128)(2,1)S(1)}, u32[]{:S(2)}, u32[]{:S(2)}) collective-permute-start(bf16[128,1024]{1,0:T(8,128)(2,1)S(1)} %columns.6), channel_id=1, source_target_pairs={{0,16},{1,17},{8,9},{9,8},{16,0},{17,1},{24,25},{25,24},{2,18},{3,... | collective-permute-start | bytes 786440 | tf_op jit(solution)/shard_map/ppermute | solution.py:61
  48.3 8.6 %collective-permute-start.19 = (bf16[128,512]{1,0:T(8,128)(2,1)S(1)}, bf16[128,512]{1,0:T(8,128)(2,1)S(1)}, u32[]{:S(2)}, u32[]{:S(2)}) collective-permute-start(bf16[128,512]{1,0:T(8,128)(2,1)S(1)} %get-tuple-element.79), channel_id=1, source_target_pairs={{0,6},{2,0},{4,2},{6,4},{1,7},{3,1},{5,3},{7,5},{8,14},{10,8},{12,... | collective-permute-start | bytes 393224 | tf_op jit(solution)/shard_map/ppermute | solution.py:42
  50.8 12.6 %collective-permute-start.20 = (bf16[128,512]{1,0:T(8,128)(2,1)S(1)}, bf16[128,512]{1,0:T(8,128)(2,1)S(1)}, u32[]{:S(2)}, u32[]{:S(2)}) collective-permute-start(bf16[128,512]{1,0:T(8,128)(2,1)S(1)} %get-tuple-element.80), channel_id=1, source_target_pairs={{0,4},{2,6},{4,0},{6,2},{1,5},{3,7},{5,1},{7,3},{8,12},{10,14},{12... | collective-permute-start | bytes 393224 | tf_op jit(solution)/shard_map/ppermute | solution.py:42
  53.3 10.1 %collective-permute-start.21 = (bf16[128,512]{1,0:T(8,128)(2,1)S(1)}, bf16[128,512]{1,0:T(8,128)(2,1)S(1)}, u32[]{:S(2)}, u32[]{:S(2)}) collective-permute-start(bf16[128,512]{1,0:T(8,128)(2,1)S(1)} %get-tuple-element.81), channel_id=1, source_target_pairs={{0,2},{2,4},{4,6},{6,0},{1,3},{3,5},{5,7},{7,1},{8,10},{10,12},{12... | collective-permute-start | bytes 393224 | tf_op jit(solution)/shard_map/ppermute | solution.py:42
  55.2 8.9 %collective-permute-start.18 = (bf16[128,1024]{1,0:T(8,128)(2,1)S(1)}, bf16[128,1024]{1,0:T(8,128)(2,1)S(1)}, u32[]{:S(2)}, u32[]{:S(2)}) collective-permute-start(bf16[128,1024]{1,0:T(8,128)(2,1)S(1)} %columns.7), channel_id=1, source_target_pairs={{0,17},{1,16},{8,25},{9,24},{16,1},{17,0},{24,9},{25,8},{2,19},{3,... | collective-permute-start | bytes 786440 | tf_op jit(solution)/shard_map/ppermute | solution.py:61

commit v10 on v9

--- a/solution.py
+++ b/solution.py
@@ -1,5 +1,4 @@
 import functools
-import itertools
 import math
 
 import jax
@@ -46,24 +45,17 @@
     return lax.ppermute(block, "twin", [(0, 1), (1, 0)])
 
 
-def flips(far, core):
-    return (0, 0) if far == 0 else (1, 1) if far == 3 else (core, 1 - core) if far == 1 else (1 - core, core)
+def flips(far):
+    return far // SPLIT, far % SPLIT
 
 
 def to_member(block, far):
-    def index(side, core, pair):
-        return (side * TWIN + core) * SPLIT + pair
-
-    pairs = []
-    for side, core, pair in itertools.product(range(SPLIT), range(TWIN), range(SPLIT)):
-        over, across = flips(far, core)
-        pairs.append((index(side, core, pair), index(side ^ over, core, pair ^ across)))
-    return lax.ppermute(block, ("side", "twin", "pair"), pairs)
+    return lax.ppermute(block, ("side", "pair"), [(i, i ^ far) for i in range(MEMBERS)])
 
 
 def run_of(part, far):
     line, core = lax.axis_size("line"), lax.axis_index("twin")
-    over, across = flips(far, core)
+    over, across = flips(far)
     place = lax.rem(lax.axis_index("line") + line - part // TWIN, line)
     side, pair = lax.axis_index("side") ^ over, lax.axis_index("pair") ^ across
     return ((place * SPLIT + pair) * SPLIT + side) * TWIN + (core ^ (part % TWIN))

time: 65.2 us -> 64.7 us (level)
  waiting for transfers between devices: 26.7 us -> 22.5 us
  starting transfers between devices: 27.5 us -> 31.2 us
    ppermute x12, waiting for transfers between devices: 15.1 us -> 12.2 us  [to_member(): lax.ppermute(block, ('side', 'pair'), [(i, i ^ far) for i in range(MEMBER...]
    ppermute x4, starting transfers between devices: 9.48 us -> 11.8 us  [rotated(): lax.ppermute(block, axis, [(i, (i + step) % size) for i in range(size)])]
    ppermute x12, starting transfers between devices: 13.7 us -> 15 us  [to_member(): lax.ppermute(block, ('side', 'pair'), [(i, i ^ far) for i in range(MEMBER...]
    ppermute x4, waiting for transfers between devices: 11.3 us -> 9.94 us  [rotated(): lax.ppermute(block, axis, [(i, (i + step) % size) for i in range(size)])]
  transfers between devices with their start and end apart: 22 -> 22, of which waited for: 8 -> 9; matrix products, arithmetic and copies ran while one was open for 0% -> 0% of each run, Pallas kernels for 9% -> 9%
where the time goes in v10:
time: 64.7 us; the launch traced here: 64.5 us
  starting transfers between devices  31.2 us (48%)
  waiting for transfers between devices  22.5 us (35%)
  Pallas kernels  8.85 us (14%)
  local copies, waits for them, and re-layouts  1.23 us (2%)
  between operations  0.79 us (1%)
    ppermute x12, starting transfers between devices, to_member(): lax.ppermute(block, ('side', 'pair'), [(i, i ^ far) for i in range(MEMBER...  15 us
    ppermute x12, waiting for transfers between devices, to_member(): lax.ppermute(block, ('side', 'pair'), [(i, i ^ far) for i in range(MEMBER...  12.2 us
    ppermute x4, starting transfers between devices, rotated(): lax.ppermute(block, axis, [(i, (i + step) % size) for i in range(size)])  11.8 us
    ppermute x4, waiting for transfers between devices, rotated(): lax.ppermute(block, axis, [(i, (i + step) % size) for i in range(size)])  9.94 us
    pallas_call x17, Pallas kernels, local_call(): pl.pallas_call(body, name=name, out_shape=out_shapes, in_specs=[pl.BlockS...  7.02 us
    ppermute x1, starting transfers between devices, parted(): return lax.ppermute(block, ('twin', 'line'), list(enumerate(to)))  3.08 us
    pallas_call x2, Pallas kernels, unpack(): pl.pallas_call(functools.partial(unpack_body, fars), name='unpack', out_s...  1.83 us
  transfers between devices with their start and end apart: 22, of which 9 were waited for; matrix products, arithmetic and copies ran while one was open for 0% of the time, Pallas kernels for 9%

profile of v10, /device:TPU:0, one launch (start us, length us, event | category | flops | bytes accessed | tf_op | source)
XLA Modules:
  0.0 64.5 jit_solution(10643521741622677707)
XLA Ops:
  0.6 1.0 %front.1 = (bf16[256,512]{1,0:T(8,128)(2,1)S(1)}, bf16[128,512]{1,0:T(8,128)(2,1)S(1)}) custom-call(bf16[512,512]{1,0:T(8,128)(2,1)} %shard.1), custom_call_target="tpu_custom_call" | custom-call | bytes 524288 | tf_op jit(solution)/shard_map/front/pallas_call | solution.py:27
  1.6 3.1 %collective-permute-start = (bf16[256,512]{1,0:T(8,128)(2,1)S(1)}, bf16[256,512]{1,0:T(8,128)(2,1)S(1)}, u32[]{:S(2)}, u32[]{:S(2)}) collective-permute-start(bf16[256,512]{1,0:T(8,128)(2,1)S(1)} %get-tuple-element.47.refs_0_), channel_id=1, source_target_pairs={{0,2},{2,4},{4,6},{6,0},{8,14},{10,8},{12,10},{14,12},{1,3},{3,5},... | collective-permute-start | bytes 786440 | tf_op jit(solution)/shard_map/ppermute | solution.py:138
  4.7 2.6 %collective-permute-start.1 = (bf16[128,512]{1,0:T(8,128)(2,1)S(1)}, bf16[128,512]{1,0:T(8,128)(2,1)S(1)}, u32[]{:S(2)}, u32[]{:S(2)}) collective-permute-start(bf16[128,512]{1,0:T(8,128)(2,1)S(1)} %get-tuple-element.48), channel_id=1, source_target_pairs={{0,4},{2,6},{4,0},{6,2},{1,5},{3,7},{5,1},{7,3},{8,12},{10,14},{12... | collective-permute-start | bytes 393224 | tf_op jit(solution)/shard_map/ppermute | solution.py:41
  7.3 1.2 %copy-done = bf16[128,4096]{1,0:T(8,128)(2,1)S(1)} copy-done((bf16[128,4096]{1,0:T(8,128)(2,1)S(1)}, bf16[128,4096]{1,0:T(8,128)(2,1)}, u32[]{:S(2)}) %copy-start) | copy-done | bytes 1048600
  8.8 1.6 %collective-permute-start.4 = (bf16[128,1024]{1,0:T(8,128)(2,1)S(1)}, bf16[128,1024]{1,0:T(8,128)(2,1)S(1)}, u32[]{:S(2)}, u32[]{:S(2)}) collective-permute-start(bf16[128,1024]{1,0:T(8,128)(2,1)S(1)} %get-tuple-element.52), channel_id=1, source_target_pairs={{0,1},{1,0},{16,17},{17,16},{2,3},{3,2},{18,19},{19,18},{4,5},{5,4... | collective-permute-start | bytes 786440 | tf_op jit(solution)/shard_map/ppermute | solution.py:53
  10.4 1.5 %collective-permute-start.5 = (bf16[128,1024]{1,0:T(8,128)(2,1)S(1)}, bf16[128,1024]{1,0:T(8,128)(2,1)S(1)}, u32[]{:S(2)}, u32[]{:S(2)}) collective-permute-start(bf16[128,1024]{1,0:T(8,128)(2,1)S(1)} %get-tuple-element.53), channel_id=1, source_target_pairs={{0,16},{1,17},{16,0},{17,1},{2,18},{3,19},{18,2},{19,3},{4,20},{5,... | collective-permute-start | bytes 786440 | tf_op jit(solution)/shard_map/ppermute | solution.py:53
  12.4 4.8 %collective-permute-done.1.refs_1_.refs_2_ = bf16[128,512]{1,0:T(8,128)(2,1)S(1)} collective-permute-done((bf16[128,512]{1,0:T(8,128)(2,1)S(1)}, bf16[128,512]{1,0:T(8,128)(2,1)S(1)}, u32[]{:S(2)}, u32[]{:S(2)}) %collective-permute-start.1) | collective-permute-done | bytes 131104 | tf_op jit(solution)/shard_map/ppermute | solution.py:41
  17.2 0.5 collective-permute-start.2
  17.8 1.8 %collective-permute-done.5.block.refs_2_ = bf16[128,1024]{1,0:T(8,128)(2,1)S(1)} collective-permute-done((bf16[128,1024]{1,0:T(8,128)(2,1)S(1)}, bf16[128,1024]{1,0:T(8,128)(2,1)S(1)}, u32[]{:S(2)}, u32[]{:S(2)}) %collective-permute-start.5) | collective-permute-done | bytes 262176 | tf_op jit(solution)/shard_map/ppermute | solution.py:53
  19.7 3.2 %collective-permute-done.6.block.refs_3_ = bf16[128,1024]{1,0:T(8,128)(2,1)S(1)} collective-permute-done((bf16[128,1024]{1,0:T(8,128)(2,1)S(1)}, bf16[128,1024]{1,0:T(8,128)(2,1)S(1)}, u32[]{:S(2)}, u32[]{:S(2)}) %collective-permute-start.6) | collective-permute-done | bytes 262176 | tf_op jit(solution)/shard_map/ppermute | solution.py:53
  24.0 2.5 %collective-permute-start.7 = (bf16[128,512]{1,0:T(8,128)(2,1)S(1)}, bf16[128,512]{1,0:T(8,128)(2,1)S(1)}, u32[]{:S(2)}, u32[]{:S(2)}) collective-permute-start(bf16[128,512]{1,0:T(8,128)(2,1)S(1)} %share.5), channel_id=1, source_target_pairs={{0,17},{1,16},{16,1},{17,0},{2,19},{3,18},{18,3},{19,2},{4,21},{5,... | collective-permute-start | bytes 393224 | tf_op jit(solution)/shard_map/ppermute | solution.py:53
  26.5 0.5 collective-permute-start.8
  27.0 0.5 collective-permute-start.9
  27.8 2.8 %collective-permute-done.7.refs_1_ = bf16[128,512]{1,0:T(8,128)(2,1)S(1)} collective-permute-done((bf16[128,512]{1,0:T(8,128)(2,1)S(1)}, bf16[128,512]{1,0:T(8,128)(2,1)S(1)}, u32[]{:S(2)}, u32[]{:S(2)}) %collective-permute-start.7) | collective-permute-done | bytes 131104 | tf_op jit(solution)/shard_map/ppermute | solution.py:53
  30.6 1.5 %collective-permute-done.8.refs_2_ = bf16[128,512]{1,0:T(8,128)(2,1)S(1)} collective-permute-done((bf16[128,512]{1,0:T(8,128)(2,1)S(1)}, bf16[128,512]{1,0:T(8,128)(2,1)S(1)}, u32[]{:S(2)}, u32[]{:S(2)}) %collective-permute-start.8) | collective-permute-done | bytes 131104 | tf_op jit(solution)/shard_map/ppermute | solution.py:53
  32.4 1.4 %collective-permute-start.10 = (bf16[128,512]{1,0:T(8,128)(2,1)S(1)}, bf16[128,512]{1,0:T(8,128)(2,1)S(1)}, u32[]{:S(2)}, u32[]{:S(2)}) collective-permute-start(bf16[128,512]{1,0:T(8,128)(2,1)S(1)} %get-tuple-element.61.grad.refs_4_), channel_id=1, source_target_pairs={{0,1},{1,0},{16,17},{17,16},{2,3},{3,2},{18,19},{19,18},{4,5},{5,4... | collective-permute-start | bytes 393224 | tf_op jit(solution)/shard_map/ppermute | solution.py:53
  33.8 1.1 %collective-permute-start.12 = (bf16[128,512]{1,0:T(8,128)(2,1)S(1)}, bf16[128,512]{1,0:T(8,128)(2,1)S(1)}, u32[]{:S(2)}, u32[]{:S(2)}) collective-permute-start(bf16[128,512]{1,0:T(8,128)(2,1)S(1)} %get-tuple-element.61.grad.refs_4_), channel_id=1, source_target_pairs={{0,17},{1,16},{16,1},{17,0},{2,19},{3,18},{18,3},{19,2},{4,21},{5,... | collective-permute-start | bytes 393224 | tf_op jit(solution)/shard_map/ppermute | solution.py:53
  34.9 1.1 %collective-permute-start.11 = (bf16[128,512]{1,0:T(8,128)(2,1)S(1)}, bf16[128,512]{1,0:T(8,128)(2,1)S(1)}, u32[]{:S(2)}, u32[]{:S(2)}) collective-permute-start(bf16[128,512]{1,0:T(8,128)(2,1)S(1)} %get-tuple-element.61.grad.refs_4_), channel_id=1, source_target_pairs={{0,16},{1,17},{16,0},{17,1},{2,18},{3,19},{18,2},{19,3},{4,20},{5,... | collective-permute-start | bytes 393224 | tf_op jit(solution)/shard_map/ppermute | solution.py:53
  36.0 1.5 %collective-permute-done.10.grad.refs_5_ = bf16[128,512]{1,0:T(8,128)(2,1)S(1)} collective-permute-done((bf16[128,512]{1,0:T(8,128)(2,1)S(1)}, bf16[128,512]{1,0:T(8,128)(2,1)S(1)}, u32[]{:S(2)}, u32[]{:S(2)}) %collective-permute-start.10) | collective-permute-done | bytes 131104 | tf_op jit(solution)/shard_map/ppermute | solution.py:53
  37.9 1.4 %collective-permute-start.16 = (bf16[128,1024]{1,0:T(8,128)(2,1)S(1)}, bf16[128,1024]{1,0:T(8,128)(2,1)S(1)}, u32[]{:S(2)}, u32[]{:S(2)}) collective-permute-start(bf16[128,1024]{1,0:T(8,128)(2,1)S(1)} %columns.5), channel_id=1, source_target_pairs={{0,1},{1,0},{16,17},{17,16},{2,3},{3,2},{18,19},{19,18},{4,5},{5,4... | collective-permute-start | bytes 786440 | tf_op jit(solution)/shard_map/ppermute | solution.py:53
  39.8 0.7 %emit.1 = bf16[128,512]{1,0:T(8,128)(2,1)} custom-call(bf16[128,512]{1,0:T(8,128)(2,1)S(1)} %get-tuple-element.62.held), custom_call_target="tpu_custom_call" | custom-call | bytes 131072 | tf_op jit(solution)/shard_map/emit/pallas_call | solution.py:27
  40.4 0.7 %terms.1 = (f32[4,128,512]{2,1,0:T(8,128)S(1)}, bf16[192,512]{1,0:T(8,128)(2,1)S(1)}, bf16[192,512]{1,0:T(8,128)(2,1)S(1)}, bf16[128,512]{1,0:T(8,128)(2,1)S(1)}) custom-call(bf16[128,1024]{1,0:T(8,128)(2,1)S(1)} %get-tuple-element.55.block.refs_0_, bf16[128,1024]{1,0:T(8,128)(2,1)S(1)} %collective-permute-done.4.block.refs_1_, ...), custom_call_target="tpu_custom_call" | custom-call | tf_op jit(solution)/shard_map/terms/pallas_call | solution.py:27
  43.2 1.3 %collective-permute-done.16.refs_1_ = bf16[128,1024]{1,0:T(8,128)(2,1)S(1)} collective-permute-done((bf16[128,1024]{1,0:T(8,128)(2,1)S(1)}, bf16[128,1024]{1,0:T(8,128)(2,1)S(1)}, u32[]{:S(2)}, u32[]{:S(2)}) %collective-permute-start.16) | collective-permute-done | bytes 262176 | tf_op jit(solution)/shard_map/ppermute | solution.py:53
  44.5 1.1 %collective-permute-start.17 = (bf16[128,1024]{1,0:T(8,128)(2,1)S(1)}, bf16[128,1024]{1,0:T(8,128)(2,1)S(1)}, u32[]{:S(2)}, u32[]{:S(2)}) collective-permute-start(bf16[128,1024]{1,0:T(8,128)(2,1)S(1)} %columns.6), channel_id=1, source_target_pairs={{0,16},{1,17},{16,0},{17,1},{2,18},{3,19},{18,2},{19,3},{4,20},{5,... | collective-permute-start | bytes 786440 | tf_op jit(solution)/shard_map/ppermute | solution.py:53
  45.7 5.2 %collective-permute-start.19 = (bf16[128,512]{1,0:T(8,128)(2,1)S(1)}, bf16[128,512]{1,0:T(8,128)(2,1)S(1)}, u32[]{:S(2)}, u32[]{:S(2)}) collective-permute-start(bf16[128,512]{1,0:T(8,128)(2,1)S(1)} %get-tuple-element.79), channel_id=1, source_target_pairs={{0,6},{2,0},{4,2},{6,4},{1,7},{3,1},{5,3},{7,5},{8,14},{10,8},{12,... | collective-permute-start | bytes 393224 | tf_op jit(solution)/shard_map/ppermute | solution.py:41
  50.8 2.1 %collective-permute-start.20 = (bf16[128,512]{1,0:T(8,128)(2,1)S(1)}, bf16[128,512]{1,0:T(8,128)(2,1)S(1)}, u32[]{:S(2)}, u32[]{:S(2)}) collective-permute-start(bf16[128,512]{1,0:T(8,128)(2,1)S(1)} %get-tuple-element.80), channel_id=1, source_target_pairs={{0,4},{2,6},{4,0},{6,2},{1,5},{3,7},{5,1},{7,3},{8,12},{10,14},{12... | collective-permute-start | bytes 393224 | tf_op jit(solution)/shard_map/ppermute | solution.py:41
  53.0 1.9 %collective-permute-start.21 = (bf16[128,512]{1,0:T(8,128)(2,1)S(1)}, bf16[128,512]{1,0:T(8,128)(2,1)S(1)}, u32[]{:S(2)}, u32[]{:S(2)}) collective-permute-start(bf16[128,512]{1,0:T(8,128)(2,1)S(1)} %get-tuple-element.81), channel_id=1, source_target_pairs={{0,2},{2,4},{4,6},{6,0},{1,3},{3,5},{5,7},{7,1},{8,10},{10,12},{12... | collective-permute-start | bytes 393224 | tf_op jit(solution)/shard_map/ppermute | solution.py:41
  54.9 1.9 %collective-permute-start.18 = (bf16[128,1024]{1,0:T(8,128)(2,1)S(1)}, bf16[128,1024]{1,0:T(8,128)(2,1)S(1)}, u32[]{:S(2)}, u32[]{:S(2)}) collective-permute-start(bf16[128,1024]{1,0:T(8,128)(2,1)S(1)} %columns.7), channel_id=1, source_target_pairs={{0,17},{1,16},{16,1},{17,0},{2,19},{3,18},{18,3},{19,2},{4,21},{5,... | collective-permute-start | bytes 786440 | tf_op jit(solution)/shard_map/ppermute | solution.py:53
  56.8 0.9 %unpack.2.refs_2_ = bf16[128,4096]{1,0:T(8,128)(2,1)} custom-call(bf16[128,1024]{1,0:T(8,128)(2,1)S(1)} %columns.4.refs_0_, bf16[128,1024]{1,0:T(8,128)(2,1)S(1)} %collective-permute-done.16.refs_1_), custom_call_target="tpu_custom_call" | custom-call | tf_op jit(solution)/shard_map/unpack/pallas_call | solution.py:106
  57.7 5.1 %collective-permute-done.20.refs_2_ = bf16[128,512]{1,0:T(8,128)(2,1)S(1)} collective-permute-done((bf16[128,512]{1,0:T(8,128)(2,1)S(1)}, bf16[128,512]{1,0:T(8,128)(2,1)S(1)}, u32[]{:S(2)}, u32[]{:S(2)}) %collective-permute-start.20) | collective-permute-done | bytes 131104 | tf_op jit(solution)/shard_map/ppermute | solution.py:41
  62.9 0.8 %final_sum.1 = f32[128,512]{1,0:T(8,128)} custom-call(f32[128,512]{1,0:T(8,128)S(1)} %get-tuple-element.83.refs_0_, bf16[128,512]{1,0:T(8,128)(2,1)S(1)} %collective-permute-done.19.refs_1_, bf16[128,512]{1,0:T(8,128)(2,1)S(1)} %collective-permute-done.20.refs_2_, bf16[128,512]{1,0:T(8,128)(2,1)S(1)} %collective-permute-done.21.refs_3_), custom_call_target="tpu_custom_call" | custom-call | flops 2147483648 | bytes 655360 | tf_op jit(solution)/shard_map/final_sum/pallas_call | solution.py:27
  63.6 0.9 %unpack.3 = bf16[128,4096]{1,0:T(8,128)(2,1)} custom-call(bf16[128,1024]{1,0:T(8,128)(2,1)S(1)} %collective-permute-done.17.refs_0_, bf16[128,1024]{1,0:T(8,128)(2,1)S(1)} %collective-permute-done.18.refs_1_, bf16[128,4096]{1,0:T(8,128)(2,1)} %unpack.2.refs_2_), custom_call_target="tpu_custom_call", output_to_operand_aliasing={{}: (2, {})} | custom-call | tf_op jit(solution)/shard_map/unpack/pallas_call | solution.py:106
  (35 shorter events, 5.4 us)
Async XLA Ops:
  1.6 15.6 %collective-permute-start = (bf16[256,512]{1,0:T(8,128)(2,1)S(1)}, bf16[256,512]{1,0:T(8,128)(2,1)S(1)}, u32[]{:S(2)}, u32[]{:S(2)}) collective-permute-start(bf16[256,512]{1,0:T(8,128)(2,1)S(1)} %get-tuple-element.47.refs_0_), channel_id=1, source_target_pairs={{0,2},{2,4},{4,6},{6,0},{8,14},{10,8},{12,10},{14,12},{1,3},{3,5},... | collective-permute-start | bytes 786440 | tf_op jit(solution)/shard_map/ppermute | solution.py:138
  4.7 12.5 %collective-permute-start.1 = (bf16[128,512]{1,0:T(8,128)(2,1)S(1)}, bf16[128,512]{1,0:T(8,128)(2,1)S(1)}, u32[]{:S(2)}, u32[]{:S(2)}) collective-permute-start(bf16[128,512]{1,0:T(8,128)(2,1)S(1)} %get-tuple-element.48), channel_id=1, source_target_pairs={{0,4},{2,6},{4,0},{6,2},{1,5},{3,7},{5,1},{7,3},{8,12},{10,14},{12... | collective-permute-start | bytes 393224 | tf_op jit(solution)/shard_map/ppermute | solution.py:41
  7.3 1.2 %copy-start = (bf16[128,4096]{1,0:T(8,128)(2,1)S(1)}, bf16[128,4096]{1,0:T(8,128)(2,1)}, u32[]{:S(2)}) copy-start(bf16[128,4096]{1,0:T(8,128)(2,1)} %tokens.1) | copy-start | bytes 3145732
  8.8 9.0 %collective-permute-start.4 = (bf16[128,1024]{1,0:T(8,128)(2,1)S(1)}, bf16[128,1024]{1,0:T(8,128)(2,1)S(1)}, u32[]{:S(2)}, u32[]{:S(2)}) collective-permute-start(bf16[128,1024]{1,0:T(8,128)(2,1)S(1)} %get-tuple-element.52), channel_id=1, source_target_pairs={{0,1},{1,0},{16,17},{17,16},{2,3},{3,2},{18,19},{19,18},{4,5},{5,4... | collective-permute-start | bytes 786440 | tf_op jit(solution)/shard_map/ppermute | solution.py:53
  10.4 9.2 %collective-permute-start.5 = (bf16[128,1024]{1,0:T(8,128)(2,1)S(1)}, bf16[128,1024]{1,0:T(8,128)(2,1)S(1)}, u32[]{:S(2)}, u32[]{:S(2)}) collective-permute-start(bf16[128,1024]{1,0:T(8,128)(2,1)S(1)} %get-tuple-element.53), channel_id=1, source_target_pairs={{0,16},{1,17},{16,0},{17,1},{2,18},{3,19},{18,2},{19,3},{4,20},{5,... | collective-permute-start | bytes 786440 | tf_op jit(solution)/shard_map/ppermute | solution.py:53
  11.9 11.0 %collective-permute-start.6 = (bf16[128,1024]{1,0:T(8,128)(2,1)S(1)}, bf16[128,1024]{1,0:T(8,128)(2,1)S(1)}, u32[]{:S(2)}, u32[]{:S(2)}) collective-permute-start(bf16[128,1024]{1,0:T(8,128)(2,1)S(1)} %get-tuple-element.54), channel_id=1, source_target_pairs={{0,17},{1,16},{16,1},{17,0},{2,19},{3,18},{18,3},{19,2},{4,21},{5,... | collective-permute-start | bytes 786440 | tf_op jit(solution)/shard_map/ppermute | solution.py:53
  17.2 5.6 %collective-permute-start.2 = (bf16[192,512]{1,0:T(8,128)(2,1)S(1)}, bf16[192,512]{1,0:T(8,128)(2,1)S(1)}, u32[]{:S(2)}, u32[]{:S(2)}) collective-permute-start(bf16[192,512]{1,0:T(8,128)(2,1)S(1)} %get-tuple-element.49), channel_id=1, source_target_pairs={{0,8},{8,0},{1,9},{9,1},{2,10},{10,2},{3,11},{11,3},{4,12},{12,4},... | collective-permute-start | bytes 589832 | tf_op jit(solution)/shard_map/ppermute | solution.py:45
  17.7 5.2 %collective-permute-start.3 = (bf16[192,512]{1,0:T(8,128)(2,1)S(1)}, bf16[192,512]{1,0:T(8,128)(2,1)S(1)}, u32[]{:S(2)}, u32[]{:S(2)}) collective-permute-start(bf16[192,512]{1,0:T(8,128)(2,1)S(1)} %get-tuple-element.50), channel_id=1, source_target_pairs={{0,8},{8,0},{1,9},{9,1},{2,10},{10,2},{3,11},{11,3},{4,12},{12,4},... | collective-permute-start | bytes 589832 | tf_op jit(solution)/shard_map/ppermute | solution.py:45
  23.9 8.2 %copy-start.1 = (bf16[128,512]{1,0:T(8,128)(2,1)S(1)}, bf16[128,512]{1,0:T(8,128)(2,1)}, u32[]{:S(2)}) copy-start(bf16[128,512]{1,0:T(8,128)(2,1)} %refs_4_.1) | copy-start | bytes 393220
  24.0 6.6 %collective-permute-start.7 = (bf16[128,512]{1,0:T(8,128)(2,1)S(1)}, bf16[128,512]{1,0:T(8,128)(2,1)S(1)}, u32[]{:S(2)}, u32[]{:S(2)}) collective-permute-start(bf16[128,512]{1,0:T(8,128)(2,1)S(1)} %share.5), channel_id=1, source_target_pairs={{0,17},{1,16},{16,1},{17,0},{2,19},{3,18},{18,3},{19,2},{4,21},{5,... | collective-permute-start | bytes 393224 | tf_op jit(solution)/shard_map/ppermute | solution.py:53
  26.5 5.7 %collective-permute-start.8 = (bf16[128,512]{1,0:T(8,128)(2,1)S(1)}, bf16[128,512]{1,0:T(8,128)(2,1)S(1)}, u32[]{:S(2)}, u32[]{:S(2)}) collective-permute-start(bf16[128,512]{1,0:T(8,128)(2,1)S(1)} %share.6), channel_id=1, source_target_pairs={{0,1},{1,0},{16,17},{17,16},{2,3},{3,2},{18,19},{19,18},{4,5},{5,4... | collective-permute-start | bytes 393224 | tf_op jit(solution)/shard_map/ppermute | solution.py:53
  27.0 5.2 %collective-permute-start.9 = (bf16[128,512]{1,0:T(8,128)(2,1)S(1)}, bf16[128,512]{1,0:T(8,128)(2,1)S(1)}, u32[]{:S(2)}, u32[]{:S(2)}) collective-permute-start(bf16[128,512]{1,0:T(8,128)(2,1)S(1)} %share.7), channel_id=1, source_target_pairs={{0,16},{1,17},{16,0},{17,1},{2,18},{3,19},{18,2},{19,3},{4,20},{5,... | collective-permute-start | bytes 393224 | tf_op jit(solution)/shard_map/ppermute | solution.py:53
  32.4 5.0 %collective-permute-start.10 = (bf16[128,512]{1,0:T(8,128)(2,1)S(1)}, bf16[128,512]{1,0:T(8,128)(2,1)S(1)}, u32[]{:S(2)}, u32[]{:S(2)}) collective-permute-start(bf16[128,512]{1,0:T(8,128)(2,1)S(1)} %get-tuple-element.61.grad.refs_4_), channel_id=1, source_target_pairs={{0,1},{1,0},{16,17},{17,16},{2,3},{3,2},{18,19},{19,18},{4,5},{5,4... | collective-permute-start | bytes 393224 | tf_op jit(solution)/shard_map/ppermute | solution.py:53
  33.8 6.7 %collective-permute-start.12 = (bf16[128,512]{1,0:T(8,128)(2,1)S(1)}, bf16[128,512]{1,0:T(8,128)(2,1)S(1)}, u32[]{:S(2)}, u32[]{:S(2)}) collective-permute-start(bf16[128,512]{1,0:T(8,128)(2,1)S(1)} %get-tuple-element.61.grad.refs_4_), channel_id=1, source_target_pairs={{0,17},{1,16},{16,1},{17,0},{2,19},{3,18},{18,3},{19,2},{4,21},{5,... | collective-permute-start | bytes 393224 | tf_op jit(solution)/shard_map/ppermute | solution.py:53
  34.9 5.6 %collective-permute-start.11 = (bf16[128,512]{1,0:T(8,128)(2,1)S(1)}, bf16[128,512]{1,0:T(8,128)(2,1)S(1)}, u32[]{:S(2)}, u32[]{:S(2)}) collective-permute-start(bf16[128,512]{1,0:T(8,128)(2,1)S(1)} %get-tuple-element.61.grad.refs_4_), channel_id=1, source_target_pairs={{0,16},{1,17},{16,0},{17,1},{2,18},{3,19},{18,2},{19,3},{4,20},{5,... | collective-permute-start | bytes 393224 | tf_op jit(solution)/shard_map/ppermute | solution.py:53
  37.9 6.6 %collective-permute-start.16 = (bf16[128,1024]{1,0:T(8,128)(2,1)S(1)}, bf16[128,1024]{1,0:T(8,128)(2,1)S(1)}, u32[]{:S(2)}, u32[]{:S(2)}) collective-permute-start(bf16[128,1024]{1,0:T(8,128)(2,1)S(1)} %columns.5), channel_id=1, source_target_pairs={{0,1},{1,0},{16,17},{17,16},{2,3},{3,2},{18,19},{19,18},{4,5},{5,4... | collective-permute-start | bytes 786440 | tf_op jit(solution)/shard_map/ppermute | solution.py:53
  41.2 2.0 %collective-permute-start.13 = (bf16[192,512]{1,0:T(8,128)(2,1)S(1)}, bf16[192,512]{1,0:T(8,128)(2,1)S(1)}, u32[]{:S(2)}, u32[]{:S(2)}) collective-permute-start(bf16[192,512]{1,0:T(8,128)(2,1)S(1)} %get-tuple-element.66), channel_id=1, source_target_pairs={{0,8},{8,0},{1,9},{9,1},{2,10},{10,2},{3,11},{11,3},{4,12},{12,4},... | collective-permute-start | bytes 589832 | tf_op jit(solution)/shard_map/ppermute | solution.py:45
  41.3 1.9 %collective-permute-start.14 = (bf16[192,512]{1,0:T(8,128)(2,1)S(1)}, bf16[192,512]{1,0:T(8,128)(2,1)S(1)}, u32[]{:S(2)}, u32[]{:S(2)}) collective-permute-start(bf16[192,512]{1,0:T(8,128)(2,1)S(1)} %get-tuple-element.67), channel_id=1, source_target_pairs={{0,8},{8,0},{1,9},{9,1},{2,10},{10,2},{3,11},{11,3},{4,12},{12,4},... | collective-permute-start | bytes 589832 | tf_op jit(solution)/shard_map/ppermute | solution.py:45
  41.8 1.4 %collective-permute-start.15 = (bf16[128,512]{1,0:T(8,128)(2,1)S(1)}, bf16[128,512]{1,0:T(8,128)(2,1)S(1)}, u32[]{:S(2)}, u32[]{:S(2)}) collective-permute-start(bf16[128,512]{1,0:T(8,128)(2,1)S(1)} %get-tuple-element.68), channel_id=1, source_target_pairs={{0,8},{8,0},{1,9},{9,1},{2,10},{10,2},{3,11},{11,3},{4,12},{12,4},... | collective-permute-start | bytes 393224 | tf_op jit(solution)/shard_map/ppermute | solution.py:45
  44.5 10.4 %collective-permute-start.17 = (bf16[128,1024]{1,0:T(8,128)(2,1)S(1)}, bf16[128,1024]{1,0:T(8,128)(2,1)S(1)}, u32[]{:S(2)}, u32[]{:S(2)}) collective-permute-start(bf16[128,1024]{1,0:T(8,128)(2,1)S(1)} %columns.6), channel_id=1, source_target_pairs={{0,16},{1,17},{16,0},{17,1},{2,18},{3,19},{18,2},{19,3},{4,20},{5,... | collective-permute-start | bytes 786440 | tf_op jit(solution)/shard_map/ppermute | solution.py:53
  45.7 12.1 %collective-permute-start.19 = (bf16[128,512]{1,0:T(8,128)(2,1)S(1)}, bf16[128,512]{1,0:T(8,128)(2,1)S(1)}, u32[]{:S(2)}, u32[]{:S(2)}) collective-permute-start(bf16[128,512]{1,0:T(8,128)(2,1)S(1)} %get-tuple-element.79), channel_id=1, source_target_pairs={{0,6},{2,0},{4,2},{6,4},{1,7},{3,1},{5,3},{7,5},{8,14},{10,8},{12,... | collective-permute-start | bytes 393224 | tf_op jit(solution)/shard_map/ppermute | solution.py:41
  50.8 12.0 %collective-permute-start.20 = (bf16[128,512]{1,0:T(8,128)(2,1)S(1)}, bf16[128,512]{1,0:T(8,128)(2,1)S(1)}, u32[]{:S(2)}, u32[]{:S(2)}) collective-permute-start(bf16[128,512]{1,0:T(8,128)(2,1)S(1)} %get-tuple-element.80), channel_id=1, source_target_pairs={{0,4},{2,6},{4,0},{6,2},{1,5},{3,7},{5,1},{7,3},{8,12},{10,14},{12... | collective-permute-start | bytes 393224 | tf_op jit(solution)/shard_map/ppermute | solution.py:41
  53.0 9.9 %collective-permute-start.21 = (bf16[128,512]{1,0:T(8,128)(2,1)S(1)}, bf16[128,512]{1,0:T(8,128)(2,1)S(1)}, u32[]{:S(2)}, u32[]{:S(2)}) collective-permute-start(bf16[128,512]{1,0:T(8,128)(2,1)S(1)} %get-tuple-element.81), channel_id=1, source_target_pairs={{0,2},{2,4},{4,6},{6,0},{1,3},{3,5},{5,7},{7,1},{8,10},{10,12},{12... | collective-permute-start | bytes 393224 | tf_op jit(solution)/shard_map/ppermute | solution.py:41
  54.9 8.7 %collective-permute-start.18 = (bf16[128,1024]{1,0:T(8,128)(2,1)S(1)}, bf16[128,1024]{1,0:T(8,128)(2,1)S(1)}, u32[]{:S(2)}, u32[]{:S(2)}) collective-permute-start(bf16[128,1024]{1,0:T(8,128)(2,1)S(1)} %columns.7), channel_id=1, source_target_pairs={{0,17},{1,16},{16,1},{17,0},{2,19},{3,18},{18,3},{19,2},{4,21},{5,... | collective-permute-start | bytes 786440 | tf_op jit(solution)/shard_map/ppermute | solution.py:53

commit v11 on v10

--- a/solution.py
+++ b/solution.py
@@ -265,7 +265,9 @@
         room=53.4,
     )
     packed = local_call("pack", pack_body, [block_shape] * MEMBERS, tokens)
-    blocks = [packed[0]] + [to_member(packed[far], far) for far in range(1, MEMBERS)]
+    blocks = [packed[0], None, None, None]
+    for far in (3, 1, 2):
+        blocks[far] = to_member(packed[far], far)
     passed = [parted(both, step) for step in range(1, (line + 1) // 2)]
     if line % 2 == 0:
         passed.append(rotated(mine, "line", line // 2))
@@ -279,7 +281,8 @@
         flops=8 * flops,
     )
     theirs = [to_twin(piece) for piece in relayed]
-    theirs, blocks = lax.optimization_barrier((theirs, blocks))
+    *blocks, theirs = lax.optimization_barrier((*blocks[::-1], theirs))
+    blocks = blocks[::-1]
     weight = local_call(
         "join",
         functools.partial(join_body, line, 2),
@@ -299,19 +302,18 @@
 
     grad_3, grad_1, grad_2 = (to_member(key_grad, far) for far in (3, 1, 2))
 
-    def columns(grad):
-        return local_call("columns", columns_body, block_shape, grad, weight, moved=0)
-
-    column_0, column_1 = columns(key_grad), columns(grad_1)
-    back_1 = to_member(column_1, 1)
-    column_0, _, key_out, grad_2, grad_3 = lax.optimization_barrier(
-        (column_0, column_1, key_out, grad_2, grad_3)
-    )
-    terms = local_call(
+    def columns(grad, **cost):
+        return local_call("columns", columns_body, block_shape, grad, weight, **cost)
+
+    column_0, column_3 = columns(key_grad, flops=flops), columns(grad_3, flops=flops)
+    column_0, column_3, key_out, grad_1, grad_2 = lax.optimization_barrier(
+        (column_0, column_3, key_out, grad_1, grad_2)
+    )
+    kept, *theirs = local_call(
         "terms",
         functools.partial(terms_body, grad_scale),
         [shape((line, rows, key_cols), f32)]
-        + [shape((end - start, key_cols), bf16) for start, end in cuts(line * rows, 3)],
+        + [shape((end - start, key_cols), bf16) for start, end in cuts(line * rows, 2)],
         *blocks,
         key_grad,
         grad_1,
@@ -319,30 +321,27 @@
         grad_3,
         moved=0,
     )
-    kept, *theirs = terms
     theirs = [to_twin(piece) for piece in theirs]
-    column_2, column_3 = columns(grad_2), columns(grad_3)
-    theirs, back_1, column_2, column_3 = lax.optimization_barrier((theirs, back_1, column_2, column_3))
     sums = local_call(
         "merge",
-        functools.partial(merge_body, 3),
+        functools.partial(merge_body, 2),
         [shape((rows, key_cols), f32)] + [shape((rows, key_cols), bf16)] * (line - 1),
         kept,
         *theirs,
         moved=0,
     )
+
     met = [sums[0]] + [rotated(sums[step], "line", -step) for step in range(1, line)]
-    input_grad = unpack((0, 1), (column_0, back_1), shape((tok_rows, width), bf16))
+    back_1, back_2 = to_member(columns(grad_1, flops=flops), 1), to_member(columns(grad_2, flops=flops), 2)
+    column_3, back_1, back_2, _ = lax.optimization_barrier((column_3, back_1, back_2, sums))
+    back_3 = to_member(column_3, 3)
+    input_grad = unpack((0, 1, 2), (column_0, back_1, back_2), shape((tok_rows, width), bf16))
     met, input_grad = lax.optimization_barrier((met, input_grad))
-    weight_grad = local_call("final_sum", sum_body, shape((rows, key_cols), f32), *met, flops=16 * flops)
+    weight_grad = local_call("final_sum", sum_body, shape((rows, key_cols), f32), *met, flops=24 * flops)
+    back_3, weight_grad = lax.optimization_barrier((back_3, weight_grad))
     if outer > 1:
         weight_grad = lax.psum_scatter(weight_grad, "outer", scatter_dimension=0, tiled=True)
-
-    back_2 = to_member(column_2, 2)
-    column_3, back_1, back_2 = lax.optimization_barrier((column_3, back_1, back_2))
-    back_3 = to_member(column_3, 3)
-    back_2, back_3, weight_grad = lax.optimization_barrier((back_2, back_3, weight_grad))
-    input_grad = unpack((2, 3), (back_2, back_3), shape((tok_rows, width), bf16), input_grad)
+    input_grad = unpack((3,), (back_3,), shape((tok_rows, width), bf16), input_grad)
     if outer > 1:
         input_grad = join_runs(input_grad, outer)
     return (key_out, input_grad, weight_grad)

time: 64.7 us -> 63 us (0.974)
  starting transfers between devices: 31.2 us -> 26 us
  waiting for transfers between devices: 22.5 us -> 25.9 us
    ppermute x12, waiting for transfers between devices: 12.2 us -> 16.9 us  [to_member(): lax.ppermute(block, ('side', 'pair'), [(i, i ^ far) for i in range(MEMBER...]
    ppermute x4, starting transfers between devices: 11.8 us -> 7.27 us  [rotated(): lax.ppermute(block, axis, [(i, (i + step) % size) for i in range(size)])]
    ppermute x4, waiting for transfers between devices: 9.94 us -> 9 us  [rotated(): lax.ppermute(block, axis, [(i, (i + step) % size) for i in range(size)])]
    ppermute x12, starting transfers between devices: 15 us -> 14.2 us  [to_member(): lax.ppermute(block, ('side', 'pair'), [(i, i ^ far) for i in range(MEMBER...]
    ppermute x5 -> x4, starting transfers between devices: 1.23 us -> 1.44 us  [to_twin(): return lax.ppermute(block, 'twin', [(0, 1), (1, 0)])]
  transfers between devices with their start and end apart: 22 -> 21, of which waited for: 9 -> 12; matrix products, arithmetic and copies ran while one was open for 0% -> 0% of each run, Pallas kernels for 9% -> 8%
where the time goes in v11:
time: 63 us; the launch traced here: 62.8 us
  starting transfers between devices  26 us (41%)
  waiting for transfers between devices  25.9 us (41%)
  Pallas kernels  8.86 us (14%)
  local copies, waits for them, and re-layouts  1.23 us (2%)
  between operations  0.8 us (1%)
    ppermute x12, waiting for transfers between devices, to_member(): lax.ppermute(block, ('side', 'pair'), [(i, i ^ far) for i in range(MEMBER...  16.9 us
    ppermute x12, starting transfers between devices, to_member(): lax.ppermute(block, ('side', 'pair'), [(i, i ^ far) for i in range(MEMBER...  14.2 us
    ppermute x4, waiting for transfers between devices, rotated(): lax.ppermute(block, axis, [(i, (i + step) % size) for i in range(size)])  9 us
    ppermute x4, starting transfers between devices, rotated(): lax.ppermute(block, axis, [(i, (i + step) % size) for i in range(size)])  7.27 us
    pallas_call x17, Pallas kernels, local_call(): pl.pallas_call(body, name=name, out_shape=out_shapes, in_specs=[pl.BlockS...  7.03 us
    ppermute x1, starting transfers between devices, parted(): return lax.ppermute(block, ('twin', 'line'), list(enumerate(to)))  3.08 us
    pallas_call x2, Pallas kernels, unpack(): pl.pallas_call(functools.partial(unpack_body, fars), name='unpack', out_s...  1.83 us
    ppermute x4, starting transfers between devices, to_twin(): return lax.ppermute(block, 'twin', [(0, 1), (1, 0)])  1.44 us
  transfers between devices with their start and end apart: 21, of which 12 were waited for; matrix products, arithmetic and copies ran while one was open for 0% of the time, Pallas kernels for 8%

profile of v11, /device:TPU:0, one launch (start us, length us, event | category | flops | bytes accessed | tf_op | source)
XLA Modules:
  0.0 62.8 jit_solution(2188900282419464128)
XLA Ops:
  0.6 1.0 %front.1 = (bf16[256,512]{1,0:T(8,128)(2,1)S(1)}, bf16[128,512]{1,0:T(8,128)(2,1)S(1)}) custom-call(bf16[512,512]{1,0:T(8,128)(2,1)} %shard.1), custom_call_target="tpu_custom_call" | custom-call | bytes 524288 | tf_op jit(solution)/shard_map/front/pallas_call | solution.py:27
  1.6 3.1 %collective-permute-start.3 = (bf16[256,512]{1,0:T(8,128)(2,1)S(1)}, bf16[256,512]{1,0:T(8,128)(2,1)S(1)}, u32[]{:S(2)}, u32[]{:S(2)}) collective-permute-start(bf16[256,512]{1,0:T(8,128)(2,1)S(1)} %get-tuple-element.45.refs_0_), channel_id=1, source_target_pairs={{0,2},{2,4},{4,6},{6,0},{8,14},{10,8},{12,10},{14,12},{1,3},{3,5},... | collective-permute-start | bytes 786440 | tf_op jit(solution)/shard_map/ppermute | solution.py:138
  4.7 2.6 %collective-permute-start.4 = (bf16[128,512]{1,0:T(8,128)(2,1)S(1)}, bf16[128,512]{1,0:T(8,128)(2,1)S(1)}, u32[]{:S(2)}, u32[]{:S(2)}) collective-permute-start(bf16[128,512]{1,0:T(8,128)(2,1)S(1)} %get-tuple-element.46), channel_id=1, source_target_pairs={{0,4},{2,6},{4,0},{6,2},{1,5},{3,7},{5,1},{7,3},{8,12},{10,14},{12... | collective-permute-start | bytes 393224 | tf_op jit(solution)/shard_map/ppermute | solution.py:41
  7.3 1.2 %copy-done = bf16[128,4096]{1,0:T(8,128)(2,1)S(1)} copy-done((bf16[128,4096]{1,0:T(8,128)(2,1)S(1)}, bf16[128,4096]{1,0:T(8,128)(2,1)}, u32[]{:S(2)}) %copy-start) | copy-done | bytes 1048600
  8.8 2.5 %collective-permute-start = (bf16[128,1024]{1,0:T(8,128)(2,1)S(1)}, bf16[128,1024]{1,0:T(8,128)(2,1)S(1)}, u32[]{:S(2)}, u32[]{:S(2)}) collective-permute-start(bf16[128,1024]{1,0:T(8,128)(2,1)S(1)} %get-tuple-element.41), channel_id=1, source_target_pairs={{0,17},{1,16},{16,1},{17,0},{2,19},{3,18},{18,3},{19,2},{4,21},{5,... | collective-permute-start | bytes 786440 | tf_op jit(solution)/shard_map/ppermute | solution.py:53
  12.4 4.8 %collective-permute-done.4.refs_1_.refs_2_ = bf16[128,512]{1,0:T(8,128)(2,1)S(1)} collective-permute-done((bf16[128,512]{1,0:T(8,128)(2,1)S(1)}, bf16[128,512]{1,0:T(8,128)(2,1)S(1)}, u32[]{:S(2)}, u32[]{:S(2)}) %collective-permute-start.4) | collective-permute-done | bytes 131104 | tf_op jit(solution)/shard_map/ppermute | solution.py:41
  17.2 0.8 %collective-permute-start.5 = (bf16[192,512]{1,0:T(8,128)(2,1)S(1)}, bf16[192,512]{1,0:T(8,128)(2,1)S(1)}, u32[]{:S(2)}, u32[]{:S(2)}) collective-permute-start(bf16[192,512]{1,0:T(8,128)(2,1)S(1)} %get-tuple-element.47), channel_id=1, source_target_pairs={{0,8},{8,0},{1,9},{9,1},{2,10},{10,2},{3,11},{11,3},{4,12},{12,4},... | collective-permute-start | bytes 589832 | tf_op jit(solution)/shard_map/ppermute | solution.py:45
  18.1 1.0 %collective-permute-done.block.refs_3_ = bf16[128,1024]{1,0:T(8,128)(2,1)S(1)} collective-permute-done((bf16[128,1024]{1,0:T(8,128)(2,1)S(1)}, bf16[128,1024]{1,0:T(8,128)(2,1)S(1)}, u32[]{:S(2)}, u32[]{:S(2)}) %collective-permute-start) | collective-permute-done | bytes 262176 | tf_op jit(solution)/shard_map/ppermute | solution.py:53
  19.1 3.6 %collective-permute-done.1.block.refs_2_ = bf16[128,1024]{1,0:T(8,128)(2,1)S(1)} collective-permute-done((bf16[128,1024]{1,0:T(8,128)(2,1)S(1)}, bf16[128,1024]{1,0:T(8,128)(2,1)S(1)}, u32[]{:S(2)}, u32[]{:S(2)}) %collective-permute-start.1) | collective-permute-done | bytes 262176 | tf_op jit(solution)/shard_map/ppermute | solution.py:53
  23.8 2.4 %collective-permute-start.7 = (bf16[128,512]{1,0:T(8,128)(2,1)S(1)}, bf16[128,512]{1,0:T(8,128)(2,1)S(1)}, u32[]{:S(2)}, u32[]{:S(2)}) collective-permute-start(bf16[128,512]{1,0:T(8,128)(2,1)S(1)} %share.5), channel_id=1, source_target_pairs={{0,17},{1,16},{16,1},{17,0},{2,19},{3,18},{18,3},{19,2},{4,21},{5,... | collective-permute-start | bytes 393224 | tf_op jit(solution)/shard_map/ppermute | solution.py:53
  26.2 0.6 collective-permute-start.8
  27.6 2.5 %collective-permute-done.7.refs_1_ = bf16[128,512]{1,0:T(8,128)(2,1)S(1)} collective-permute-done((bf16[128,512]{1,0:T(8,128)(2,1)S(1)}, bf16[128,512]{1,0:T(8,128)(2,1)S(1)}, u32[]{:S(2)}, u32[]{:S(2)}) %collective-permute-start.7) | collective-permute-done | bytes 131104 | tf_op jit(solution)/shard_map/ppermute | solution.py:53
  30.1 2.6 %collective-permute-done.8.refs_2_ = bf16[128,512]{1,0:T(8,128)(2,1)S(1)} collective-permute-done((bf16[128,512]{1,0:T(8,128)(2,1)S(1)}, bf16[128,512]{1,0:T(8,128)(2,1)S(1)}, u32[]{:S(2)}, u32[]{:S(2)}) %collective-permute-start.8) | collective-permute-done | bytes 131104 | tf_op jit(solution)/shard_map/ppermute | solution.py:53
  33.2 1.6 %collective-permute-start.10 = (bf16[128,512]{1,0:T(8,128)(2,1)S(1)}, bf16[128,512]{1,0:T(8,128)(2,1)S(1)}, u32[]{:S(2)}, u32[]{:S(2)}) collective-permute-start(bf16[128,512]{1,0:T(8,128)(2,1)S(1)} %get-tuple-element.55.grad.refs_4_), channel_id=1, source_target_pairs={{0,17},{1,16},{16,1},{17,0},{2,19},{3,18},{18,3},{19,2},{4,21},{5,... | collective-permute-start | bytes 393224 | tf_op jit(solution)/shard_map/ppermute | solution.py:53
  34.8 1.4 %collective-permute-start.12 = (bf16[128,512]{1,0:T(8,128)(2,1)S(1)}, bf16[128,512]{1,0:T(8,128)(2,1)S(1)}, u32[]{:S(2)}, u32[]{:S(2)}) collective-permute-start(bf16[128,512]{1,0:T(8,128)(2,1)S(1)} %get-tuple-element.55.grad.refs_4_), channel_id=1, source_target_pairs={{0,16},{1,17},{16,0},{17,1},{2,18},{3,19},{18,2},{19,3},{4,20},{5,... | collective-permute-start | bytes 393224 | tf_op jit(solution)/shard_map/ppermute | solution.py:53
  36.2 0.6 collective-permute-start.11
  36.8 0.7 %emit.1 = bf16[128,512]{1,0:T(8,128)(2,1)} custom-call(bf16[128,512]{1,0:T(8,128)(2,1)S(1)} %get-tuple-element.56.held), custom_call_target="tpu_custom_call" | custom-call | bytes 131072 | tf_op jit(solution)/shard_map/emit/pallas_call | solution.py:27
  37.9 2.7 %collective-permute-done.10.grad.refs_7_ = bf16[128,512]{1,0:T(8,128)(2,1)S(1)} collective-permute-done((bf16[128,512]{1,0:T(8,128)(2,1)S(1)}, bf16[128,512]{1,0:T(8,128)(2,1)S(1)}, u32[]{:S(2)}, u32[]{:S(2)}) %collective-permute-start.10) | collective-permute-done | bytes 131104 | tf_op jit(solution)/shard_map/ppermute | solution.py:53
  41.0 1.3 %collective-permute-done.12.grad.refs_6_ = bf16[128,512]{1,0:T(8,128)(2,1)S(1)} collective-permute-done((bf16[128,512]{1,0:T(8,128)(2,1)S(1)}, bf16[128,512]{1,0:T(8,128)(2,1)S(1)}, u32[]{:S(2)}, u32[]{:S(2)}) %collective-permute-start.12) | collective-permute-done | bytes 131104 | tf_op jit(solution)/shard_map/ppermute | solution.py:53
  42.4 0.7 %terms.1 = (f32[4,128,512]{2,1,0:T(8,128)S(1)}, bf16[256,512]{1,0:T(8,128)(2,1)S(1)}, bf16[256,512]{1,0:T(8,128)(2,1)S(1)}) custom-call(bf16[128,1024]{1,0:T(8,128)(2,1)S(1)} %get-tuple-element.49.block.refs_0_, bf16[128,1024]{1,0:T(8,128)(2,1)S(1)} %collective-permute-done.2.block.refs_1_, bf16[128,1024]{1,0:T(8,128)(2,1)S(1)} %collective-permute-done.1.block.refs_2_, ...), custom_call_target="tpu_custom_call" | custom-call | tf_op jit(solution)/shard_map/terms/pallas_call | solution.py:27
  44.7 1.3 %collective-permute-start.14 = (bf16[128,1024]{1,0:T(8,128)(2,1)S(1)}, bf16[128,1024]{1,0:T(8,128)(2,1)S(1)}, u32[]{:S(2)}, u32[]{:S(2)}) collective-permute-start(bf16[128,1024]{1,0:T(8,128)(2,1)S(1)} %columns.7), channel_id=1, source_target_pairs={{0,16},{1,17},{16,0},{17,1},{2,18},{3,19},{18,2},{19,3},{4,20},{5,... | collective-permute-start | bytes 786440 | tf_op jit(solution)/shard_map/ppermute | solution.py:53
  46.0 0.6 collective-permute-start.13
  46.6 1.1 %collective-permute-start.18 = (bf16[128,512]{1,0:T(8,128)(2,1)S(1)}, bf16[128,512]{1,0:T(8,128)(2,1)S(1)}, u32[]{:S(2)}, u32[]{:S(2)}) collective-permute-start(bf16[128,512]{1,0:T(8,128)(2,1)S(1)} %get-tuple-element.65), channel_id=1, source_target_pairs={{0,6},{2,0},{4,2},{6,4},{1,7},{3,1},{5,3},{7,5},{8,14},{10,8},{12,... | collective-permute-start | bytes 393224 | tf_op jit(solution)/shard_map/ppermute | solution.py:41
  47.7 1.6 %collective-permute-start.19 = (bf16[128,512]{1,0:T(8,128)(2,1)S(1)}, bf16[128,512]{1,0:T(8,128)(2,1)S(1)}, u32[]{:S(2)}, u32[]{:S(2)}) collective-permute-start(bf16[128,512]{1,0:T(8,128)(2,1)S(1)} %get-tuple-element.66), channel_id=1, source_target_pairs={{0,4},{2,6},{4,0},{6,2},{1,5},{3,7},{5,1},{7,3},{8,12},{10,14},{12... | collective-permute-start | bytes 393224 | tf_op jit(solution)/shard_map/ppermute | solution.py:41
  49.4 1.9 %collective-permute-start.20 = (bf16[128,512]{1,0:T(8,128)(2,1)S(1)}, bf16[128,512]{1,0:T(8,128)(2,1)S(1)}, u32[]{:S(2)}, u32[]{:S(2)}) collective-permute-start(bf16[128,512]{1,0:T(8,128)(2,1)S(1)} %get-tuple-element.67), channel_id=1, source_target_pairs={{0,2},{2,4},{4,6},{6,0},{1,3},{3,5},{5,7},{7,1},{8,10},{10,12},{12... | collective-permute-start | bytes 393224 | tf_op jit(solution)/shard_map/ppermute | solution.py:41
  51.3 1.7 %collective-permute-done.14.refs_2_ = bf16[128,1024]{1,0:T(8,128)(2,1)S(1)} collective-permute-done((bf16[128,1024]{1,0:T(8,128)(2,1)S(1)}, bf16[128,1024]{1,0:T(8,128)(2,1)S(1)}, u32[]{:S(2)}, u32[]{:S(2)}) %collective-permute-start.14) | collective-permute-done | bytes 262176 | tf_op jit(solution)/shard_map/ppermute | solution.py:53
  53.0 1.0 %collective-permute-done.13.refs_1_ = bf16[128,1024]{1,0:T(8,128)(2,1)S(1)} collective-permute-done((bf16[128,1024]{1,0:T(8,128)(2,1)S(1)}, bf16[128,1024]{1,0:T(8,128)(2,1)S(1)}, u32[]{:S(2)}, u32[]{:S(2)}) %collective-permute-start.13) | collective-permute-done | bytes 262176 | tf_op jit(solution)/shard_map/ppermute | solution.py:53
  54.0 1.7 %collective-permute-start.17 = (bf16[128,1024]{1,0:T(8,128)(2,1)S(1)}, bf16[128,1024]{1,0:T(8,128)(2,1)S(1)}, u32[]{:S(2)}, u32[]{:S(2)}) collective-permute-start(bf16[128,1024]{1,0:T(8,128)(2,1)S(1)} %columns.5), channel_id=1, source_target_pairs={{0,17},{1,16},{16,1},{17,0},{2,19},{3,18},{18,3},{19,2},{4,21},{5,... | collective-permute-start | bytes 786440 | tf_op jit(solution)/shard_map/ppermute | solution.py:53
  55.7 1.1 %unpack.2.refs_1_ = bf16[128,4096]{1,0:T(8,128)(2,1)} custom-call(bf16[128,1024]{1,0:T(8,128)(2,1)S(1)} %columns.4.refs_0_, bf16[128,1024]{1,0:T(8,128)(2,1)S(1)} %collective-permute-done.13.refs_1_, bf16[128,1024]{1,0:T(8,128)(2,1)S(1)} %collective-permute-done.14.refs_2_), custom_call_target="tpu_custom_call" | custom-call | tf_op jit(solution)/shard_map/unpack/pallas_call | solution.py:106
  56.7 4.2 %collective-permute-done.19.refs_2_ = bf16[128,512]{1,0:T(8,128)(2,1)S(1)} collective-permute-done((bf16[128,512]{1,0:T(8,128)(2,1)S(1)}, bf16[128,512]{1,0:T(8,128)(2,1)S(1)}, u32[]{:S(2)}, u32[]{:S(2)}) %collective-permute-start.19) | collective-permute-done | bytes 131104 | tf_op jit(solution)/shard_map/ppermute | solution.py:41
  60.9 0.8 %final_sum.1 = f32[128,512]{1,0:T(8,128)} custom-call(f32[128,512]{1,0:T(8,128)S(1)} %get-tuple-element.72.refs_0_, bf16[128,512]{1,0:T(8,128)(2,1)S(1)} %collective-permute-done.18.refs_1_, bf16[128,512]{1,0:T(8,128)(2,1)S(1)} %collective-permute-done.19.refs_2_, bf16[128,512]{1,0:T(8,128)(2,1)S(1)} %collective-permute-done.20.refs_3_), custom_call_target="tpu_custom_call" | custom-call | flops 3221225472 | bytes 655360 | tf_op jit(solution)/shard_map/final_sum/pallas_call | solution.py:27
  62.0 0.8 %unpack.3 = bf16[128,4096]{1,0:T(8,128)(2,1)} custom-call(bf16[128,1024]{1,0:T(8,128)(2,1)S(1)} %collective-permute-done.17.refs_0_, bf16[128,4096]{1,0:T(8,128)(2,1)} %unpack.2.refs_1_), custom_call_target="tpu_custom_call", output_to_operand_aliasing={{}: (1, {})} | custom-call | tf_op jit(solution)/shard_map/unpack/pallas_call | solution.py:106
  (33 shorter events, 6.7 us)
Async XLA Ops:
  1.6 15.6 %collective-permute-start.3 = (bf16[256,512]{1,0:T(8,128)(2,1)S(1)}, bf16[256,512]{1,0:T(8,128)(2,1)S(1)}, u32[]{:S(2)}, u32[]{:S(2)}) collective-permute-start(bf16[256,512]{1,0:T(8,128)(2,1)S(1)} %get-tuple-element.45.refs_0_), channel_id=1, source_target_pairs={{0,2},{2,4},{4,6},{6,0},{8,14},{10,8},{12,10},{14,12},{1,3},{3,5},... | collective-permute-start | bytes 786440 | tf_op jit(solution)/shard_map/ppermute | solution.py:138
  4.7 12.5 %collective-permute-start.4 = (bf16[128,512]{1,0:T(8,128)(2,1)S(1)}, bf16[128,512]{1,0:T(8,128)(2,1)S(1)}, u32[]{:S(2)}, u32[]{:S(2)}) collective-permute-start(bf16[128,512]{1,0:T(8,128)(2,1)S(1)} %get-tuple-element.46), channel_id=1, source_target_pairs={{0,4},{2,6},{4,0},{6,2},{1,5},{3,7},{5,1},{7,3},{8,12},{10,14},{12... | collective-permute-start | bytes 393224 | tf_op jit(solution)/shard_map/ppermute | solution.py:41
  7.3 1.2 %copy-start = (bf16[128,4096]{1,0:T(8,128)(2,1)S(1)}, bf16[128,4096]{1,0:T(8,128)(2,1)}, u32[]{:S(2)}) copy-start(bf16[128,4096]{1,0:T(8,128)(2,1)} %tokens.1) | copy-start | bytes 3145732
  8.8 10.3 %collective-permute-start = (bf16[128,1024]{1,0:T(8,128)(2,1)S(1)}, bf16[128,1024]{1,0:T(8,128)(2,1)S(1)}, u32[]{:S(2)}, u32[]{:S(2)}) collective-permute-start(bf16[128,1024]{1,0:T(8,128)(2,1)S(1)} %get-tuple-element.41), channel_id=1, source_target_pairs={{0,17},{1,16},{16,1},{17,0},{2,19},{3,18},{18,3},{19,2},{4,21},{5,... | collective-permute-start | bytes 786440 | tf_op jit(solution)/shard_map/ppermute | solution.py:53
  11.3 11.4 %collective-permute-start.1 = (bf16[128,1024]{1,0:T(8,128)(2,1)S(1)}, bf16[128,1024]{1,0:T(8,128)(2,1)S(1)}, u32[]{:S(2)}, u32[]{:S(2)}) collective-permute-start(bf16[128,1024]{1,0:T(8,128)(2,1)S(1)} %get-tuple-element.42), channel_id=1, source_target_pairs={{0,16},{1,17},{16,0},{17,1},{2,18},{3,19},{18,2},{19,3},{4,20},{5,... | collective-permute-start | bytes 786440 | tf_op jit(solution)/shard_map/ppermute | solution.py:53
  11.9 10.8 %collective-permute-start.2 = (bf16[128,1024]{1,0:T(8,128)(2,1)S(1)}, bf16[128,1024]{1,0:T(8,128)(2,1)S(1)}, u32[]{:S(2)}, u32[]{:S(2)}) collective-permute-start(bf16[128,1024]{1,0:T(8,128)(2,1)S(1)} %get-tuple-element.43), channel_id=1, source_target_pairs={{0,1},{1,0},{16,17},{17,16},{2,3},{3,2},{18,19},{19,18},{4,5},{5,4... | collective-permute-start | bytes 786440 | tf_op jit(solution)/shard_map/ppermute | solution.py:53
  17.2 5.5 %collective-permute-start.5 = (bf16[192,512]{1,0:T(8,128)(2,1)S(1)}, bf16[192,512]{1,0:T(8,128)(2,1)S(1)}, u32[]{:S(2)}, u32[]{:S(2)}) collective-permute-start(bf16[192,512]{1,0:T(8,128)(2,1)S(1)} %get-tuple-element.47), channel_id=1, source_target_pairs={{0,8},{8,0},{1,9},{9,1},{2,10},{10,2},{3,11},{11,3},{4,12},{12,4},... | collective-permute-start | bytes 589832 | tf_op jit(solution)/shard_map/ppermute | solution.py:45
  18.0 4.7 %collective-permute-start.6 = (bf16[192,512]{1,0:T(8,128)(2,1)S(1)}, bf16[192,512]{1,0:T(8,128)(2,1)S(1)}, u32[]{:S(2)}, u32[]{:S(2)}) collective-permute-start(bf16[192,512]{1,0:T(8,128)(2,1)S(1)} %get-tuple-element.48), channel_id=1, source_target_pairs={{0,8},{8,0},{1,9},{9,1},{2,10},{10,2},{3,11},{11,3},{4,12},{12,4},... | collective-permute-start | bytes 589832 | tf_op jit(solution)/shard_map/ppermute | solution.py:45
  23.8 9.2 %copy-start.1 = (bf16[128,512]{1,0:T(8,128)(2,1)S(1)}, bf16[128,512]{1,0:T(8,128)(2,1)}, u32[]{:S(2)}) copy-start(bf16[128,512]{1,0:T(8,128)(2,1)} %refs_4_.1) | copy-start | bytes 393220
  23.8 6.3 %collective-permute-start.7 = (bf16[128,512]{1,0:T(8,128)(2,1)S(1)}, bf16[128,512]{1,0:T(8,128)(2,1)S(1)}, u32[]{:S(2)}, u32[]{:S(2)}) collective-permute-start(bf16[128,512]{1,0:T(8,128)(2,1)S(1)} %share.5), channel_id=1, source_target_pairs={{0,17},{1,16},{16,1},{17,0},{2,19},{3,18},{18,3},{19,2},{4,21},{5,... | collective-permute-start | bytes 393224 | tf_op jit(solution)/shard_map/ppermute | solution.py:53
  26.2 6.5 %collective-permute-start.8 = (bf16[128,512]{1,0:T(8,128)(2,1)S(1)}, bf16[128,512]{1,0:T(8,128)(2,1)S(1)}, u32[]{:S(2)}, u32[]{:S(2)}) collective-permute-start(bf16[128,512]{1,0:T(8,128)(2,1)S(1)} %share.6), channel_id=1, source_target_pairs={{0,1},{1,0},{16,17},{17,16},{2,3},{3,2},{18,19},{19,18},{4,5},{5,4... | collective-permute-start | bytes 393224 | tf_op jit(solution)/shard_map/ppermute | solution.py:53
  26.8 6.2 %collective-permute-start.9 = (bf16[128,512]{1,0:T(8,128)(2,1)S(1)}, bf16[128,512]{1,0:T(8,128)(2,1)S(1)}, u32[]{:S(2)}, u32[]{:S(2)}) collective-permute-start(bf16[128,512]{1,0:T(8,128)(2,1)S(1)} %share.7), channel_id=1, source_target_pairs={{0,16},{1,17},{16,0},{17,1},{2,18},{3,19},{18,2},{19,3},{4,20},{5,... | collective-permute-start | bytes 393224 | tf_op jit(solution)/shard_map/ppermute | solution.py:53
  33.2 7.4 %collective-permute-start.10 = (bf16[128,512]{1,0:T(8,128)(2,1)S(1)}, bf16[128,512]{1,0:T(8,128)(2,1)S(1)}, u32[]{:S(2)}, u32[]{:S(2)}) collective-permute-start(bf16[128,512]{1,0:T(8,128)(2,1)S(1)} %get-tuple-element.55.grad.refs_4_), channel_id=1, source_target_pairs={{0,17},{1,16},{16,1},{17,0},{2,19},{3,18},{18,3},{19,2},{4,21},{5,... | collective-permute-start | bytes 393224 | tf_op jit(solution)/shard_map/ppermute | solution.py:53
  34.8 7.6 %collective-permute-start.12 = (bf16[128,512]{1,0:T(8,128)(2,1)S(1)}, bf16[128,512]{1,0:T(8,128)(2,1)S(1)}, u32[]{:S(2)}, u32[]{:S(2)}) collective-permute-start(bf16[128,512]{1,0:T(8,128)(2,1)S(1)} %get-tuple-element.55.grad.refs_4_), channel_id=1, source_target_pairs={{0,16},{1,17},{16,0},{17,1},{2,18},{3,19},{18,2},{19,3},{4,20},{5,... | collective-permute-start | bytes 393224 | tf_op jit(solution)/shard_map/ppermute | solution.py:53
  36.2 6.2 %collective-permute-start.11 = (bf16[128,512]{1,0:T(8,128)(2,1)S(1)}, bf16[128,512]{1,0:T(8,128)(2,1)S(1)}, u32[]{:S(2)}, u32[]{:S(2)}) collective-permute-start(bf16[128,512]{1,0:T(8,128)(2,1)S(1)} %get-tuple-element.55.grad.refs_4_), channel_id=1, source_target_pairs={{0,1},{1,0},{16,17},{17,16},{2,3},{3,2},{18,19},{19,18},{4,5},{5,4... | collective-permute-start | bytes 393224 | tf_op jit(solution)/shard_map/ppermute | solution.py:53
  43.1 3.4 %collective-permute-start.15 = (bf16[256,512]{1,0:T(8,128)(2,1)S(1)}, bf16[256,512]{1,0:T(8,128)(2,1)S(1)}, u32[]{:S(2)}, u32[]{:S(2)}) collective-permute-start(bf16[256,512]{1,0:T(8,128)(2,1)S(1)} %get-tuple-element.62), channel_id=1, source_target_pairs={{0,8},{8,0},{1,9},{9,1},{2,10},{10,2},{3,11},{11,3},{4,12},{12,4},... | collective-permute-start | bytes 786440 | tf_op jit(solution)/shard_map/ppermute | solution.py:45
  43.2 3.3 %collective-permute-start.16 = (bf16[256,512]{1,0:T(8,128)(2,1)S(1)}, bf16[256,512]{1,0:T(8,128)(2,1)S(1)}, u32[]{:S(2)}, u32[]{:S(2)}) collective-permute-start(bf16[256,512]{1,0:T(8,128)(2,1)S(1)} %get-tuple-element.63), channel_id=1, source_target_pairs={{0,8},{8,0},{1,9},{9,1},{2,10},{10,2},{3,11},{11,3},{4,12},{12,4},... | collective-permute-start | bytes 786440 | tf_op jit(solution)/shard_map/ppermute | solution.py:45
  44.7 8.3 %collective-permute-start.14 = (bf16[128,1024]{1,0:T(8,128)(2,1)S(1)}, bf16[128,1024]{1,0:T(8,128)(2,1)S(1)}, u32[]{:S(2)}, u32[]{:S(2)}) collective-permute-start(bf16[128,1024]{1,0:T(8,128)(2,1)S(1)} %columns.7), channel_id=1, source_target_pairs={{0,16},{1,17},{16,0},{17,1},{2,18},{3,19},{18,2},{19,3},{4,20},{5,... | collective-permute-start | bytes 786440 | tf_op jit(solution)/shard_map/ppermute | solution.py:53
  46.0 8.0 %collective-permute-start.13 = (bf16[128,1024]{1,0:T(8,128)(2,1)S(1)}, bf16[128,1024]{1,0:T(8,128)(2,1)S(1)}, u32[]{:S(2)}, u32[]{:S(2)}) collective-permute-start(bf16[128,1024]{1,0:T(8,128)(2,1)S(1)} %columns.6), channel_id=1, source_target_pairs={{0,1},{1,0},{16,17},{17,16},{2,3},{3,2},{18,19},{19,18},{4,5},{5,4... | collective-permute-start | bytes 786440 | tf_op jit(solution)/shard_map/ppermute | solution.py:53
  46.6 10.1 %collective-permute-start.18 = (bf16[128,512]{1,0:T(8,128)(2,1)S(1)}, bf16[128,512]{1,0:T(8,128)(2,1)S(1)}, u32[]{:S(2)}, u32[]{:S(2)}) collective-permute-start(bf16[128,512]{1,0:T(8,128)(2,1)S(1)} %get-tuple-element.65), channel_id=1, source_target_pairs={{0,6},{2,0},{4,2},{6,4},{1,7},{3,1},{5,3},{7,5},{8,14},{10,8},{12,... | collective-permute-start | bytes 393224 | tf_op jit(solution)/shard_map/ppermute | solution.py:41
  47.7 13.2 %collective-permute-start.19 = (bf16[128,512]{1,0:T(8,128)(2,1)S(1)}, bf16[128,512]{1,0:T(8,128)(2,1)S(1)}, u32[]{:S(2)}, u32[]{:S(2)}) collective-permute-start(bf16[128,512]{1,0:T(8,128)(2,1)S(1)} %get-tuple-element.66), channel_id=1, source_target_pairs={{0,4},{2,6},{4,0},{6,2},{1,5},{3,7},{5,1},{7,3},{8,12},{10,14},{12... | collective-permute-start | bytes 393224 | tf_op jit(solution)/shard_map/ppermute | solution.py:41
  49.4 11.5 %collective-permute-start.20 = (bf16[128,512]{1,0:T(8,128)(2,1)S(1)}, bf16[128,512]{1,0:T(8,128)(2,1)S(1)}, u32[]{:S(2)}, u32[]{:S(2)}) collective-permute-start(bf16[128,512]{1,0:T(8,128)(2,1)S(1)} %get-tuple-element.67), channel_id=1, source_target_pairs={{0,2},{2,4},{4,6},{6,0},{1,3},{3,5},{5,7},{7,1},{8,10},{10,12},{12... | collective-permute-start | bytes 393224 | tf_op jit(solution)/shard_map/ppermute | solution.py:41
  54.0 8.0 %collective-permute-start.17 = (bf16[128,1024]{1,0:T(8,128)(2,1)S(1)}, bf16[128,1024]{1,0:T(8,128)(2,1)S(1)}, u32[]{:S(2)}, u32[]{:S(2)}) collective-permute-start(bf16[128,1024]{1,0:T(8,128)(2,1)S(1)} %columns.5), channel_id=1, source_target_pairs={{0,17},{1,16},{16,1},{17,0},{2,19},{3,18},{18,3},{19,2},{4,21},{5,... | collective-permute-start | bytes 786440 | tf_op jit(solution)/shard_map/ppermute | solution.py:53

commit v12 on v11

--- a/solution.py
+++ b/solution.py
@@ -175,18 +175,24 @@
         put(line // 2, 1 - core, others[others.shape[0] - rows :])
 
 
-def share_body(block, weight, out):
-    out[...] = jnp.dot(block[...], weight[...], preferred_element_type=f32).astype(out.dtype)
-
-
-def columns_body(grad, weight, out):
-    out[...] = lax.dot_general(
-        grad[...], weight[...], (((1,), (1,)), ((), ())), preferred_element_type=f32
-    ).astype(out.dtype)
-
-
-def add_body(first, second, out):
-    out[...] = (first[...].astype(f32) + second[...].astype(f32)).astype(out.dtype)
+def share_body(*refs):
+    *blocks, weight = refs[: len(refs) // 2 + 1]
+    outs = refs[len(blocks) + 1 :]
+    stacked = jnp.concatenate([block[...] for block in blocks], axis=0)
+    product = jnp.dot(stacked, weight[...], preferred_element_type=f32)
+    for i, out in enumerate(outs):
+        out[...] = product[i * out.shape[0] : (i + 1) * out.shape[0]].astype(out.dtype)
+
+
+def columns_body(*refs):
+    *grads, weight = refs[: len(refs) // 2 + 1]
+    outs = refs[len(grads) + 1 :]
+    stacked = jnp.concatenate([grad[...] for grad in grads], axis=0)
+    product = lax.dot_general(
+        stacked, weight[...], (((1,), (1,)), ((), ())), preferred_element_type=f32
+    )
+    for i, out in enumerate(outs):
+        out[...] = product[i * out.shape[0] : (i + 1) * out.shape[0]].astype(out.dtype)
 
 
 def emit_body(held, out):
@@ -292,20 +298,21 @@
         *theirs,
     )
 
-    def share(far, kind):
-        shaped = shape((tok_rows, key_cols), kind)
-        return local_call("share", share_body, shaped, blocks[far], weight, flops=flops)
-
-    shares = [to_member(share(far, bf16), far) for far in (3, 1, 2)]
-    normed, key_grad = local_call("norm", norm_body, [head_shape] * 2, share(0, f32), *shares, cotangent)
+    def share(fars, kind):
+        shaped = [shape((tok_rows, key_cols), kind)] * len(fars)
+        return local_call("share", share_body, shaped, *[blocks[far] for far in fars], weight, flops=flops)
+
+    order = (3, 1, 2)
+    shares = [to_member(part, far) for far, part in zip(order, share(order, bf16))]
+    normed, key_grad = local_call("norm", norm_body, [head_shape] * 2, *share((0,), f32), *shares, cotangent)
     key_out = local_call("emit", emit_body, head_shape, normed)
 
     grad_3, grad_1, grad_2 = (to_member(key_grad, far) for far in (3, 1, 2))
 
-    def columns(grad, **cost):
-        return local_call("columns", columns_body, block_shape, grad, weight, **cost)
-
-    column_0, column_3 = columns(key_grad, flops=flops), columns(grad_3, flops=flops)
+    def columns(*grads):
+        return local_call("columns", columns_body, [block_shape] * len(grads), *grads, weight, flops=flops)
+
+    (column_0,), (column_3,) = columns(key_grad), columns(grad_3)
     column_0, column_3, key_out, grad_1, grad_2 = lax.optimization_barrier(
         (column_0, column_3, key_out, grad_1, grad_2)
     )
@@ -332,8 +339,8 @@
     )
 
     met = [sums[0]] + [rotated(sums[step], "line", -step) for step in range(1, line)]
-    back_1, back_2 = to_member(columns(grad_1, flops=flops), 1), to_member(columns(grad_2, flops=flops), 2)
-    column_3, back_1, back_2, _ = lax.optimization_barrier((column_3, back_1, back_2, sums))
+    back_1, back_2 = (to_member(column, far) for far, column in zip((1, 2), columns(grad_1, grad_2)))
+    column_3, back_2, _ = lax.optimization_barrier((column_3, back_2, sums))
     back_3 = to_member(column_3, 3)
     input_grad = unpack((0, 1, 2), (column_0, back_1, back_2), shape((tok_rows, width), bf16))
     met, input_grad = lax.optimization_barrier((met, input_grad))

time: 63 us -> 61.7 us (0.979)
  Pallas kernels: 8.86 us -> 8 us
    ppermute x4, waiting for transfers between devices: 9 us -> 10.4 us  [rotated(): lax.ppermute(block, axis, [(i, (i + step) % size) for i in range(size)])]
    ppermute x12, waiting for transfers between devices: 16.9 us -> 15.6 us  [to_member(): lax.ppermute(block, ('side', 'pair'), [(i, i ^ far) for i in range(MEMBER...]
    pallas_call x17 -> x14, Pallas kernels: 7.03 us -> 6.17 us  [local_call(): pl.pallas_call(body, name=name, out_shape=out_shapes, in_specs=[pl.BlockS...]
  transfers between devices with their start and end apart: 21 -> 21, of which waited for: 12 -> 10; matrix products, arithmetic and copies ran while one was open for 0% -> 0% of each run, Pallas kernels for 8% -> 7%
where the time goes in v12:
time: 61.7 us; the launch traced here: 61.5 us
  waiting for transfers between devices  26 us (42%)
  starting transfers between devices  25.6 us (41%)
  Pallas kernels  8 us (13%)
  local copies, waits for them, and re-layouts  1.23 us (2%)
  between operations  0.77 us (1%)
    ppermute x12, waiting for transfers between devices, to_member(): lax.ppermute(block, ('side', 'pair'), [(i, i ^ far) for i in range(MEMBER...  15.6 us
    ppermute x12, starting transfers between devices, to_member(): lax.ppermute(block, ('side', 'pair'), [(i, i ^ far) for i in range(MEMBER...  13.8 us
    ppermute x4, waiting for transfers between devices, rotated(): lax.ppermute(block, axis, [(i, (i + step) % size) for i in range(size)])  10.4 us
    ppermute x4, starting transfers between devices, rotated(): lax.ppermute(block, axis, [(i, (i + step) % size) for i in range(size)])  7.27 us
    pallas_call x14, Pallas kernels, local_call(): pl.pallas_call(body, name=name, out_shape=out_shapes, in_specs=[pl.BlockS...  6.17 us
    ppermute x1, starting transfers between devices, parted(): return lax.ppermute(block, ('twin', 'line'), list(enumerate(to)))  3.08 us
    pallas_call x2, Pallas kernels, unpack(): pl.pallas_call(functools.partial(unpack_body, fars), name='unpack', out_s...  1.83 us
    ppermute x4, starting transfers between devices, to_twin(): return lax.ppermute(block, 'twin', [(0, 1), (1, 0)])  1.44 us
  transfers between devices with their start and end apart: 21, of which 10 were waited for; matrix products, arithmetic and copies ran while one was open for 0% of the time, Pallas kernels for 7%

profile of v12, /device:TPU:0, one launch (start us, length us, event | category | flops | bytes accessed | tf_op | source)
XLA Modules:
  0.0 61.5 jit_solution(11524553179804129753)
XLA Ops:
  0.6 1.0 %front.1 = (bf16[256,512]{1,0:T(8,128)(2,1)S(1)}, bf16[128,512]{1,0:T(8,128)(2,1)S(1)}) custom-call(bf16[512,512]{1,0:T(8,128)(2,1)} %shard.1), custom_call_target="tpu_custom_call" | custom-call | bytes 524288 | tf_op jit(solution)/shard_map/front/pallas_call | solution.py:27
  1.6 3.1 %collective-permute-start.3 = (bf16[256,512]{1,0:T(8,128)(2,1)S(1)}, bf16[256,512]{1,0:T(8,128)(2,1)S(1)}, u32[]{:S(2)}, u32[]{:S(2)}) collective-permute-start(bf16[256,512]{1,0:T(8,128)(2,1)S(1)} %get-tuple-element.49.refs_0_), channel_id=1, source_target_pairs={{0,2},{2,4},{4,6},{6,0},{8,14},{10,8},{12,10},{14,12},{1,3},{3,5},... | collective-permute-start | bytes 786440 | tf_op jit(solution)/shard_map/ppermute | solution.py:138
  4.7 2.6 %collective-permute-start.4 = (bf16[128,512]{1,0:T(8,128)(2,1)S(1)}, bf16[128,512]{1,0:T(8,128)(2,1)S(1)}, u32[]{:S(2)}, u32[]{:S(2)}) collective-permute-start(bf16[128,512]{1,0:T(8,128)(2,1)S(1)} %get-tuple-element.50), channel_id=1, source_target_pairs={{0,4},{2,6},{4,0},{6,2},{1,5},{3,7},{5,1},{7,3},{8,12},{10,14},{12... | collective-permute-start | bytes 393224 | tf_op jit(solution)/shard_map/ppermute | solution.py:41
  7.3 1.2 %copy-done = bf16[128,4096]{1,0:T(8,128)(2,1)S(1)} copy-done((bf16[128,4096]{1,0:T(8,128)(2,1)S(1)}, bf16[128,4096]{1,0:T(8,128)(2,1)}, u32[]{:S(2)}) %copy-start) | copy-done | bytes 1048600
  8.8 2.5 %collective-permute-start = (bf16[128,1024]{1,0:T(8,128)(2,1)S(1)}, bf16[128,1024]{1,0:T(8,128)(2,1)S(1)}, u32[]{:S(2)}, u32[]{:S(2)}) collective-permute-start(bf16[128,1024]{1,0:T(8,128)(2,1)S(1)} %get-tuple-element.45), channel_id=1, source_target_pairs={{0,17},{1,16},{16,1},{17,0},{2,19},{3,18},{18,3},{19,2},{4,21},{5,... | collective-permute-start | bytes 786440 | tf_op jit(solution)/shard_map/ppermute | solution.py:53
  12.4 4.8 %collective-permute-done.4.refs_1_.refs_2_ = bf16[128,512]{1,0:T(8,128)(2,1)S(1)} collective-permute-done((bf16[128,512]{1,0:T(8,128)(2,1)S(1)}, bf16[128,512]{1,0:T(8,128)(2,1)S(1)}, u32[]{:S(2)}, u32[]{:S(2)}) %collective-permute-start.4) | collective-permute-done | bytes 131104 | tf_op jit(solution)/shard_map/ppermute | solution.py:41
  17.2 0.8 %collective-permute-start.5 = (bf16[192,512]{1,0:T(8,128)(2,1)S(1)}, bf16[192,512]{1,0:T(8,128)(2,1)S(1)}, u32[]{:S(2)}, u32[]{:S(2)}) collective-permute-start(bf16[192,512]{1,0:T(8,128)(2,1)S(1)} %get-tuple-element.51), channel_id=1, source_target_pairs={{0,8},{8,0},{1,9},{9,1},{2,10},{10,2},{3,11},{11,3},{4,12},{12,4},... | collective-permute-start | bytes 589832 | tf_op jit(solution)/shard_map/ppermute | solution.py:45
  18.1 1.0 %collective-permute-done.refs_0_.refs_3_ = bf16[128,1024]{1,0:T(8,128)(2,1)S(1)} collective-permute-done((bf16[128,1024]{1,0:T(8,128)(2,1)S(1)}, bf16[128,1024]{1,0:T(8,128)(2,1)S(1)}, u32[]{:S(2)}, u32[]{:S(2)}) %collective-permute-start) | collective-permute-done | bytes 262176 | tf_op jit(solution)/shard_map/ppermute | solution.py:53
  19.1 3.6 %collective-permute-done.1.refs_2_ = bf16[128,1024]{1,0:T(8,128)(2,1)S(1)} collective-permute-done((bf16[128,1024]{1,0:T(8,128)(2,1)S(1)}, bf16[128,1024]{1,0:T(8,128)(2,1)S(1)}, u32[]{:S(2)}, u32[]{:S(2)}) %collective-permute-start.1) | collective-permute-done | bytes 262176 | tf_op jit(solution)/shard_map/ppermute | solution.py:53
  22.8 0.6 share.3
  23.4 2.4 %collective-permute-start.7 = (bf16[128,512]{1,0:T(8,128)(2,1)S(1)}, bf16[128,512]{1,0:T(8,128)(2,1)S(1)}, u32[]{:S(2)}, u32[]{:S(2)}) collective-permute-start(bf16[128,512]{1,0:T(8,128)(2,1)S(1)} %get-tuple-element.59), channel_id=1, source_target_pairs={{0,17},{1,16},{16,1},{17,0},{2,19},{3,18},{18,3},{19,2},{4,21},{5,... | collective-permute-start | bytes 393224 | tf_op jit(solution)/shard_map/ppermute | solution.py:53
  25.8 0.6 %collective-permute-start.8 = (bf16[128,512]{1,0:T(8,128)(2,1)S(1)}, bf16[128,512]{1,0:T(8,128)(2,1)S(1)}, u32[]{:S(2)}, u32[]{:S(2)}) collective-permute-start(bf16[128,512]{1,0:T(8,128)(2,1)S(1)} %get-tuple-element.60), channel_id=1, source_target_pairs={{0,1},{1,0},{16,17},{17,16},{2,3},{3,2},{18,19},{19,18},{4,5},{5,4... | collective-permute-start | bytes 393224 | tf_op jit(solution)/shard_map/ppermute | solution.py:53
  27.3 2.5 %collective-permute-done.7.refs_1_ = bf16[128,512]{1,0:T(8,128)(2,1)S(1)} collective-permute-done((bf16[128,512]{1,0:T(8,128)(2,1)S(1)}, bf16[128,512]{1,0:T(8,128)(2,1)S(1)}, u32[]{:S(2)}, u32[]{:S(2)}) %collective-permute-start.7) | collective-permute-done | bytes 131104 | tf_op jit(solution)/shard_map/ppermute | solution.py:53
  29.7 2.6 %collective-permute-done.8.refs_2_ = bf16[128,512]{1,0:T(8,128)(2,1)S(1)} collective-permute-done((bf16[128,512]{1,0:T(8,128)(2,1)S(1)}, bf16[128,512]{1,0:T(8,128)(2,1)S(1)}, u32[]{:S(2)}, u32[]{:S(2)}) %collective-permute-start.8) | collective-permute-done | bytes 131104 | tf_op jit(solution)/shard_map/ppermute | solution.py:53
  32.8 1.6 %collective-permute-start.10 = (bf16[128,512]{1,0:T(8,128)(2,1)S(1)}, bf16[128,512]{1,0:T(8,128)(2,1)S(1)}, u32[]{:S(2)}, u32[]{:S(2)}) collective-permute-start(bf16[128,512]{1,0:T(8,128)(2,1)S(1)} %get-tuple-element.62.refs_0_.refs_4_), channel_id=1, source_target_pairs={{0,17},{1,16},{16,1},{17,0},{2,19},{3,18},{18,3},{19,2},{4,21},{5,... | collective-permute-start | bytes 393224 | tf_op jit(solution)/shard_map/ppermute | solution.py:53
  34.4 1.4 %collective-permute-start.12 = (bf16[128,512]{1,0:T(8,128)(2,1)S(1)}, bf16[128,512]{1,0:T(8,128)(2,1)S(1)}, u32[]{:S(2)}, u32[]{:S(2)}) collective-permute-start(bf16[128,512]{1,0:T(8,128)(2,1)S(1)} %get-tuple-element.62.refs_0_.refs_4_), channel_id=1, source_target_pairs={{0,16},{1,17},{16,0},{17,1},{2,18},{3,19},{18,2},{19,3},{4,20},{5,... | collective-permute-start | bytes 393224 | tf_op jit(solution)/shard_map/ppermute | solution.py:53
  35.8 0.6 collective-permute-start.11
  36.4 0.7 %emit.1 = bf16[128,512]{1,0:T(8,128)(2,1)} custom-call(bf16[128,512]{1,0:T(8,128)(2,1)S(1)} %get-tuple-element.63.held), custom_call_target="tpu_custom_call" | custom-call | bytes 131072 | tf_op jit(solution)/shard_map/emit/pallas_call | solution.py:27
  37.5 2.7 %collective-permute-done.10.refs_0_.refs_7_ = bf16[128,512]{1,0:T(8,128)(2,1)S(1)} collective-permute-done((bf16[128,512]{1,0:T(8,128)(2,1)S(1)}, bf16[128,512]{1,0:T(8,128)(2,1)S(1)}, u32[]{:S(2)}, u32[]{:S(2)}) %collective-permute-start.10) | collective-permute-done | bytes 131104 | tf_op jit(solution)/shard_map/ppermute | solution.py:53
  40.6 1.3 %collective-permute-done.12.refs_1_.refs_6_ = bf16[128,512]{1,0:T(8,128)(2,1)S(1)} collective-permute-done((bf16[128,512]{1,0:T(8,128)(2,1)S(1)}, bf16[128,512]{1,0:T(8,128)(2,1)S(1)}, u32[]{:S(2)}, u32[]{:S(2)}) %collective-permute-start.12) | collective-permute-done | bytes 131104 | tf_op jit(solution)/shard_map/ppermute | solution.py:53
  42.0 0.7 %terms.1 = (f32[4,128,512]{2,1,0:T(8,128)S(1)}, bf16[256,512]{1,0:T(8,128)(2,1)S(1)}, bf16[256,512]{1,0:T(8,128)(2,1)S(1)}) custom-call(bf16[128,1024]{1,0:T(8,128)(2,1)S(1)} %get-tuple-element.53.refs_0_, bf16[128,1024]{1,0:T(8,128)(2,1)S(1)} %collective-permute-done.2.refs_1_, bf16[128,1024]{1,0:T(8,128)(2,1)S(1)} %collective-permute-done.1.refs_2_, ...), custom_call_target="tpu_custom_call" | custom-call | tf_op jit(solution)/shard_map/terms/pallas_call | solution.py:27
  43.8 1.3 %collective-permute-start.13 = (bf16[128,1024]{1,0:T(8,128)(2,1)S(1)}, bf16[128,1024]{1,0:T(8,128)(2,1)S(1)}, u32[]{:S(2)}, u32[]{:S(2)}) collective-permute-start(bf16[128,1024]{1,0:T(8,128)(2,1)S(1)} %get-tuple-element.68), channel_id=1, source_target_pairs={{0,16},{1,17},{16,0},{17,1},{2,18},{3,19},{18,2},{19,3},{4,20},{5,... | collective-permute-start | bytes 786440 | tf_op jit(solution)/shard_map/ppermute | solution.py:53
  45.1 0.6 collective-permute-start.20
  45.8 1.1 %collective-permute-start.17 = (bf16[128,512]{1,0:T(8,128)(2,1)S(1)}, bf16[128,512]{1,0:T(8,128)(2,1)S(1)}, u32[]{:S(2)}, u32[]{:S(2)}) collective-permute-start(bf16[128,512]{1,0:T(8,128)(2,1)S(1)} %get-tuple-element.73), channel_id=1, source_target_pairs={{0,6},{2,0},{4,2},{6,4},{1,7},{3,1},{5,3},{7,5},{8,14},{10,8},{12,... | collective-permute-start | bytes 393224 | tf_op jit(solution)/shard_map/ppermute | solution.py:41
  46.8 1.7 %collective-permute-start.18 = (bf16[128,512]{1,0:T(8,128)(2,1)S(1)}, bf16[128,512]{1,0:T(8,128)(2,1)S(1)}, u32[]{:S(2)}, u32[]{:S(2)}) collective-permute-start(bf16[128,512]{1,0:T(8,128)(2,1)S(1)} %get-tuple-element.74), channel_id=1, source_target_pairs={{0,4},{2,6},{4,0},{6,2},{1,5},{3,7},{5,1},{7,3},{8,12},{10,14},{12... | collective-permute-start | bytes 393224 | tf_op jit(solution)/shard_map/ppermute | solution.py:41
  48.5 1.9 %collective-permute-start.19 = (bf16[128,512]{1,0:T(8,128)(2,1)S(1)}, bf16[128,512]{1,0:T(8,128)(2,1)S(1)}, u32[]{:S(2)}, u32[]{:S(2)}) collective-permute-start(bf16[128,512]{1,0:T(8,128)(2,1)S(1)} %get-tuple-element.75), channel_id=1, source_target_pairs={{0,2},{2,4},{4,6},{6,0},{1,3},{3,5},{5,7},{7,1},{8,10},{10,12},{12... | collective-permute-start | bytes 393224 | tf_op jit(solution)/shard_map/ppermute | solution.py:41
  50.4 1.7 %collective-permute-done.13.refs_2_ = bf16[128,1024]{1,0:T(8,128)(2,1)S(1)} collective-permute-done((bf16[128,1024]{1,0:T(8,128)(2,1)S(1)}, bf16[128,1024]{1,0:T(8,128)(2,1)S(1)}, u32[]{:S(2)}, u32[]{:S(2)}) %collective-permute-start.13) | collective-permute-done | bytes 262176 | tf_op jit(solution)/shard_map/ppermute | solution.py:53
  52.1 1.3 %collective-permute-start.16 = (bf16[128,1024]{1,0:T(8,128)(2,1)S(1)}, bf16[128,1024]{1,0:T(8,128)(2,1)S(1)}, u32[]{:S(2)}, u32[]{:S(2)}) collective-permute-start(bf16[128,1024]{1,0:T(8,128)(2,1)S(1)} %columns.4), channel_id=1, source_target_pairs={{0,17},{1,16},{16,1},{17,0},{2,19},{3,18},{18,3},{19,2},{4,21},{5,... | collective-permute-start | bytes 786440 | tf_op jit(solution)/shard_map/ppermute | solution.py:53
  53.4 1.1 %unpack.2.refs_1_ = bf16[128,4096]{1,0:T(8,128)(2,1)} custom-call(bf16[128,1024]{1,0:T(8,128)(2,1)S(1)} %columns.3.refs_0_, bf16[128,1024]{1,0:T(8,128)(2,1)S(1)} %collective-permute-done.20.refs_1_, bf16[128,1024]{1,0:T(8,128)(2,1)S(1)} %collective-permute-done.13.refs_2_), custom_call_target="tpu_custom_call" | custom-call | tf_op jit(solution)/shard_map/unpack/pallas_call | solution.py:106
  54.5 5.5 %collective-permute-done.18.refs_2_ = bf16[128,512]{1,0:T(8,128)(2,1)S(1)} collective-permute-done((bf16[128,512]{1,0:T(8,128)(2,1)S(1)}, bf16[128,512]{1,0:T(8,128)(2,1)S(1)}, u32[]{:S(2)}, u32[]{:S(2)}) %collective-permute-start.18) | collective-permute-done | bytes 131104 | tf_op jit(solution)/shard_map/ppermute | solution.py:41
  60.0 0.8 %final_sum.1 = f32[128,512]{1,0:T(8,128)} custom-call(f32[128,512]{1,0:T(8,128)S(1)} %get-tuple-element.80.refs_0_, bf16[128,512]{1,0:T(8,128)(2,1)S(1)} %collective-permute-done.17.refs_1_, bf16[128,512]{1,0:T(8,128)(2,1)S(1)} %collective-permute-done.18.refs_2_, bf16[128,512]{1,0:T(8,128)(2,1)S(1)} %collective-permute-done.19.refs_3_), custom_call_target="tpu_custom_call" | custom-call | flops 3221225472 | bytes 655360 | tf_op jit(solution)/shard_map/final_sum/pallas_call | solution.py:27
  60.8 0.8 %unpack.3 = bf16[128,4096]{1,0:T(8,128)(2,1)} custom-call(bf16[128,1024]{1,0:T(8,128)(2,1)S(1)} %collective-permute-done.16.refs_0_, bf16[128,4096]{1,0:T(8,128)(2,1)} %unpack.2.refs_1_), custom_call_target="tpu_custom_call", output_to_operand_aliasing={{}: (1, {})} | custom-call | tf_op jit(solution)/shard_map/unpack/pallas_call | solution.py:106
  (30 shorter events, 4.9 us)
Async XLA Ops:
  1.6 15.6 %collective-permute-start.3 = (bf16[256,512]{1,0:T(8,128)(2,1)S(1)}, bf16[256,512]{1,0:T(8,128)(2,1)S(1)}, u32[]{:S(2)}, u32[]{:S(2)}) collective-permute-start(bf16[256,512]{1,0:T(8,128)(2,1)S(1)} %get-tuple-element.49.refs_0_), channel_id=1, source_target_pairs={{0,2},{2,4},{4,6},{6,0},{8,14},{10,8},{12,10},{14,12},{1,3},{3,5},... | collective-permute-start | bytes 786440 | tf_op jit(solution)/shard_map/ppermute | solution.py:138
  4.7 12.5 %collective-permute-start.4 = (bf16[128,512]{1,0:T(8,128)(2,1)S(1)}, bf16[128,512]{1,0:T(8,128)(2,1)S(1)}, u32[]{:S(2)}, u32[]{:S(2)}) collective-permute-start(bf16[128,512]{1,0:T(8,128)(2,1)S(1)} %get-tuple-element.50), channel_id=1, source_target_pairs={{0,4},{2,6},{4,0},{6,2},{1,5},{3,7},{5,1},{7,3},{8,12},{10,14},{12... | collective-permute-start | bytes 393224 | tf_op jit(solution)/shard_map/ppermute | solution.py:41
  7.3 1.2 %copy-start = (bf16[128,4096]{1,0:T(8,128)(2,1)S(1)}, bf16[128,4096]{1,0:T(8,128)(2,1)}, u32[]{:S(2)}) copy-start(bf16[128,4096]{1,0:T(8,128)(2,1)} %tokens.1) | copy-start | bytes 3145732
  8.8 10.3 %collective-permute-start = (bf16[128,1024]{1,0:T(8,128)(2,1)S(1)}, bf16[128,1024]{1,0:T(8,128)(2,1)S(1)}, u32[]{:S(2)}, u32[]{:S(2)}) collective-permute-start(bf16[128,1024]{1,0:T(8,128)(2,1)S(1)} %get-tuple-element.45), channel_id=1, source_target_pairs={{0,17},{1,16},{16,1},{17,0},{2,19},{3,18},{18,3},{19,2},{4,21},{5,... | collective-permute-start | bytes 786440 | tf_op jit(solution)/shard_map/ppermute | solution.py:53
  11.3 11.4 %collective-permute-start.1 = (bf16[128,1024]{1,0:T(8,128)(2,1)S(1)}, bf16[128,1024]{1,0:T(8,128)(2,1)S(1)}, u32[]{:S(2)}, u32[]{:S(2)}) collective-permute-start(bf16[128,1024]{1,0:T(8,128)(2,1)S(1)} %get-tuple-element.46), channel_id=1, source_target_pairs={{0,16},{1,17},{16,0},{17,1},{2,18},{3,19},{18,2},{19,3},{4,20},{5,... | collective-permute-start | bytes 786440 | tf_op jit(solution)/shard_map/ppermute | solution.py:53
  11.9 10.8 %collective-permute-start.2 = (bf16[128,1024]{1,0:T(8,128)(2,1)S(1)}, bf16[128,1024]{1,0:T(8,128)(2,1)S(1)}, u32[]{:S(2)}, u32[]{:S(2)}) collective-permute-start(bf16[128,1024]{1,0:T(8,128)(2,1)S(1)} %get-tuple-element.47), channel_id=1, source_target_pairs={{0,1},{1,0},{16,17},{17,16},{2,3},{3,2},{18,19},{19,18},{4,5},{5,4... | collective-permute-start | bytes 786440 | tf_op jit(solution)/shard_map/ppermute | solution.py:53
  17.2 5.5 %collective-permute-start.5 = (bf16[192,512]{1,0:T(8,128)(2,1)S(1)}, bf16[192,512]{1,0:T(8,128)(2,1)S(1)}, u32[]{:S(2)}, u32[]{:S(2)}) collective-permute-start(bf16[192,512]{1,0:T(8,128)(2,1)S(1)} %get-tuple-element.51), channel_id=1, source_target_pairs={{0,8},{8,0},{1,9},{9,1},{2,10},{10,2},{3,11},{11,3},{4,12},{12,4},... | collective-permute-start | bytes 589832 | tf_op jit(solution)/shard_map/ppermute | solution.py:45
  18.0 4.7 %collective-permute-start.6 = (bf16[192,512]{1,0:T(8,128)(2,1)S(1)}, bf16[192,512]{1,0:T(8,128)(2,1)S(1)}, u32[]{:S(2)}, u32[]{:S(2)}) collective-permute-start(bf16[192,512]{1,0:T(8,128)(2,1)S(1)} %get-tuple-element.52), channel_id=1, source_target_pairs={{0,8},{8,0},{1,9},{9,1},{2,10},{10,2},{3,11},{11,3},{4,12},{12,4},... | collective-permute-start | bytes 589832 | tf_op jit(solution)/shard_map/ppermute | solution.py:45
  23.4 6.3 %collective-permute-start.7 = (bf16[128,512]{1,0:T(8,128)(2,1)S(1)}, bf16[128,512]{1,0:T(8,128)(2,1)S(1)}, u32[]{:S(2)}, u32[]{:S(2)}) collective-permute-start(bf16[128,512]{1,0:T(8,128)(2,1)S(1)} %get-tuple-element.59), channel_id=1, source_target_pairs={{0,17},{1,16},{16,1},{17,0},{2,19},{3,18},{18,3},{19,2},{4,21},{5,... | collective-permute-start | bytes 393224 | tf_op jit(solution)/shard_map/ppermute | solution.py:53
  25.8 6.5 %collective-permute-start.8 = (bf16[128,512]{1,0:T(8,128)(2,1)S(1)}, bf16[128,512]{1,0:T(8,128)(2,1)S(1)}, u32[]{:S(2)}, u32[]{:S(2)}) collective-permute-start(bf16[128,512]{1,0:T(8,128)(2,1)S(1)} %get-tuple-element.60), channel_id=1, source_target_pairs={{0,1},{1,0},{16,17},{17,16},{2,3},{3,2},{18,19},{19,18},{4,5},{5,4... | collective-permute-start | bytes 393224 | tf_op jit(solution)/shard_map/ppermute | solution.py:53
  26.4 6.2 %copy-start.1 = (bf16[128,512]{1,0:T(8,128)(2,1)S(1)}, bf16[128,512]{1,0:T(8,128)(2,1)}, u32[]{:S(2)}) copy-start(bf16[128,512]{1,0:T(8,128)(2,1)} %refs_4_.1) | copy-start | bytes 393220
  26.4 6.1 %collective-permute-start.9 = (bf16[128,512]{1,0:T(8,128)(2,1)S(1)}, bf16[128,512]{1,0:T(8,128)(2,1)S(1)}, u32[]{:S(2)}, u32[]{:S(2)}) collective-permute-start(bf16[128,512]{1,0:T(8,128)(2,1)S(1)} %get-tuple-element.61), channel_id=1, source_target_pairs={{0,16},{1,17},{16,0},{17,1},{2,18},{3,19},{18,2},{19,3},{4,20},{5,... | collective-permute-start | bytes 393224 | tf_op jit(solution)/shard_map/ppermute | solution.py:53
  32.8 7.4 %collective-permute-start.10 = (bf16[128,512]{1,0:T(8,128)(2,1)S(1)}, bf16[128,512]{1,0:T(8,128)(2,1)S(1)}, u32[]{:S(2)}, u32[]{:S(2)}) collective-permute-start(bf16[128,512]{1,0:T(8,128)(2,1)S(1)} %get-tuple-element.62.refs_0_.refs_4_), channel_id=1, source_target_pairs={{0,17},{1,16},{16,1},{17,0},{2,19},{3,18},{18,3},{19,2},{4,21},{5,... | collective-permute-start | bytes 393224 | tf_op jit(solution)/shard_map/ppermute | solution.py:53
  34.4 7.6 %collective-permute-start.12 = (bf16[128,512]{1,0:T(8,128)(2,1)S(1)}, bf16[128,512]{1,0:T(8,128)(2,1)S(1)}, u32[]{:S(2)}, u32[]{:S(2)}) collective-permute-start(bf16[128,512]{1,0:T(8,128)(2,1)S(1)} %get-tuple-element.62.refs_0_.refs_4_), channel_id=1, source_target_pairs={{0,16},{1,17},{16,0},{17,1},{2,18},{3,19},{18,2},{19,3},{4,20},{5,... | collective-permute-start | bytes 393224 | tf_op jit(solution)/shard_map/ppermute | solution.py:53
  35.8 6.2 %collective-permute-start.11 = (bf16[128,512]{1,0:T(8,128)(2,1)S(1)}, bf16[128,512]{1,0:T(8,128)(2,1)S(1)}, u32[]{:S(2)}, u32[]{:S(2)}) collective-permute-start(bf16[128,512]{1,0:T(8,128)(2,1)S(1)} %get-tuple-element.62.refs_0_.refs_4_), channel_id=1, source_target_pairs={{0,1},{1,0},{16,17},{17,16},{2,3},{3,2},{18,19},{19,18},{4,5},{5,4... | collective-permute-start | bytes 393224 | tf_op jit(solution)/shard_map/ppermute | solution.py:53
  42.7 2.9 %collective-permute-start.14 = (bf16[256,512]{1,0:T(8,128)(2,1)S(1)}, bf16[256,512]{1,0:T(8,128)(2,1)S(1)}, u32[]{:S(2)}, u32[]{:S(2)}) collective-permute-start(bf16[256,512]{1,0:T(8,128)(2,1)S(1)} %get-tuple-element.70), channel_id=1, source_target_pairs={{0,8},{8,0},{1,9},{9,1},{2,10},{10,2},{3,11},{11,3},{4,12},{12,4},... | collective-permute-start | bytes 786440 | tf_op jit(solution)/shard_map/ppermute | solution.py:45
  42.8 2.9 %collective-permute-start.15 = (bf16[256,512]{1,0:T(8,128)(2,1)S(1)}, bf16[256,512]{1,0:T(8,128)(2,1)S(1)}, u32[]{:S(2)}, u32[]{:S(2)}) collective-permute-start(bf16[256,512]{1,0:T(8,128)(2,1)S(1)} %get-tuple-element.71), channel_id=1, source_target_pairs={{0,8},{8,0},{1,9},{9,1},{2,10},{10,2},{3,11},{11,3},{4,12},{12,4},... | collective-permute-start | bytes 786440 | tf_op jit(solution)/shard_map/ppermute | solution.py:45
  43.8 8.4 %collective-permute-start.13 = (bf16[128,1024]{1,0:T(8,128)(2,1)S(1)}, bf16[128,1024]{1,0:T(8,128)(2,1)S(1)}, u32[]{:S(2)}, u32[]{:S(2)}) collective-permute-start(bf16[128,1024]{1,0:T(8,128)(2,1)S(1)} %get-tuple-element.68), channel_id=1, source_target_pairs={{0,16},{1,17},{16,0},{17,1},{2,18},{3,19},{18,2},{19,3},{4,20},{5,... | collective-permute-start | bytes 786440 | tf_op jit(solution)/shard_map/ppermute | solution.py:53
  45.1 8.3 %collective-permute-start.20 = (bf16[128,1024]{1,0:T(8,128)(2,1)S(1)}, bf16[128,1024]{1,0:T(8,128)(2,1)S(1)}, u32[]{:S(2)}, u32[]{:S(2)}) collective-permute-start(bf16[128,1024]{1,0:T(8,128)(2,1)S(1)} %get-tuple-element.78), channel_id=1, source_target_pairs={{0,1},{1,0},{16,17},{17,16},{2,3},{3,2},{18,19},{19,18},{4,5},{5,4... | collective-permute-start | bytes 786440 | tf_op jit(solution)/shard_map/ppermute | solution.py:53
  45.8 8.7 %collective-permute-start.17 = (bf16[128,512]{1,0:T(8,128)(2,1)S(1)}, bf16[128,512]{1,0:T(8,128)(2,1)S(1)}, u32[]{:S(2)}, u32[]{:S(2)}) collective-permute-start(bf16[128,512]{1,0:T(8,128)(2,1)S(1)} %get-tuple-element.73), channel_id=1, source_target_pairs={{0,6},{2,0},{4,2},{6,4},{1,7},{3,1},{5,3},{7,5},{8,14},{10,8},{12,... | collective-permute-start | bytes 393224 | tf_op jit(solution)/shard_map/ppermute | solution.py:41
  46.8 13.2 %collective-permute-start.18 = (bf16[128,512]{1,0:T(8,128)(2,1)S(1)}, bf16[128,512]{1,0:T(8,128)(2,1)S(1)}, u32[]{:S(2)}, u32[]{:S(2)}) collective-permute-start(bf16[128,512]{1,0:T(8,128)(2,1)S(1)} %get-tuple-element.74), channel_id=1, source_target_pairs={{0,4},{2,6},{4,0},{6,2},{1,5},{3,7},{5,1},{7,3},{8,12},{10,14},{12... | collective-permute-start | bytes 393224 | tf_op jit(solution)/shard_map/ppermute | solution.py:41
  48.5 11.5 %collective-permute-start.19 = (bf16[128,512]{1,0:T(8,128)(2,1)S(1)}, bf16[128,512]{1,0:T(8,128)(2,1)S(1)}, u32[]{:S(2)}, u32[]{:S(2)}) collective-permute-start(bf16[128,512]{1,0:T(8,128)(2,1)S(1)} %get-tuple-element.75), channel_id=1, source_target_pairs={{0,2},{2,4},{4,6},{6,0},{1,3},{3,5},{5,7},{7,1},{8,10},{10,12},{12... | collective-permute-start | bytes 393224 | tf_op jit(solution)/shard_map/ppermute | solution.py:41
  52.1 8.7 %collective-permute-start.16 = (bf16[128,1024]{1,0:T(8,128)(2,1)S(1)}, bf16[128,1024]{1,0:T(8,128)(2,1)S(1)}, u32[]{:S(2)}, u32[]{:S(2)}) collective-permute-start(bf16[128,1024]{1,0:T(8,128)(2,1)S(1)} %columns.4), channel_id=1, source_target_pairs={{0,17},{1,16},{16,1},{17,0},{2,19},{3,18},{18,3},{19,2},{4,21},{5,... | collective-permute-start | bytes 786440 | tf_op jit(solution)/shard_map/ppermute | solution.py:53

commit v13 on v12

--- a/solution.py
+++ b/solution.py
@@ -36,9 +36,8 @@
     )(*args)
 
 
-def rotated(block, axis, step):
-    size = lax.axis_size(axis)
-    return lax.ppermute(block, axis, [(i, (i + step) % size) for i in range(size)])
+def along(block, step):
+    return lax.ppermute(block, "line", [(i, i ^ step) for i in range(lax.axis_size("line"))])
 
 
 def to_twin(block):
@@ -54,9 +53,9 @@
 
 
 def run_of(part, far):
-    line, core = lax.axis_size("line"), lax.axis_index("twin")
+    core = lax.axis_index("twin")
     over, across = flips(far)
-    place = lax.rem(lax.axis_index("line") + line - part // TWIN, line)
+    place = lax.axis_index("line") ^ (part // TWIN)
     side, pair = lax.axis_index("side") ^ over, lax.axis_index("pair") ^ across
     return ((place * SPLIT + pair) * SPLIT + side) * TWIN + (core ^ (part % TWIN))
 
@@ -83,16 +82,15 @@
             block[:, part * run : (part + 1) * run] = tokens[:, pl.ds(start, run)]
 
 
-def unpack_body(fars, *refs):
-    blocks = refs[: len(fars)]
-    whole, done = refs[-2:]
+def unpack_moves(far, block, whole):
     parts = lax.axis_size("line") * TWIN
-    run = blocks[0].shape[1] // parts
-    moves = []
-    for far, block in zip(fars, blocks):
-        for part in range(parts):
-            start = pl.multiple_of(run_of(part, far) * run, run)
-            moves.append((block.at[:, pl.ds(part * run, run)], whole.at[:, pl.ds(start, run)]))
+    run = block.shape[1] // parts
+    for part in range(parts):
+        start = pl.multiple_of(run_of(part, far) * run, run)
+        yield block.at[:, pl.ds(part * run, run)], whole.at[:, pl.ds(start, run)]
+
+
+def run_copies(moves, done):
     copies = [pltpu.make_async_copy(*move, done.at[i]) for i, move in enumerate(moves)]
     for copy in copies:
         copy.start()
@@ -100,17 +98,26 @@
         copy.wait()
 
 
-def unpack(fars, blocks, shape, whole=None):
-    vmem, hbm = pl.BlockSpec(memory_space=pltpu.VMEM), pl.BlockSpec(memory_space=pl.ANY)
-    held = [] if whole is None else [whole]
+def unpack_body(*refs):
+    *blocks, whole, done = refs
+    run_copies([move for far, block in enumerate(blocks) for move in unpack_moves(far, block, whole)], done)
+
+
+def finish_body(block, total, _, whole, weight_grad, done):
+    run_copies([(total, weight_grad), *unpack_moves(MEMBERS - 1, block, whole)], done)
+
+
+def placing_call(name, body, out_shapes, blocks, held=()):
+    parts = lax.axis_size("line") * TWIN
     return pl.pallas_call(
-        functools.partial(unpack_body, fars),
-        name="unpack",
-        out_shape=shape,
-        in_specs=[vmem] * len(blocks) + [hbm] * len(held),
-        out_specs=hbm,
+        body,
+        name=name,
+        out_shape=out_shapes,
+        in_specs=[pl.BlockSpec(memory_space=pltpu.VMEM)] * len(blocks)
+        + [pl.BlockSpec(memory_space=pl.ANY)] * len(held),
+        out_specs=[pl.BlockSpec(memory_space=pl.ANY)] * len(out_shapes),
         input_output_aliases={len(blocks): 0} if held else {},
-        scratch_shapes=[pltpu.SemaphoreType.DMA((len(blocks) * lax.axis_size("line") * TWIN,))],
+        scratch_shapes=[pltpu.SemaphoreType.DMA((len(blocks) * parts,))],
         compiler_params=pltpu.CompilerParams(vmem_limit_bytes=32 << 20),
         cost_estimate=pl.CostEstimate(flops=0, bytes_accessed=0, transcendentals=0),
     )(*blocks, *held)
@@ -134,7 +141,7 @@
 
 def parted(block, step):
     line = lax.axis_size("line")
-    to = [core * line + (i + (line - step if core else step)) % line for core in range(TWIN) for i in range(line)]
+    to = [core * line + (i ^ (line - step if core else step)) for core in range(TWIN) for i in range(line)]
     return lax.ppermute(block, ("twin", "line"), list(enumerate(to)))
 
 
@@ -238,7 +245,7 @@
         if step == 0:
             own[...] = piece
         else:
-            leaving[step - 1][...] = piece.astype(bf16)
+            leaving[-step][...] = piece.astype(bf16)
 
 
 def sum_body(*refs):
@@ -276,7 +283,7 @@
         blocks[far] = to_member(packed[far], far)
     passed = [parted(both, step) for step in range(1, (line + 1) // 2)]
     if line % 2 == 0:
-        passed.append(rotated(mine, "line", line // 2))
+        passed.append(along(mine, line // 2))
     pieces = [both]
     reach = shard_rows // SPLIT * (line - 1) // TWIN
     relayed = local_call(
@@ -338,17 +345,19 @@
         moved=0,
     )
 
-    met = [sums[0]] + [rotated(sums[step], "line", -step) for step in range(1, line)]
+    met = [sums[0]] + [along(sums[line - step], step) for step in range(line - 1, 0, -1)]
     back_1, back_2 = (to_member(column, far) for far, column in zip((1, 2), columns(grad_1, grad_2)))
     column_3, back_2, _ = lax.optimization_barrier((column_3, back_2, sums))
     back_3 = to_member(column_3, 3)
-    input_grad = unpack((0, 1, 2), (column_0, back_1, back_2), shape((tok_rows, width), bf16))
+    whole_shape = shape((tok_rows, width), bf16)
+    (input_grad,) = placing_call("unpack", unpack_body, [whole_shape], (column_0, back_1, back_2))
     met, input_grad = lax.optimization_barrier((met, input_grad))
-    weight_grad = local_call("final_sum", sum_body, shape((rows, key_cols), f32), *met, flops=24 * flops)
-    back_3, weight_grad = lax.optimization_barrier((back_3, weight_grad))
+    total = local_call("final_sum", sum_body, shape((rows, key_cols), f32), *met, flops=24 * flops)
+    input_grad, weight_grad = placing_call(
+        "finish", finish_body, [whole_shape, shape(total.shape, f32)], (back_3, total), (input_grad,)
+    )
     if outer > 1:
         weight_grad = lax.psum_scatter(weight_grad, "outer", scatter_dimension=0, tiled=True)
-    input_grad = unpack((3,), (back_3,), shape((tok_rows, width), bf16), input_grad)
     if outer > 1:
         input_grad = join_runs(input_grad, outer)
     return (key_out, input_grad, weight_grad)

time: 61.7 us -> 61.6 us (level)
  starting transfers between devices: 25.6 us -> 26.4 us
    ppermute x4, starting transfers between devices: 1.44 us -> 2.47 us  [to_twin(): return lax.ppermute(block, 'twin', [(0, 1), (1, 0)])]
    ppermute x4, waiting for transfers between devices: 10.4 us -> 9.36 us  [along(): lax.ppermute(block, 'line', [(i, i ^ step) for i in range(lax.axis_size('...]
    pallas_call x14, Pallas kernels: 6.17 us -> 5.46 us  [local_call(): pl.pallas_call(body, name=name, out_shape=out_shapes, in_specs=[pl.BlockS...]
  transfers between devices with their start and end apart: 21 -> 21, of which waited for: 10 -> 11; matrix products, arithmetic and copies ran while one was open for 0% -> 0% of each run, Pallas kernels for 7% -> 6%
where the time goes in v13:
time: 61.6 us; the launch traced here: 61.4 us
  starting transfers between devices  26.4 us (43%)
  waiting for transfers between devices  25.6 us (42%)
  Pallas kernels  7.45 us (12%)
  local copies, waits for them, and re-layouts  1.23 us (2%)
  between operations  0.77 us (1%)
    ppermute x12, waiting for transfers between devices, to_member(): lax.ppermute(block, ('side', 'pair'), [(i, i ^ far) for i in range(MEMBER...  16.2 us
    ppermute x12, starting transfers between devices, to_member(): lax.ppermute(block, ('side', 'pair'), [(i, i ^ far) for i in range(MEMBER...  13.8 us
    ppermute x4, waiting for transfers between devices, along(): lax.ppermute(block, 'line', [(i, i ^ step) for i in range(lax.axis_size('...  9.36 us
    ppermute x4, starting transfers between devices, along(): lax.ppermute(block, 'line', [(i, i ^ step) for i in range(lax.axis_size('...  7.04 us
    pallas_call x14, Pallas kernels, local_call(): pl.pallas_call(body, name=name, out_shape=out_shapes, in_specs=[pl.BlockS...  5.46 us
    ppermute x1, starting transfers between devices, parted(): return lax.ppermute(block, ('twin', 'line'), list(enumerate(to)))  3.09 us
    ppermute x4, starting transfers between devices, to_twin(): return lax.ppermute(block, 'twin', [(0, 1), (1, 0)])  2.47 us
    pallas_call x2, Pallas kernels, placing_call(): pl.pallas_call(body, name=name, out_shape=out_shapes, in_specs=[pl.BlockS...  1.99 us
  transfers between devices with their start and end apart: 21, of which 11 were waited for; matrix products, arithmetic and copies ran while one was open for 0% of the time, Pallas kernels for 6%

profile of v13, /device:TPU:0, one launch (start us, length us, event | category | flops | bytes accessed | tf_op | source)
XLA Modules:
  0.0 61.4 jit_solution(10251672155539039621)
XLA Ops:
  0.6 1.0 %front.1 = (bf16[256,512]{1,0:T(8,128)(2,1)S(1)}, bf16[128,512]{1,0:T(8,128)(2,1)S(1)}) custom-call(bf16[512,512]{1,0:T(8,128)(2,1)} %shard.1), custom_call_target="tpu_custom_call" | custom-call | bytes 524288 | tf_op jit(solution)/shard_map/front/pallas_call | solution.py:27
  1.6 3.1 %collective-permute-start.3 = (bf16[256,512]{1,0:T(8,128)(2,1)S(1)}, bf16[256,512]{1,0:T(8,128)(2,1)S(1)}, u32[]{:S(2)}, u32[]{:S(2)}) collective-permute-start(bf16[256,512]{1,0:T(8,128)(2,1)S(1)} %get-tuple-element.49.refs_0_), channel_id=1, source_target_pairs={{0,2},{2,0},{4,6},{6,4},{8,14},{10,12},{12,10},{14,8},{1,3},{3,1},... | collective-permute-start | bytes 786440 | tf_op jit(solution)/shard_map/ppermute | solution.py:145
  4.7 2.6 %collective-permute-start.4 = (bf16[128,512]{1,0:T(8,128)(2,1)S(1)}, bf16[128,512]{1,0:T(8,128)(2,1)S(1)}, u32[]{:S(2)}, u32[]{:S(2)}) collective-permute-start(bf16[128,512]{1,0:T(8,128)(2,1)S(1)} %get-tuple-element.50), channel_id=1, source_target_pairs={{0,4},{2,6},{4,0},{6,2},{1,5},{3,7},{5,1},{7,3},{8,12},{10,14},{12... | collective-permute-start | bytes 393224 | tf_op jit(solution)/shard_map/ppermute | solution.py:40
  7.3 1.2 %copy-done = bf16[128,4096]{1,0:T(8,128)(2,1)S(1)} copy-done((bf16[128,4096]{1,0:T(8,128)(2,1)S(1)}, bf16[128,4096]{1,0:T(8,128)(2,1)}, u32[]{:S(2)}) %copy-start) | copy-done | bytes 1048600
  8.8 2.5 %collective-permute-start = (bf16[128,1024]{1,0:T(8,128)(2,1)S(1)}, bf16[128,1024]{1,0:T(8,128)(2,1)S(1)}, u32[]{:S(2)}, u32[]{:S(2)}) collective-permute-start(bf16[128,1024]{1,0:T(8,128)(2,1)S(1)} %get-tuple-element.45), channel_id=1, source_target_pairs={{0,17},{1,16},{16,1},{17,0},{2,19},{3,18},{18,3},{19,2},{4,21},{5,... | collective-permute-start | bytes 786440 | tf_op jit(solution)/shard_map/ppermute | solution.py:52
  12.4 3.8 %collective-permute-done.4.refs_1_.refs_2_ = bf16[128,512]{1,0:T(8,128)(2,1)S(1)} collective-permute-done((bf16[128,512]{1,0:T(8,128)(2,1)S(1)}, bf16[128,512]{1,0:T(8,128)(2,1)S(1)}, u32[]{:S(2)}, u32[]{:S(2)}) %collective-permute-start.4) | collective-permute-done | bytes 131104 | tf_op jit(solution)/shard_map/ppermute | solution.py:40
  16.2 1.8 %collective-permute-start.5 = (bf16[192,512]{1,0:T(8,128)(2,1)S(1)}, bf16[192,512]{1,0:T(8,128)(2,1)S(1)}, u32[]{:S(2)}, u32[]{:S(2)}) collective-permute-start(bf16[192,512]{1,0:T(8,128)(2,1)S(1)} %get-tuple-element.51), channel_id=1, source_target_pairs={{0,8},{8,0},{1,9},{9,1},{2,10},{10,2},{3,11},{11,3},{4,12},{12,4},... | collective-permute-start | bytes 589832 | tf_op jit(solution)/shard_map/ppermute | solution.py:44
  18.1 1.0 %collective-permute-done.refs_0_.refs_3_ = bf16[128,1024]{1,0:T(8,128)(2,1)S(1)} collective-permute-done((bf16[128,1024]{1,0:T(8,128)(2,1)S(1)}, bf16[128,1024]{1,0:T(8,128)(2,1)S(1)}, u32[]{:S(2)}, u32[]{:S(2)}) %collective-permute-start) | collective-permute-done | bytes 262176 | tf_op jit(solution)/shard_map/ppermute | solution.py:52
  19.1 3.6 %collective-permute-done.1.refs_2_ = bf16[128,1024]{1,0:T(8,128)(2,1)S(1)} collective-permute-done((bf16[128,1024]{1,0:T(8,128)(2,1)S(1)}, bf16[128,1024]{1,0:T(8,128)(2,1)S(1)}, u32[]{:S(2)}, u32[]{:S(2)}) %collective-permute-start.1) | collective-permute-done | bytes 262176 | tf_op jit(solution)/shard_map/ppermute | solution.py:52
  22.8 0.6 share.3
  23.4 2.4 %collective-permute-start.7 = (bf16[128,512]{1,0:T(8,128)(2,1)S(1)}, bf16[128,512]{1,0:T(8,128)(2,1)S(1)}, u32[]{:S(2)}, u32[]{:S(2)}) collective-permute-start(bf16[128,512]{1,0:T(8,128)(2,1)S(1)} %get-tuple-element.59), channel_id=1, source_target_pairs={{0,17},{1,16},{16,1},{17,0},{2,19},{3,18},{18,3},{19,2},{4,21},{5,... | collective-permute-start | bytes 393224 | tf_op jit(solution)/shard_map/ppermute | solution.py:52
  25.8 0.6 %collective-permute-start.8 = (bf16[128,512]{1,0:T(8,128)(2,1)S(1)}, bf16[128,512]{1,0:T(8,128)(2,1)S(1)}, u32[]{:S(2)}, u32[]{:S(2)}) collective-permute-start(bf16[128,512]{1,0:T(8,128)(2,1)S(1)} %get-tuple-element.60), channel_id=1, source_target_pairs={{0,1},{1,0},{16,17},{17,16},{2,3},{3,2},{18,19},{19,18},{4,5},{5,4... | collective-permute-start | bytes 393224 | tf_op jit(solution)/shard_map/ppermute | solution.py:52
  26.4 0.5 collective-permute-start.9
  27.3 2.5 %collective-permute-done.7.refs_1_ = bf16[128,512]{1,0:T(8,128)(2,1)S(1)} collective-permute-done((bf16[128,512]{1,0:T(8,128)(2,1)S(1)}, bf16[128,512]{1,0:T(8,128)(2,1)S(1)}, u32[]{:S(2)}, u32[]{:S(2)}) %collective-permute-start.7) | collective-permute-done | bytes 131104 | tf_op jit(solution)/shard_map/ppermute | solution.py:52
  29.7 2.6 %collective-permute-done.8.refs_2_ = bf16[128,512]{1,0:T(8,128)(2,1)S(1)} collective-permute-done((bf16[128,512]{1,0:T(8,128)(2,1)S(1)}, bf16[128,512]{1,0:T(8,128)(2,1)S(1)}, u32[]{:S(2)}, u32[]{:S(2)}) %collective-permute-start.8) | collective-permute-done | bytes 131104 | tf_op jit(solution)/shard_map/ppermute | solution.py:52
  32.8 1.6 %collective-permute-start.10 = (bf16[128,512]{1,0:T(8,128)(2,1)S(1)}, bf16[128,512]{1,0:T(8,128)(2,1)S(1)}, u32[]{:S(2)}, u32[]{:S(2)}) collective-permute-start(bf16[128,512]{1,0:T(8,128)(2,1)S(1)} %get-tuple-element.62.refs_0_.refs_4_), channel_id=1, source_target_pairs={{0,17},{1,16},{16,1},{17,0},{2,19},{3,18},{18,3},{19,2},{4,21},{5,... | collective-permute-start | bytes 393224 | tf_op jit(solution)/shard_map/ppermute | solution.py:52
  34.4 1.4 %collective-permute-start.12 = (bf16[128,512]{1,0:T(8,128)(2,1)S(1)}, bf16[128,512]{1,0:T(8,128)(2,1)S(1)}, u32[]{:S(2)}, u32[]{:S(2)}) collective-permute-start(bf16[128,512]{1,0:T(8,128)(2,1)S(1)} %get-tuple-element.62.refs_0_.refs_4_), channel_id=1, source_target_pairs={{0,16},{1,17},{16,0},{17,1},{2,18},{3,19},{18,2},{19,3},{4,20},{5,... | collective-permute-start | bytes 393224 | tf_op jit(solution)/shard_map/ppermute | solution.py:52
  35.8 0.6 collective-permute-start.11
  36.4 0.7 %emit.1 = bf16[128,512]{1,0:T(8,128)(2,1)} custom-call(bf16[128,512]{1,0:T(8,128)(2,1)S(1)} %get-tuple-element.63.held), custom_call_target="tpu_custom_call" | custom-call | bytes 131072 | tf_op jit(solution)/shard_map/emit/pallas_call | solution.py:27
  37.5 2.7 %collective-permute-done.10.refs_0_.refs_7_ = bf16[128,512]{1,0:T(8,128)(2,1)S(1)} collective-permute-done((bf16[128,512]{1,0:T(8,128)(2,1)S(1)}, bf16[128,512]{1,0:T(8,128)(2,1)S(1)}, u32[]{:S(2)}, u32[]{:S(2)}) %collective-permute-start.10) | collective-permute-done | bytes 131104 | tf_op jit(solution)/shard_map/ppermute | solution.py:52
  40.7 1.3 %collective-permute-done.12.refs_1_.refs_6_ = bf16[128,512]{1,0:T(8,128)(2,1)S(1)} collective-permute-done((bf16[128,512]{1,0:T(8,128)(2,1)S(1)}, bf16[128,512]{1,0:T(8,128)(2,1)S(1)}, u32[]{:S(2)}, u32[]{:S(2)}) %collective-permute-start.12) | collective-permute-done | bytes 131104 | tf_op jit(solution)/shard_map/ppermute | solution.py:52
  42.0 0.7 %terms.1 = (f32[4,128,512]{2,1,0:T(8,128)S(1)}, bf16[256,512]{1,0:T(8,128)(2,1)S(1)}, bf16[256,512]{1,0:T(8,128)(2,1)S(1)}) custom-call(bf16[128,1024]{1,0:T(8,128)(2,1)S(1)} %get-tuple-element.53.refs_0_, bf16[128,1024]{1,0:T(8,128)(2,1)S(1)} %collective-permute-done.2.refs_1_, bf16[128,1024]{1,0:T(8,128)(2,1)S(1)} %collective-permute-done.1.refs_2_, ...), custom_call_target="tpu_custom_call" | custom-call | tf_op jit(solution)/shard_map/terms/pallas_call | solution.py:27
  43.8 1.3 %collective-permute-start.13 = (bf16[128,1024]{1,0:T(8,128)(2,1)S(1)}, bf16[128,1024]{1,0:T(8,128)(2,1)S(1)}, u32[]{:S(2)}, u32[]{:S(2)}) collective-permute-start(bf16[128,1024]{1,0:T(8,128)(2,1)S(1)} %get-tuple-element.68), channel_id=1, source_target_pairs={{0,16},{1,17},{16,0},{17,1},{2,18},{3,19},{18,2},{19,3},{4,20},{5,... | collective-permute-start | bytes 786440 | tf_op jit(solution)/shard_map/ppermute | solution.py:52
  45.1 0.6 collective-permute-start.20
  45.8 1.9 %collective-permute-start.17 = (bf16[128,512]{1,0:T(8,128)(2,1)S(1)}, bf16[128,512]{1,0:T(8,128)(2,1)S(1)}, u32[]{:S(2)}, u32[]{:S(2)}) collective-permute-start(bf16[128,512]{1,0:T(8,128)(2,1)S(1)} %get-tuple-element.73), channel_id=1, source_target_pairs={{0,6},{2,4},{4,2},{6,0},{1,7},{3,5},{5,3},{7,1},{8,14},{10,12},{12... | collective-permute-start | bytes 393224 | tf_op jit(solution)/shard_map/ppermute | solution.py:40
  47.6 0.9 %collective-permute-start.18 = (bf16[128,512]{1,0:T(8,128)(2,1)S(1)}, bf16[128,512]{1,0:T(8,128)(2,1)S(1)}, u32[]{:S(2)}, u32[]{:S(2)}) collective-permute-start(bf16[128,512]{1,0:T(8,128)(2,1)S(1)} %get-tuple-element.74), channel_id=1, source_target_pairs={{0,4},{2,6},{4,0},{6,2},{1,5},{3,7},{5,1},{7,3},{8,12},{10,14},{12... | collective-permute-start | bytes 393224 | tf_op jit(solution)/shard_map/ppermute | solution.py:40
  48.5 1.7 %collective-permute-start.19 = (bf16[128,512]{1,0:T(8,128)(2,1)S(1)}, bf16[128,512]{1,0:T(8,128)(2,1)S(1)}, u32[]{:S(2)}, u32[]{:S(2)}) collective-permute-start(bf16[128,512]{1,0:T(8,128)(2,1)S(1)} %get-tuple-element.75), channel_id=1, source_target_pairs={{0,2},{2,0},{4,6},{6,4},{1,3},{3,1},{5,7},{7,5},{8,10},{10,8},{12,... | collective-permute-start | bytes 393224 | tf_op jit(solution)/shard_map/ppermute | solution.py:40
  50.2 1.9 %collective-permute-done.13.refs_2_ = bf16[128,1024]{1,0:T(8,128)(2,1)S(1)} collective-permute-done((bf16[128,1024]{1,0:T(8,128)(2,1)S(1)}, bf16[128,1024]{1,0:T(8,128)(2,1)S(1)}, u32[]{:S(2)}, u32[]{:S(2)}) %collective-permute-start.13) | collective-permute-done | bytes 262176 | tf_op jit(solution)/shard_map/ppermute | solution.py:52
  52.1 1.3 %collective-permute-start.16 = (bf16[128,1024]{1,0:T(8,128)(2,1)S(1)}, bf16[128,1024]{1,0:T(8,128)(2,1)S(1)}, u32[]{:S(2)}, u32[]{:S(2)}) collective-permute-start(bf16[128,1024]{1,0:T(8,128)(2,1)S(1)} %columns.4), channel_id=1, source_target_pairs={{0,17},{1,16},{16,1},{17,0},{2,19},{3,18},{18,3},{19,2},{4,21},{5,... | collective-permute-start | bytes 786440 | tf_op jit(solution)/shard_map/ppermute | solution.py:52
  53.4 1.1 %unpack.1._ = bf16[128,4096]{1,0:T(8,128)(2,1)} custom-call(bf16[128,1024]{1,0:T(8,128)(2,1)S(1)} %columns.3.refs_0_, bf16[128,1024]{1,0:T(8,128)(2,1)S(1)} %collective-permute-done.20.refs_1_, bf16[128,1024]{1,0:T(8,128)(2,1)S(1)} %collective-permute-done.13.refs_2_), custom_call_target="tpu_custom_call" | custom-call | tf_op jit(solution)/shard_map/unpack/pallas_call | solution.py:112
  54.5 5.6 %collective-permute-done.18.refs_2_ = bf16[128,512]{1,0:T(8,128)(2,1)S(1)} collective-permute-done((bf16[128,512]{1,0:T(8,128)(2,1)S(1)}, bf16[128,512]{1,0:T(8,128)(2,1)S(1)}, u32[]{:S(2)}, u32[]{:S(2)}) %collective-permute-start.18) | collective-permute-done | bytes 131104 | tf_op jit(solution)/shard_map/ppermute | solution.py:40
  60.5 0.9 %finish.1 = (bf16[128,4096]{1,0:T(8,128)(2,1)}, f32[128,512]{1,0:T(8,128)}) custom-call(bf16[128,1024]{1,0:T(8,128)(2,1)S(1)} %collective-permute-done.16.block, f32[128,512]{1,0:T(8,128)S(1)} %final_sum.1.total, bf16[128,4096]{1,0:T(8,128)(2,1)} %unpack.1._), custom_call_target="tpu_custom_call", output_to_operand_aliasing={{0}: (2, {})} | custom-call | tf_op jit(solution)/shard_map/finish/pallas_call | solution.py:112
  (30 shorter events, 4.8 us)
Async XLA Ops:
  1.6 14.5 %collective-permute-start.3 = (bf16[256,512]{1,0:T(8,128)(2,1)S(1)}, bf16[256,512]{1,0:T(8,128)(2,1)S(1)}, u32[]{:S(2)}, u32[]{:S(2)}) collective-permute-start(bf16[256,512]{1,0:T(8,128)(2,1)S(1)} %get-tuple-element.49.refs_0_), channel_id=1, source_target_pairs={{0,2},{2,0},{4,6},{6,4},{8,14},{10,12},{12,10},{14,8},{1,3},{3,1},... | collective-permute-start | bytes 786440 | tf_op jit(solution)/shard_map/ppermute | solution.py:145
  4.7 11.5 %collective-permute-start.4 = (bf16[128,512]{1,0:T(8,128)(2,1)S(1)}, bf16[128,512]{1,0:T(8,128)(2,1)S(1)}, u32[]{:S(2)}, u32[]{:S(2)}) collective-permute-start(bf16[128,512]{1,0:T(8,128)(2,1)S(1)} %get-tuple-element.50), channel_id=1, source_target_pairs={{0,4},{2,6},{4,0},{6,2},{1,5},{3,7},{5,1},{7,3},{8,12},{10,14},{12... | collective-permute-start | bytes 393224 | tf_op jit(solution)/shard_map/ppermute | solution.py:40
  7.3 1.2 %copy-start = (bf16[128,4096]{1,0:T(8,128)(2,1)S(1)}, bf16[128,4096]{1,0:T(8,128)(2,1)}, u32[]{:S(2)}) copy-start(bf16[128,4096]{1,0:T(8,128)(2,1)} %tokens.1) | copy-start | bytes 3145732
  8.8 10.3 %collective-permute-start = (bf16[128,1024]{1,0:T(8,128)(2,1)S(1)}, bf16[128,1024]{1,0:T(8,128)(2,1)S(1)}, u32[]{:S(2)}, u32[]{:S(2)}) collective-permute-start(bf16[128,1024]{1,0:T(8,128)(2,1)S(1)} %get-tuple-element.45), channel_id=1, source_target_pairs={{0,17},{1,16},{16,1},{17,0},{2,19},{3,18},{18,3},{19,2},{4,21},{5,... | collective-permute-start | bytes 786440 | tf_op jit(solution)/shard_map/ppermute | solution.py:52
  11.4 11.4 %collective-permute-start.1 = (bf16[128,1024]{1,0:T(8,128)(2,1)S(1)}, bf16[128,1024]{1,0:T(8,128)(2,1)S(1)}, u32[]{:S(2)}, u32[]{:S(2)}) collective-permute-start(bf16[128,1024]{1,0:T(8,128)(2,1)S(1)} %get-tuple-element.46), channel_id=1, source_target_pairs={{0,16},{1,17},{16,0},{17,1},{2,18},{3,19},{18,2},{19,3},{4,20},{5,... | collective-permute-start | bytes 786440 | tf_op jit(solution)/shard_map/ppermute | solution.py:52
  11.9 10.8 %collective-permute-start.2 = (bf16[128,1024]{1,0:T(8,128)(2,1)S(1)}, bf16[128,1024]{1,0:T(8,128)(2,1)S(1)}, u32[]{:S(2)}, u32[]{:S(2)}) collective-permute-start(bf16[128,1024]{1,0:T(8,128)(2,1)S(1)} %get-tuple-element.47), channel_id=1, source_target_pairs={{0,1},{1,0},{16,17},{17,16},{2,3},{3,2},{18,19},{19,18},{4,5},{5,4... | collective-permute-start | bytes 786440 | tf_op jit(solution)/shard_map/ppermute | solution.py:52
  16.2 6.5 %collective-permute-start.5 = (bf16[192,512]{1,0:T(8,128)(2,1)S(1)}, bf16[192,512]{1,0:T(8,128)(2,1)S(1)}, u32[]{:S(2)}, u32[]{:S(2)}) collective-permute-start(bf16[192,512]{1,0:T(8,128)(2,1)S(1)} %get-tuple-element.51), channel_id=1, source_target_pairs={{0,8},{8,0},{1,9},{9,1},{2,10},{10,2},{3,11},{11,3},{4,12},{12,4},... | collective-permute-start | bytes 589832 | tf_op jit(solution)/shard_map/ppermute | solution.py:44
  18.1 4.7 %collective-permute-start.6 = (bf16[192,512]{1,0:T(8,128)(2,1)S(1)}, bf16[192,512]{1,0:T(8,128)(2,1)S(1)}, u32[]{:S(2)}, u32[]{:S(2)}) collective-permute-start(bf16[192,512]{1,0:T(8,128)(2,1)S(1)} %get-tuple-element.52), channel_id=1, source_target_pairs={{0,8},{8,0},{1,9},{9,1},{2,10},{10,2},{3,11},{11,3},{4,12},{12,4},... | collective-permute-start | bytes 589832 | tf_op jit(solution)/shard_map/ppermute | solution.py:44
  23.4 6.3 %collective-permute-start.7 = (bf16[128,512]{1,0:T(8,128)(2,1)S(1)}, bf16[128,512]{1,0:T(8,128)(2,1)S(1)}, u32[]{:S(2)}, u32[]{:S(2)}) collective-permute-start(bf16[128,512]{1,0:T(8,128)(2,1)S(1)} %get-tuple-element.59), channel_id=1, source_target_pairs={{0,17},{1,16},{16,1},{17,0},{2,19},{3,18},{18,3},{19,2},{4,21},{5,... | collective-permute-start | bytes 393224 | tf_op jit(solution)/shard_map/ppermute | solution.py:52
  25.8 6.5 %collective-permute-start.8 = (bf16[128,512]{1,0:T(8,128)(2,1)S(1)}, bf16[128,512]{1,0:T(8,128)(2,1)S(1)}, u32[]{:S(2)}, u32[]{:S(2)}) collective-permute-start(bf16[128,512]{1,0:T(8,128)(2,1)S(1)} %get-tuple-element.60), channel_id=1, source_target_pairs={{0,1},{1,0},{16,17},{17,16},{2,3},{3,2},{18,19},{19,18},{4,5},{5,4... | collective-permute-start | bytes 393224 | tf_op jit(solution)/shard_map/ppermute | solution.py:52
  26.4 6.2 %copy-start.1 = (bf16[128,512]{1,0:T(8,128)(2,1)S(1)}, bf16[128,512]{1,0:T(8,128)(2,1)}, u32[]{:S(2)}) copy-start(bf16[128,512]{1,0:T(8,128)(2,1)} %refs_4_.1) | copy-start | bytes 393220
  26.4 6.1 %collective-permute-start.9 = (bf16[128,512]{1,0:T(8,128)(2,1)S(1)}, bf16[128,512]{1,0:T(8,128)(2,1)S(1)}, u32[]{:S(2)}, u32[]{:S(2)}) collective-permute-start(bf16[128,512]{1,0:T(8,128)(2,1)S(1)} %get-tuple-element.61), channel_id=1, source_target_pairs={{0,16},{1,17},{16,0},{17,1},{2,18},{3,19},{18,2},{19,3},{4,20},{5,... | collective-permute-start | bytes 393224 | tf_op jit(solution)/shard_map/ppermute | solution.py:52
  32.8 7.4 %collective-permute-start.10 = (bf16[128,512]{1,0:T(8,128)(2,1)S(1)}, bf16[128,512]{1,0:T(8,128)(2,1)S(1)}, u32[]{:S(2)}, u32[]{:S(2)}) collective-permute-start(bf16[128,512]{1,0:T(8,128)(2,1)S(1)} %get-tuple-element.62.refs_0_.refs_4_), channel_id=1, source_target_pairs={{0,17},{1,16},{16,1},{17,0},{2,19},{3,18},{18,3},{19,2},{4,21},{5,... | collective-permute-start | bytes 393224 | tf_op jit(solution)/shard_map/ppermute | solution.py:52
  34.4 7.6 %collective-permute-start.12 = (bf16[128,512]{1,0:T(8,128)(2,1)S(1)}, bf16[128,512]{1,0:T(8,128)(2,1)S(1)}, u32[]{:S(2)}, u32[]{:S(2)}) collective-permute-start(bf16[128,512]{1,0:T(8,128)(2,1)S(1)} %get-tuple-element.62.refs_0_.refs_4_), channel_id=1, source_target_pairs={{0,16},{1,17},{16,0},{17,1},{2,18},{3,19},{18,2},{19,3},{4,20},{5,... | collective-permute-start | bytes 393224 | tf_op jit(solution)/shard_map/ppermute | solution.py:52
  35.8 6.2 %collective-permute-start.11 = (bf16[128,512]{1,0:T(8,128)(2,1)S(1)}, bf16[128,512]{1,0:T(8,128)(2,1)S(1)}, u32[]{:S(2)}, u32[]{:S(2)}) collective-permute-start(bf16[128,512]{1,0:T(8,128)(2,1)S(1)} %get-tuple-element.62.refs_0_.refs_4_), channel_id=1, source_target_pairs={{0,1},{1,0},{16,17},{17,16},{2,3},{3,2},{18,19},{19,18},{4,5},{5,4... | collective-permute-start | bytes 393224 | tf_op jit(solution)/shard_map/ppermute | solution.py:52
  42.7 2.9 %collective-permute-start.14 = (bf16[256,512]{1,0:T(8,128)(2,1)S(1)}, bf16[256,512]{1,0:T(8,128)(2,1)S(1)}, u32[]{:S(2)}, u32[]{:S(2)}) collective-permute-start(bf16[256,512]{1,0:T(8,128)(2,1)S(1)} %get-tuple-element.70), channel_id=1, source_target_pairs={{0,8},{8,0},{1,9},{9,1},{2,10},{10,2},{3,11},{11,3},{4,12},{12,4},... | collective-permute-start | bytes 786440 | tf_op jit(solution)/shard_map/ppermute | solution.py:44
  42.8 2.9 %collective-permute-start.15 = (bf16[256,512]{1,0:T(8,128)(2,1)S(1)}, bf16[256,512]{1,0:T(8,128)(2,1)S(1)}, u32[]{:S(2)}, u32[]{:S(2)}) collective-permute-start(bf16[256,512]{1,0:T(8,128)(2,1)S(1)} %get-tuple-element.71), channel_id=1, source_target_pairs={{0,8},{8,0},{1,9},{9,1},{2,10},{10,2},{3,11},{11,3},{4,12},{12,4},... | collective-permute-start | bytes 786440 | tf_op jit(solution)/shard_map/ppermute | solution.py:44
  43.8 8.4 %collective-permute-start.13 = (bf16[128,1024]{1,0:T(8,128)(2,1)S(1)}, bf16[128,1024]{1,0:T(8,128)(2,1)S(1)}, u32[]{:S(2)}, u32[]{:S(2)}) collective-permute-start(bf16[128,1024]{1,0:T(8,128)(2,1)S(1)} %get-tuple-element.68), channel_id=1, source_target_pairs={{0,16},{1,17},{16,0},{17,1},{2,18},{3,19},{18,2},{19,3},{4,20},{5,... | collective-permute-start | bytes 786440 | tf_op jit(solution)/shard_map/ppermute | solution.py:52
  45.1 8.3 %collective-permute-start.20 = (bf16[128,1024]{1,0:T(8,128)(2,1)S(1)}, bf16[128,1024]{1,0:T(8,128)(2,1)S(1)}, u32[]{:S(2)}, u32[]{:S(2)}) collective-permute-start(bf16[128,1024]{1,0:T(8,128)(2,1)S(1)} %get-tuple-element.78), channel_id=1, source_target_pairs={{0,1},{1,0},{16,17},{17,16},{2,3},{3,2},{18,19},{19,18},{4,5},{5,4... | collective-permute-start | bytes 786440 | tf_op jit(solution)/shard_map/ppermute | solution.py:52
  45.8 8.7 %collective-permute-start.17 = (bf16[128,512]{1,0:T(8,128)(2,1)S(1)}, bf16[128,512]{1,0:T(8,128)(2,1)S(1)}, u32[]{:S(2)}, u32[]{:S(2)}) collective-permute-start(bf16[128,512]{1,0:T(8,128)(2,1)S(1)} %get-tuple-element.73), channel_id=1, source_target_pairs={{0,6},{2,4},{4,2},{6,0},{1,7},{3,5},{5,3},{7,1},{8,14},{10,12},{12... | collective-permute-start | bytes 393224 | tf_op jit(solution)/shard_map/ppermute | solution.py:40
  47.6 12.4 %collective-permute-start.18 = (bf16[128,512]{1,0:T(8,128)(2,1)S(1)}, bf16[128,512]{1,0:T(8,128)(2,1)S(1)}, u32[]{:S(2)}, u32[]{:S(2)}) collective-permute-start(bf16[128,512]{1,0:T(8,128)(2,1)S(1)} %get-tuple-element.74), channel_id=1, source_target_pairs={{0,4},{2,6},{4,0},{6,2},{1,5},{3,7},{5,1},{7,3},{8,12},{10,14},{12... | collective-permute-start | bytes 393224 | tf_op jit(solution)/shard_map/ppermute | solution.py:40
  48.5 11.5 %collective-permute-start.19 = (bf16[128,512]{1,0:T(8,128)(2,1)S(1)}, bf16[128,512]{1,0:T(8,128)(2,1)S(1)}, u32[]{:S(2)}, u32[]{:S(2)}) collective-permute-start(bf16[128,512]{1,0:T(8,128)(2,1)S(1)} %get-tuple-element.75), channel_id=1, source_target_pairs={{0,2},{2,0},{4,6},{6,4},{1,3},{3,1},{5,7},{7,5},{8,10},{10,8},{12,... | collective-permute-start | bytes 393224 | tf_op jit(solution)/shard_map/ppermute | solution.py:40
  52.1 8.3 %collective-permute-start.16 = (bf16[128,1024]{1,0:T(8,128)(2,1)S(1)}, bf16[128,1024]{1,0:T(8,128)(2,1)S(1)}, u32[]{:S(2)}, u32[]{:S(2)}) collective-permute-start(bf16[128,1024]{1,0:T(8,128)(2,1)S(1)} %columns.4), channel_id=1, source_target_pairs={{0,17},{1,16},{16,1},{17,0},{2,19},{3,18},{18,3},{19,2},{4,21},{5,... | collective-permute-start | bytes 786440 | tf_op jit(solution)/shard_map/ppermute | solution.py:52

commit v14 on v13

--- a/solution.py
+++ b/solution.py
@@ -60,26 +60,24 @@
     return ((place * SPLIT + pair) * SPLIT + side) * TWIN + (core ^ (part % TWIN))
 
 
-def front_body(shard, both, mine, arrived):
+def front_body(tokens, shard, both, mine, *refs):
+    *blocks, arrived = refs
     rows, half = mine.shape[0], both.shape[0]
     first = lax.axis_index("side") * half
-    copies = []
+    moves = []
     for target, start in ((both, first), (mine, first + lax.axis_index("twin") * rows)):
-        source = shard.at[pl.ds(pl.multiple_of(start, rows), target.shape[0])]
-        copies.append(pltpu.make_async_copy(source, target, arrived.at[len(copies)]))
-    for copy in copies:
-        copy.start()
-    for copy in copies:
-        copy.wait()
-
-
-def pack_body(tokens, *blocks):
+        moves.append((shard.at[pl.ds(pl.multiple_of(start, rows), target.shape[0])], target))
     parts = lax.axis_size("line") * TWIN
     run = blocks[0].shape[1] // parts
     for far, block in enumerate(blocks):
         for part in range(parts):
             start = pl.multiple_of(run_of(part, far) * run, run)
-            block[:, part * run : (part + 1) * run] = tokens[:, pl.ds(start, run)]
+            moves.append((tokens.at[:, pl.ds(start, run)], block.at[:, pl.ds(part * run, run)]))
+    copies = [pltpu.make_async_copy(*move, arrived.at[i]) for i, move in enumerate(moves)]
+    for copy in copies:
+        copy.start()
+    for copy in copies:
+        copy.wait()
 
 
 def unpack_moves(far, block, whole):
@@ -268,16 +266,16 @@
         key_weight = cut.transpose(1, 0, 2, 3).reshape(shard_rows, key_cols)
         tokens = split_runs(tokens, outer)
 
-    both, mine = local_call(
+    both, mine, *packed = local_call(
         "front",
         front_body,
-        [shape((TWIN * rows, key_cols), bf16), shape((rows, key_cols), bf16)],
+        [shape((TWIN * rows, key_cols), bf16), shape((rows, key_cols), bf16)] + [block_shape] * MEMBERS,
+        tokens,
         key_weight,
         space=pltpu.HBM,
-        scratch=[pltpu.SemaphoreType.DMA((2,))],
-        room=53.4,
-    )
-    packed = local_call("pack", pack_body, [block_shape] * MEMBERS, tokens)
+        room=53,
+        scratch=[pltpu.SemaphoreType.DMA((2 + MEMBERS * parts,))],
+    )
     blocks = [packed[0], None, None, None]
     for far in (3, 1, 2):
         blocks[far] = to_member(packed[far], far)
@@ -286,6 +284,7 @@
         passed.append(along(mine, line // 2))
     pieces = [both]
     reach = shard_rows // SPLIT * (line - 1) // TWIN
+    blocks[3], *passed = lax.optimization_barrier((blocks[3], *passed))
     relayed = local_call(
         "relay",
         functools.partial(relay_body, 2),

time: 61.6 us -> 60.9 us (0.989)
  local copies, waits for them, and re-layouts: 1.23 us -> 0.01 us
  Pallas kernels: 7.45 us -> 8.52 us
  waiting for transfers between devices: 25.6 us -> 24.9 us
    ppermute x12, waiting for transfers between devices: 16.2 us -> 11.9 us  [to_member(): lax.ppermute(block, ('side', 'pair'), [(i, i ^ far) for i in range(MEMBER...]
    ppermute x4, waiting for transfers between devices: 9.36 us -> 11.7 us  [along(): lax.ppermute(block, 'line', [(i, i ^ step) for i in range(lax.axis_size('...]
    ppermute x12, starting transfers between devices: 13.8 us -> 15.7 us  [to_member(): lax.ppermute(block, ('side', 'pair'), [(i, i ^ far) for i in range(MEMBER...]
    ppermute x1, starting transfers between devices: 3.09 us -> 1.58 us  [parted(): return lax.ppermute(block, ('twin', 'line'), list(enumerate(to)))]
    ppermute x4, waiting for transfers between devices: 0.01 us -> 1.36 us  [to_twin(): return lax.ppermute(block, 'twin', [(0, 1), (1, 0)])]
    unnamed x4 -> x2, local copies, waits for them, and re-layouts: 1.23 us -> 0.01 us
    pallas_call x14 -> x13, Pallas kernels: 5.46 us -> 6.54 us  [local_call(): pl.pallas_call(body, name=name, out_shape=out_shapes, in_specs=[pl.BlockS...]
  transfers between devices with their start and end apart: 21 -> 21, of which waited for: 11 -> 10; matrix products, arithmetic and copies ran while one was open for 0% -> 0% of each run, Pallas kernels for 6% -> 6%
where the time goes in v14:
time: 60.9 us; the launch traced here: 60.8 us
  starting transfers between devices  26.5 us (44%)
  waiting for transfers between devices  24.9 us (41%)
  Pallas kernels  8.52 us (14%)
  between operations  0.75 us (1%)
    ppermute x12, starting transfers between devices, to_member(): lax.ppermute(block, ('side', 'pair'), [(i, i ^ far) for i in range(MEMBER...  15.7 us
    ppermute x12, waiting for transfers between devices, to_member(): lax.ppermute(block, ('side', 'pair'), [(i, i ^ far) for i in range(MEMBER...  11.9 us
    ppermute x4, waiting for transfers between devices, along(): lax.ppermute(block, 'line', [(i, i ^ step) for i in range(lax.axis_size('...  11.7 us
    ppermute x4, starting transfers between devices, along(): lax.ppermute(block, 'line', [(i, i ^ step) for i in range(lax.axis_size('...  7.04 us
    pallas_call x13, Pallas kernels, local_call(): pl.pallas_call(body, name=name, out_shape=out_shapes, in_specs=[pl.BlockS...  6.54 us
    ppermute x4, starting transfers between devices, to_twin(): return lax.ppermute(block, 'twin', [(0, 1), (1, 0)])  2.19 us
    pallas_call x2, Pallas kernels, placing_call(): pl.pallas_call(body, name=name, out_shape=out_shapes, in_specs=[pl.BlockS...  1.99 us
    ppermute x1, starting transfers between devices, parted(): return lax.ppermute(block, ('twin', 'line'), list(enumerate(to)))  1.58 us
  transfers between devices with their start and end apart: 21, of which 10 were waited for; matrix products, arithmetic and copies ran while one was open for 0% of the time, Pallas kernels for 6%

profile of v14, /device:TPU:0, one launch (start us, length us, event | category | flops | bytes accessed | tf_op | source)
XLA Modules:
  0.0 60.8 jit_solution(16085501538444641452)
XLA Ops:
  0.6 2.4 %front.1 = (bf16[256,512]{1,0:T(8,128)(2,1)S(1)}, bf16[128,512]{1,0:T(8,128)(2,1)S(1)}, bf16[128,1024]{1,0:T(8,128)(2,1)S(1)}, bf16[128,1024]{1,0:T(8,128)(2,1)S...) custom-call(bf16[128,4096]{1,0:T(8,128)(2,1)} %tokens.1, bf16[512,512]{1,0:T(8,128)(2,1)} %shard.1), custom_call_target="tpu_custom_call" | custom-call | bytes 1572864 | tf_op jit(solution)/shard_map/front/pallas_call | solution.py:27
  3.0 4.0 %collective-permute-start = (bf16[128,1024]{1,0:T(8,128)(2,1)}, bf16[128,1024]{1,0:T(8,128)(2,1)S(1)}, u32[]{:S(2)}, u32[]{:S(2)}) collective-permute-start(bf16[128,1024]{1,0:T(8,128)(2,1)} %get-tuple-element.48), channel_id=1, source_target_pairs={{0,17},{1,16},{16,1},{17,0},{2,19},{3,18},{18,3},{19,2},{4,21},{5,... | collective-permute-start | bytes 786440 | tf_op jit(solution)/shard_map/ppermute | solution.py:52
  7.0 1.6 %collective-permute-start.1 = (bf16[256,512]{1,0:T(8,128)(2,1)S(1)}, bf16[256,512]{1,0:T(8,128)(2,1)S(1)}, u32[]{:S(2)}, u32[]{:S(2)}) collective-permute-start(bf16[256,512]{1,0:T(8,128)(2,1)S(1)} %get-tuple-element.49.refs_0_), channel_id=1, source_target_pairs={{0,2},{2,0},{4,6},{6,4},{8,14},{10,12},{12,10},{14,8},{1,3},{3,1},... | collective-permute-start | bytes 786440 | tf_op jit(solution)/shard_map/ppermute | solution.py:143
  8.5 2.6 %collective-permute-start.2 = (bf16[128,512]{1,0:T(8,128)(2,1)S(1)}, bf16[128,512]{1,0:T(8,128)(2,1)S(1)}, u32[]{:S(2)}, u32[]{:S(2)}) collective-permute-start(bf16[128,512]{1,0:T(8,128)(2,1)S(1)} %get-tuple-element.50), channel_id=1, source_target_pairs={{0,4},{2,6},{4,0},{6,2},{1,5},{3,7},{5,1},{7,3},{8,12},{10,14},{12... | collective-permute-start | bytes 393224 | tf_op jit(solution)/shard_map/ppermute | solution.py:40
  11.1 0.5 collective-permute-start.3
  11.7 0.5 collective-permute-start.4
  12.2 7.5 %collective-permute-done.2.refs_1_.refs_2_ = bf16[128,512]{1,0:T(8,128)(2,1)S(1)} collective-permute-done((bf16[128,512]{1,0:T(8,128)(2,1)S(1)}, bf16[128,512]{1,0:T(8,128)(2,1)S(1)}, u32[]{:S(2)}, u32[]{:S(2)}) %collective-permute-start.2) | collective-permute-done | bytes 131104 | tf_op jit(solution)/shard_map/ppermute | solution.py:40
  19.7 1.5 %collective-permute-start.5 = (bf16[192,512]{1,0:T(8,128)(2,1)S(1)}, bf16[192,512]{1,0:T(8,128)(2,1)S(1)}, u32[]{:S(2)}, u32[]{:S(2)}) collective-permute-start(bf16[192,512]{1,0:T(8,128)(2,1)S(1)} %get-tuple-element.57), channel_id=1, source_target_pairs={{0,8},{8,0},{1,9},{9,1},{2,10},{10,2},{3,11},{11,3},{4,12},{12,4},... | collective-permute-start | bytes 589832 | tf_op jit(solution)/shard_map/ppermute | solution.py:44
  21.4 1.0 %collective-permute-done.5.refs_3_ = bf16[192,512]{1,0:T(8,128)(2,1)S(1)} collective-permute-done((bf16[192,512]{1,0:T(8,128)(2,1)S(1)}, bf16[192,512]{1,0:T(8,128)(2,1)S(1)}, u32[]{:S(2)}, u32[]{:S(2)}) %collective-permute-start.5) | collective-permute-done | bytes 196640 | tf_op jit(solution)/shard_map/ppermute | solution.py:44
  22.8 0.6 share.3
  23.4 0.5 collective-permute-start.7
  23.9 1.5 %collective-permute-start.8 = (bf16[128,512]{1,0:T(8,128)(2,1)S(1)}, bf16[128,512]{1,0:T(8,128)(2,1)S(1)}, u32[]{:S(2)}, u32[]{:S(2)}) collective-permute-start(bf16[128,512]{1,0:T(8,128)(2,1)S(1)} %get-tuple-element.66), channel_id=1, source_target_pairs={{0,1},{1,0},{16,17},{17,16},{2,3},{3,2},{18,19},{19,18},{4,5},{5,4... | collective-permute-start | bytes 393224 | tf_op jit(solution)/shard_map/ppermute | solution.py:52
  25.4 1.5 %collective-permute-start.9 = (bf16[128,512]{1,0:T(8,128)(2,1)S(1)}, bf16[128,512]{1,0:T(8,128)(2,1)S(1)}, u32[]{:S(2)}, u32[]{:S(2)}) collective-permute-start(bf16[128,512]{1,0:T(8,128)(2,1)S(1)} %get-tuple-element.67), channel_id=1, source_target_pairs={{0,16},{1,17},{16,0},{17,1},{2,18},{3,19},{18,2},{19,3},{4,20},{5,... | collective-permute-start | bytes 393224 | tf_op jit(solution)/shard_map/ppermute | solution.py:52
  27.3 3.5 %collective-permute-done.7.refs_1_ = bf16[128,512]{1,0:T(8,128)(2,1)S(1)} collective-permute-done((bf16[128,512]{1,0:T(8,128)(2,1)S(1)}, bf16[128,512]{1,0:T(8,128)(2,1)S(1)}, u32[]{:S(2)}, u32[]{:S(2)}) %collective-permute-start.7) | collective-permute-done | bytes 131104 | tf_op jit(solution)/shard_map/ppermute | solution.py:52
  30.7 1.4 %collective-permute-done.8.refs_2_ = bf16[128,512]{1,0:T(8,128)(2,1)S(1)} collective-permute-done((bf16[128,512]{1,0:T(8,128)(2,1)S(1)}, bf16[128,512]{1,0:T(8,128)(2,1)S(1)}, u32[]{:S(2)}, u32[]{:S(2)}) %collective-permute-start.8) | collective-permute-done | bytes 131104 | tf_op jit(solution)/shard_map/ppermute | solution.py:52
  32.4 1.3 %collective-permute-start.10 = (bf16[128,512]{1,0:T(8,128)(2,1)S(1)}, bf16[128,512]{1,0:T(8,128)(2,1)S(1)}, u32[]{:S(2)}, u32[]{:S(2)}) collective-permute-start(bf16[128,512]{1,0:T(8,128)(2,1)S(1)} %get-tuple-element.68.refs_0_.refs_4_), channel_id=1, source_target_pairs={{0,17},{1,16},{16,1},{17,0},{2,19},{3,18},{18,3},{19,2},{4,21},{5,... | collective-permute-start | bytes 393224 | tf_op jit(solution)/shard_map/ppermute | solution.py:52
  33.7 1.5 %collective-permute-start.12 = (bf16[128,512]{1,0:T(8,128)(2,1)S(1)}, bf16[128,512]{1,0:T(8,128)(2,1)S(1)}, u32[]{:S(2)}, u32[]{:S(2)}) collective-permute-start(bf16[128,512]{1,0:T(8,128)(2,1)S(1)} %get-tuple-element.68.refs_0_.refs_4_), channel_id=1, source_target_pairs={{0,16},{1,17},{16,0},{17,1},{2,18},{3,19},{18,2},{19,3},{4,20},{5,... | collective-permute-start | bytes 393224 | tf_op jit(solution)/shard_map/ppermute | solution.py:52
  35.2 0.7 %collective-permute-start.11 = (bf16[128,512]{1,0:T(8,128)(2,1)S(1)}, bf16[128,512]{1,0:T(8,128)(2,1)S(1)}, u32[]{:S(2)}, u32[]{:S(2)}) collective-permute-start(bf16[128,512]{1,0:T(8,128)(2,1)S(1)} %get-tuple-element.68.refs_0_.refs_4_), channel_id=1, source_target_pairs={{0,1},{1,0},{16,17},{17,16},{2,3},{3,2},{18,19},{19,18},{4,5},{5,4... | collective-permute-start | bytes 393224 | tf_op jit(solution)/shard_map/ppermute | solution.py:52
  35.9 0.7 %emit.1 = bf16[128,512]{1,0:T(8,128)(2,1)} custom-call(bf16[128,512]{1,0:T(8,128)(2,1)S(1)} %get-tuple-element.69.held), custom_call_target="tpu_custom_call" | custom-call | bytes 131072 | tf_op jit(solution)/shard_map/emit/pallas_call | solution.py:27
  37.1 2.6 %collective-permute-done.10.refs_0_.refs_7_ = bf16[128,512]{1,0:T(8,128)(2,1)S(1)} collective-permute-done((bf16[128,512]{1,0:T(8,128)(2,1)S(1)}, bf16[128,512]{1,0:T(8,128)(2,1)S(1)}, u32[]{:S(2)}, u32[]{:S(2)}) %collective-permute-start.10) | collective-permute-done | bytes 131104 | tf_op jit(solution)/shard_map/ppermute | solution.py:52
  40.2 1.1 %collective-permute-done.12.refs_1_.refs_6_ = bf16[128,512]{1,0:T(8,128)(2,1)S(1)} collective-permute-done((bf16[128,512]{1,0:T(8,128)(2,1)S(1)}, bf16[128,512]{1,0:T(8,128)(2,1)S(1)}, u32[]{:S(2)}, u32[]{:S(2)}) %collective-permute-start.12) | collective-permute-done | bytes 131104 | tf_op jit(solution)/shard_map/ppermute | solution.py:52
  41.3 0.7 %terms.1 = (f32[4,128,512]{2,1,0:T(8,128)S(1)}, bf16[256,512]{1,0:T(8,128)(2,1)S(1)}, bf16[256,512]{1,0:T(8,128)(2,1)S(1)}) custom-call(bf16[128,1024]{1,0:T(8,128)(2,1)S(1)} %get-tuple-element.59.refs_0_, bf16[128,1024]{1,0:T(8,128)(2,1)S(1)} %collective-permute-done.4.refs_1_, bf16[128,1024]{1,0:T(8,128)(2,1)S(1)} %collective-permute-done.3.refs_2_, ...), custom_call_target="tpu_custom_call" | custom-call | tf_op jit(solution)/shard_map/terms/pallas_call | solution.py:27
  43.1 1.6 %collective-permute-start.13 = (bf16[128,1024]{1,0:T(8,128)(2,1)S(1)}, bf16[128,1024]{1,0:T(8,128)(2,1)S(1)}, u32[]{:S(2)}, u32[]{:S(2)}) collective-permute-start(bf16[128,1024]{1,0:T(8,128)(2,1)S(1)} %get-tuple-element.74), channel_id=1, source_target_pairs={{0,16},{1,17},{16,0},{17,1},{2,18},{3,19},{18,2},{19,3},{4,20},{5,... | collective-permute-start | bytes 786440 | tf_op jit(solution)/shard_map/ppermute | solution.py:52
  44.7 0.6 collective-permute-start.20
  45.4 2.6 %collective-permute-start.17 = (bf16[128,512]{1,0:T(8,128)(2,1)S(1)}, bf16[128,512]{1,0:T(8,128)(2,1)S(1)}, u32[]{:S(2)}, u32[]{:S(2)}) collective-permute-start(bf16[128,512]{1,0:T(8,128)(2,1)S(1)} %get-tuple-element.79), channel_id=1, source_target_pairs={{0,6},{2,4},{4,2},{6,0},{1,7},{3,5},{5,3},{7,1},{8,14},{10,12},{12... | collective-permute-start | bytes 393224 | tf_op jit(solution)/shard_map/ppermute | solution.py:40
  47.9 1.9 %collective-permute-start.19 = (bf16[128,512]{1,0:T(8,128)(2,1)S(1)}, bf16[128,512]{1,0:T(8,128)(2,1)S(1)}, u32[]{:S(2)}, u32[]{:S(2)}) collective-permute-start(bf16[128,512]{1,0:T(8,128)(2,1)S(1)} %get-tuple-element.81), channel_id=1, source_target_pairs={{0,2},{2,0},{4,6},{6,4},{1,3},{3,1},{5,7},{7,5},{8,10},{10,8},{12,... | collective-permute-start | bytes 393224 | tf_op jit(solution)/shard_map/ppermute | solution.py:40
  49.8 1.7 %collective-permute-done.13.refs_2_ = bf16[128,1024]{1,0:T(8,128)(2,1)S(1)} collective-permute-done((bf16[128,1024]{1,0:T(8,128)(2,1)S(1)}, bf16[128,1024]{1,0:T(8,128)(2,1)S(1)}, u32[]{:S(2)}, u32[]{:S(2)}) %collective-permute-start.13) | collective-permute-done | bytes 262176 | tf_op jit(solution)/shard_map/ppermute | solution.py:52
  51.5 1.5 %collective-permute-start.16 = (bf16[128,1024]{1,0:T(8,128)(2,1)S(1)}, bf16[128,1024]{1,0:T(8,128)(2,1)S(1)}, u32[]{:S(2)}, u32[]{:S(2)}) collective-permute-start(bf16[128,1024]{1,0:T(8,128)(2,1)S(1)} %columns.4), channel_id=1, source_target_pairs={{0,17},{1,16},{16,1},{17,0},{2,19},{3,18},{18,3},{19,2},{4,21},{5,... | collective-permute-start | bytes 786440 | tf_op jit(solution)/shard_map/ppermute | solution.py:52
  53.0 1.1 %unpack.1._ = bf16[128,4096]{1,0:T(8,128)(2,1)} custom-call(bf16[128,1024]{1,0:T(8,128)(2,1)S(1)} %columns.3.refs_0_, bf16[128,1024]{1,0:T(8,128)(2,1)S(1)} %collective-permute-done.20.refs_1_, bf16[128,1024]{1,0:T(8,128)(2,1)S(1)} %collective-permute-done.13.refs_2_), custom_call_target="tpu_custom_call" | custom-call | tf_op jit(solution)/shard_map/unpack/pallas_call | solution.py:110
  54.1 4.1 %collective-permute-done.18.refs_2_ = bf16[128,512]{1,0:T(8,128)(2,1)S(1)} collective-permute-done((bf16[128,512]{1,0:T(8,128)(2,1)S(1)}, bf16[128,512]{1,0:T(8,128)(2,1)S(1)}, u32[]{:S(2)}, u32[]{:S(2)}) %collective-permute-start.18) | collective-permute-done | bytes 131104 | tf_op jit(solution)/shard_map/ppermute | solution.py:40
  58.3 1.6 %collective-permute-done.16.block = bf16[128,1024]{1,0:T(8,128)(2,1)S(1)} collective-permute-done((bf16[128,1024]{1,0:T(8,128)(2,1)S(1)}, bf16[128,1024]{1,0:T(8,128)(2,1)S(1)}, u32[]{:S(2)}, u32[]{:S(2)}) %collective-permute-start.16) | collective-permute-done | bytes 262176 | tf_op jit(solution)/shard_map/ppermute | solution.py:52
  59.8 0.9 %finish.1 = (bf16[128,4096]{1,0:T(8,128)(2,1)}, f32[128,512]{1,0:T(8,128)}) custom-call(bf16[128,1024]{1,0:T(8,128)(2,1)S(1)} %collective-permute-done.16.block, f32[128,512]{1,0:T(8,128)S(1)} %final_sum.1.total, bf16[128,4096]{1,0:T(8,128)(2,1)} %unpack.1._), custom_call_target="tpu_custom_call", output_to_operand_aliasing={{0}: (2, {})} | custom-call | tf_op jit(solution)/shard_map/finish/pallas_call | solution.py:110
  (27 shorter events, 3.2 us)
Async XLA Ops:
  3.0 16.7 %collective-permute-start = (bf16[128,1024]{1,0:T(8,128)(2,1)}, bf16[128,1024]{1,0:T(8,128)(2,1)S(1)}, u32[]{:S(2)}, u32[]{:S(2)}) collective-permute-start(bf16[128,1024]{1,0:T(8,128)(2,1)} %get-tuple-element.48), channel_id=1, source_target_pairs={{0,17},{1,16},{16,1},{17,0},{2,19},{3,18},{18,3},{19,2},{4,21},{5,... | collective-permute-start | bytes 786440 | tf_op jit(solution)/shard_map/ppermute | solution.py:52
  7.0 12.7 %collective-permute-start.1 = (bf16[256,512]{1,0:T(8,128)(2,1)S(1)}, bf16[256,512]{1,0:T(8,128)(2,1)S(1)}, u32[]{:S(2)}, u32[]{:S(2)}) collective-permute-start(bf16[256,512]{1,0:T(8,128)(2,1)S(1)} %get-tuple-element.49.refs_0_), channel_id=1, source_target_pairs={{0,2},{2,0},{4,6},{6,4},{8,14},{10,12},{12,10},{14,8},{1,3},{3,1},... | collective-permute-start | bytes 786440 | tf_op jit(solution)/shard_map/ppermute | solution.py:143
  8.5 11.2 %collective-permute-start.2 = (bf16[128,512]{1,0:T(8,128)(2,1)S(1)}, bf16[128,512]{1,0:T(8,128)(2,1)S(1)}, u32[]{:S(2)}, u32[]{:S(2)}) collective-permute-start(bf16[128,512]{1,0:T(8,128)(2,1)S(1)} %get-tuple-element.50), channel_id=1, source_target_pairs={{0,4},{2,6},{4,0},{6,2},{1,5},{3,7},{5,1},{7,3},{8,12},{10,14},{12... | collective-permute-start | bytes 393224 | tf_op jit(solution)/shard_map/ppermute | solution.py:40
  11.1 10.2 %collective-permute-start.3 = (bf16[128,1024]{1,0:T(8,128)(2,1)}, bf16[128,1024]{1,0:T(8,128)(2,1)S(1)}, u32[]{:S(2)}, u32[]{:S(2)}) collective-permute-start(bf16[128,1024]{1,0:T(8,128)(2,1)} %get-tuple-element.52), channel_id=1, source_target_pairs={{0,16},{1,17},{16,0},{17,1},{2,18},{3,19},{18,2},{19,3},{4,20},{5,... | collective-permute-start | bytes 786440 | tf_op jit(solution)/shard_map/ppermute | solution.py:52
  11.7 9.7 %collective-permute-start.4 = (bf16[128,1024]{1,0:T(8,128)(2,1)S(1)}, bf16[128,1024]{1,0:T(8,128)(2,1)S(1)}, u32[]{:S(2)}, u32[]{:S(2)}) collective-permute-start(bf16[128,1024]{1,0:T(8,128)(2,1)S(1)} %get-tuple-element.53), channel_id=1, source_target_pairs={{0,1},{1,0},{16,17},{17,16},{2,3},{3,2},{18,19},{19,18},{4,5},{5,4... | collective-permute-start | bytes 786440 | tf_op jit(solution)/shard_map/ppermute | solution.py:52
  19.7 2.6 %collective-permute-start.5 = (bf16[192,512]{1,0:T(8,128)(2,1)S(1)}, bf16[192,512]{1,0:T(8,128)(2,1)S(1)}, u32[]{:S(2)}, u32[]{:S(2)}) collective-permute-start(bf16[192,512]{1,0:T(8,128)(2,1)S(1)} %get-tuple-element.57), channel_id=1, source_target_pairs={{0,8},{8,0},{1,9},{9,1},{2,10},{10,2},{3,11},{11,3},{4,12},{12,4},... | collective-permute-start | bytes 589832 | tf_op jit(solution)/shard_map/ppermute | solution.py:44
  21.3 1.4 %collective-permute-start.6 = (bf16[192,512]{1,0:T(8,128)(2,1)S(1)}, bf16[192,512]{1,0:T(8,128)(2,1)S(1)}, u32[]{:S(2)}, u32[]{:S(2)}) collective-permute-start(bf16[192,512]{1,0:T(8,128)(2,1)S(1)} %get-tuple-element.58), channel_id=1, source_target_pairs={{0,8},{8,0},{1,9},{9,1},{2,10},{10,2},{3,11},{11,3},{4,12},{12,4},... | collective-permute-start | bytes 589832 | tf_op jit(solution)/shard_map/ppermute | solution.py:44
  23.4 7.3 %collective-permute-start.7 = (bf16[128,512]{1,0:T(8,128)(2,1)S(1)}, bf16[128,512]{1,0:T(8,128)(2,1)S(1)}, u32[]{:S(2)}, u32[]{:S(2)}) collective-permute-start(bf16[128,512]{1,0:T(8,128)(2,1)S(1)} %get-tuple-element.65), channel_id=1, source_target_pairs={{0,17},{1,16},{16,1},{17,0},{2,19},{3,18},{18,3},{19,2},{4,21},{5,... | collective-permute-start | bytes 393224 | tf_op jit(solution)/shard_map/ppermute | solution.py:52
  23.9 8.2 %collective-permute-start.8 = (bf16[128,512]{1,0:T(8,128)(2,1)S(1)}, bf16[128,512]{1,0:T(8,128)(2,1)S(1)}, u32[]{:S(2)}, u32[]{:S(2)}) collective-permute-start(bf16[128,512]{1,0:T(8,128)(2,1)S(1)} %get-tuple-element.66), channel_id=1, source_target_pairs={{0,1},{1,0},{16,17},{17,16},{2,3},{3,2},{18,19},{19,18},{4,5},{5,4... | collective-permute-start | bytes 393224 | tf_op jit(solution)/shard_map/ppermute | solution.py:52
  25.4 6.7 %copy-start = (bf16[128,512]{1,0:T(8,128)(2,1)S(1)}, bf16[128,512]{1,0:T(8,128)(2,1)}, u32[]{:S(2)}) copy-start(bf16[128,512]{1,0:T(8,128)(2,1)} %refs_4_.1) | copy-start | bytes 393220
  25.4 6.7 %collective-permute-start.9 = (bf16[128,512]{1,0:T(8,128)(2,1)S(1)}, bf16[128,512]{1,0:T(8,128)(2,1)S(1)}, u32[]{:S(2)}, u32[]{:S(2)}) collective-permute-start(bf16[128,512]{1,0:T(8,128)(2,1)S(1)} %get-tuple-element.67), channel_id=1, source_target_pairs={{0,16},{1,17},{16,0},{17,1},{2,18},{3,19},{18,2},{19,3},{4,20},{5,... | collective-permute-start | bytes 393224 | tf_op jit(solution)/shard_map/ppermute | solution.py:52
  32.4 7.3 %collective-permute-start.10 = (bf16[128,512]{1,0:T(8,128)(2,1)S(1)}, bf16[128,512]{1,0:T(8,128)(2,1)S(1)}, u32[]{:S(2)}, u32[]{:S(2)}) collective-permute-start(bf16[128,512]{1,0:T(8,128)(2,1)S(1)} %get-tuple-element.68.refs_0_.refs_4_), channel_id=1, source_target_pairs={{0,17},{1,16},{16,1},{17,0},{2,19},{3,18},{18,3},{19,2},{4,21},{5,... | collective-permute-start | bytes 393224 | tf_op jit(solution)/shard_map/ppermute | solution.py:52
  33.7 7.6 %collective-permute-start.12 = (bf16[128,512]{1,0:T(8,128)(2,1)S(1)}, bf16[128,512]{1,0:T(8,128)(2,1)S(1)}, u32[]{:S(2)}, u32[]{:S(2)}) collective-permute-start(bf16[128,512]{1,0:T(8,128)(2,1)S(1)} %get-tuple-element.68.refs_0_.refs_4_), channel_id=1, source_target_pairs={{0,16},{1,17},{16,0},{17,1},{2,18},{3,19},{18,2},{19,3},{4,20},{5,... | collective-permute-start | bytes 393224 | tf_op jit(solution)/shard_map/ppermute | solution.py:52
  35.2 6.1 %collective-permute-start.11 = (bf16[128,512]{1,0:T(8,128)(2,1)S(1)}, bf16[128,512]{1,0:T(8,128)(2,1)S(1)}, u32[]{:S(2)}, u32[]{:S(2)}) collective-permute-start(bf16[128,512]{1,0:T(8,128)(2,1)S(1)} %get-tuple-element.68.refs_0_.refs_4_), channel_id=1, source_target_pairs={{0,1},{1,0},{16,17},{17,16},{2,3},{3,2},{18,19},{19,18},{4,5},{5,4... | collective-permute-start | bytes 393224 | tf_op jit(solution)/shard_map/ppermute | solution.py:52
  42.1 3.2 %collective-permute-start.14 = (bf16[256,512]{1,0:T(8,128)(2,1)S(1)}, bf16[256,512]{1,0:T(8,128)(2,1)S(1)}, u32[]{:S(2)}, u32[]{:S(2)}) collective-permute-start(bf16[256,512]{1,0:T(8,128)(2,1)S(1)} %get-tuple-element.76), channel_id=1, source_target_pairs={{0,8},{8,0},{1,9},{9,1},{2,10},{10,2},{3,11},{11,3},{4,12},{12,4},... | collective-permute-start | bytes 786440 | tf_op jit(solution)/shard_map/ppermute | solution.py:44
  42.2 3.1 %collective-permute-start.15 = (bf16[256,512]{1,0:T(8,128)(2,1)S(1)}, bf16[256,512]{1,0:T(8,128)(2,1)S(1)}, u32[]{:S(2)}, u32[]{:S(2)}) collective-permute-start(bf16[256,512]{1,0:T(8,128)(2,1)S(1)} %get-tuple-element.77), channel_id=1, source_target_pairs={{0,8},{8,0},{1,9},{9,1},{2,10},{10,2},{3,11},{11,3},{4,12},{12,4},... | collective-permute-start | bytes 786440 | tf_op jit(solution)/shard_map/ppermute | solution.py:44
  43.1 8.4 %collective-permute-start.13 = (bf16[128,1024]{1,0:T(8,128)(2,1)S(1)}, bf16[128,1024]{1,0:T(8,128)(2,1)S(1)}, u32[]{:S(2)}, u32[]{:S(2)}) collective-permute-start(bf16[128,1024]{1,0:T(8,128)(2,1)S(1)} %get-tuple-element.74), channel_id=1, source_target_pairs={{0,16},{1,17},{16,0},{17,1},{2,18},{3,19},{18,2},{19,3},{4,20},{5,... | collective-permute-start | bytes 786440 | tf_op jit(solution)/shard_map/ppermute | solution.py:52
  44.7 8.3 %collective-permute-start.20 = (bf16[128,1024]{1,0:T(8,128)(2,1)S(1)}, bf16[128,1024]{1,0:T(8,128)(2,1)S(1)}, u32[]{:S(2)}, u32[]{:S(2)}) collective-permute-start(bf16[128,1024]{1,0:T(8,128)(2,1)S(1)} %get-tuple-element.84), channel_id=1, source_target_pairs={{0,1},{1,0},{16,17},{17,16},{2,3},{3,2},{18,19},{19,18},{4,5},{5,4... | collective-permute-start | bytes 786440 | tf_op jit(solution)/shard_map/ppermute | solution.py:52
  45.4 8.7 %collective-permute-start.17 = (bf16[128,512]{1,0:T(8,128)(2,1)S(1)}, bf16[128,512]{1,0:T(8,128)(2,1)S(1)}, u32[]{:S(2)}, u32[]{:S(2)}) collective-permute-start(bf16[128,512]{1,0:T(8,128)(2,1)S(1)} %get-tuple-element.79), channel_id=1, source_target_pairs={{0,6},{2,4},{4,2},{6,0},{1,7},{3,5},{5,3},{7,1},{8,14},{10,12},{12... | collective-permute-start | bytes 393224 | tf_op jit(solution)/shard_map/ppermute | solution.py:40
  47.9 10.3 %collective-permute-start.18 = (bf16[128,512]{1,0:T(8,128)(2,1)S(1)}, bf16[128,512]{1,0:T(8,128)(2,1)S(1)}, u32[]{:S(2)}, u32[]{:S(2)}) collective-permute-start(bf16[128,512]{1,0:T(8,128)(2,1)S(1)} %get-tuple-element.80), channel_id=1, source_target_pairs={{0,4},{2,6},{4,0},{6,2},{1,5},{3,7},{5,1},{7,3},{8,12},{10,14},{12... | collective-permute-start | bytes 393224 | tf_op jit(solution)/shard_map/ppermute | solution.py:40
  47.9 10.3 %collective-permute-start.19 = (bf16[128,512]{1,0:T(8,128)(2,1)S(1)}, bf16[128,512]{1,0:T(8,128)(2,1)S(1)}, u32[]{:S(2)}, u32[]{:S(2)}) collective-permute-start(bf16[128,512]{1,0:T(8,128)(2,1)S(1)} %get-tuple-element.81), channel_id=1, source_target_pairs={{0,2},{2,0},{4,6},{6,4},{1,3},{3,1},{5,7},{7,5},{8,10},{10,8},{12,... | collective-permute-start | bytes 393224 | tf_op jit(solution)/shard_map/ppermute | solution.py:40
  51.5 8.3 %collective-permute-start.16 = (bf16[128,1024]{1,0:T(8,128)(2,1)S(1)}, bf16[128,1024]{1,0:T(8,128)(2,1)S(1)}, u32[]{:S(2)}, u32[]{:S(2)}) collective-permute-start(bf16[128,1024]{1,0:T(8,128)(2,1)S(1)} %columns.4), channel_id=1, source_target_pairs={{0,17},{1,16},{16,1},{17,0},{2,19},{3,18},{18,3},{19,2},{4,21},{5,... | collective-permute-start | bytes 786440 | tf_op jit(solution)/shard_map/ppermute | solution.py:52

commit v15 on v14

--- a/solution.py
+++ b/solution.py
@@ -344,14 +344,18 @@
         moved=0,
     )
 
-    met = [sums[0]] + [along(sums[line - step], step) for step in range(line - 1, 0, -1)]
     back_1, back_2 = (to_member(column, far) for far, column in zip((1, 2), columns(grad_1, grad_2)))
-    column_3, back_2, _ = lax.optimization_barrier((column_3, back_2, sums))
+    column_3, _ = lax.optimization_barrier((column_3, sums))
     back_3 = to_member(column_3, 3)
+    *sums, closest = sums
+    closest, back_2 = lax.optimization_barrier((closest, back_2))
+    met = [sums[0]] + [along(piece, line - i) for i, piece in enumerate(sums) if i]
     whole_shape = shape((tok_rows, width), bf16)
     (input_grad,) = placing_call("unpack", unpack_body, [whole_shape], (column_0, back_1, back_2))
     met, input_grad = lax.optimization_barrier((met, input_grad))
-    total = local_call("final_sum", sum_body, shape((rows, key_cols), f32), *met, flops=24 * flops)
+    sum_shape = shape((rows, key_cols), f32)
+    far_sum = local_call("far_sum", sum_body, sum_shape, *met, flops=24 * flops)
+    total = local_call("final_sum", sum_body, sum_shape, far_sum, along(closest, 1), moved=0)
     input_grad, weight_grad = placing_call(
         "finish", finish_body, [whole_shape, shape(total.shape, f32)], (back_3, total), (input_grad,)
     )

time: 60.9 us -> 60.7 us (level)
  starting transfers between devices: 26.5 us -> 24.6 us
  waiting for transfers between devices: 24.9 us -> 26.7 us
    ppermute x12, waiting for transfers between devices: 11.9 us -> 17.6 us  [to_member(): lax.ppermute(block, ('side', 'pair'), [(i, i ^ far) for i in range(MEMBER...]
    ppermute x4, waiting for transfers between devices: 11.7 us -> 7.67 us  [along(): lax.ppermute(block, 'line', [(i, i ^ step) for i in range(lax.axis_size('...]
    ppermute x4, starting transfers between devices: 7.04 us -> 5.16 us  [along(): lax.ppermute(block, 'line', [(i, i ^ step) for i in range(lax.axis_size('...]
    pallas_call x13 -> x14, Pallas kernels: 6.54 us -> 6.54 us  [local_call(): pl.pallas_call(body, name=name, out_shape=out_shapes, in_specs=[pl.BlockS...]
where the time goes in v15:
time: 60.7 us; the launch traced here: 60.6 us
  waiting for transfers between devices  26.7 us (44%)
  starting transfers between devices  24.6 us (41%)
  Pallas kernels  8.53 us (14%)
  between operations  0.78 us (1%)
    ppermute x12, waiting for transfers between devices, to_member(): lax.ppermute(block, ('side', 'pair'), [(i, i ^ far) for i in range(MEMBER...  17.6 us
    ppermute x12, starting transfers between devices, to_member(): lax.ppermute(block, ('side', 'pair'), [(i, i ^ far) for i in range(MEMBER...  15.7 us
    ppermute x4, waiting for transfers between devices, along(): lax.ppermute(block, 'line', [(i, i ^ step) for i in range(lax.axis_size('...  7.67 us
    pallas_call x14, Pallas kernels, local_call(): pl.pallas_call(body, name=name, out_shape=out_shapes, in_specs=[pl.BlockS...  6.54 us
    ppermute x4, starting transfers between devices, along(): lax.ppermute(block, 'line', [(i, i ^ step) for i in range(lax.axis_size('...  5.16 us
    ppermute x4, starting transfers between devices, to_twin(): return lax.ppermute(block, 'twin', [(0, 1), (1, 0)])  2.19 us
    pallas_call x2, Pallas kernels, placing_call(): pl.pallas_call(body, name=name, out_shape=out_shapes, in_specs=[pl.BlockS...  1.99 us
    ppermute x1, starting transfers between devices, parted(): return lax.ppermute(block, ('twin', 'line'), list(enumerate(to)))  1.58 us
  transfers between devices with their start and end apart: 21, of which 10 were waited for; matrix products, arithmetic and copies ran while one was open for 0% of the time, Pallas kernels for 6%

profile of v15, /device:TPU:0, one launch (start us, length us, event | category | flops | bytes accessed | tf_op | source)
XLA Modules:
  0.0 60.6 jit_solution(11360167106205735071)
XLA Ops:
  0.6 2.4 %front.1 = (bf16[256,512]{1,0:T(8,128)(2,1)S(1)}, bf16[128,512]{1,0:T(8,128)(2,1)S(1)}, bf16[128,1024]{1,0:T(8,128)(2,1)S(1)}, bf16[128,1024]{1,0:T(8,128)(2,1)S...) custom-call(bf16[128,4096]{1,0:T(8,128)(2,1)} %tokens.1, bf16[512,512]{1,0:T(8,128)(2,1)} %shard.1), custom_call_target="tpu_custom_call" | custom-call | bytes 1572864 | tf_op jit(solution)/shard_map/front/pallas_call | solution.py:27
  3.0 4.0 %collective-permute-start = (bf16[128,1024]{1,0:T(8,128)(2,1)}, bf16[128,1024]{1,0:T(8,128)(2,1)S(1)}, u32[]{:S(2)}, u32[]{:S(2)}) collective-permute-start(bf16[128,1024]{1,0:T(8,128)(2,1)} %get-tuple-element.48), channel_id=1, source_target_pairs={{0,17},{1,16},{16,1},{17,0},{2,19},{3,18},{18,3},{19,2},{4,21},{5,... | collective-permute-start | bytes 786440 | tf_op jit(solution)/shard_map/ppermute | solution.py:52
  7.0 1.6 %collective-permute-start.1 = (bf16[256,512]{1,0:T(8,128)(2,1)S(1)}, bf16[256,512]{1,0:T(8,128)(2,1)S(1)}, u32[]{:S(2)}, u32[]{:S(2)}) collective-permute-start(bf16[256,512]{1,0:T(8,128)(2,1)S(1)} %get-tuple-element.49.refs_0_), channel_id=1, source_target_pairs={{0,2},{2,0},{4,6},{6,4},{8,14},{10,12},{12,10},{14,8},{1,3},{3,1},... | collective-permute-start | bytes 786440 | tf_op jit(solution)/shard_map/ppermute | solution.py:143
  8.5 2.6 %collective-permute-start.2 = (bf16[128,512]{1,0:T(8,128)(2,1)S(1)}, bf16[128,512]{1,0:T(8,128)(2,1)S(1)}, u32[]{:S(2)}, u32[]{:S(2)}) collective-permute-start(bf16[128,512]{1,0:T(8,128)(2,1)S(1)} %get-tuple-element.50), channel_id=1, source_target_pairs={{0,4},{2,6},{4,0},{6,2},{1,5},{3,7},{5,1},{7,3},{8,12},{10,14},{12... | collective-permute-start | bytes 393224 | tf_op jit(solution)/shard_map/ppermute | solution.py:40
  11.1 0.5 collective-permute-start.3
  11.7 0.5 collective-permute-start.4
  12.2 7.5 %collective-permute-done.2.refs_1_.refs_2_ = bf16[128,512]{1,0:T(8,128)(2,1)S(1)} collective-permute-done((bf16[128,512]{1,0:T(8,128)(2,1)S(1)}, bf16[128,512]{1,0:T(8,128)(2,1)S(1)}, u32[]{:S(2)}, u32[]{:S(2)}) %collective-permute-start.2) | collective-permute-done | bytes 131104 | tf_op jit(solution)/shard_map/ppermute | solution.py:40
  19.7 1.5 %collective-permute-start.5 = (bf16[192,512]{1,0:T(8,128)(2,1)S(1)}, bf16[192,512]{1,0:T(8,128)(2,1)S(1)}, u32[]{:S(2)}, u32[]{:S(2)}) collective-permute-start(bf16[192,512]{1,0:T(8,128)(2,1)S(1)} %get-tuple-element.57), channel_id=1, source_target_pairs={{0,8},{8,0},{1,9},{9,1},{2,10},{10,2},{3,11},{11,3},{4,12},{12,4},... | collective-permute-start | bytes 589832 | tf_op jit(solution)/shard_map/ppermute | solution.py:44
  21.4 1.0 %collective-permute-done.5.refs_3_ = bf16[192,512]{1,0:T(8,128)(2,1)S(1)} collective-permute-done((bf16[192,512]{1,0:T(8,128)(2,1)S(1)}, bf16[192,512]{1,0:T(8,128)(2,1)S(1)}, u32[]{:S(2)}, u32[]{:S(2)}) %collective-permute-start.5) | collective-permute-done | bytes 196640 | tf_op jit(solution)/shard_map/ppermute | solution.py:44
  22.8 0.6 share.3
  23.4 0.5 collective-permute-start.7
  23.9 1.5 %collective-permute-start.8 = (bf16[128,512]{1,0:T(8,128)(2,1)S(1)}, bf16[128,512]{1,0:T(8,128)(2,1)S(1)}, u32[]{:S(2)}, u32[]{:S(2)}) collective-permute-start(bf16[128,512]{1,0:T(8,128)(2,1)S(1)} %get-tuple-element.66), channel_id=1, source_target_pairs={{0,1},{1,0},{16,17},{17,16},{2,3},{3,2},{18,19},{19,18},{4,5},{5,4... | collective-permute-start | bytes 393224 | tf_op jit(solution)/shard_map/ppermute | solution.py:52
  25.4 1.5 %collective-permute-start.9 = (bf16[128,512]{1,0:T(8,128)(2,1)S(1)}, bf16[128,512]{1,0:T(8,128)(2,1)S(1)}, u32[]{:S(2)}, u32[]{:S(2)}) collective-permute-start(bf16[128,512]{1,0:T(8,128)(2,1)S(1)} %get-tuple-element.67), channel_id=1, source_target_pairs={{0,16},{1,17},{16,0},{17,1},{2,18},{3,19},{18,2},{19,3},{4,20},{5,... | collective-permute-start | bytes 393224 | tf_op jit(solution)/shard_map/ppermute | solution.py:52
  27.3 3.5 %collective-permute-done.7.refs_1_ = bf16[128,512]{1,0:T(8,128)(2,1)S(1)} collective-permute-done((bf16[128,512]{1,0:T(8,128)(2,1)S(1)}, bf16[128,512]{1,0:T(8,128)(2,1)S(1)}, u32[]{:S(2)}, u32[]{:S(2)}) %collective-permute-start.7) | collective-permute-done | bytes 131104 | tf_op jit(solution)/shard_map/ppermute | solution.py:52
  30.7 1.4 %collective-permute-done.8.refs_2_ = bf16[128,512]{1,0:T(8,128)(2,1)S(1)} collective-permute-done((bf16[128,512]{1,0:T(8,128)(2,1)S(1)}, bf16[128,512]{1,0:T(8,128)(2,1)S(1)}, u32[]{:S(2)}, u32[]{:S(2)}) %collective-permute-start.8) | collective-permute-done | bytes 131104 | tf_op jit(solution)/shard_map/ppermute | solution.py:52
  32.4 1.3 %collective-permute-start.10 = (bf16[128,512]{1,0:T(8,128)(2,1)S(1)}, bf16[128,512]{1,0:T(8,128)(2,1)S(1)}, u32[]{:S(2)}, u32[]{:S(2)}) collective-permute-start(bf16[128,512]{1,0:T(8,128)(2,1)S(1)} %get-tuple-element.68.refs_0_.refs_4_), channel_id=1, source_target_pairs={{0,17},{1,16},{16,1},{17,0},{2,19},{3,18},{18,3},{19,2},{4,21},{5,... | collective-permute-start | bytes 393224 | tf_op jit(solution)/shard_map/ppermute | solution.py:52
  33.7 1.5 %collective-permute-start.12 = (bf16[128,512]{1,0:T(8,128)(2,1)S(1)}, bf16[128,512]{1,0:T(8,128)(2,1)S(1)}, u32[]{:S(2)}, u32[]{:S(2)}) collective-permute-start(bf16[128,512]{1,0:T(8,128)(2,1)S(1)} %get-tuple-element.68.refs_0_.refs_4_), channel_id=1, source_target_pairs={{0,16},{1,17},{16,0},{17,1},{2,18},{3,19},{18,2},{19,3},{4,20},{5,... | collective-permute-start | bytes 393224 | tf_op jit(solution)/shard_map/ppermute | solution.py:52
  35.2 0.7 %collective-permute-start.11 = (bf16[128,512]{1,0:T(8,128)(2,1)S(1)}, bf16[128,512]{1,0:T(8,128)(2,1)S(1)}, u32[]{:S(2)}, u32[]{:S(2)}) collective-permute-start(bf16[128,512]{1,0:T(8,128)(2,1)S(1)} %get-tuple-element.68.refs_0_.refs_4_), channel_id=1, source_target_pairs={{0,1},{1,0},{16,17},{17,16},{2,3},{3,2},{18,19},{19,18},{4,5},{5,4... | collective-permute-start | bytes 393224 | tf_op jit(solution)/shard_map/ppermute | solution.py:52
  35.9 0.7 %emit.1 = bf16[128,512]{1,0:T(8,128)(2,1)} custom-call(bf16[128,512]{1,0:T(8,128)(2,1)S(1)} %get-tuple-element.69.held), custom_call_target="tpu_custom_call" | custom-call | bytes 131072 | tf_op jit(solution)/shard_map/emit/pallas_call | solution.py:27
  36.6 0.5 columns.3.refs_0_
  37.1 2.6 %collective-permute-done.10.refs_0_.refs_7_ = bf16[128,512]{1,0:T(8,128)(2,1)S(1)} collective-permute-done((bf16[128,512]{1,0:T(8,128)(2,1)S(1)}, bf16[128,512]{1,0:T(8,128)(2,1)S(1)}, u32[]{:S(2)}, u32[]{:S(2)}) %collective-permute-start.10) | collective-permute-done | bytes 131104 | tf_op jit(solution)/shard_map/ppermute | solution.py:52
  40.2 1.1 %collective-permute-done.12.refs_6_.refs_1_ = bf16[128,512]{1,0:T(8,128)(2,1)S(1)} collective-permute-done((bf16[128,512]{1,0:T(8,128)(2,1)S(1)}, bf16[128,512]{1,0:T(8,128)(2,1)S(1)}, u32[]{:S(2)}, u32[]{:S(2)}) %collective-permute-start.12) | collective-permute-done | bytes 131104 | tf_op jit(solution)/shard_map/ppermute | solution.py:52
  41.3 0.7 %terms.1 = (f32[4,128,512]{2,1,0:T(8,128)S(1)}, bf16[256,512]{1,0:T(8,128)(2,1)S(1)}, bf16[256,512]{1,0:T(8,128)(2,1)S(1)}) custom-call(bf16[128,1024]{1,0:T(8,128)(2,1)S(1)} %get-tuple-element.59.refs_0_, bf16[128,1024]{1,0:T(8,128)(2,1)S(1)} %collective-permute-done.4.refs_1_, bf16[128,1024]{1,0:T(8,128)(2,1)S(1)} %collective-permute-done.3.refs_2_, ...), custom_call_target="tpu_custom_call" | custom-call | tf_op jit(solution)/shard_map/terms/pallas_call | solution.py:27
  42.2 0.5 collective-permute-start.14
  43.1 1.6 %collective-permute-start.19 = (bf16[128,1024]{1,0:T(8,128)(2,1)S(1)}, bf16[128,1024]{1,0:T(8,128)(2,1)S(1)}, u32[]{:S(2)}, u32[]{:S(2)}) collective-permute-start(bf16[128,1024]{1,0:T(8,128)(2,1)S(1)} %get-tuple-element.84), channel_id=1, source_target_pairs={{0,16},{1,17},{16,0},{17,1},{2,18},{3,19},{18,2},{19,3},{4,20},{5,... | collective-permute-start | bytes 786440 | tf_op jit(solution)/shard_map/ppermute | solution.py:52
  44.7 0.6 collective-permute-start.18
  45.4 2.6 %collective-permute-start.16 = (bf16[128,512]{1,0:T(8,128)(2,1)S(1)}, bf16[128,512]{1,0:T(8,128)(2,1)S(1)}, u32[]{:S(2)}, u32[]{:S(2)}) collective-permute-start(bf16[128,512]{1,0:T(8,128)(2,1)S(1)} %get-tuple-element.78), channel_id=1, source_target_pairs={{0,6},{2,4},{4,2},{6,0},{1,7},{3,5},{5,3},{7,1},{8,14},{10,12},{12... | collective-permute-start | bytes 393224 | tf_op jit(solution)/shard_map/ppermute | solution.py:40
  47.9 1.4 %collective-permute-start.15 = (bf16[128,1024]{1,0:T(8,128)(2,1)S(1)}, bf16[128,1024]{1,0:T(8,128)(2,1)S(1)}, u32[]{:S(2)}, u32[]{:S(2)}) collective-permute-start(bf16[128,1024]{1,0:T(8,128)(2,1)S(1)} %columns.4), channel_id=1, source_target_pairs={{0,17},{1,16},{16,1},{17,0},{2,19},{3,18},{18,3},{19,2},{4,21},{5,... | collective-permute-start | bytes 786440 | tf_op jit(solution)/shard_map/ppermute | solution.py:52
  49.4 2.9 %collective-permute-done.19.refs_2_ = bf16[128,1024]{1,0:T(8,128)(2,1)S(1)} collective-permute-done((bf16[128,1024]{1,0:T(8,128)(2,1)S(1)}, bf16[128,1024]{1,0:T(8,128)(2,1)S(1)}, u32[]{:S(2)}, u32[]{:S(2)}) %collective-permute-start.19) | collective-permute-done | bytes 262176 | tf_op jit(solution)/shard_map/ppermute | solution.py:52
  52.3 6.1 %collective-permute-done.18.refs_1_ = bf16[128,1024]{1,0:T(8,128)(2,1)S(1)} collective-permute-done((bf16[128,1024]{1,0:T(8,128)(2,1)S(1)}, bf16[128,1024]{1,0:T(8,128)(2,1)S(1)}, u32[]{:S(2)}, u32[]{:S(2)}) %collective-permute-start.18) | collective-permute-done | bytes 262176 | tf_op jit(solution)/shard_map/ppermute | solution.py:52
  58.3 1.1 %unpack.1._ = bf16[128,4096]{1,0:T(8,128)(2,1)} custom-call(bf16[128,1024]{1,0:T(8,128)(2,1)S(1)} %columns.3.refs_0_, bf16[128,1024]{1,0:T(8,128)(2,1)S(1)} %collective-permute-done.18.refs_1_, bf16[128,1024]{1,0:T(8,128)(2,1)S(1)} %collective-permute-done.19.refs_2_), custom_call_target="tpu_custom_call" | custom-call | tf_op jit(solution)/shard_map/unpack/pallas_call | solution.py:110
  59.6 0.9 %finish.1 = (bf16[128,4096]{1,0:T(8,128)(2,1)}, f32[128,512]{1,0:T(8,128)}) custom-call(bf16[128,1024]{1,0:T(8,128)(2,1)S(1)} %collective-permute-done.15.block, f32[128,512]{1,0:T(8,128)S(1)} %final_sum.1.total, bf16[128,4096]{1,0:T(8,128)(2,1)} %unpack.1._), custom_call_target="tpu_custom_call", output_to_operand_aliasing={{0}: (2, {})} | custom-call | tf_op jit(solution)/shard_map/finish/pallas_call | solution.py:110
  (28 shorter events, 2.4 us)
Async XLA Ops:
  3.0 16.7 %collective-permute-start = (bf16[128,1024]{1,0:T(8,128)(2,1)}, bf16[128,1024]{1,0:T(8,128)(2,1)S(1)}, u32[]{:S(2)}, u32[]{:S(2)}) collective-permute-start(bf16[128,1024]{1,0:T(8,128)(2,1)} %get-tuple-element.48), channel_id=1, source_target_pairs={{0,17},{1,16},{16,1},{17,0},{2,19},{3,18},{18,3},{19,2},{4,21},{5,... | collective-permute-start | bytes 786440 | tf_op jit(solution)/shard_map/ppermute | solution.py:52
  7.0 12.7 %collective-permute-start.1 = (bf16[256,512]{1,0:T(8,128)(2,1)S(1)}, bf16[256,512]{1,0:T(8,128)(2,1)S(1)}, u32[]{:S(2)}, u32[]{:S(2)}) collective-permute-start(bf16[256,512]{1,0:T(8,128)(2,1)S(1)} %get-tuple-element.49.refs_0_), channel_id=1, source_target_pairs={{0,2},{2,0},{4,6},{6,4},{8,14},{10,12},{12,10},{14,8},{1,3},{3,1},... | collective-permute-start | bytes 786440 | tf_op jit(solution)/shard_map/ppermute | solution.py:143
  8.5 11.2 %collective-permute-start.2 = (bf16[128,512]{1,0:T(8,128)(2,1)S(1)}, bf16[128,512]{1,0:T(8,128)(2,1)S(1)}, u32[]{:S(2)}, u32[]{:S(2)}) collective-permute-start(bf16[128,512]{1,0:T(8,128)(2,1)S(1)} %get-tuple-element.50), channel_id=1, source_target_pairs={{0,4},{2,6},{4,0},{6,2},{1,5},{3,7},{5,1},{7,3},{8,12},{10,14},{12... | collective-permute-start | bytes 393224 | tf_op jit(solution)/shard_map/ppermute | solution.py:40
  11.1 10.2 %collective-permute-start.3 = (bf16[128,1024]{1,0:T(8,128)(2,1)}, bf16[128,1024]{1,0:T(8,128)(2,1)S(1)}, u32[]{:S(2)}, u32[]{:S(2)}) collective-permute-start(bf16[128,1024]{1,0:T(8,128)(2,1)} %get-tuple-element.52), channel_id=1, source_target_pairs={{0,16},{1,17},{16,0},{17,1},{2,18},{3,19},{18,2},{19,3},{4,20},{5,... | collective-permute-start | bytes 786440 | tf_op jit(solution)/shard_map/ppermute | solution.py:52
  11.7 9.7 %collective-permute-start.4 = (bf16[128,1024]{1,0:T(8,128)(2,1)S(1)}, bf16[128,1024]{1,0:T(8,128)(2,1)S(1)}, u32[]{:S(2)}, u32[]{:S(2)}) collective-permute-start(bf16[128,1024]{1,0:T(8,128)(2,1)S(1)} %get-tuple-element.53), channel_id=1, source_target_pairs={{0,1},{1,0},{16,17},{17,16},{2,3},{3,2},{18,19},{19,18},{4,5},{5,4... | collective-permute-start | bytes 786440 | tf_op jit(solution)/shard_map/ppermute | solution.py:52
  19.7 2.6 %collective-permute-start.5 = (bf16[192,512]{1,0:T(8,128)(2,1)S(1)}, bf16[192,512]{1,0:T(8,128)(2,1)S(1)}, u32[]{:S(2)}, u32[]{:S(2)}) collective-permute-start(bf16[192,512]{1,0:T(8,128)(2,1)S(1)} %get-tuple-element.57), channel_id=1, source_target_pairs={{0,8},{8,0},{1,9},{9,1},{2,10},{10,2},{3,11},{11,3},{4,12},{12,4},... | collective-permute-start | bytes 589832 | tf_op jit(solution)/shard_map/ppermute | solution.py:44
  21.3 1.4 %collective-permute-start.6 = (bf16[192,512]{1,0:T(8,128)(2,1)S(1)}, bf16[192,512]{1,0:T(8,128)(2,1)S(1)}, u32[]{:S(2)}, u32[]{:S(2)}) collective-permute-start(bf16[192,512]{1,0:T(8,128)(2,1)S(1)} %get-tuple-element.58), channel_id=1, source_target_pairs={{0,8},{8,0},{1,9},{9,1},{2,10},{10,2},{3,11},{11,3},{4,12},{12,4},... | collective-permute-start | bytes 589832 | tf_op jit(solution)/shard_map/ppermute | solution.py:44
  23.4 7.3 %collective-permute-start.7 = (bf16[128,512]{1,0:T(8,128)(2,1)S(1)}, bf16[128,512]{1,0:T(8,128)(2,1)S(1)}, u32[]{:S(2)}, u32[]{:S(2)}) collective-permute-start(bf16[128,512]{1,0:T(8,128)(2,1)S(1)} %get-tuple-element.65), channel_id=1, source_target_pairs={{0,17},{1,16},{16,1},{17,0},{2,19},{3,18},{18,3},{19,2},{4,21},{5,... | collective-permute-start | bytes 393224 | tf_op jit(solution)/shard_map/ppermute | solution.py:52
  23.9 8.2 %collective-permute-start.8 = (bf16[128,512]{1,0:T(8,128)(2,1)S(1)}, bf16[128,512]{1,0:T(8,128)(2,1)S(1)}, u32[]{:S(2)}, u32[]{:S(2)}) collective-permute-start(bf16[128,512]{1,0:T(8,128)(2,1)S(1)} %get-tuple-element.66), channel_id=1, source_target_pairs={{0,1},{1,0},{16,17},{17,16},{2,3},{3,2},{18,19},{19,18},{4,5},{5,4... | collective-permute-start | bytes 393224 | tf_op jit(solution)/shard_map/ppermute | solution.py:52
  25.4 6.7 %copy-start = (bf16[128,512]{1,0:T(8,128)(2,1)S(1)}, bf16[128,512]{1,0:T(8,128)(2,1)}, u32[]{:S(2)}) copy-start(bf16[128,512]{1,0:T(8,128)(2,1)} %refs_4_.1) | copy-start | bytes 393220
  25.4 6.7 %collective-permute-start.9 = (bf16[128,512]{1,0:T(8,128)(2,1)S(1)}, bf16[128,512]{1,0:T(8,128)(2,1)S(1)}, u32[]{:S(2)}, u32[]{:S(2)}) collective-permute-start(bf16[128,512]{1,0:T(8,128)(2,1)S(1)} %get-tuple-element.67), channel_id=1, source_target_pairs={{0,16},{1,17},{16,0},{17,1},{2,18},{3,19},{18,2},{19,3},{4,20},{5,... | collective-permute-start | bytes 393224 | tf_op jit(solution)/shard_map/ppermute | solution.py:52
  32.4 7.3 %collective-permute-start.10 = (bf16[128,512]{1,0:T(8,128)(2,1)S(1)}, bf16[128,512]{1,0:T(8,128)(2,1)S(1)}, u32[]{:S(2)}, u32[]{:S(2)}) collective-permute-start(bf16[128,512]{1,0:T(8,128)(2,1)S(1)} %get-tuple-element.68.refs_0_.refs_4_), channel_id=1, source_target_pairs={{0,17},{1,16},{16,1},{17,0},{2,19},{3,18},{18,3},{19,2},{4,21},{5,... | collective-permute-start | bytes 393224 | tf_op jit(solution)/shard_map/ppermute | solution.py:52
  33.7 7.6 %collective-permute-start.12 = (bf16[128,512]{1,0:T(8,128)(2,1)S(1)}, bf16[128,512]{1,0:T(8,128)(2,1)S(1)}, u32[]{:S(2)}, u32[]{:S(2)}) collective-permute-start(bf16[128,512]{1,0:T(8,128)(2,1)S(1)} %get-tuple-element.68.refs_0_.refs_4_), channel_id=1, source_target_pairs={{0,16},{1,17},{16,0},{17,1},{2,18},{3,19},{18,2},{19,3},{4,20},{5,... | collective-permute-start | bytes 393224 | tf_op jit(solution)/shard_map/ppermute | solution.py:52
  35.2 6.1 %collective-permute-start.11 = (bf16[128,512]{1,0:T(8,128)(2,1)S(1)}, bf16[128,512]{1,0:T(8,128)(2,1)S(1)}, u32[]{:S(2)}, u32[]{:S(2)}) collective-permute-start(bf16[128,512]{1,0:T(8,128)(2,1)S(1)} %get-tuple-element.68.refs_0_.refs_4_), channel_id=1, source_target_pairs={{0,1},{1,0},{16,17},{17,16},{2,3},{3,2},{18,19},{19,18},{4,5},{5,4... | collective-permute-start | bytes 393224 | tf_op jit(solution)/shard_map/ppermute | solution.py:52
  42.1 3.2 %collective-permute-start.13 = (bf16[256,512]{1,0:T(8,128)(2,1)S(1)}, bf16[256,512]{1,0:T(8,128)(2,1)S(1)}, u32[]{:S(2)}, u32[]{:S(2)}) collective-permute-start(bf16[256,512]{1,0:T(8,128)(2,1)S(1)} %get-tuple-element.75), channel_id=1, source_target_pairs={{0,8},{8,0},{1,9},{9,1},{2,10},{10,2},{3,11},{11,3},{4,12},{12,4},... | collective-permute-start | bytes 786440 | tf_op jit(solution)/shard_map/ppermute | solution.py:44
  42.2 3.1 %collective-permute-start.14 = (bf16[256,512]{1,0:T(8,128)(2,1)S(1)}, bf16[256,512]{1,0:T(8,128)(2,1)S(1)}, u32[]{:S(2)}, u32[]{:S(2)}) collective-permute-start(bf16[256,512]{1,0:T(8,128)(2,1)S(1)} %get-tuple-element.76), channel_id=1, source_target_pairs={{0,8},{8,0},{1,9},{9,1},{2,10},{10,2},{3,11},{11,3},{4,12},{12,4},... | collective-permute-start | bytes 786440 | tf_op jit(solution)/shard_map/ppermute | solution.py:44
  43.1 9.1 %collective-permute-start.19 = (bf16[128,1024]{1,0:T(8,128)(2,1)S(1)}, bf16[128,1024]{1,0:T(8,128)(2,1)S(1)}, u32[]{:S(2)}, u32[]{:S(2)}) collective-permute-start(bf16[128,1024]{1,0:T(8,128)(2,1)S(1)} %get-tuple-element.84), channel_id=1, source_target_pairs={{0,16},{1,17},{16,0},{17,1},{2,18},{3,19},{18,2},{19,3},{4,20},{5,... | collective-permute-start | bytes 786440 | tf_op jit(solution)/shard_map/ppermute | solution.py:52
  44.7 13.6 %collective-permute-start.18 = (bf16[128,1024]{1,0:T(8,128)(2,1)S(1)}, bf16[128,1024]{1,0:T(8,128)(2,1)S(1)}, u32[]{:S(2)}, u32[]{:S(2)}) collective-permute-start(bf16[128,1024]{1,0:T(8,128)(2,1)S(1)} %get-tuple-element.83), channel_id=1, source_target_pairs={{0,1},{1,0},{16,17},{17,16},{2,3},{3,2},{18,19},{19,18},{4,5},{5,4... | collective-permute-start | bytes 786440 | tf_op jit(solution)/shard_map/ppermute | solution.py:52
  45.4 14.0 %collective-permute-start.16 = (bf16[128,512]{1,0:T(8,128)(2,1)S(1)}, bf16[128,512]{1,0:T(8,128)(2,1)S(1)}, u32[]{:S(2)}, u32[]{:S(2)}) collective-permute-start(bf16[128,512]{1,0:T(8,128)(2,1)S(1)} %get-tuple-element.78), channel_id=1, source_target_pairs={{0,6},{2,4},{4,2},{6,0},{1,7},{3,5},{5,3},{7,1},{8,14},{10,12},{12... | collective-permute-start | bytes 393224 | tf_op jit(solution)/shard_map/ppermute | solution.py:40
  47.9 11.5 %collective-permute-start.17 = (bf16[128,512]{1,0:T(8,128)(2,1)S(1)}, bf16[128,512]{1,0:T(8,128)(2,1)S(1)}, u32[]{:S(2)}, u32[]{:S(2)}) collective-permute-start(bf16[128,512]{1,0:T(8,128)(2,1)S(1)} %get-tuple-element.79), channel_id=1, source_target_pairs={{0,4},{2,6},{4,0},{6,2},{1,5},{3,7},{5,1},{7,3},{8,12},{10,14},{12... | collective-permute-start | bytes 393224 | tf_op jit(solution)/shard_map/ppermute | solution.py:40
  47.9 11.7 %collective-permute-start.15 = (bf16[128,1024]{1,0:T(8,128)(2,1)S(1)}, bf16[128,1024]{1,0:T(8,128)(2,1)S(1)}, u32[]{:S(2)}, u32[]{:S(2)}) collective-permute-start(bf16[128,1024]{1,0:T(8,128)(2,1)S(1)} %columns.4), channel_id=1, source_target_pairs={{0,17},{1,16},{16,1},{17,0},{2,19},{3,18},{18,3},{19,2},{4,21},{5,... | collective-permute-start | bytes 786440 | tf_op jit(solution)/shard_map/ppermute | solution.py:52
  52.3 7.3 %collective-permute-start.20 = (bf16[128,512]{1,0:T(8,128)(2,1)S(1)}, bf16[128,512]{1,0:T(8,128)(2,1)S(1)}, u32[]{:S(2)}, u32[]{:S(2)}) collective-permute-start(bf16[128,512]{1,0:T(8,128)(2,1)S(1)} %get-tuple-element.89), channel_id=1, source_target_pairs={{0,2},{2,0},{4,6},{6,4},{1,3},{3,1},{5,7},{7,5},{8,10},{10,8},{12,... | collective-permute-start | bytes 393224 | tf_op jit(solution)/shard_map/ppermute | solution.py:40

commit v16 on v15

--- a/solution.py
+++ b/solution.py
@@ -96,13 +96,15 @@
         copy.wait()
 
 
-def unpack_body(*refs):
+def unpack_body(fars, *refs):
     *blocks, whole, done = refs
-    run_copies([move for far, block in enumerate(blocks) for move in unpack_moves(far, block, whole)], done)
-
-
-def finish_body(block, total, _, whole, weight_grad, done):
-    run_copies([(total, weight_grad), *unpack_moves(MEMBERS - 1, block, whole)], done)
+    run_copies([move for far, block in zip(fars, blocks) for move in unpack_moves(far, block, whole)], done)
+
+
+def finish_body(fars, *refs):
+    *blocks, total, _, whole, weight_grad, done = refs
+    moves = [move for far, block in zip(fars, blocks) for move in unpack_moves(far, block, whole)]
+    run_copies([(total, weight_grad), *moves], done)
 
 
 def placing_call(name, body, out_shapes, blocks, held=()):
@@ -351,13 +353,19 @@
     closest, back_2 = lax.optimization_barrier((closest, back_2))
     met = [sums[0]] + [along(piece, line - i) for i, piece in enumerate(sums) if i]
     whole_shape = shape((tok_rows, width), bf16)
-    (input_grad,) = placing_call("unpack", unpack_body, [whole_shape], (column_0, back_1, back_2))
-    met, input_grad = lax.optimization_barrier((met, input_grad))
+    (input_grad,) = placing_call(
+        "unpack", functools.partial(unpack_body, (0, 2)), [whole_shape], (column_0, back_2)
+    )
+    met, back_1, input_grad = lax.optimization_barrier((met, back_1, input_grad))
     sum_shape = shape((rows, key_cols), f32)
     far_sum = local_call("far_sum", sum_body, sum_shape, *met, flops=24 * flops)
     total = local_call("final_sum", sum_body, sum_shape, far_sum, along(closest, 1), moved=0)
     input_grad, weight_grad = placing_call(
-        "finish", finish_body, [whole_shape, shape(total.shape, f32)], (back_3, total), (input_grad,)
+        "finish",
+        functools.partial(finish_body, (1, 3)),
+        [whole_shape, shape(total.shape, f32)],
+        (back_1, back_3, total),
+        (input_grad,),
     )
     if outer > 1:
         weight_grad = lax.psum_scatter(weight_grad, "outer", scatter_dimension=0, tiled=True)

time: 60.7 us -> 60.9 us (level)
    ppermute x4, waiting for transfers between devices: 7.67 us -> 8.76 us  [along(): lax.ppermute(block, 'line', [(i, i ^ step) for i in range(lax.axis_size('...]
    ppermute x12, waiting for transfers between devices: 17.6 us -> 16.7 us  [to_member(): lax.ppermute(block, ('side', 'pair'), [(i, i ^ far) for i in range(MEMBER...]
where the time goes in v16:
time: 60.9 us; the launch traced here: 60.7 us
  waiting for transfers between devices  26.8 us (44%)
  starting transfers between devices  24.6 us (40%)
  Pallas kernels  8.53 us (14%)
  between operations  0.76 us (1%)
    ppermute x12, waiting for transfers between devices, to_member(): lax.ppermute(block, ('side', 'pair'), [(i, i ^ far) for i in range(MEMBER...  16.7 us
    ppermute x12, starting transfers between devices, to_member(): lax.ppermute(block, ('side', 'pair'), [(i, i ^ far) for i in range(MEMBER...  15.7 us
    ppermute x4, waiting for transfers between devices, along(): lax.ppermute(block, 'line', [(i, i ^ step) for i in range(lax.axis_size('...  8.76 us
    pallas_call x14, Pallas kernels, local_call(): pl.pallas_call(body, name=name, out_shape=out_shapes, in_specs=[pl.BlockS...  6.54 us
    ppermute x4, starting transfers between devices, along(): lax.ppermute(block, 'line', [(i, i ^ step) for i in range(lax.axis_size('...  5.16 us
    ppermute x4, starting transfers between devices, to_twin(): return lax.ppermute(block, 'twin', [(0, 1), (1, 0)])  2.19 us
    pallas_call x2, Pallas kernels, placing_call(): pl.pallas_call(body, name=name, out_shape=out_shapes, in_specs=[pl.BlockS...  1.99 us
    ppermute x1, starting transfers between devices, parted(): return lax.ppermute(block, ('twin', 'line'), list(enumerate(to)))  1.58 us
  transfers between devices with their start and end apart: 21, of which 10 were waited for; matrix products, arithmetic and copies ran while one was open for 0% of the time, Pallas kernels for 6%

profile of v16, /device:TPU:0, one launch (start us, length us, event | category | flops | bytes accessed | tf_op | source)
XLA Modules:
  0.0 60.7 jit_solution(5379266530304067599)
XLA Ops:
  0.6 2.4 %front.1 = (bf16[256,512]{1,0:T(8,128)(2,1)S(1)}, bf16[128,512]{1,0:T(8,128)(2,1)S(1)}, bf16[128,1024]{1,0:T(8,128)(2,1)S(1)}, bf16[128,1024]{1,0:T(8,128)(2,1)S...) custom-call(bf16[128,4096]{1,0:T(8,128)(2,1)} %tokens.1, bf16[512,512]{1,0:T(8,128)(2,1)} %shard.1), custom_call_target="tpu_custom_call" | custom-call | bytes 1572864 | tf_op jit(solution)/shard_map/front/pallas_call | solution.py:27
  3.0 4.0 %collective-permute-start = (bf16[128,1024]{1,0:T(8,128)(2,1)}, bf16[128,1024]{1,0:T(8,128)(2,1)S(1)}, u32[]{:S(2)}, u32[]{:S(2)}) collective-permute-start(bf16[128,1024]{1,0:T(8,128)(2,1)} %get-tuple-element.49), channel_id=1, source_target_pairs={{0,17},{1,16},{16,1},{17,0},{2,19},{3,18},{18,3},{19,2},{4,21},{5,... | collective-permute-start | bytes 786440 | tf_op jit(solution)/shard_map/ppermute | solution.py:52
  7.0 1.6 %collective-permute-start.1 = (bf16[256,512]{1,0:T(8,128)(2,1)S(1)}, bf16[256,512]{1,0:T(8,128)(2,1)S(1)}, u32[]{:S(2)}, u32[]{:S(2)}) collective-permute-start(bf16[256,512]{1,0:T(8,128)(2,1)S(1)} %get-tuple-element.50.refs_0_), channel_id=1, source_target_pairs={{0,2},{2,0},{4,6},{6,4},{8,14},{10,12},{12,10},{14,8},{1,3},{3,1},... | collective-permute-start | bytes 786440 | tf_op jit(solution)/shard_map/ppermute | solution.py:145
  8.5 2.6 %collective-permute-start.2 = (bf16[128,512]{1,0:T(8,128)(2,1)S(1)}, bf16[128,512]{1,0:T(8,128)(2,1)S(1)}, u32[]{:S(2)}, u32[]{:S(2)}) collective-permute-start(bf16[128,512]{1,0:T(8,128)(2,1)S(1)} %get-tuple-element.51), channel_id=1, source_target_pairs={{0,4},{2,6},{4,0},{6,2},{1,5},{3,7},{5,1},{7,3},{8,12},{10,14},{12... | collective-permute-start | bytes 393224 | tf_op jit(solution)/shard_map/ppermute | solution.py:40
  11.1 0.5 collective-permute-start.3
  11.7 0.5 collective-permute-start.4
  12.2 7.5 %collective-permute-done.2.refs_1_.refs_2_ = bf16[128,512]{1,0:T(8,128)(2,1)S(1)} collective-permute-done((bf16[128,512]{1,0:T(8,128)(2,1)S(1)}, bf16[128,512]{1,0:T(8,128)(2,1)S(1)}, u32[]{:S(2)}, u32[]{:S(2)}) %collective-permute-start.2) | collective-permute-done | bytes 131104 | tf_op jit(solution)/shard_map/ppermute | solution.py:40
  19.7 1.5 %collective-permute-start.5 = (bf16[192,512]{1,0:T(8,128)(2,1)S(1)}, bf16[192,512]{1,0:T(8,128)(2,1)S(1)}, u32[]{:S(2)}, u32[]{:S(2)}) collective-permute-start(bf16[192,512]{1,0:T(8,128)(2,1)S(1)} %get-tuple-element.58), channel_id=1, source_target_pairs={{0,8},{8,0},{1,9},{9,1},{2,10},{10,2},{3,11},{11,3},{4,12},{12,4},... | collective-permute-start | bytes 589832 | tf_op jit(solution)/shard_map/ppermute | solution.py:44
  21.4 1.0 %collective-permute-done.5.refs_3_ = bf16[192,512]{1,0:T(8,128)(2,1)S(1)} collective-permute-done((bf16[192,512]{1,0:T(8,128)(2,1)S(1)}, bf16[192,512]{1,0:T(8,128)(2,1)S(1)}, u32[]{:S(2)}, u32[]{:S(2)}) %collective-permute-start.5) | collective-permute-done | bytes 196640 | tf_op jit(solution)/shard_map/ppermute | solution.py:44
  22.8 0.6 share.3
  23.4 0.5 collective-permute-start.7
  23.9 1.5 %collective-permute-start.8 = (bf16[128,512]{1,0:T(8,128)(2,1)S(1)}, bf16[128,512]{1,0:T(8,128)(2,1)S(1)}, u32[]{:S(2)}, u32[]{:S(2)}) collective-permute-start(bf16[128,512]{1,0:T(8,128)(2,1)S(1)} %get-tuple-element.67), channel_id=1, source_target_pairs={{0,1},{1,0},{16,17},{17,16},{2,3},{3,2},{18,19},{19,18},{4,5},{5,4... | collective-permute-start | bytes 393224 | tf_op jit(solution)/shard_map/ppermute | solution.py:52
  25.4 1.5 %collective-permute-start.9 = (bf16[128,512]{1,0:T(8,128)(2,1)S(1)}, bf16[128,512]{1,0:T(8,128)(2,1)S(1)}, u32[]{:S(2)}, u32[]{:S(2)}) collective-permute-start(bf16[128,512]{1,0:T(8,128)(2,1)S(1)} %get-tuple-element.68), channel_id=1, source_target_pairs={{0,16},{1,17},{16,0},{17,1},{2,18},{3,19},{18,2},{19,3},{4,20},{5,... | collective-permute-start | bytes 393224 | tf_op jit(solution)/shard_map/ppermute | solution.py:52
  27.3 3.5 %collective-permute-done.7.refs_1_ = bf16[128,512]{1,0:T(8,128)(2,1)S(1)} collective-permute-done((bf16[128,512]{1,0:T(8,128)(2,1)S(1)}, bf16[128,512]{1,0:T(8,128)(2,1)S(1)}, u32[]{:S(2)}, u32[]{:S(2)}) %collective-permute-start.7) | collective-permute-done | bytes 131104 | tf_op jit(solution)/shard_map/ppermute | solution.py:52
  30.7 1.4 %collective-permute-done.8.refs_2_ = bf16[128,512]{1,0:T(8,128)(2,1)S(1)} collective-permute-done((bf16[128,512]{1,0:T(8,128)(2,1)S(1)}, bf16[128,512]{1,0:T(8,128)(2,1)S(1)}, u32[]{:S(2)}, u32[]{:S(2)}) %collective-permute-start.8) | collective-permute-done | bytes 131104 | tf_op jit(solution)/shard_map/ppermute | solution.py:52
  32.4 1.3 %collective-permute-start.10 = (bf16[128,512]{1,0:T(8,128)(2,1)S(1)}, bf16[128,512]{1,0:T(8,128)(2,1)S(1)}, u32[]{:S(2)}, u32[]{:S(2)}) collective-permute-start(bf16[128,512]{1,0:T(8,128)(2,1)S(1)} %get-tuple-element.69.refs_0_.refs_4_), channel_id=1, source_target_pairs={{0,17},{1,16},{16,1},{17,0},{2,19},{3,18},{18,3},{19,2},{4,21},{5,... | collective-permute-start | bytes 393224 | tf_op jit(solution)/shard_map/ppermute | solution.py:52
  33.7 1.5 %collective-permute-start.12 = (bf16[128,512]{1,0:T(8,128)(2,1)S(1)}, bf16[128,512]{1,0:T(8,128)(2,1)S(1)}, u32[]{:S(2)}, u32[]{:S(2)}) collective-permute-start(bf16[128,512]{1,0:T(8,128)(2,1)S(1)} %get-tuple-element.69.refs_0_.refs_4_), channel_id=1, source_target_pairs={{0,16},{1,17},{16,0},{17,1},{2,18},{3,19},{18,2},{19,3},{4,20},{5,... | collective-permute-start | bytes 393224 | tf_op jit(solution)/shard_map/ppermute | solution.py:52
  35.2 0.7 %collective-permute-start.11 = (bf16[128,512]{1,0:T(8,128)(2,1)S(1)}, bf16[128,512]{1,0:T(8,128)(2,1)S(1)}, u32[]{:S(2)}, u32[]{:S(2)}) collective-permute-start(bf16[128,512]{1,0:T(8,128)(2,1)S(1)} %get-tuple-element.69.refs_0_.refs_4_), channel_id=1, source_target_pairs={{0,1},{1,0},{16,17},{17,16},{2,3},{3,2},{18,19},{19,18},{4,5},{5,4... | collective-permute-start | bytes 393224 | tf_op jit(solution)/shard_map/ppermute | solution.py:52
  35.9 0.7 %emit.1 = bf16[128,512]{1,0:T(8,128)(2,1)} custom-call(bf16[128,512]{1,0:T(8,128)(2,1)S(1)} %get-tuple-element.70.held), custom_call_target="tpu_custom_call" | custom-call | bytes 131072 | tf_op jit(solution)/shard_map/emit/pallas_call | solution.py:27
  37.1 2.6 %collective-permute-done.10.refs_0_.refs_7_ = bf16[128,512]{1,0:T(8,128)(2,1)S(1)} collective-permute-done((bf16[128,512]{1,0:T(8,128)(2,1)S(1)}, bf16[128,512]{1,0:T(8,128)(2,1)S(1)}, u32[]{:S(2)}, u32[]{:S(2)}) %collective-permute-start.10) | collective-permute-done | bytes 131104 | tf_op jit(solution)/shard_map/ppermute | solution.py:52
  40.2 1.1 %collective-permute-done.12.refs_6_.refs_1_ = bf16[128,512]{1,0:T(8,128)(2,1)S(1)} collective-permute-done((bf16[128,512]{1,0:T(8,128)(2,1)S(1)}, bf16[128,512]{1,0:T(8,128)(2,1)S(1)}, u32[]{:S(2)}, u32[]{:S(2)}) %collective-permute-start.12) | collective-permute-done | bytes 131104 | tf_op jit(solution)/shard_map/ppermute | solution.py:52
  41.3 0.7 %terms.1 = (f32[4,128,512]{2,1,0:T(8,128)S(1)}, bf16[256,512]{1,0:T(8,128)(2,1)S(1)}, bf16[256,512]{1,0:T(8,128)(2,1)S(1)}) custom-call(bf16[128,1024]{1,0:T(8,128)(2,1)S(1)} %get-tuple-element.60.refs_0_, bf16[128,1024]{1,0:T(8,128)(2,1)S(1)} %collective-permute-done.4.refs_1_, bf16[128,1024]{1,0:T(8,128)(2,1)S(1)} %collective-permute-done.3.refs_2_, ...), custom_call_target="tpu_custom_call" | custom-call | tf_op jit(solution)/shard_map/terms/pallas_call | solution.py:27
  42.2 0.5 collective-permute-start.14
  43.1 1.6 %collective-permute-start.18 = (bf16[128,1024]{1,0:T(8,128)(2,1)S(1)}, bf16[128,1024]{1,0:T(8,128)(2,1)S(1)}, u32[]{:S(2)}, u32[]{:S(2)}) collective-permute-start(bf16[128,1024]{1,0:T(8,128)(2,1)S(1)} %get-tuple-element.83), channel_id=1, source_target_pairs={{0,16},{1,17},{16,0},{17,1},{2,18},{3,19},{18,2},{19,3},{4,20},{5,... | collective-permute-start | bytes 786440 | tf_op jit(solution)/shard_map/ppermute | solution.py:52
  44.7 0.6 collective-permute-start.17
  45.4 2.6 %collective-permute-start.15 = (bf16[128,512]{1,0:T(8,128)(2,1)S(1)}, bf16[128,512]{1,0:T(8,128)(2,1)S(1)}, u32[]{:S(2)}, u32[]{:S(2)}) collective-permute-start(bf16[128,512]{1,0:T(8,128)(2,1)S(1)} %get-tuple-element.78), channel_id=1, source_target_pairs={{0,6},{2,4},{4,2},{6,0},{1,7},{3,5},{5,3},{7,1},{8,14},{10,12},{12... | collective-permute-start | bytes 393224 | tf_op jit(solution)/shard_map/ppermute | solution.py:40
  47.9 1.4 %collective-permute-start.19 = (bf16[128,1024]{1,0:T(8,128)(2,1)S(1)}, bf16[128,1024]{1,0:T(8,128)(2,1)S(1)}, u32[]{:S(2)}, u32[]{:S(2)}) collective-permute-start(bf16[128,1024]{1,0:T(8,128)(2,1)S(1)} %columns.4), channel_id=1, source_target_pairs={{0,17},{1,16},{16,1},{17,0},{2,19},{3,18},{18,3},{19,2},{4,21},{5,... | collective-permute-start | bytes 786440 | tf_op jit(solution)/shard_map/ppermute | solution.py:52
  49.4 2.9 %collective-permute-done.18.refs_1_ = bf16[128,1024]{1,0:T(8,128)(2,1)S(1)} collective-permute-done((bf16[128,1024]{1,0:T(8,128)(2,1)S(1)}, bf16[128,1024]{1,0:T(8,128)(2,1)S(1)}, u32[]{:S(2)}, u32[]{:S(2)}) %collective-permute-start.18) | collective-permute-done | bytes 262176 | tf_op jit(solution)/shard_map/ppermute | solution.py:52
  52.3 0.9 %unpack.1.refs_3_ = bf16[128,4096]{1,0:T(8,128)(2,1)} custom-call(bf16[128,1024]{1,0:T(8,128)(2,1)S(1)} %columns.3.refs_0_, bf16[128,1024]{1,0:T(8,128)(2,1)S(1)} %collective-permute-done.18.refs_1_), custom_call_target="tpu_custom_call" | custom-call | tf_op jit(solution)/shard_map/unpack/pallas_call | solution.py:112
  53.2 5.1 %collective-permute-done.17.refs_0_ = bf16[128,1024]{1,0:T(8,128)(2,1)S(1)} collective-permute-done((bf16[128,1024]{1,0:T(8,128)(2,1)S(1)}, bf16[128,1024]{1,0:T(8,128)(2,1)S(1)}, u32[]{:S(2)}, u32[]{:S(2)}) %collective-permute-start.17) | collective-permute-done | bytes 262176 | tf_op jit(solution)/shard_map/ppermute | solution.py:52
  58.4 1.2 %collective-permute-done.20.refs_1_ = bf16[128,512]{1,0:T(8,128)(2,1)S(1)} collective-permute-done((bf16[128,512]{1,0:T(8,128)(2,1)S(1)}, bf16[128,512]{1,0:T(8,128)(2,1)S(1)}, u32[]{:S(2)}, u32[]{:S(2)}) %collective-permute-start.20) | collective-permute-done | bytes 131104 | tf_op jit(solution)/shard_map/ppermute | solution.py:40
  59.6 1.1 %finish.1 = (bf16[128,4096]{1,0:T(8,128)(2,1)}, f32[128,512]{1,0:T(8,128)}) custom-call(bf16[128,1024]{1,0:T(8,128)(2,1)S(1)} %collective-permute-done.17.refs_0_, bf16[128,1024]{1,0:T(8,128)(2,1)S(1)} %collective-permute-done.19.refs_1_, f32[128,512]{1,0:T(8,128)S(1)} %final_sum.1.refs_2_, ...), custom_call_target="tpu_custom_call", output_to_operand_aliasing={{0}: (3, {})} | custom-call | tf_op jit(solution)/shard_map/finish/pallas_call | solution.py:112
  (28 shorter events, 2.8 us)
Async XLA Ops:
  3.0 16.7 %collective-permute-start = (bf16[128,1024]{1,0:T(8,128)(2,1)}, bf16[128,1024]{1,0:T(8,128)(2,1)S(1)}, u32[]{:S(2)}, u32[]{:S(2)}) collective-permute-start(bf16[128,1024]{1,0:T(8,128)(2,1)} %get-tuple-element.49), channel_id=1, source_target_pairs={{0,17},{1,16},{16,1},{17,0},{2,19},{3,18},{18,3},{19,2},{4,21},{5,... | collective-permute-start | bytes 786440 | tf_op jit(solution)/shard_map/ppermute | solution.py:52
  7.0 12.7 %collective-permute-start.1 = (bf16[256,512]{1,0:T(8,128)(2,1)S(1)}, bf16[256,512]{1,0:T(8,128)(2,1)S(1)}, u32[]{:S(2)}, u32[]{:S(2)}) collective-permute-start(bf16[256,512]{1,0:T(8,128)(2,1)S(1)} %get-tuple-element.50.refs_0_), channel_id=1, source_target_pairs={{0,2},{2,0},{4,6},{6,4},{8,14},{10,12},{12,10},{14,8},{1,3},{3,1},... | collective-permute-start | bytes 786440 | tf_op jit(solution)/shard_map/ppermute | solution.py:145
  8.5 11.2 %collective-permute-start.2 = (bf16[128,512]{1,0:T(8,128)(2,1)S(1)}, bf16[128,512]{1,0:T(8,128)(2,1)S(1)}, u32[]{:S(2)}, u32[]{:S(2)}) collective-permute-start(bf16[128,512]{1,0:T(8,128)(2,1)S(1)} %get-tuple-element.51), channel_id=1, source_target_pairs={{0,4},{2,6},{4,0},{6,2},{1,5},{3,7},{5,1},{7,3},{8,12},{10,14},{12... | collective-permute-start | bytes 393224 | tf_op jit(solution)/shard_map/ppermute | solution.py:40
  11.1 10.2 %collective-permute-start.3 = (bf16[128,1024]{1,0:T(8,128)(2,1)}, bf16[128,1024]{1,0:T(8,128)(2,1)S(1)}, u32[]{:S(2)}, u32[]{:S(2)}) collective-permute-start(bf16[128,1024]{1,0:T(8,128)(2,1)} %get-tuple-element.53), channel_id=1, source_target_pairs={{0,16},{1,17},{16,0},{17,1},{2,18},{3,19},{18,2},{19,3},{4,20},{5,... | collective-permute-start | bytes 786440 | tf_op jit(solution)/shard_map/ppermute | solution.py:52
  11.7 9.7 %collective-permute-start.4 = (bf16[128,1024]{1,0:T(8,128)(2,1)S(1)}, bf16[128,1024]{1,0:T(8,128)(2,1)S(1)}, u32[]{:S(2)}, u32[]{:S(2)}) collective-permute-start(bf16[128,1024]{1,0:T(8,128)(2,1)S(1)} %get-tuple-element.54), channel_id=1, source_target_pairs={{0,1},{1,0},{16,17},{17,16},{2,3},{3,2},{18,19},{19,18},{4,5},{5,4... | collective-permute-start | bytes 786440 | tf_op jit(solution)/shard_map/ppermute | solution.py:52
  19.7 2.6 %collective-permute-start.5 = (bf16[192,512]{1,0:T(8,128)(2,1)S(1)}, bf16[192,512]{1,0:T(8,128)(2,1)S(1)}, u32[]{:S(2)}, u32[]{:S(2)}) collective-permute-start(bf16[192,512]{1,0:T(8,128)(2,1)S(1)} %get-tuple-element.58), channel_id=1, source_target_pairs={{0,8},{8,0},{1,9},{9,1},{2,10},{10,2},{3,11},{11,3},{4,12},{12,4},... | collective-permute-start | bytes 589832 | tf_op jit(solution)/shard_map/ppermute | solution.py:44
  21.3 1.4 %collective-permute-start.6 = (bf16[192,512]{1,0:T(8,128)(2,1)S(1)}, bf16[192,512]{1,0:T(8,128)(2,1)S(1)}, u32[]{:S(2)}, u32[]{:S(2)}) collective-permute-start(bf16[192,512]{1,0:T(8,128)(2,1)S(1)} %get-tuple-element.59), channel_id=1, source_target_pairs={{0,8},{8,0},{1,9},{9,1},{2,10},{10,2},{3,11},{11,3},{4,12},{12,4},... | collective-permute-start | bytes 589832 | tf_op jit(solution)/shard_map/ppermute | solution.py:44
  23.4 7.3 %collective-permute-start.7 = (bf16[128,512]{1,0:T(8,128)(2,1)S(1)}, bf16[128,512]{1,0:T(8,128)(2,1)S(1)}, u32[]{:S(2)}, u32[]{:S(2)}) collective-permute-start(bf16[128,512]{1,0:T(8,128)(2,1)S(1)} %get-tuple-element.66), channel_id=1, source_target_pairs={{0,17},{1,16},{16,1},{17,0},{2,19},{3,18},{18,3},{19,2},{4,21},{5,... | collective-permute-start | bytes 393224 | tf_op jit(solution)/shard_map/ppermute | solution.py:52
  23.9 8.2 %collective-permute-start.8 = (bf16[128,512]{1,0:T(8,128)(2,1)S(1)}, bf16[128,512]{1,0:T(8,128)(2,1)S(1)}, u32[]{:S(2)}, u32[]{:S(2)}) collective-permute-start(bf16[128,512]{1,0:T(8,128)(2,1)S(1)} %get-tuple-element.67), channel_id=1, source_target_pairs={{0,1},{1,0},{16,17},{17,16},{2,3},{3,2},{18,19},{19,18},{4,5},{5,4... | collective-permute-start | bytes 393224 | tf_op jit(solution)/shard_map/ppermute | solution.py:52
  25.4 6.7 %copy-start = (bf16[128,512]{1,0:T(8,128)(2,1)S(1)}, bf16[128,512]{1,0:T(8,128)(2,1)}, u32[]{:S(2)}) copy-start(bf16[128,512]{1,0:T(8,128)(2,1)} %refs_4_.1) | copy-start | bytes 393220
  25.4 6.7 %collective-permute-start.9 = (bf16[128,512]{1,0:T(8,128)(2,1)S(1)}, bf16[128,512]{1,0:T(8,128)(2,1)S(1)}, u32[]{:S(2)}, u32[]{:S(2)}) collective-permute-start(bf16[128,512]{1,0:T(8,128)(2,1)S(1)} %get-tuple-element.68), channel_id=1, source_target_pairs={{0,16},{1,17},{16,0},{17,1},{2,18},{3,19},{18,2},{19,3},{4,20},{5,... | collective-permute-start | bytes 393224 | tf_op jit(solution)/shard_map/ppermute | solution.py:52
  32.4 7.3 %collective-permute-start.10 = (bf16[128,512]{1,0:T(8,128)(2,1)S(1)}, bf16[128,512]{1,0:T(8,128)(2,1)S(1)}, u32[]{:S(2)}, u32[]{:S(2)}) collective-permute-start(bf16[128,512]{1,0:T(8,128)(2,1)S(1)} %get-tuple-element.69.refs_0_.refs_4_), channel_id=1, source_target_pairs={{0,17},{1,16},{16,1},{17,0},{2,19},{3,18},{18,3},{19,2},{4,21},{5,... | collective-permute-start | bytes 393224 | tf_op jit(solution)/shard_map/ppermute | solution.py:52
  33.7 7.6 %collective-permute-start.12 = (bf16[128,512]{1,0:T(8,128)(2,1)S(1)}, bf16[128,512]{1,0:T(8,128)(2,1)S(1)}, u32[]{:S(2)}, u32[]{:S(2)}) collective-permute-start(bf16[128,512]{1,0:T(8,128)(2,1)S(1)} %get-tuple-element.69.refs_0_.refs_4_), channel_id=1, source_target_pairs={{0,16},{1,17},{16,0},{17,1},{2,18},{3,19},{18,2},{19,3},{4,20},{5,... | collective-permute-start | bytes 393224 | tf_op jit(solution)/shard_map/ppermute | solution.py:52
  35.2 6.1 %collective-permute-start.11 = (bf16[128,512]{1,0:T(8,128)(2,1)S(1)}, bf16[128,512]{1,0:T(8,128)(2,1)S(1)}, u32[]{:S(2)}, u32[]{:S(2)}) collective-permute-start(bf16[128,512]{1,0:T(8,128)(2,1)S(1)} %get-tuple-element.69.refs_0_.refs_4_), channel_id=1, source_target_pairs={{0,1},{1,0},{16,17},{17,16},{2,3},{3,2},{18,19},{19,18},{4,5},{5,4... | collective-permute-start | bytes 393224 | tf_op jit(solution)/shard_map/ppermute | solution.py:52
  42.1 3.2 %collective-permute-start.13 = (bf16[256,512]{1,0:T(8,128)(2,1)S(1)}, bf16[256,512]{1,0:T(8,128)(2,1)S(1)}, u32[]{:S(2)}, u32[]{:S(2)}) collective-permute-start(bf16[256,512]{1,0:T(8,128)(2,1)S(1)} %get-tuple-element.75), channel_id=1, source_target_pairs={{0,8},{8,0},{1,9},{9,1},{2,10},{10,2},{3,11},{11,3},{4,12},{12,4},... | collective-permute-start | bytes 786440 | tf_op jit(solution)/shard_map/ppermute | solution.py:44
  42.2 3.1 %collective-permute-start.14 = (bf16[256,512]{1,0:T(8,128)(2,1)S(1)}, bf16[256,512]{1,0:T(8,128)(2,1)S(1)}, u32[]{:S(2)}, u32[]{:S(2)}) collective-permute-start(bf16[256,512]{1,0:T(8,128)(2,1)S(1)} %get-tuple-element.76), channel_id=1, source_target_pairs={{0,8},{8,0},{1,9},{9,1},{2,10},{10,2},{3,11},{11,3},{4,12},{12,4},... | collective-permute-start | bytes 786440 | tf_op jit(solution)/shard_map/ppermute | solution.py:44
  43.1 9.1 %collective-permute-start.18 = (bf16[128,1024]{1,0:T(8,128)(2,1)S(1)}, bf16[128,1024]{1,0:T(8,128)(2,1)S(1)}, u32[]{:S(2)}, u32[]{:S(2)}) collective-permute-start(bf16[128,1024]{1,0:T(8,128)(2,1)S(1)} %get-tuple-element.83), channel_id=1, source_target_pairs={{0,16},{1,17},{16,0},{17,1},{2,18},{3,19},{18,2},{19,3},{4,20},{5,... | collective-permute-start | bytes 786440 | tf_op jit(solution)/shard_map/ppermute | solution.py:52
  44.7 13.6 %collective-permute-start.17 = (bf16[128,1024]{1,0:T(8,128)(2,1)S(1)}, bf16[128,1024]{1,0:T(8,128)(2,1)S(1)}, u32[]{:S(2)}, u32[]{:S(2)}) collective-permute-start(bf16[128,1024]{1,0:T(8,128)(2,1)S(1)} %get-tuple-element.80), channel_id=1, source_target_pairs={{0,1},{1,0},{16,17},{17,16},{2,3},{3,2},{18,19},{19,18},{4,5},{5,4... | collective-permute-start | bytes 786440 | tf_op jit(solution)/shard_map/ppermute | solution.py:52
  45.4 13.0 %collective-permute-start.15 = (bf16[128,512]{1,0:T(8,128)(2,1)S(1)}, bf16[128,512]{1,0:T(8,128)(2,1)S(1)}, u32[]{:S(2)}, u32[]{:S(2)}) collective-permute-start(bf16[128,512]{1,0:T(8,128)(2,1)S(1)} %get-tuple-element.78), channel_id=1, source_target_pairs={{0,6},{2,4},{4,2},{6,0},{1,7},{3,5},{5,3},{7,1},{8,14},{10,12},{12... | collective-permute-start | bytes 393224 | tf_op jit(solution)/shard_map/ppermute | solution.py:40
  47.9 10.4 %collective-permute-start.16 = (bf16[128,512]{1,0:T(8,128)(2,1)S(1)}, bf16[128,512]{1,0:T(8,128)(2,1)S(1)}, u32[]{:S(2)}, u32[]{:S(2)}) collective-permute-start(bf16[128,512]{1,0:T(8,128)(2,1)S(1)} %get-tuple-element.79), channel_id=1, source_target_pairs={{0,4},{2,6},{4,0},{6,2},{1,5},{3,7},{5,1},{7,3},{8,12},{10,14},{12... | collective-permute-start | bytes 393224 | tf_op jit(solution)/shard_map/ppermute | solution.py:40
  47.9 11.7 %collective-permute-start.19 = (bf16[128,1024]{1,0:T(8,128)(2,1)S(1)}, bf16[128,1024]{1,0:T(8,128)(2,1)S(1)}, u32[]{:S(2)}, u32[]{:S(2)}) collective-permute-start(bf16[128,1024]{1,0:T(8,128)(2,1)S(1)} %columns.4), channel_id=1, source_target_pairs={{0,17},{1,16},{16,1},{17,0},{2,19},{3,18},{18,3},{19,2},{4,21},{5,... | collective-permute-start | bytes 786440 | tf_op jit(solution)/shard_map/ppermute | solution.py:52
  52.3 7.3 %collective-permute-start.20 = (bf16[128,512]{1,0:T(8,128)(2,1)S(1)}, bf16[128,512]{1,0:T(8,128)(2,1)S(1)}, u32[]{:S(2)}, u32[]{:S(2)}) collective-permute-start(bf16[128,512]{1,0:T(8,128)(2,1)S(1)} %get-tuple-element.91), channel_id=1, source_target_pairs={{0,2},{2,0},{4,6},{6,4},{1,3},{3,1},{5,7},{7,5},{8,10},{10,8},{12,... | collective-permute-start | bytes 393224 | tf_op jit(solution)/shard_map/ppermute | solution.py:40

commit v17 on v16

--- a/solution.py
+++ b/solution.py
@@ -16,6 +16,7 @@
 SPLIT = 2
 TWIN = 2
 MEMBERS = SPLIT * SPLIT
+MIXED = (4, 5)
 bf16, f32 = jnp.bfloat16, jnp.float32
 
 
@@ -45,11 +46,26 @@
 
 
 def flips(far):
+    if far in MIXED:
+        core = lax.axis_index("twin")
+        return (1 - core, core) if far == MIXED[0] else (core, 1 - core)
     return far // SPLIT, far % SPLIT
 
 
 def to_member(block, far):
     return lax.ppermute(block, ("side", "pair"), [(i, i ^ far) for i in range(MEMBERS)])
+
+
+def to_mixed(block, far):
+    def index(side, core, pair):
+        return (side * TWIN + core) * SPLIT + pair
+
+    pairs = []
+    for i in range(MEMBERS * TWIN):
+        side, core, pair = i // (TWIN * SPLIT), i // SPLIT % TWIN, i % SPLIT
+        over = 1 - core if far == MIXED[0] else core
+        pairs.append((i, index(side ^ over, core, pair ^ (1 - over))))
+    return lax.ppermute(block, ("side", "twin", "pair"), pairs)
 
 
 def run_of(part, far):
@@ -202,6 +218,17 @@
         out[...] = product[i * out.shape[0] : (i + 1) * out.shape[0]].astype(out.dtype)
 
 
+def mixed_columns_body(grad_1, grad_2, weight, first, second):
+    rows = first.shape[0]
+    stacked = jnp.concatenate([grad_1[...], grad_2[...]], axis=0)
+    product = lax.dot_general(
+        stacked, weight[...], (((1,), (1,)), ((), ())), preferred_element_type=f32
+    )
+    core = lax.axis_index("twin")
+    first[...] = jnp.where(core == 0, product[rows:], product[:rows]).astype(first.dtype)
+    second[...] = jnp.where(core == 0, product[:rows], product[rows:]).astype(second.dtype)
+
+
 def emit_body(held, out):
     out[...] = held[...]
 
@@ -346,7 +373,10 @@
         moved=0,
     )
 
-    back_1, back_2 = (to_member(column, far) for far, column in zip((1, 2), columns(grad_1, grad_2)))
+    mixed = local_call(
+        "columns", mixed_columns_body, [block_shape] * 2, grad_1, grad_2, weight, flops=flops
+    )
+    back_2, back_1 = (to_mixed(column, far) for far, column in zip(MIXED, mixed))
     column_3, _ = lax.optimization_barrier((column_3, sums))
     back_3 = to_member(column_3, 3)
     *sums, closest = sums
@@ -354,7 +384,7 @@
     met = [sums[0]] + [along(piece, line - i) for i, piece in enumerate(sums) if i]
     whole_shape = shape((tok_rows, width), bf16)
     (input_grad,) = placing_call(
-        "unpack", functools.partial(unpack_body, (0, 2)), [whole_shape], (column_0, back_2)
+        "unpack", functools.partial(unpack_body, (0, MIXED[0])), [whole_shape], (column_0, back_2)
     )
     met, back_1, input_grad = lax.optimization_barrier((met, back_1, input_grad))
     sum_shape = shape((rows, key_cols), f32)
@@ -362,7 +392,7 @@
     total = local_call("final_sum", sum_body, sum_shape, far_sum, along(closest, 1), moved=0)
     input_grad, weight_grad = placing_call(
         "finish",
-        functools.partial(finish_body, (1, 3)),
+        functools.partial(finish_body, (MIXED[1], 3)),
         [whole_shape, shape(total.shape, f32)],
         (back_1, back_3, total),
         (input_grad,),

time: 60.9 us -> 60.5 us (level)
    ppermute x12 -> x10, waiting for transfers between devices: 16.7 us -> 8.67 us  [to_member(): lax.ppermute(block, ('side', 'pair'), [(i, i ^ far) for i in range(MEMBER...]
    ppermute x4, waiting for transfers between devices: 8.76 us -> 13.7 us  [along(): lax.ppermute(block, 'line', [(i, i ^ step) for i in range(lax.axis_size('...]
    ppermute x0 -> x2, waiting for transfers between devices: none -> 2.73 us  [to_mixed(): return lax.ppermute(block, ('side', 'twin', 'pair'), pairs)]
    ppermute x0 -> x2, starting transfers between devices: none -> 2.12 us  [to_mixed(): return lax.ppermute(block, ('side', 'twin', 'pair'), pairs)]
    ppermute x12 -> x10, starting transfers between devices: 15.7 us -> 13.5 us  [to_member(): lax.ppermute(block, ('side', 'pair'), [(i, i ^ far) for i in range(MEMBER...]
  transfers between devices with their start and end apart: 21 -> 21, of which waited for: 10 -> 11; matrix products, arithmetic and copies ran while one was open for 0% -> 0% of each run, Pallas kernels for 6% -> 6%
where the time goes in v17:
time: 60.5 us; the launch traced here: 60.3 us
  waiting for transfers between devices  26.4 us (44%)
  starting transfers between devices  24.6 us (41%)
  Pallas kernels  8.54 us (14%)
  between operations  0.76 us (1%)
    ppermute x4, waiting for transfers between devices, along(): lax.ppermute(block, 'line', [(i, i ^ step) for i in range(lax.axis_size('...  13.7 us
    ppermute x10, starting transfers between devices, to_member(): lax.ppermute(block, ('side', 'pair'), [(i, i ^ far) for i in range(MEMBER...  13.5 us
    ppermute x10, waiting for transfers between devices, to_member(): lax.ppermute(block, ('side', 'pair'), [(i, i ^ far) for i in range(MEMBER...  8.67 us
    pallas_call x14, Pallas kernels, local_call(): pl.pallas_call(body, name=name, out_shape=out_shapes, in_specs=[pl.BlockS...  6.54 us
    ppermute x4, starting transfers between devices, along(): lax.ppermute(block, 'line', [(i, i ^ step) for i in range(lax.axis_size('...  5.16 us
    ppermute x2, waiting for transfers between devices, to_mixed(): return lax.ppermute(block, ('side', 'twin', 'pair'), pairs)  2.73 us
    ppermute x4, starting transfers between devices, to_twin(): return lax.ppermute(block, 'twin', [(0, 1), (1, 0)])  2.19 us
    ppermute x2, starting transfers between devices, to_mixed(): return lax.ppermute(block, ('side', 'twin', 'pair'), pairs)  2.12 us
  transfers between devices with their start and end apart: 21, of which 11 were waited for; matrix products, arithmetic and copies ran while one was open for 0% of the time, Pallas kernels for 6%

profile of v17, /device:TPU:0, one launch (start us, length us, event | category | flops | bytes accessed | tf_op | source)
XLA Modules:
  0.0 60.3 jit_solution(17312448288832202166)
XLA Ops:
  0.6 2.4 %front.1 = (bf16[256,512]{1,0:T(8,128)(2,1)S(1)}, bf16[128,512]{1,0:T(8,128)(2,1)S(1)}, bf16[128,1024]{1,0:T(8,128)(2,1)S(1)}, bf16[128,1024]{1,0:T(8,128)(2,1)S...) custom-call(bf16[128,4096]{1,0:T(8,128)(2,1)} %tokens.1, bf16[512,512]{1,0:T(8,128)(2,1)} %shard.1), custom_call_target="tpu_custom_call" | custom-call | bytes 1572864 | tf_op jit(solution)/shard_map/front/pallas_call | solution.py:28
  3.0 4.0 %collective-permute-start = (bf16[128,1024]{1,0:T(8,128)(2,1)}, bf16[128,1024]{1,0:T(8,128)(2,1)S(1)}, u32[]{:S(2)}, u32[]{:S(2)}) collective-permute-start(bf16[128,1024]{1,0:T(8,128)(2,1)} %get-tuple-element.49), channel_id=1, source_target_pairs={{0,17},{1,16},{16,1},{17,0},{2,19},{3,18},{18,3},{19,2},{4,21},{5,... | collective-permute-start | bytes 786440 | tf_op jit(solution)/shard_map/ppermute | solution.py:56
  7.0 1.6 %collective-permute-start.1 = (bf16[256,512]{1,0:T(8,128)(2,1)S(1)}, bf16[256,512]{1,0:T(8,128)(2,1)S(1)}, u32[]{:S(2)}, u32[]{:S(2)}) collective-permute-start(bf16[256,512]{1,0:T(8,128)(2,1)S(1)} %get-tuple-element.50.refs_0_), channel_id=1, source_target_pairs={{0,2},{2,0},{4,6},{6,4},{8,14},{10,12},{12,10},{14,8},{1,3},{3,1},... | collective-permute-start | bytes 786440 | tf_op jit(solution)/shard_map/ppermute | solution.py:161
  8.5 2.6 %collective-permute-start.2 = (bf16[128,512]{1,0:T(8,128)(2,1)S(1)}, bf16[128,512]{1,0:T(8,128)(2,1)S(1)}, u32[]{:S(2)}, u32[]{:S(2)}) collective-permute-start(bf16[128,512]{1,0:T(8,128)(2,1)S(1)} %get-tuple-element.51), channel_id=1, source_target_pairs={{0,4},{2,6},{4,0},{6,2},{1,5},{3,7},{5,1},{7,3},{8,12},{10,14},{12... | collective-permute-start | bytes 393224 | tf_op jit(solution)/shard_map/ppermute | solution.py:41
  11.1 0.5 collective-permute-start.3
  11.7 0.5 collective-permute-start.4
  12.2 7.5 %collective-permute-done.2.refs_1_.refs_2_ = bf16[128,512]{1,0:T(8,128)(2,1)S(1)} collective-permute-done((bf16[128,512]{1,0:T(8,128)(2,1)S(1)}, bf16[128,512]{1,0:T(8,128)(2,1)S(1)}, u32[]{:S(2)}, u32[]{:S(2)}) %collective-permute-start.2) | collective-permute-done | bytes 131104 | tf_op jit(solution)/shard_map/ppermute | solution.py:41
  19.7 1.5 %collective-permute-start.5 = (bf16[192,512]{1,0:T(8,128)(2,1)S(1)}, bf16[192,512]{1,0:T(8,128)(2,1)S(1)}, u32[]{:S(2)}, u32[]{:S(2)}) collective-permute-start(bf16[192,512]{1,0:T(8,128)(2,1)S(1)} %get-tuple-element.58), channel_id=1, source_target_pairs={{0,8},{8,0},{1,9},{9,1},{2,10},{10,2},{3,11},{11,3},{4,12},{12,4},... | collective-permute-start | bytes 589832 | tf_op jit(solution)/shard_map/ppermute | solution.py:45
  21.4 1.0 %collective-permute-done.5.refs_3_ = bf16[192,512]{1,0:T(8,128)(2,1)S(1)} collective-permute-done((bf16[192,512]{1,0:T(8,128)(2,1)S(1)}, bf16[192,512]{1,0:T(8,128)(2,1)S(1)}, u32[]{:S(2)}, u32[]{:S(2)}) %collective-permute-start.5) | collective-permute-done | bytes 196640 | tf_op jit(solution)/shard_map/ppermute | solution.py:45
  22.8 0.6 share.3
  23.4 0.5 collective-permute-start.7
  23.9 1.5 %collective-permute-start.8 = (bf16[128,512]{1,0:T(8,128)(2,1)S(1)}, bf16[128,512]{1,0:T(8,128)(2,1)S(1)}, u32[]{:S(2)}, u32[]{:S(2)}) collective-permute-start(bf16[128,512]{1,0:T(8,128)(2,1)S(1)} %get-tuple-element.67), channel_id=1, source_target_pairs={{0,1},{1,0},{16,17},{17,16},{2,3},{3,2},{18,19},{19,18},{4,5},{5,4... | collective-permute-start | bytes 393224 | tf_op jit(solution)/shard_map/ppermute | solution.py:56
  25.4 1.5 %collective-permute-start.9 = (bf16[128,512]{1,0:T(8,128)(2,1)S(1)}, bf16[128,512]{1,0:T(8,128)(2,1)S(1)}, u32[]{:S(2)}, u32[]{:S(2)}) collective-permute-start(bf16[128,512]{1,0:T(8,128)(2,1)S(1)} %get-tuple-element.68), channel_id=1, source_target_pairs={{0,16},{1,17},{16,0},{17,1},{2,18},{3,19},{18,2},{19,3},{4,20},{5,... | collective-permute-start | bytes 393224 | tf_op jit(solution)/shard_map/ppermute | solution.py:56
  27.3 3.5 %collective-permute-done.7.refs_1_ = bf16[128,512]{1,0:T(8,128)(2,1)S(1)} collective-permute-done((bf16[128,512]{1,0:T(8,128)(2,1)S(1)}, bf16[128,512]{1,0:T(8,128)(2,1)S(1)}, u32[]{:S(2)}, u32[]{:S(2)}) %collective-permute-start.7) | collective-permute-done | bytes 131104 | tf_op jit(solution)/shard_map/ppermute | solution.py:56
  30.7 1.4 %collective-permute-done.8.refs_2_ = bf16[128,512]{1,0:T(8,128)(2,1)S(1)} collective-permute-done((bf16[128,512]{1,0:T(8,128)(2,1)S(1)}, bf16[128,512]{1,0:T(8,128)(2,1)S(1)}, u32[]{:S(2)}, u32[]{:S(2)}) %collective-permute-start.8) | collective-permute-done | bytes 131104 | tf_op jit(solution)/shard_map/ppermute | solution.py:56
  32.4 1.3 %collective-permute-start.10 = (bf16[128,512]{1,0:T(8,128)(2,1)S(1)}, bf16[128,512]{1,0:T(8,128)(2,1)S(1)}, u32[]{:S(2)}, u32[]{:S(2)}) collective-permute-start(bf16[128,512]{1,0:T(8,128)(2,1)S(1)} %get-tuple-element.69.refs_0_.refs_4_), channel_id=1, source_target_pairs={{0,17},{1,16},{16,1},{17,0},{2,19},{3,18},{18,3},{19,2},{4,21},{5,... | collective-permute-start | bytes 393224 | tf_op jit(solution)/shard_map/ppermute | solution.py:56
  33.7 1.5 %collective-permute-start.12 = (bf16[128,512]{1,0:T(8,128)(2,1)S(1)}, bf16[128,512]{1,0:T(8,128)(2,1)S(1)}, u32[]{:S(2)}, u32[]{:S(2)}) collective-permute-start(bf16[128,512]{1,0:T(8,128)(2,1)S(1)} %get-tuple-element.69.refs_0_.refs_4_), channel_id=1, source_target_pairs={{0,16},{1,17},{16,0},{17,1},{2,18},{3,19},{18,2},{19,3},{4,20},{5,... | collective-permute-start | bytes 393224 | tf_op jit(solution)/shard_map/ppermute | solution.py:56
  35.2 0.7 %collective-permute-start.11 = (bf16[128,512]{1,0:T(8,128)(2,1)S(1)}, bf16[128,512]{1,0:T(8,128)(2,1)S(1)}, u32[]{:S(2)}, u32[]{:S(2)}) collective-permute-start(bf16[128,512]{1,0:T(8,128)(2,1)S(1)} %get-tuple-element.69.refs_0_.refs_4_), channel_id=1, source_target_pairs={{0,1},{1,0},{16,17},{17,16},{2,3},{3,2},{18,19},{19,18},{4,5},{5,4... | collective-permute-start | bytes 393224 | tf_op jit(solution)/shard_map/ppermute | solution.py:56
  35.9 0.7 %emit.1 = bf16[128,512]{1,0:T(8,128)(2,1)} custom-call(bf16[128,512]{1,0:T(8,128)(2,1)S(1)} %get-tuple-element.70.held), custom_call_target="tpu_custom_call" | custom-call | bytes 131072 | tf_op jit(solution)/shard_map/emit/pallas_call | solution.py:28
  37.1 2.6 %collective-permute-done.10.refs_0_.refs_7_ = bf16[128,512]{1,0:T(8,128)(2,1)S(1)} collective-permute-done((bf16[128,512]{1,0:T(8,128)(2,1)S(1)}, bf16[128,512]{1,0:T(8,128)(2,1)S(1)}, u32[]{:S(2)}, u32[]{:S(2)}) %collective-permute-start.10) | collective-permute-done | bytes 131104 | tf_op jit(solution)/shard_map/ppermute | solution.py:56
  40.2 1.1 %collective-permute-done.12.refs_6_.grad_2 = bf16[128,512]{1,0:T(8,128)(2,1)S(1)} collective-permute-done((bf16[128,512]{1,0:T(8,128)(2,1)S(1)}, bf16[128,512]{1,0:T(8,128)(2,1)S(1)}, u32[]{:S(2)}, u32[]{:S(2)}) %collective-permute-start.12) | collective-permute-done | bytes 131104 | tf_op jit(solution)/shard_map/ppermute | solution.py:56
  41.3 0.7 %terms.1 = (f32[4,128,512]{2,1,0:T(8,128)S(1)}, bf16[256,512]{1,0:T(8,128)(2,1)S(1)}, bf16[256,512]{1,0:T(8,128)(2,1)S(1)}) custom-call(bf16[128,1024]{1,0:T(8,128)(2,1)S(1)} %get-tuple-element.60.refs_0_, bf16[128,1024]{1,0:T(8,128)(2,1)S(1)} %collective-permute-done.4.refs_1_, bf16[128,1024]{1,0:T(8,128)(2,1)S(1)} %collective-permute-done.3.refs_2_, ...), custom_call_target="tpu_custom_call" | custom-call | tf_op jit(solution)/shard_map/terms/pallas_call | solution.py:28
  43.1 1.6 %collective-permute-start.18 = (bf16[128,1024]{1,0:T(8,128)(2,1)S(1)}, bf16[128,1024]{1,0:T(8,128)(2,1)S(1)}, u32[]{:S(2)}, u32[]{:S(2)}) collective-permute-start(bf16[128,1024]{1,0:T(8,128)(2,1)S(1)} %get-tuple-element.83), channel_id=1, source_target_pairs={{0,16},{1,17},{8,9},{9,8},{16,0},{17,1},{24,25},{25,24},{2,18},{3,... | collective-permute-start | bytes 786440 | tf_op jit(solution)/shard_map/ppermute | solution.py:68
  44.7 0.6 collective-permute-start.17
  45.4 2.6 %collective-permute-start.15 = (bf16[128,512]{1,0:T(8,128)(2,1)S(1)}, bf16[128,512]{1,0:T(8,128)(2,1)S(1)}, u32[]{:S(2)}, u32[]{:S(2)}) collective-permute-start(bf16[128,512]{1,0:T(8,128)(2,1)S(1)} %get-tuple-element.78), channel_id=1, source_target_pairs={{0,6},{2,4},{4,2},{6,0},{1,7},{3,5},{5,3},{7,1},{8,14},{10,12},{12... | collective-permute-start | bytes 393224 | tf_op jit(solution)/shard_map/ppermute | solution.py:41
  47.9 1.4 %collective-permute-start.19 = (bf16[128,1024]{1,0:T(8,128)(2,1)S(1)}, bf16[128,1024]{1,0:T(8,128)(2,1)S(1)}, u32[]{:S(2)}, u32[]{:S(2)}) collective-permute-start(bf16[128,1024]{1,0:T(8,128)(2,1)S(1)} %columns.4), channel_id=1, source_target_pairs={{0,17},{1,16},{16,1},{17,0},{2,19},{3,18},{18,3},{19,2},{4,21},{5,... | collective-permute-start | bytes 786440 | tf_op jit(solution)/shard_map/ppermute | solution.py:56
  49.4 2.7 %collective-permute-done.18.refs_1_ = bf16[128,1024]{1,0:T(8,128)(2,1)S(1)} collective-permute-done((bf16[128,1024]{1,0:T(8,128)(2,1)S(1)}, bf16[128,1024]{1,0:T(8,128)(2,1)S(1)}, u32[]{:S(2)}, u32[]{:S(2)}) %collective-permute-start.18) | collective-permute-done | bytes 262176 | tf_op jit(solution)/shard_map/ppermute | solution.py:68
  52.1 0.9 %unpack.1.refs_3_ = bf16[128,4096]{1,0:T(8,128)(2,1)} custom-call(bf16[128,1024]{1,0:T(8,128)(2,1)S(1)} %columns.3.refs_0_, bf16[128,1024]{1,0:T(8,128)(2,1)S(1)} %collective-permute-done.18.refs_1_), custom_call_target="tpu_custom_call" | custom-call | tf_op jit(solution)/shard_map/unpack/pallas_call | solution.py:128
  53.0 0.7 %collective-permute-done.15.refs_1_ = bf16[128,512]{1,0:T(8,128)(2,1)S(1)} collective-permute-done((bf16[128,512]{1,0:T(8,128)(2,1)S(1)}, bf16[128,512]{1,0:T(8,128)(2,1)S(1)}, u32[]{:S(2)}, u32[]{:S(2)}) %collective-permute-start.15) | collective-permute-done | bytes 131104 | tf_op jit(solution)/shard_map/ppermute | solution.py:41
  53.8 4.5 %collective-permute-done.16.refs_2_ = bf16[128,512]{1,0:T(8,128)(2,1)S(1)} collective-permute-done((bf16[128,512]{1,0:T(8,128)(2,1)S(1)}, bf16[128,512]{1,0:T(8,128)(2,1)S(1)}, u32[]{:S(2)}, u32[]{:S(2)}) %collective-permute-start.16) | collective-permute-done | bytes 131104 | tf_op jit(solution)/shard_map/ppermute | solution.py:41
  58.3 0.9 %collective-permute-done.20.refs_1_ = bf16[128,512]{1,0:T(8,128)(2,1)S(1)} collective-permute-done((bf16[128,512]{1,0:T(8,128)(2,1)S(1)}, bf16[128,512]{1,0:T(8,128)(2,1)S(1)}, u32[]{:S(2)}, u32[]{:S(2)}) %collective-permute-start.20) | collective-permute-done | bytes 131104 | tf_op jit(solution)/shard_map/ppermute | solution.py:41
  59.2 1.1 %finish.1 = (bf16[128,4096]{1,0:T(8,128)(2,1)}, f32[128,512]{1,0:T(8,128)}) custom-call(bf16[128,1024]{1,0:T(8,128)(2,1)S(1)} %collective-permute-done.17.refs_0_, bf16[128,1024]{1,0:T(8,128)(2,1)S(1)} %collective-permute-done.19.refs_1_, f32[128,512]{1,0:T(8,128)S(1)} %final_sum.1.refs_2_, ...), custom_call_target="tpu_custom_call", output_to_operand_aliasing={{0}: (3, {})} | custom-call | tf_op jit(solution)/shard_map/finish/pallas_call | solution.py:128
  (28 shorter events, 3.3 us)
Async XLA Ops:
  3.0 16.7 %collective-permute-start = (bf16[128,1024]{1,0:T(8,128)(2,1)}, bf16[128,1024]{1,0:T(8,128)(2,1)S(1)}, u32[]{:S(2)}, u32[]{:S(2)}) collective-permute-start(bf16[128,1024]{1,0:T(8,128)(2,1)} %get-tuple-element.49), channel_id=1, source_target_pairs={{0,17},{1,16},{16,1},{17,0},{2,19},{3,18},{18,3},{19,2},{4,21},{5,... | collective-permute-start | bytes 786440 | tf_op jit(solution)/shard_map/ppermute | solution.py:56
  7.0 12.7 %collective-permute-start.1 = (bf16[256,512]{1,0:T(8,128)(2,1)S(1)}, bf16[256,512]{1,0:T(8,128)(2,1)S(1)}, u32[]{:S(2)}, u32[]{:S(2)}) collective-permute-start(bf16[256,512]{1,0:T(8,128)(2,1)S(1)} %get-tuple-element.50.refs_0_), channel_id=1, source_target_pairs={{0,2},{2,0},{4,6},{6,4},{8,14},{10,12},{12,10},{14,8},{1,3},{3,1},... | collective-permute-start | bytes 786440 | tf_op jit(solution)/shard_map/ppermute | solution.py:161
  8.5 11.2 %collective-permute-start.2 = (bf16[128,512]{1,0:T(8,128)(2,1)S(1)}, bf16[128,512]{1,0:T(8,128)(2,1)S(1)}, u32[]{:S(2)}, u32[]{:S(2)}) collective-permute-start(bf16[128,512]{1,0:T(8,128)(2,1)S(1)} %get-tuple-element.51), channel_id=1, source_target_pairs={{0,4},{2,6},{4,0},{6,2},{1,5},{3,7},{5,1},{7,3},{8,12},{10,14},{12... | collective-permute-start | bytes 393224 | tf_op jit(solution)/shard_map/ppermute | solution.py:41
  11.1 10.2 %collective-permute-start.3 = (bf16[128,1024]{1,0:T(8,128)(2,1)}, bf16[128,1024]{1,0:T(8,128)(2,1)S(1)}, u32[]{:S(2)}, u32[]{:S(2)}) collective-permute-start(bf16[128,1024]{1,0:T(8,128)(2,1)} %get-tuple-element.53), channel_id=1, source_target_pairs={{0,16},{1,17},{16,0},{17,1},{2,18},{3,19},{18,2},{19,3},{4,20},{5,... | collective-permute-start | bytes 786440 | tf_op jit(solution)/shard_map/ppermute | solution.py:56
  11.7 9.7 %collective-permute-start.4 = (bf16[128,1024]{1,0:T(8,128)(2,1)S(1)}, bf16[128,1024]{1,0:T(8,128)(2,1)S(1)}, u32[]{:S(2)}, u32[]{:S(2)}) collective-permute-start(bf16[128,1024]{1,0:T(8,128)(2,1)S(1)} %get-tuple-element.54), channel_id=1, source_target_pairs={{0,1},{1,0},{16,17},{17,16},{2,3},{3,2},{18,19},{19,18},{4,5},{5,4... | collective-permute-start | bytes 786440 | tf_op jit(solution)/shard_map/ppermute | solution.py:56
  19.7 2.6 %collective-permute-start.5 = (bf16[192,512]{1,0:T(8,128)(2,1)S(1)}, bf16[192,512]{1,0:T(8,128)(2,1)S(1)}, u32[]{:S(2)}, u32[]{:S(2)}) collective-permute-start(bf16[192,512]{1,0:T(8,128)(2,1)S(1)} %get-tuple-element.58), channel_id=1, source_target_pairs={{0,8},{8,0},{1,9},{9,1},{2,10},{10,2},{3,11},{11,3},{4,12},{12,4},... | collective-permute-start | bytes 589832 | tf_op jit(solution)/shard_map/ppermute | solution.py:45
  21.3 1.4 %collective-permute-start.6 = (bf16[192,512]{1,0:T(8,128)(2,1)S(1)}, bf16[192,512]{1,0:T(8,128)(2,1)S(1)}, u32[]{:S(2)}, u32[]{:S(2)}) collective-permute-start(bf16[192,512]{1,0:T(8,128)(2,1)S(1)} %get-tuple-element.59), channel_id=1, source_target_pairs={{0,8},{8,0},{1,9},{9,1},{2,10},{10,2},{3,11},{11,3},{4,12},{12,4},... | collective-permute-start | bytes 589832 | tf_op jit(solution)/shard_map/ppermute | solution.py:45
  23.4 7.3 %collective-permute-start.7 = (bf16[128,512]{1,0:T(8,128)(2,1)S(1)}, bf16[128,512]{1,0:T(8,128)(2,1)S(1)}, u32[]{:S(2)}, u32[]{:S(2)}) collective-permute-start(bf16[128,512]{1,0:T(8,128)(2,1)S(1)} %get-tuple-element.66), channel_id=1, source_target_pairs={{0,17},{1,16},{16,1},{17,0},{2,19},{3,18},{18,3},{19,2},{4,21},{5,... | collective-permute-start | bytes 393224 | tf_op jit(solution)/shard_map/ppermute | solution.py:56
  23.9 8.2 %collective-permute-start.8 = (bf16[128,512]{1,0:T(8,128)(2,1)S(1)}, bf16[128,512]{1,0:T(8,128)(2,1)S(1)}, u32[]{:S(2)}, u32[]{:S(2)}) collective-permute-start(bf16[128,512]{1,0:T(8,128)(2,1)S(1)} %get-tuple-element.67), channel_id=1, source_target_pairs={{0,1},{1,0},{16,17},{17,16},{2,3},{3,2},{18,19},{19,18},{4,5},{5,4... | collective-permute-start | bytes 393224 | tf_op jit(solution)/shard_map/ppermute | solution.py:56
  25.4 6.7 %copy-start = (bf16[128,512]{1,0:T(8,128)(2,1)S(1)}, bf16[128,512]{1,0:T(8,128)(2,1)}, u32[]{:S(2)}) copy-start(bf16[128,512]{1,0:T(8,128)(2,1)} %refs_4_.1) | copy-start | bytes 393220
  25.4 6.7 %collective-permute-start.9 = (bf16[128,512]{1,0:T(8,128)(2,1)S(1)}, bf16[128,512]{1,0:T(8,128)(2,1)S(1)}, u32[]{:S(2)}, u32[]{:S(2)}) collective-permute-start(bf16[128,512]{1,0:T(8,128)(2,1)S(1)} %get-tuple-element.68), channel_id=1, source_target_pairs={{0,16},{1,17},{16,0},{17,1},{2,18},{3,19},{18,2},{19,3},{4,20},{5,... | collective-permute-start | bytes 393224 | tf_op jit(solution)/shard_map/ppermute | solution.py:56
  32.4 7.3 %collective-permute-start.10 = (bf16[128,512]{1,0:T(8,128)(2,1)S(1)}, bf16[128,512]{1,0:T(8,128)(2,1)S(1)}, u32[]{:S(2)}, u32[]{:S(2)}) collective-permute-start(bf16[128,512]{1,0:T(8,128)(2,1)S(1)} %get-tuple-element.69.refs_0_.refs_4_), channel_id=1, source_target_pairs={{0,17},{1,16},{16,1},{17,0},{2,19},{3,18},{18,3},{19,2},{4,21},{5,... | collective-permute-start | bytes 393224 | tf_op jit(solution)/shard_map/ppermute | solution.py:56
  33.7 7.6 %collective-permute-start.12 = (bf16[128,512]{1,0:T(8,128)(2,1)S(1)}, bf16[128,512]{1,0:T(8,128)(2,1)S(1)}, u32[]{:S(2)}, u32[]{:S(2)}) collective-permute-start(bf16[128,512]{1,0:T(8,128)(2,1)S(1)} %get-tuple-element.69.refs_0_.refs_4_), channel_id=1, source_target_pairs={{0,16},{1,17},{16,0},{17,1},{2,18},{3,19},{18,2},{19,3},{4,20},{5,... | collective-permute-start | bytes 393224 | tf_op jit(solution)/shard_map/ppermute | solution.py:56
  35.2 6.1 %collective-permute-start.11 = (bf16[128,512]{1,0:T(8,128)(2,1)S(1)}, bf16[128,512]{1,0:T(8,128)(2,1)S(1)}, u32[]{:S(2)}, u32[]{:S(2)}) collective-permute-start(bf16[128,512]{1,0:T(8,128)(2,1)S(1)} %get-tuple-element.69.refs_0_.refs_4_), channel_id=1, source_target_pairs={{0,1},{1,0},{16,17},{17,16},{2,3},{3,2},{18,19},{19,18},{4,5},{5,4... | collective-permute-start | bytes 393224 | tf_op jit(solution)/shard_map/ppermute | solution.py:56
  42.1 3.2 %collective-permute-start.13 = (bf16[256,512]{1,0:T(8,128)(2,1)S(1)}, bf16[256,512]{1,0:T(8,128)(2,1)S(1)}, u32[]{:S(2)}, u32[]{:S(2)}) collective-permute-start(bf16[256,512]{1,0:T(8,128)(2,1)S(1)} %get-tuple-element.75), channel_id=1, source_target_pairs={{0,8},{8,0},{1,9},{9,1},{2,10},{10,2},{3,11},{11,3},{4,12},{12,4},... | collective-permute-start | bytes 786440 | tf_op jit(solution)/shard_map/ppermute | solution.py:45
  42.2 3.1 %collective-permute-start.14 = (bf16[256,512]{1,0:T(8,128)(2,1)S(1)}, bf16[256,512]{1,0:T(8,128)(2,1)S(1)}, u32[]{:S(2)}, u32[]{:S(2)}) collective-permute-start(bf16[256,512]{1,0:T(8,128)(2,1)S(1)} %get-tuple-element.76), channel_id=1, source_target_pairs={{0,8},{8,0},{1,9},{9,1},{2,10},{10,2},{3,11},{11,3},{4,12},{12,4},... | collective-permute-start | bytes 786440 | tf_op jit(solution)/shard_map/ppermute | solution.py:45
  43.1 9.0 %collective-permute-start.18 = (bf16[128,1024]{1,0:T(8,128)(2,1)S(1)}, bf16[128,1024]{1,0:T(8,128)(2,1)S(1)}, u32[]{:S(2)}, u32[]{:S(2)}) collective-permute-start(bf16[128,1024]{1,0:T(8,128)(2,1)S(1)} %get-tuple-element.83), channel_id=1, source_target_pairs={{0,16},{1,17},{8,9},{9,8},{16,0},{17,1},{24,25},{25,24},{2,18},{3,... | collective-permute-start | bytes 786440 | tf_op jit(solution)/shard_map/ppermute | solution.py:68
  44.7 8.3 %collective-permute-start.17 = (bf16[128,1024]{1,0:T(8,128)(2,1)S(1)}, bf16[128,1024]{1,0:T(8,128)(2,1)S(1)}, u32[]{:S(2)}, u32[]{:S(2)}) collective-permute-start(bf16[128,1024]{1,0:T(8,128)(2,1)S(1)} %get-tuple-element.80), channel_id=1, source_target_pairs={{0,1},{1,0},{8,24},{9,25},{16,17},{17,16},{24,8},{25,9},{2,3},{3,2... | collective-permute-start | bytes 786440 | tf_op jit(solution)/shard_map/ppermute | solution.py:68
  45.4 8.4 %collective-permute-start.15 = (bf16[128,512]{1,0:T(8,128)(2,1)S(1)}, bf16[128,512]{1,0:T(8,128)(2,1)S(1)}, u32[]{:S(2)}, u32[]{:S(2)}) collective-permute-start(bf16[128,512]{1,0:T(8,128)(2,1)S(1)} %get-tuple-element.78), channel_id=1, source_target_pairs={{0,6},{2,4},{4,2},{6,0},{1,7},{3,5},{5,3},{7,1},{8,14},{10,12},{12... | collective-permute-start | bytes 393224 | tf_op jit(solution)/shard_map/ppermute | solution.py:41
  47.9 10.3 %collective-permute-start.16 = (bf16[128,512]{1,0:T(8,128)(2,1)S(1)}, bf16[128,512]{1,0:T(8,128)(2,1)S(1)}, u32[]{:S(2)}, u32[]{:S(2)}) collective-permute-start(bf16[128,512]{1,0:T(8,128)(2,1)S(1)} %get-tuple-element.79), channel_id=1, source_target_pairs={{0,4},{2,6},{4,0},{6,2},{1,5},{3,7},{5,1},{7,3},{8,12},{10,14},{12... | collective-permute-start | bytes 393224 | tf_op jit(solution)/shard_map/ppermute | solution.py:41
  47.9 11.3 %collective-permute-start.19 = (bf16[128,1024]{1,0:T(8,128)(2,1)S(1)}, bf16[128,1024]{1,0:T(8,128)(2,1)S(1)}, u32[]{:S(2)}, u32[]{:S(2)}) collective-permute-start(bf16[128,1024]{1,0:T(8,128)(2,1)S(1)} %columns.4), channel_id=1, source_target_pairs={{0,17},{1,16},{16,1},{17,0},{2,19},{3,18},{18,3},{19,2},{4,21},{5,... | collective-permute-start | bytes 786440 | tf_op jit(solution)/shard_map/ppermute | solution.py:56
  52.1 7.1 %collective-permute-start.20 = (bf16[128,512]{1,0:T(8,128)(2,1)S(1)}, bf16[128,512]{1,0:T(8,128)(2,1)S(1)}, u32[]{:S(2)}, u32[]{:S(2)}) collective-permute-start(bf16[128,512]{1,0:T(8,128)(2,1)S(1)} %get-tuple-element.91), channel_id=1, source_target_pairs={{0,2},{2,0},{4,6},{6,4},{1,3},{3,1},{5,7},{7,5},{8,10},{10,8},{12,... | collective-permute-start | bytes 393224 | tf_op jit(solution)/shard_map/ppermute | solution.py:41

commit v18 on v17

--- a/solution.py
+++ b/solution.py
@@ -384,17 +384,17 @@
     met = [sums[0]] + [along(piece, line - i) for i, piece in enumerate(sums) if i]
     whole_shape = shape((tok_rows, width), bf16)
     (input_grad,) = placing_call(
-        "unpack", functools.partial(unpack_body, (0, MIXED[0])), [whole_shape], (column_0, back_2)
-    )
-    met, back_1, input_grad = lax.optimization_barrier((met, back_1, input_grad))
+        "unpack", functools.partial(unpack_body, (0, *MIXED)), [whole_shape], (column_0, back_2, back_1)
+    )
+    met, input_grad = lax.optimization_barrier((met, input_grad))
     sum_shape = shape((rows, key_cols), f32)
     far_sum = local_call("far_sum", sum_body, sum_shape, *met, flops=24 * flops)
     total = local_call("final_sum", sum_body, sum_shape, far_sum, along(closest, 1), moved=0)
     input_grad, weight_grad = placing_call(
         "finish",
-        functools.partial(finish_body, (MIXED[1], 3)),
+        functools.partial(finish_body, (3,)),
         [whole_shape, shape(total.shape, f32)],
-        (back_1, back_3, total),
+        (back_3, total),
         (input_grad,),
     )
     if outer > 1:

time: 60.5 us -> 60.3 us (level)
  no operation moved by 1% of the time
where the time goes in v18:
time: 60.3 us; the launch traced here: 60.2 us
  waiting for transfers between devices  26.3 us (44%)
  starting transfers between devices  24.6 us (41%)
  Pallas kernels  8.54 us (14%)
  between operations  0.76 us (1%)
    ppermute x10, starting transfers between devices, to_member(): lax.ppermute(block, ('side', 'pair'), [(i, i ^ far) for i in range(MEMBER...  13.5 us
    ppermute x4, waiting for transfers between devices, along(): lax.ppermute(block, 'line', [(i, i ^ step) for i in range(lax.axis_size('...  13.5 us
    ppermute x10, waiting for transfers between devices, to_member(): lax.ppermute(block, ('side', 'pair'), [(i, i ^ far) for i in range(MEMBER...  8.67 us
    pallas_call x14, Pallas kernels, local_call(): pl.pallas_call(body, name=name, out_shape=out_shapes, in_specs=[pl.BlockS...  6.54 us
    ppermute x4, starting transfers between devices, along(): lax.ppermute(block, 'line', [(i, i ^ step) for i in range(lax.axis_size('...  5.16 us
    ppermute x2, waiting for transfers between devices, to_mixed(): return lax.ppermute(block, ('side', 'twin', 'pair'), pairs)  2.73 us
    ppermute x4, starting transfers between devices, to_twin(): return lax.ppermute(block, 'twin', [(0, 1), (1, 0)])  2.19 us
    ppermute x2, starting transfers between devices, to_mixed(): return lax.ppermute(block, ('side', 'twin', 'pair'), pairs)  2.12 us
  transfers between devices with their start and end apart: 21, of which 11 were waited for; matrix products, arithmetic and copies ran while one was open for 0% of the time, Pallas kernels for 6%

profile of v18, /device:TPU:0, one launch (start us, length us, event | category | flops | bytes accessed | tf_op | source)
XLA Modules:
  0.0 60.2 jit_solution(10551513304743683885)
XLA Ops:
  0.6 2.4 %front.1 = (bf16[256,512]{1,0:T(8,128)(2,1)S(1)}, bf16[128,512]{1,0:T(8,128)(2,1)S(1)}, bf16[128,1024]{1,0:T(8,128)(2,1)S(1)}, bf16[128,1024]{1,0:T(8,128)(2,1)S...) custom-call(bf16[128,4096]{1,0:T(8,128)(2,1)} %tokens.1, bf16[512,512]{1,0:T(8,128)(2,1)} %shard.1), custom_call_target="tpu_custom_call" | custom-call | bytes 1572864 | tf_op jit(solution)/shard_map/front/pallas_call | solution.py:28
  3.0 4.0 %collective-permute-start = (bf16[128,1024]{1,0:T(8,128)(2,1)}, bf16[128,1024]{1,0:T(8,128)(2,1)S(1)}, u32[]{:S(2)}, u32[]{:S(2)}) collective-permute-start(bf16[128,1024]{1,0:T(8,128)(2,1)} %get-tuple-element.48), channel_id=1, source_target_pairs={{0,17},{1,16},{16,1},{17,0},{2,19},{3,18},{18,3},{19,2},{4,21},{5,... | collective-permute-start | bytes 786440 | tf_op jit(solution)/shard_map/ppermute | solution.py:56
  7.0 1.6 %collective-permute-start.1 = (bf16[256,512]{1,0:T(8,128)(2,1)S(1)}, bf16[256,512]{1,0:T(8,128)(2,1)S(1)}, u32[]{:S(2)}, u32[]{:S(2)}) collective-permute-start(bf16[256,512]{1,0:T(8,128)(2,1)S(1)} %get-tuple-element.49.refs_0_), channel_id=1, source_target_pairs={{0,2},{2,0},{4,6},{6,4},{8,14},{10,12},{12,10},{14,8},{1,3},{3,1},... | collective-permute-start | bytes 786440 | tf_op jit(solution)/shard_map/ppermute | solution.py:161
  8.5 2.6 %collective-permute-start.2 = (bf16[128,512]{1,0:T(8,128)(2,1)S(1)}, bf16[128,512]{1,0:T(8,128)(2,1)S(1)}, u32[]{:S(2)}, u32[]{:S(2)}) collective-permute-start(bf16[128,512]{1,0:T(8,128)(2,1)S(1)} %get-tuple-element.50), channel_id=1, source_target_pairs={{0,4},{2,6},{4,0},{6,2},{1,5},{3,7},{5,1},{7,3},{8,12},{10,14},{12... | collective-permute-start | bytes 393224 | tf_op jit(solution)/shard_map/ppermute | solution.py:41
  11.1 0.5 collective-permute-start.3
  11.7 0.5 collective-permute-start.4
  12.2 7.5 %collective-permute-done.2.refs_1_.refs_2_ = bf16[128,512]{1,0:T(8,128)(2,1)S(1)} collective-permute-done((bf16[128,512]{1,0:T(8,128)(2,1)S(1)}, bf16[128,512]{1,0:T(8,128)(2,1)S(1)}, u32[]{:S(2)}, u32[]{:S(2)}) %collective-permute-start.2) | collective-permute-done | bytes 131104 | tf_op jit(solution)/shard_map/ppermute | solution.py:41
  19.7 1.5 %collective-permute-start.5 = (bf16[192,512]{1,0:T(8,128)(2,1)S(1)}, bf16[192,512]{1,0:T(8,128)(2,1)S(1)}, u32[]{:S(2)}, u32[]{:S(2)}) collective-permute-start(bf16[192,512]{1,0:T(8,128)(2,1)S(1)} %get-tuple-element.57), channel_id=1, source_target_pairs={{0,8},{8,0},{1,9},{9,1},{2,10},{10,2},{3,11},{11,3},{4,12},{12,4},... | collective-permute-start | bytes 589832 | tf_op jit(solution)/shard_map/ppermute | solution.py:45
  21.4 1.0 %collective-permute-done.5.refs_3_ = bf16[192,512]{1,0:T(8,128)(2,1)S(1)} collective-permute-done((bf16[192,512]{1,0:T(8,128)(2,1)S(1)}, bf16[192,512]{1,0:T(8,128)(2,1)S(1)}, u32[]{:S(2)}, u32[]{:S(2)}) %collective-permute-start.5) | collective-permute-done | bytes 196640 | tf_op jit(solution)/shard_map/ppermute | solution.py:45
  22.8 0.6 share.3
  23.4 0.5 collective-permute-start.7
  23.9 1.5 %collective-permute-start.8 = (bf16[128,512]{1,0:T(8,128)(2,1)S(1)}, bf16[128,512]{1,0:T(8,128)(2,1)S(1)}, u32[]{:S(2)}, u32[]{:S(2)}) collective-permute-start(bf16[128,512]{1,0:T(8,128)(2,1)S(1)} %get-tuple-element.66), channel_id=1, source_target_pairs={{0,1},{1,0},{16,17},{17,16},{2,3},{3,2},{18,19},{19,18},{4,5},{5,4... | collective-permute-start | bytes 393224 | tf_op jit(solution)/shard_map/ppermute | solution.py:56
  25.4 1.5 %collective-permute-start.9 = (bf16[128,512]{1,0:T(8,128)(2,1)S(1)}, bf16[128,512]{1,0:T(8,128)(2,1)S(1)}, u32[]{:S(2)}, u32[]{:S(2)}) collective-permute-start(bf16[128,512]{1,0:T(8,128)(2,1)S(1)} %get-tuple-element.67), channel_id=1, source_target_pairs={{0,16},{1,17},{16,0},{17,1},{2,18},{3,19},{18,2},{19,3},{4,20},{5,... | collective-permute-start | bytes 393224 | tf_op jit(solution)/shard_map/ppermute | solution.py:56
  27.3 3.5 %collective-permute-done.7.refs_1_ = bf16[128,512]{1,0:T(8,128)(2,1)S(1)} collective-permute-done((bf16[128,512]{1,0:T(8,128)(2,1)S(1)}, bf16[128,512]{1,0:T(8,128)(2,1)S(1)}, u32[]{:S(2)}, u32[]{:S(2)}) %collective-permute-start.7) | collective-permute-done | bytes 131104 | tf_op jit(solution)/shard_map/ppermute | solution.py:56
  30.7 1.4 %collective-permute-done.8.refs_2_ = bf16[128,512]{1,0:T(8,128)(2,1)S(1)} collective-permute-done((bf16[128,512]{1,0:T(8,128)(2,1)S(1)}, bf16[128,512]{1,0:T(8,128)(2,1)S(1)}, u32[]{:S(2)}, u32[]{:S(2)}) %collective-permute-start.8) | collective-permute-done | bytes 131104 | tf_op jit(solution)/shard_map/ppermute | solution.py:56
  32.4 1.3 %collective-permute-start.10 = (bf16[128,512]{1,0:T(8,128)(2,1)S(1)}, bf16[128,512]{1,0:T(8,128)(2,1)S(1)}, u32[]{:S(2)}, u32[]{:S(2)}) collective-permute-start(bf16[128,512]{1,0:T(8,128)(2,1)S(1)} %get-tuple-element.68.refs_0_.refs_4_), channel_id=1, source_target_pairs={{0,17},{1,16},{16,1},{17,0},{2,19},{3,18},{18,3},{19,2},{4,21},{5,... | collective-permute-start | bytes 393224 | tf_op jit(solution)/shard_map/ppermute | solution.py:56
  33.7 1.5 %collective-permute-start.12 = (bf16[128,512]{1,0:T(8,128)(2,1)S(1)}, bf16[128,512]{1,0:T(8,128)(2,1)S(1)}, u32[]{:S(2)}, u32[]{:S(2)}) collective-permute-start(bf16[128,512]{1,0:T(8,128)(2,1)S(1)} %get-tuple-element.68.refs_0_.refs_4_), channel_id=1, source_target_pairs={{0,16},{1,17},{16,0},{17,1},{2,18},{3,19},{18,2},{19,3},{4,20},{5,... | collective-permute-start | bytes 393224 | tf_op jit(solution)/shard_map/ppermute | solution.py:56
  35.2 0.7 %collective-permute-start.11 = (bf16[128,512]{1,0:T(8,128)(2,1)S(1)}, bf16[128,512]{1,0:T(8,128)(2,1)S(1)}, u32[]{:S(2)}, u32[]{:S(2)}) collective-permute-start(bf16[128,512]{1,0:T(8,128)(2,1)S(1)} %get-tuple-element.68.refs_0_.refs_4_), channel_id=1, source_target_pairs={{0,1},{1,0},{16,17},{17,16},{2,3},{3,2},{18,19},{19,18},{4,5},{5,4... | collective-permute-start | bytes 393224 | tf_op jit(solution)/shard_map/ppermute | solution.py:56
  35.9 0.7 %emit.1 = bf16[128,512]{1,0:T(8,128)(2,1)} custom-call(bf16[128,512]{1,0:T(8,128)(2,1)S(1)} %get-tuple-element.69.held), custom_call_target="tpu_custom_call" | custom-call | bytes 131072 | tf_op jit(solution)/shard_map/emit/pallas_call | solution.py:28
  37.1 2.6 %collective-permute-done.10.refs_0_.refs_7_ = bf16[128,512]{1,0:T(8,128)(2,1)S(1)} collective-permute-done((bf16[128,512]{1,0:T(8,128)(2,1)S(1)}, bf16[128,512]{1,0:T(8,128)(2,1)S(1)}, u32[]{:S(2)}, u32[]{:S(2)}) %collective-permute-start.10) | collective-permute-done | bytes 131104 | tf_op jit(solution)/shard_map/ppermute | solution.py:56
  40.2 1.1 %collective-permute-done.12.refs_6_.grad_2 = bf16[128,512]{1,0:T(8,128)(2,1)S(1)} collective-permute-done((bf16[128,512]{1,0:T(8,128)(2,1)S(1)}, bf16[128,512]{1,0:T(8,128)(2,1)S(1)}, u32[]{:S(2)}, u32[]{:S(2)}) %collective-permute-start.12) | collective-permute-done | bytes 131104 | tf_op jit(solution)/shard_map/ppermute | solution.py:56
  41.3 0.7 %terms.1 = (f32[4,128,512]{2,1,0:T(8,128)S(1)}, bf16[256,512]{1,0:T(8,128)(2,1)S(1)}, bf16[256,512]{1,0:T(8,128)(2,1)S(1)}) custom-call(bf16[128,1024]{1,0:T(8,128)(2,1)S(1)} %get-tuple-element.59.refs_0_, bf16[128,1024]{1,0:T(8,128)(2,1)S(1)} %collective-permute-done.4.refs_1_, bf16[128,1024]{1,0:T(8,128)(2,1)S(1)} %collective-permute-done.3.refs_2_, ...), custom_call_target="tpu_custom_call" | custom-call | tf_op jit(solution)/shard_map/terms/pallas_call | solution.py:28
  43.1 1.6 %collective-permute-start.18 = (bf16[128,1024]{1,0:T(8,128)(2,1)S(1)}, bf16[128,1024]{1,0:T(8,128)(2,1)S(1)}, u32[]{:S(2)}, u32[]{:S(2)}) collective-permute-start(bf16[128,1024]{1,0:T(8,128)(2,1)S(1)} %get-tuple-element.83), channel_id=1, source_target_pairs={{0,16},{1,17},{8,9},{9,8},{16,0},{17,1},{24,25},{25,24},{2,18},{3,... | collective-permute-start | bytes 786440 | tf_op jit(solution)/shard_map/ppermute | solution.py:68
  44.7 0.6 collective-permute-start.19
  45.4 2.6 %collective-permute-start.16 = (bf16[128,512]{1,0:T(8,128)(2,1)S(1)}, bf16[128,512]{1,0:T(8,128)(2,1)S(1)}, u32[]{:S(2)}, u32[]{:S(2)}) collective-permute-start(bf16[128,512]{1,0:T(8,128)(2,1)S(1)} %get-tuple-element.78), channel_id=1, source_target_pairs={{0,6},{2,4},{4,2},{6,0},{1,7},{3,5},{5,3},{7,1},{8,14},{10,12},{12... | collective-permute-start | bytes 393224 | tf_op jit(solution)/shard_map/ppermute | solution.py:41
  47.9 1.4 %collective-permute-start.15 = (bf16[128,1024]{1,0:T(8,128)(2,1)S(1)}, bf16[128,1024]{1,0:T(8,128)(2,1)S(1)}, u32[]{:S(2)}, u32[]{:S(2)}) collective-permute-start(bf16[128,1024]{1,0:T(8,128)(2,1)S(1)} %columns.4), channel_id=1, source_target_pairs={{0,17},{1,16},{16,1},{17,0},{2,19},{3,18},{18,3},{19,2},{4,21},{5,... | collective-permute-start | bytes 786440 | tf_op jit(solution)/shard_map/ppermute | solution.py:56
  49.4 2.7 %collective-permute-done.18.refs_1_ = bf16[128,1024]{1,0:T(8,128)(2,1)S(1)} collective-permute-done((bf16[128,1024]{1,0:T(8,128)(2,1)S(1)}, bf16[128,1024]{1,0:T(8,128)(2,1)S(1)}, u32[]{:S(2)}, u32[]{:S(2)}) %collective-permute-start.18) | collective-permute-done | bytes 262176 | tf_op jit(solution)/shard_map/ppermute | solution.py:68
  52.1 1.1 %unpack.1.refs_2_ = bf16[128,4096]{1,0:T(8,128)(2,1)} custom-call(bf16[128,1024]{1,0:T(8,128)(2,1)S(1)} %columns.3.refs_0_, bf16[128,1024]{1,0:T(8,128)(2,1)S(1)} %collective-permute-done.18.refs_1_, bf16[128,1024]{1,0:T(8,128)(2,1)S(1)} %collective-permute-done.19.refs_2_), custom_call_target="tpu_custom_call" | custom-call | tf_op jit(solution)/shard_map/unpack/pallas_call | solution.py:128
  53.2 0.6 collective-permute-done.16.refs_1_
  53.8 4.5 %collective-permute-done.17.refs_2_ = bf16[128,512]{1,0:T(8,128)(2,1)S(1)} collective-permute-done((bf16[128,512]{1,0:T(8,128)(2,1)S(1)}, bf16[128,512]{1,0:T(8,128)(2,1)S(1)}, u32[]{:S(2)}, u32[]{:S(2)}) %collective-permute-start.17) | collective-permute-done | bytes 131104 | tf_op jit(solution)/shard_map/ppermute | solution.py:41
  58.3 0.9 %collective-permute-done.20.refs_1_ = bf16[128,512]{1,0:T(8,128)(2,1)S(1)} collective-permute-done((bf16[128,512]{1,0:T(8,128)(2,1)S(1)}, bf16[128,512]{1,0:T(8,128)(2,1)S(1)}, u32[]{:S(2)}, u32[]{:S(2)}) %collective-permute-start.20) | collective-permute-done | bytes 131104 | tf_op jit(solution)/shard_map/ppermute | solution.py:41
  59.2 0.9 %finish.1 = (bf16[128,4096]{1,0:T(8,128)(2,1)}, f32[128,512]{1,0:T(8,128)}) custom-call(bf16[128,1024]{1,0:T(8,128)(2,1)S(1)} %collective-permute-done.15.refs_0_, f32[128,512]{1,0:T(8,128)S(1)} %final_sum.1.refs_1_, bf16[128,4096]{1,0:T(8,128)(2,1)} %unpack.1.refs_2_), custom_call_target="tpu_custom_call", output_to_operand_aliasing={{0}: (2, {})} | custom-call | tf_op jit(solution)/shard_map/finish/pallas_call | solution.py:128
  (28 shorter events, 3.3 us)
Async XLA Ops:
  3.0 16.7 %collective-permute-start = (bf16[128,1024]{1,0:T(8,128)(2,1)}, bf16[128,1024]{1,0:T(8,128)(2,1)S(1)}, u32[]{:S(2)}, u32[]{:S(2)}) collective-permute-start(bf16[128,1024]{1,0:T(8,128)(2,1)} %get-tuple-element.48), channel_id=1, source_target_pairs={{0,17},{1,16},{16,1},{17,0},{2,19},{3,18},{18,3},{19,2},{4,21},{5,... | collective-permute-start | bytes 786440 | tf_op jit(solution)/shard_map/ppermute | solution.py:56
  7.0 12.7 %collective-permute-start.1 = (bf16[256,512]{1,0:T(8,128)(2,1)S(1)}, bf16[256,512]{1,0:T(8,128)(2,1)S(1)}, u32[]{:S(2)}, u32[]{:S(2)}) collective-permute-start(bf16[256,512]{1,0:T(8,128)(2,1)S(1)} %get-tuple-element.49.refs_0_), channel_id=1, source_target_pairs={{0,2},{2,0},{4,6},{6,4},{8,14},{10,12},{12,10},{14,8},{1,3},{3,1},... | collective-permute-start | bytes 786440 | tf_op jit(solution)/shard_map/ppermute | solution.py:161
  8.5 11.2 %collective-permute-start.2 = (bf16[128,512]{1,0:T(8,128)(2,1)S(1)}, bf16[128,512]{1,0:T(8,128)(2,1)S(1)}, u32[]{:S(2)}, u32[]{:S(2)}) collective-permute-start(bf16[128,512]{1,0:T(8,128)(2,1)S(1)} %get-tuple-element.50), channel_id=1, source_target_pairs={{0,4},{2,6},{4,0},{6,2},{1,5},{3,7},{5,1},{7,3},{8,12},{10,14},{12... | collective-permute-start | bytes 393224 | tf_op jit(solution)/shard_map/ppermute | solution.py:41
  11.1 10.2 %collective-permute-start.3 = (bf16[128,1024]{1,0:T(8,128)(2,1)}, bf16[128,1024]{1,0:T(8,128)(2,1)S(1)}, u32[]{:S(2)}, u32[]{:S(2)}) collective-permute-start(bf16[128,1024]{1,0:T(8,128)(2,1)} %get-tuple-element.52), channel_id=1, source_target_pairs={{0,16},{1,17},{16,0},{17,1},{2,18},{3,19},{18,2},{19,3},{4,20},{5,... | collective-permute-start | bytes 786440 | tf_op jit(solution)/shard_map/ppermute | solution.py:56
  11.7 9.7 %collective-permute-start.4 = (bf16[128,1024]{1,0:T(8,128)(2,1)S(1)}, bf16[128,1024]{1,0:T(8,128)(2,1)S(1)}, u32[]{:S(2)}, u32[]{:S(2)}) collective-permute-start(bf16[128,1024]{1,0:T(8,128)(2,1)S(1)} %get-tuple-element.53), channel_id=1, source_target_pairs={{0,1},{1,0},{16,17},{17,16},{2,3},{3,2},{18,19},{19,18},{4,5},{5,4... | collective-permute-start | bytes 786440 | tf_op jit(solution)/shard_map/ppermute | solution.py:56
  19.7 2.6 %collective-permute-start.5 = (bf16[192,512]{1,0:T(8,128)(2,1)S(1)}, bf16[192,512]{1,0:T(8,128)(2,1)S(1)}, u32[]{:S(2)}, u32[]{:S(2)}) collective-permute-start(bf16[192,512]{1,0:T(8,128)(2,1)S(1)} %get-tuple-element.57), channel_id=1, source_target_pairs={{0,8},{8,0},{1,9},{9,1},{2,10},{10,2},{3,11},{11,3},{4,12},{12,4},... | collective-permute-start | bytes 589832 | tf_op jit(solution)/shard_map/ppermute | solution.py:45
  21.3 1.4 %collective-permute-start.6 = (bf16[192,512]{1,0:T(8,128)(2,1)S(1)}, bf16[192,512]{1,0:T(8,128)(2,1)S(1)}, u32[]{:S(2)}, u32[]{:S(2)}) collective-permute-start(bf16[192,512]{1,0:T(8,128)(2,1)S(1)} %get-tuple-element.58), channel_id=1, source_target_pairs={{0,8},{8,0},{1,9},{9,1},{2,10},{10,2},{3,11},{11,3},{4,12},{12,4},... | collective-permute-start | bytes 589832 | tf_op jit(solution)/shard_map/ppermute | solution.py:45
  23.4 7.3 %collective-permute-start.7 = (bf16[128,512]{1,0:T(8,128)(2,1)S(1)}, bf16[128,512]{1,0:T(8,128)(2,1)S(1)}, u32[]{:S(2)}, u32[]{:S(2)}) collective-permute-start(bf16[128,512]{1,0:T(8,128)(2,1)S(1)} %get-tuple-element.65), channel_id=1, source_target_pairs={{0,17},{1,16},{16,1},{17,0},{2,19},{3,18},{18,3},{19,2},{4,21},{5,... | collective-permute-start | bytes 393224 | tf_op jit(solution)/shard_map/ppermute | solution.py:56
  23.9 8.2 %collective-permute-start.8 = (bf16[128,512]{1,0:T(8,128)(2,1)S(1)}, bf16[128,512]{1,0:T(8,128)(2,1)S(1)}, u32[]{:S(2)}, u32[]{:S(2)}) collective-permute-start(bf16[128,512]{1,0:T(8,128)(2,1)S(1)} %get-tuple-element.66), channel_id=1, source_target_pairs={{0,1},{1,0},{16,17},{17,16},{2,3},{3,2},{18,19},{19,18},{4,5},{5,4... | collective-permute-start | bytes 393224 | tf_op jit(solution)/shard_map/ppermute | solution.py:56
  25.4 6.7 %copy-start = (bf16[128,512]{1,0:T(8,128)(2,1)S(1)}, bf16[128,512]{1,0:T(8,128)(2,1)}, u32[]{:S(2)}) copy-start(bf16[128,512]{1,0:T(8,128)(2,1)} %refs_4_.1) | copy-start | bytes 393220
  25.4 6.7 %collective-permute-start.9 = (bf16[128,512]{1,0:T(8,128)(2,1)S(1)}, bf16[128,512]{1,0:T(8,128)(2,1)S(1)}, u32[]{:S(2)}, u32[]{:S(2)}) collective-permute-start(bf16[128,512]{1,0:T(8,128)(2,1)S(1)} %get-tuple-element.67), channel_id=1, source_target_pairs={{0,16},{1,17},{16,0},{17,1},{2,18},{3,19},{18,2},{19,3},{4,20},{5,... | collective-permute-start | bytes 393224 | tf_op jit(solution)/shard_map/ppermute | solution.py:56
  32.4 7.3 %collective-permute-start.10 = (bf16[128,512]{1,0:T(8,128)(2,1)S(1)}, bf16[128,512]{1,0:T(8,128)(2,1)S(1)}, u32[]{:S(2)}, u32[]{:S(2)}) collective-permute-start(bf16[128,512]{1,0:T(8,128)(2,1)S(1)} %get-tuple-element.68.refs_0_.refs_4_), channel_id=1, source_target_pairs={{0,17},{1,16},{16,1},{17,0},{2,19},{3,18},{18,3},{19,2},{4,21},{5,... | collective-permute-start | bytes 393224 | tf_op jit(solution)/shard_map/ppermute | solution.py:56
  33.7 7.6 %collective-permute-start.12 = (bf16[128,512]{1,0:T(8,128)(2,1)S(1)}, bf16[128,512]{1,0:T(8,128)(2,1)S(1)}, u32[]{:S(2)}, u32[]{:S(2)}) collective-permute-start(bf16[128,512]{1,0:T(8,128)(2,1)S(1)} %get-tuple-element.68.refs_0_.refs_4_), channel_id=1, source_target_pairs={{0,16},{1,17},{16,0},{17,1},{2,18},{3,19},{18,2},{19,3},{4,20},{5,... | collective-permute-start | bytes 393224 | tf_op jit(solution)/shard_map/ppermute | solution.py:56
  35.2 6.1 %collective-permute-start.11 = (bf16[128,512]{1,0:T(8,128)(2,1)S(1)}, bf16[128,512]{1,0:T(8,128)(2,1)S(1)}, u32[]{:S(2)}, u32[]{:S(2)}) collective-permute-start(bf16[128,512]{1,0:T(8,128)(2,1)S(1)} %get-tuple-element.68.refs_0_.refs_4_), channel_id=1, source_target_pairs={{0,1},{1,0},{16,17},{17,16},{2,3},{3,2},{18,19},{19,18},{4,5},{5,4... | collective-permute-start | bytes 393224 | tf_op jit(solution)/shard_map/ppermute | solution.py:56
  42.1 3.2 %collective-permute-start.13 = (bf16[256,512]{1,0:T(8,128)(2,1)S(1)}, bf16[256,512]{1,0:T(8,128)(2,1)S(1)}, u32[]{:S(2)}, u32[]{:S(2)}) collective-permute-start(bf16[256,512]{1,0:T(8,128)(2,1)S(1)} %get-tuple-element.75), channel_id=1, source_target_pairs={{0,8},{8,0},{1,9},{9,1},{2,10},{10,2},{3,11},{11,3},{4,12},{12,4},... | collective-permute-start | bytes 786440 | tf_op jit(solution)/shard_map/ppermute | solution.py:45
  42.2 3.1 %collective-permute-start.14 = (bf16[256,512]{1,0:T(8,128)(2,1)S(1)}, bf16[256,512]{1,0:T(8,128)(2,1)S(1)}, u32[]{:S(2)}, u32[]{:S(2)}) collective-permute-start(bf16[256,512]{1,0:T(8,128)(2,1)S(1)} %get-tuple-element.76), channel_id=1, source_target_pairs={{0,8},{8,0},{1,9},{9,1},{2,10},{10,2},{3,11},{11,3},{4,12},{12,4},... | collective-permute-start | bytes 786440 | tf_op jit(solution)/shard_map/ppermute | solution.py:45
  43.1 9.0 %collective-permute-start.18 = (bf16[128,1024]{1,0:T(8,128)(2,1)S(1)}, bf16[128,1024]{1,0:T(8,128)(2,1)S(1)}, u32[]{:S(2)}, u32[]{:S(2)}) collective-permute-start(bf16[128,1024]{1,0:T(8,128)(2,1)S(1)} %get-tuple-element.83), channel_id=1, source_target_pairs={{0,16},{1,17},{8,9},{9,8},{16,0},{17,1},{24,25},{25,24},{2,18},{3,... | collective-permute-start | bytes 786440 | tf_op jit(solution)/shard_map/ppermute | solution.py:68
  44.7 7.4 %collective-permute-start.19 = (bf16[128,1024]{1,0:T(8,128)(2,1)S(1)}, bf16[128,1024]{1,0:T(8,128)(2,1)S(1)}, u32[]{:S(2)}, u32[]{:S(2)}) collective-permute-start(bf16[128,1024]{1,0:T(8,128)(2,1)S(1)} %get-tuple-element.85), channel_id=1, source_target_pairs={{0,1},{1,0},{8,24},{9,25},{16,17},{17,16},{24,8},{25,9},{2,3},{3,2... | collective-permute-start | bytes 786440 | tf_op jit(solution)/shard_map/ppermute | solution.py:68
  45.4 8.4 %collective-permute-start.16 = (bf16[128,512]{1,0:T(8,128)(2,1)S(1)}, bf16[128,512]{1,0:T(8,128)(2,1)S(1)}, u32[]{:S(2)}, u32[]{:S(2)}) collective-permute-start(bf16[128,512]{1,0:T(8,128)(2,1)S(1)} %get-tuple-element.78), channel_id=1, source_target_pairs={{0,6},{2,4},{4,2},{6,0},{1,7},{3,5},{5,3},{7,1},{8,14},{10,12},{12... | collective-permute-start | bytes 393224 | tf_op jit(solution)/shard_map/ppermute | solution.py:41
  47.9 10.3 %collective-permute-start.17 = (bf16[128,512]{1,0:T(8,128)(2,1)S(1)}, bf16[128,512]{1,0:T(8,128)(2,1)S(1)}, u32[]{:S(2)}, u32[]{:S(2)}) collective-permute-start(bf16[128,512]{1,0:T(8,128)(2,1)S(1)} %get-tuple-element.79), channel_id=1, source_target_pairs={{0,4},{2,6},{4,0},{6,2},{1,5},{3,7},{5,1},{7,3},{8,12},{10,14},{12... | collective-permute-start | bytes 393224 | tf_op jit(solution)/shard_map/ppermute | solution.py:41
  47.9 11.3 %collective-permute-start.15 = (bf16[128,1024]{1,0:T(8,128)(2,1)S(1)}, bf16[128,1024]{1,0:T(8,128)(2,1)S(1)}, u32[]{:S(2)}, u32[]{:S(2)}) collective-permute-start(bf16[128,1024]{1,0:T(8,128)(2,1)S(1)} %columns.4), channel_id=1, source_target_pairs={{0,17},{1,16},{16,1},{17,0},{2,19},{3,18},{18,3},{19,2},{4,21},{5,... | collective-permute-start | bytes 786440 | tf_op jit(solution)/shard_map/ppermute | solution.py:56
  52.1 7.1 %collective-permute-start.20 = (bf16[128,512]{1,0:T(8,128)(2,1)S(1)}, bf16[128,512]{1,0:T(8,128)(2,1)S(1)}, u32[]{:S(2)}, u32[]{:S(2)}) collective-permute-start(bf16[128,512]{1,0:T(8,128)(2,1)S(1)} %get-tuple-element.89), channel_id=1, source_target_pairs={{0,2},{2,0},{4,6},{6,4},{1,3},{3,1},{5,7},{7,5},{8,10},{10,8},{12,... | collective-permute-start | bytes 393224 | tf_op jit(solution)/shard_map/ppermute | solution.py:41
